TPU v7x, 32 devices: a whole 2x2x4 slice. The times are simulated.
32 devices in a mesh: prow: 4 (over y, core), pcol: 8 (over z, x).
Axes of the slice: x: 2, y: 2, z: 4, core: 2. Of those that a mesh axis runs over, the one named last changes fastest.
Arguments:
- sigma_top: float32 [3584, 3584], P('pcol', 'prow')
- structure: int32 [1792], replicated, may hold values from 0 to 3583, as said below
- u_panel: float32 [1792, 1024], P('pcol', 'prow'), may hold values from -0.3 to 0.3
- d_term: float32 [1024, 1024], P('pcol', 'prow'), may hold values from -6 to 6
Outputs:
- sigma_sj: float32 [1792, 1024], P('pcol', 'prow')
- sigma_jj: float32 [1024, 1024], P('pcol', 'prow')
Inputs may be any that keep to these rules, and one draw needn't show every extreme that they name: sigma_top is symmetric; structure is strictly increasing; its first entry is 0 and its last is 3583; each aligned block of 896 ancestor rows holds at most 560 structure rows, and the first block holds exactly 560.
All inputs are finite; a program needn't handle non-finite values.
Results may differ from a plain program's by a relative error of at most 0.000075.
Values sent between devices are 32-bit elements; how exact they have to be, the bound alone decides.
No kernel may reach another device: no remote copies, remote signals or barrier semaphores. Data moves between devices by JAX's collectives and lax.ppermute only.
A program may use at most 64 MiB of HBM per device.

v0:
```python
import jax
import jax.numpy as jnp
from jax import lax
from jax.sharding import PartitionSpec as P


def per_device(sigma_top, structure, u_panel, d_term):
    col_count = lax.axis_size("pcol")
    col_index = lax.axis_index("pcol")
    rows_blk, cols_blk = u_panel.shape
    order = sigma_top.shape[0] * col_count
    mapped = structure.reshape(rows_blk, col_count).T.reshape(-1)
    mine = lax.dynamic_slice_in_dim(mapped, col_index * rows_blk, rows_blk)
    u_full = lax.all_gather(u_panel, "prow", axis=1, tiled=True)
    placed_cols = (
        jnp.zeros((order, cols_blk), jnp.float32)
        .at[mapped]
        .add(lax.all_gather(u_panel, "pcol", axis=0, tiled=True))
    )
    placed_mine = lax.all_to_all(placed_cols, "prow", split_axis=0, concat_axis=1, tiled=True)
    image_t = lax.psum_scatter(
        lax.dot_general(
            placed_mine,
            sigma_top,
            (((0,), (1,)), ((), ())),
            precision=lax.Precision.HIGHEST,
            preferred_element_type=jnp.float32,
        ),
        "prow",
        scatter_dimension=0,
        tiled=True,
    )
    piece = lax.all_gather(image_t, "pcol", axis=1, tiled=True)
    count = piece.shape[1]
    valid_cols = (mine >= 0) & (mine < count)
    taken = jnp.take(piece, jnp.clip(mine, 0, count - 1), axis=1)
    picked = jnp.where(valid_cols[None, :], taken, 0.0)
    sigma_sj = -picked.T
    correction = lax.psum_scatter(
        lax.dot_general(
            u_full,
            sigma_sj,
            (((0,), (0,)), ((), ())),
            precision=lax.Precision.HIGHEST,
            preferred_element_type=jnp.float32,
        ),
        "pcol",
        scatter_dimension=0,
        tiled=True,
    )
    return (sigma_sj, d_term - correction)


def solution(mesh):
    placed = (P("pcol", "prow"), P(), P("pcol", "prow"), P("pcol", "prow"))
    return jax.shard_map(
        per_device,
        mesh=mesh,
        in_specs=placed,
        out_specs=(P("pcol", "prow"), P("pcol", "prow")),
        check_vma=False,
    )
```

profile of v0, /device:TPU:0, one launch (start us, length us, event | category | flops | bytes accessed | tf_op | source)
XLA Modules:
  0.0 303.4 jit_solution(7497628943258947958)
XLA Ops:
  7.2 0.7 all-gather.3.cloned.1.call-update
  7.9 0.0 reduce-scatter.3.cloned.1.call-start
  8.0 0.8 reshape.49
  8.8 0.1 copy.8
  8.8 0.1 reshape.51
  9.0 50.2 %all-gather.3.cloned.1.call-done = f32[1792,256]{1,0:T(8,128)} async-done(((f32[224,256]{1,0:T(8,128)}), f32[1792,256]{1,0:T(8,128)}) %all-gather.3.cloned.1.call-update) | async-done | bytes 1835024 | tf_op jit(solution)/shard_map/all_gather | solution.py:18
  59.2 12.9 %scatter_custom_fusion = f32[3584,256]{1,0:T(8,128)} fusion(s32[1792]{0:T(1024)S(1)} %fusion.2, f32[1792,256]{1,0:T(8,128)} %all-gather.3.cloned.1.call-done, f32[]{:T(128)} %constant.14.clone.1), kind=kCustom, calls=%fused_computation.2 | custom fusion | flops 458752 | bytes 3670528 | tf_op jit(solution)/shard_map/scatter-add | solution.py:18
  72.1 4.6 %copy.10 = f32[4,896,256]{1,2,0:T(8,128)} copy(f32[4,896,256]{2,1,0:T(8,128)} %bitcast.12) | data formatting | bytes 7340032 | tf_op jit(solution)/shard_map/all_to_all | solution.py:20
  76.7 46.3 %all_to_all.19 = f32[4,896,256]{1,2,0:T(8,128)S(1)} all-to-all(f32[4,896,256]{1,2,0:T(8,128)} %copy.10), channel_id=1, replica_groups=mesh['prow'=4,'pcol'=8] {'prow'}, dimensions={0} | all-to-all | bytes 7340032 | tf_op jit(solution)/shard_map/all_to_all | solution.py:20
  123.0 7.2 %fusion.3 = f32[1024,448]{0,1:T(8,128)} fusion(f32[896,1024]{0,1:T(8,128)S(1)} %bitcast.11, f32[448,896]{1,0:T(8,128)S(1)} %copy-done), kind=kOutput, calls=%fused_computation.12 | convolution fusion | flops 4932501504 | bytes 7110656 | tf_op jit(solution)/shard_map/dot_general | solution.py:22
  130.2 0.0 all-gather.5.cloned.1.call-start
  130.3 28.0 %reduce-scatter.3.cloned.1.call-done = f32[256,448]{0,1:T(8,128)} async-done(((f32[1024,448]{0,1:T(8,128)}), f32[256,448]{0,1:T(8,128)}) %reduce-scatter.3.cloned.1.call-update) | async-done | bytes 458768 | tf_op jit(solution)/shard_map/reduce_scatter | solution.py:21
  158.4 0.0 reduce-scatter.5.cloned.1.call-start
  158.4 0.1 reshape.50
  158.5 0.1 compare_and_fusion
  158.6 8.9 %all_gather.11 = f32[224,1024]{1,0:T(8,128)S(1)} all-gather(f32[224,256]{1,0:T(8,128)S(1)} %copy-done.2), channel_id=1, replica_groups=mesh['prow'=4,'pcol'=8] {'prow'}, dimensions={1}, use_global_device_ids=true | all-gather | bytes 1146880 | tf_op jit(solution)/shard_map/all_gather | solution.py:14
  167.5 60.1 %all-gather.5.cloned.1.call-done = f32[256,3584]{0,1:T(8,128)} async-done(((f32[256,448]{0,1:T(8,128)}), f32[256,3584]{0,1:T(8,128)}) %all-gather.5.cloned.1.call-update) | async-done | bytes 3670032 | tf_op jit(solution)/shard_map/all_gather | solution.py:33
  227.6 2.9 gather_fusion
  230.5 0.1 select_negate_fusion
  230.7 2.0 convolution_bitcast_fusion
  232.8 0.1 copy.11
  232.8 62.4 %reduce-scatter.5.cloned.1.call-done = f32[128,256]{0,1:T(8,128)} async-done(((f32[1024,256]{0,1:T(8,128)}), f32[128,256]{0,1:T(8,128)}) %reduce-scatter.5.cloned.1.call-update) | async-done | bytes 131088 | tf_op jit(solution)/shard_map/reduce_scatter | solution.py:39
  295.2 0.9 sub.3
  296.1 0.8 copy.12
  (14 shorter events, 0.1 us)
Async XLA Ops:
  7.2 115.8 %copy-start = (f32[448,896]{1,0:T(8,128)S(1)}, f32[448,896]{1,0:T(8,128)}, u32[]{:S(2)}) copy-start(f32[448,896]{1,0:T(8,128)} %param.4) | copy-start | bytes 4816900
  7.2 52.0 %all-gather.3.cloned.1.call-start = ((), (), s32[]{:S(2)}) async-start(), calls=%async_computation.3 | async-start | bytes 2064384 | tf_op jit(solution)/shard_map/all_gather | solution.py:18
  7.9 150.4 %reduce-scatter.3.cloned.1.call-start = ((), (), s32[]{:S(2)}) async-start(), calls=%async_computation.4 | async-start | bytes 2293760 | tf_op jit(solution)/shard_map/reduce_scatter | solution.py:21
  123.0 35.6 %copy-start.2 = (f32[224,256]{1,0:T(8,128)S(1)}, f32[224,256]{1,0:T(8,128)}, u32[]{:S(2)}) copy-start(f32[224,256]{1,0:T(8,128)} %param.6) | copy-start | bytes 688132
  130.2 97.3 %all-gather.5.cloned.1.call-start = ((), (), s32[]{:S(2)}) async-start(), calls=%async_computation.5 | async-start | bytes 4128768 | tf_op jit(solution)/shard_map/all_gather | solution.py:33
  158.4 74.4 %copy-start.3 = (f32[128,256]{1,0:T(8,128)S(1)}, f32[128,256]{1,0:T(8,128)}, u32[]{:S(2)}) copy-start(f32[128,256]{1,0:T(8,128)} %param.7) | copy-start | bytes 393220
  158.4 136.9 %reduce-scatter.5.cloned.1.call-start = ((), (), s32[]{:S(2)}) async-start(), calls=%async_computation.6 | async-start | bytes 1179648 | tf_op jit(solution)/shard_map/reduce_scatter | solution.py:39
  230.7 66.2 %copy-start.1 = (f32[224,256]{1,0:T(8,128)}, f32[224,256]{1,0:T(8,128)S(1)}, u32[]{:S(2)}) copy-start(f32[224,256]{1,0:T(8,128)S(1)} %select_negate_fusion) | copy-start | bytes 688132
Sparse Core Ops, SparseCore 0:
  10.2 48.9 all-gather.2
  130.4 27.9 reduce-scatter.2
  160.8 66.7 all-gather.4
  232.9 62.3 reduce-scatter.4
where the time goes:
time: 304 us; the launch traced here: 303 us
  waiting for transfers between devices  201 us (66%)
  blocking collectives  55.2 us (18%)
  other arithmetic  14.1 us (5%)
  between operations  13.9 us (5%)
  local copies, waits for them, and re-layouts  9.46 us (3%)
  matrix products  9.24 us (3%)
    reduce_scatter x1, waiting for transfers between devices, per_device(): lax.psum_scatter(lax.dot_general(u_full, sigma_sj, (((0,), (0,)), ((), ()...  62.4 us
    all_gather x1, waiting for transfers between devices, per_device(): piece = lax.all_gather(image_t, 'pcol', axis=1, tiled=True)  60.1 us
    all_gather x1, waiting for transfers between devices, per_device(): lax.all_gather(u_panel, 'pcol', axis=0, tiled=True)  50.2 us
    all_to_all x1, blocking collectives, per_device(): lax.all_to_all(placed_cols, 'prow', split_axis=0, concat_axis=1, tiled=True)  46.3 us
    reduce_scatter x1, waiting for transfers between devices, per_device(): lax.psum_scatter(lax.dot_general(placed_mine, sigma_top, (((0,), (1,)), (...  28 us
    scatter-add x1, other arithmetic, per_device(): placed_cols = jnp.zeros((order, cols_blk), jnp.float32).at[mapped].add(la...  12.9 us
    all_gather x1, blocking collectives, per_device(): u_full = lax.all_gather(u_panel, 'prow', axis=1, tiled=True)  8.92 us
    dot_general x1, matrix products, per_device(): lax.dot_general(placed_mine, sigma_top, (((0,), (1,)), ((), ())), precisi...  7.22 us
  transfers between devices with their start and end apart: 4, of which 4 were waited for; matrix products, arithmetic and copies ran while one was open for 0% of the time, Pallas kernels for 0%

commit v1 on v0

v1 whole, which is shorter than its diff:
```python
import functools

import jax
import jax.numpy as jnp
from jax import lax
from jax.experimental import pallas as pl
from jax.experimental.pallas import tpu as pltpu
from jax.sharding import PartitionSpec as P

LANES = 128
BLOCK_CAP = 560
VMEM = pl.BlockSpec(memory_space=pltpu.VMEM)
SMEM = pl.BlockSpec(memory_space=pltpu.SMEM)
PARAMS = pltpu.CompilerParams(vmem_limit_bytes=48 * 2**20)


def split(v):
    high = v.astype(jnp.bfloat16)
    return high, (v - high.astype(jnp.float32)).astype(jnp.bfloat16)


def split3(v):
    high = v.astype(jnp.bfloat16)
    rest = v - high.astype(jnp.float32)
    mid = rest.astype(jnp.bfloat16)
    return high, mid, (rest - mid.astype(jnp.float32)).astype(jnp.bfloat16)


def dot(a, b, dims=((1,), (0,))):
    return lax.dot_general(a, b, (dims, ((), ())), preferred_element_type=jnp.float32)


def dot3(a, b, dims=((1,), (0,))):
    ah, al = a
    bh, bl = b
    return dot(ah, bh, dims) + (dot(ah, bl, dims) + dot(al, bh, dims))


def one_hot(mask):
    return jnp.where(mask, 1.0, 0.0).astype(jnp.bfloat16)


def select_kernel(cols_ref, sigma_ref, out_ref):
    rows, width = sigma_ref.shape
    cap = cols_ref.shape[1]
    place = one_hot(lax.broadcasted_iota(jnp.int32, (width, cap), 0) == cols_ref[...])
    high, low = split(sigma_ref[...])
    picked = dot(high, place) + dot(low, place)
    full = cap // LANES
    for i in range(full):
        out_ref[rows * i : rows * (i + 1), :] = picked[:, LANES * i : LANES * (i + 1)]
    tail = picked[:, LANES * full :]
    out_ref[rows * full :, :] = jnp.concatenate([tail[: rows // 2], tail[rows // 2 :]], axis=1)


def image_term(block_ref, u_rows, rows):
    cap, w = u_rows.shape
    full = cap // LANES
    half = rows // 2
    body = jnp.concatenate([block_ref[rows * i : rows * (i + 1), :] for i in range(full)], axis=1)
    term = dot3(split(body), split(u_rows[: LANES * full]))
    tail = split(block_ref[rows * full :, :])
    last = u_rows[LANES * full :]
    zero = jnp.zeros_like(last)
    top = dot3(tail, split(jnp.concatenate([last, zero], axis=0)))
    bottom = dot3(tail, split(jnp.concatenate([zero, last], axis=0)))
    return term + jnp.concatenate([top, bottom], axis=0)


def rows_from(us_ref, start, count, w):
    base = pl.multiple_of((start // 8) * 8, 8)
    size = count + 8
    lanes = [
        pltpu.roll(us_ref[k, pl.ds(base, size), :], size - (start - base), 0)[:count]
        for k in range(us_ref.shape[0])
    ]
    return jnp.concatenate(lanes, axis=1)[:, :w]


def first_kernel(n_blocks, rows, info_ref, *refs):
    nc = len(refs) - n_blocks - 2
    u_refs, block_refs = refs[:nc], refs[nc : nc + n_blocks]
    us_ref, image_ref = refs[-2:]
    m, w = u_refs[0].shape
    n = m * nc
    for k, u_ref in enumerate(u_refs):
        u = u_ref[...]
        if w % LANES:
            u = jnp.concatenate([u, jnp.zeros((m, LANES - w % LANES), jnp.float32)], axis=1)
        for i in range(us_ref.shape[0]):
            us_ref[i, pl.ds(info_ref[n_blocks + k], m, stride=nc), :] = u[:, LANES * i : LANES * (i + 1)]
    us_ref[:, n:, :] = jnp.zeros((us_ref.shape[0], us_ref.shape[1] - n, LANES), jnp.float32)
    cap = us_ref.shape[1] - n - 8
    image = None
    for b, block_ref in enumerate(block_refs):
        term = image_term(block_ref, rows_from(us_ref, info_ref[b], cap, w), rows)
        image = term if image is None else image + term
    image_ref[...] = image


def rest_kernel(n, info_ref, slot_ref, us_ref, part_ref, *refs):
    block_refs, out_ref = refs[:-1], refs[-1]
    rows, w = part_ref.shape
    cap = us_ref.shape[1] - n - 8
    image = part_ref[...]
    def add(b, block_ref, image):
        return image + image_term(block_ref, rows_from(us_ref, info_ref[b], cap, w), rows)

    if len(block_refs[0].shape) == 3:
        stack = block_refs[0]
        image = lax.fori_loop(0, stack.shape[0], lambda b, v: add(b, stack.at[b], v), image)
    else:
        for b, block_ref in enumerate(block_refs):
            image = add(b, block_ref, image)
    place = one_hot(lax.broadcasted_iota(jnp.int32, (out_ref.shape[0], rows), 0) == slot_ref[...])
    high, mid, low = split3(image)
    out_ref[...] = dot(place, high) + (dot(place, mid) + dot(place, low))


def pick_kernel(from_ref, got_ref, out_ref):
    m, k = out_ref.shape[0], got_ref.shape[0]
    place = one_hot(lax.broadcasted_iota(jnp.int32, (m, k), 1) == from_ref[...])
    high, mid, low = split3(got_ref[...])
    out_ref[...] = -(dot(place, high) + (dot(place, mid) + dot(place, low)))


def correction_kernel(info_ref, mine_ref, other_ref, *refs):
    u_refs, out_ref = refs[:-1], refs[-1]
    m = mine_ref.shape[0]
    mine, other = split(mine_ref[...]), split(other_ref[...])
    for b, u_ref in enumerate(u_refs):
        dims = ((0,), (0,))
        term = dot3(split(u_ref[:m, :]), mine, dims) + dot3(split(u_ref[m:, :]), other, dims)
        out_ref[info_ref[b]] = term


def call(kernel, out_shape, specs, *args):
    many = isinstance(out_shape, (list, tuple))
    return pl.pallas_call(
        kernel,
        out_shape=out_shape,
        in_specs=list(specs),
        out_specs=[VMEM] * len(out_shape) if many else VMEM,
        compiler_params=PARAMS,
    )(*args)


def f32(*shape):
    return jax.ShapeDtypeStruct(shape, jnp.float32)


def shift(v, axis, size, by):
    return lax.ppermute(v, axis, [(k, (k + by) % size) for k in range(size)])


def swap(v, axis, size):
    return lax.ppermute(v, axis, [(k, k ^ 1) for k in range(size)])


def spread(v, axis, size):
    blocks = [v] + [shift(v, axis, size, 2 * t) for t in range(1, size // 2)]
    out = []
    for t, block in enumerate(blocks):
        out += [(t, 0, block), (t, 1, swap(block, axis, size))]
    return out


def per_device(sigma_top, structure, u_panel, d_term):
    nc, nr = lax.axis_size("pcol"), lax.axis_size("prow")
    c, r = lax.axis_index("pcol"), lax.axis_index("prow")
    nz = nc // 2
    rows, cols = sigma_top.shape
    m, w = u_panel.shape
    n = structure.shape[0]
    cap = -(-BLOCK_CAP // 64) * 64
    slots = -(-rows // nc)
    iota = lambda size: jnp.arange(size, dtype=jnp.int32)

    from_z = [u_panel] + [shift(u_panel, "pcol", nc, 2 * t) for t in range(1, nz)]
    from_x = [swap(b, "pcol", nc) for b in from_z]
    u_blocks, u_index = [], []
    for t in range(nz):
        owner = jnp.mod(c - 2 * t, nc)
        u_blocks += [from_z[t], from_x[t]]
        u_index += [owner, jnp.bitwise_xor(owner, 1)]

    padded = jnp.concatenate([structure, jnp.full((cap,), 2**30, jnp.int32)])
    starts = jnp.sum(structure[None, :] < (iota(nr) * cols)[:, None], axis=1, dtype=jnp.int32)
    named = lax.dynamic_slice_in_dim(padded, jnp.sum(structure < r * cols, dtype=jnp.int32), cap) - r * cols
    full = cap // LANES
    packed = f32(rows * full + rows // 2, LANES)
    chosen = call(select_kernel, packed, [VMEM] * 2, named[None, :], sigma_top)
    blocks, begin = [], []
    for t, flip, block in spread(chosen, "prow", nr):
        owner = jnp.bitwise_xor(jnp.mod(r - 2 * t, nr), flip)
        blocks.append(block)
        begin.append(starts[owner])

    us, part = call(
        functools.partial(first_kernel, 2, rows),
        [f32(-(-w // LANES), n + cap + 8, LANES), f32(rows, w)],
        [SMEM] + [VMEM] * (nc + 2),
        jnp.stack(begin[:2] + u_index),
        *u_blocks,
        *blocks[:2],
    )

    order = iota(n)
    low = jnp.sum(structure < c * rows, dtype=jnp.int32)
    turn = jnp.mod(order, nc)
    ahead = (low - turn + nc - 1) // nc
    slot = turn * slots + order // nc - ahead
    match = structure[:, None] == (c * rows + iota(rows))[None, :]
    slot_of_row = jnp.max(jnp.where(match, slot[:, None], -1), axis=0)
    later = blocks[2:] if nr <= 4 else [jnp.stack(blocks[2:])]
    sent = call(
        functools.partial(rest_kernel, n),
        f32(nc * slots, w),
        [SMEM] + [VMEM] * (3 + len(later)),
        jnp.stack(begin[2:]),
        slot_of_row[None, :],
        us,
        part,
        *later,
    )
    got = lax.all_to_all(sent, "pcol", split_axis=0, concat_axis=0, tiled=True)

    mine = jnp.sum(jnp.where(iota(nc)[None, :] == c, structure.reshape(m, nc), 0), axis=1)
    source = mine // rows
    before = jnp.sum(source[None, :] < source[:, None], axis=1, dtype=jnp.int32)
    place = source * slots + iota(m) - before
    sigma_sj = call(pick_kernel, f32(m, w), [VMEM] * 2, place[:, None], got)

    wd = w // 2
    pair = jnp.concatenate([u_panel, from_x[0]], axis=0)
    pair = jnp.where(jnp.bitwise_and(c, 1) == 0, pair[:, :wd], pair[:, wd:])
    u_parts, u_where = [], []
    for t, flip, block in spread(pair, "prow", nr):
        u_parts.append(block)
        u_where.append(jnp.bitwise_xor(jnp.mod(r - 2 * t, nr), flip))
    other = swap(sigma_sj, "pcol", nc)
    parts = call(
        correction_kernel,
        f32(nr, wd, w),
        [SMEM] + [VMEM] * (2 + nr),
        jnp.stack(u_where),
        sigma_sj,
        other,
        *u_parts,
    )
    groups = [[2 * k + x for k in range(nz)] for x in range(2)]
    terms = lax.all_to_all(parts, "pcol", split_axis=0, concat_axis=0, axis_index_groups=groups, tiled=True)
    return sigma_sj, d_term - jnp.sum(terms, axis=0)


def solution(mesh):
    placed = (P("pcol", "prow"), P(), P("pcol", "prow"), P("pcol", "prow"))
    return jax.shard_map(
        per_device,
        mesh=mesh,
        in_specs=placed,
        out_specs=(P("pcol", "prow"), P("pcol", "prow")),
        check_vma=False,
    )
```

time: 304 us -> 117 us (0.38)
  waiting for transfers between devices: 201 us -> 41.6 us
  blocking collectives: 55.2 us -> 16.9 us
  starting transfers between devices: 0.16 us -> 23.1 us
  Pallas kernels: 0 us -> 12.6 us
  between operations: 13.9 us -> 2.75 us
  matrix products: 9.24 us -> 0 us
    all_gather x2 -> x0, waiting for transfers between devices: 110 us -> none  [the longest x1 60.1 us: per_device(): piece = lax.all_gather(image_t, 'pcol', axis=1, tiled=True)]
    reduce_scatter x2 -> x0, waiting for transfers between devices: 90.4 us -> none  [the longest x1 62.4 us: per_device(): lax.psum_scatter(lax.dot_general(u_full, sigma_sj, (((0,), (0,)), ((), ()...]
    ppermute x0 -> x14, waiting for transfers between devices: none -> 36.2 us  [the longest x5 22.5 us: shift(): return lax.ppermute(v, axis, [(k, (k + by) % size) for k in range(size)])]
    all_to_all x1, blocking collectives: 46.3 us -> 16.9 us  [per_device(): lax.all_to_all(parts, 'pcol', split_axis=0, concat_axis=0, axis_index_gro...]
    ppermute x0 -> x14, starting transfers between devices: none -> 17.5 us  [the longest x5 10.1 us: shift(): return lax.ppermute(v, axis, [(k, (k + by) % size) for k in range(size)])]
    scatter-add x1 -> x0, other arithmetic: 12.9 us -> none  [per_device(): placed_cols = jnp.zeros((order, cols_blk), jnp.float32).at[mapped].add(la...]
    pallas_call x0 -> x5, Pallas kernels: none -> 12.6 us  [call(): pl.pallas_call(kernel, out_shape=out_shape, in_specs=list(specs), out_spe...]
    dot_general x2 -> x0, matrix products: 9.24 us -> none  [the longest x1 7.22 us: per_device(): lax.dot_general(placed_mine, sigma_top, (((0,), (1,)), ((), ())), precisi...]
  transfers between devices with their start and end apart: 4 -> 15, of which waited for: 4 -> 7; matrix products, arithmetic and copies ran while one was open for 0% -> 10% of each run, Pallas kernels for 0% -> 4%
where the time goes in v1:
time: 117 us
  waiting for transfers between devices  41.6 us (36%)
  starting transfers between devices  23.1 us (20%)
  blocking collectives  16.9 us (14%)
  Pallas kernels  12.6 us (11%)
  other arithmetic  11.5 us (10%)
  local copies, waits for them, and re-layouts  8.33 us (7%)
  between operations  2.75 us (2%)
    ppermute x5, waiting for transfers between devices, shift(): return lax.ppermute(v, axis, [(k, (k + by) % size) for k in range(size)])  22.5 us
    all_to_all x1, blocking collectives, per_device(): lax.all_to_all(parts, 'pcol', split_axis=0, concat_axis=0, axis_index_gro...  16.9 us
    ppermute x9, waiting for transfers between devices, swap(): return lax.ppermute(v, axis, [(k, k ^ 1) for k in range(size)])  13.7 us
    pallas_call x5, Pallas kernels, call(): pl.pallas_call(kernel, out_shape=out_shape, in_specs=list(specs), out_spe...  12.6 us
    ppermute x5, starting transfers between devices, shift(): return lax.ppermute(v, axis, [(k, (k + by) % size) for k in range(size)])  10.1 us
    ppermute x9, starting transfers between devices, swap(): return lax.ppermute(v, axis, [(k, k ^ 1) for k in range(size)])  7.38 us
    all_to_all x1, starting transfers between devices, per_device(): got = lax.all_to_all(sent, 'pcol', split_axis=0, concat_axis=0, tiled=True)  5.57 us
    all_to_all x1, waiting for transfers between devices, per_device(): got = lax.all_to_all(sent, 'pcol', split_axis=0, concat_axis=0, tiled=True)  5.39 us
  transfers between devices with their start and end apart: 15, of which 7 were waited for; matrix products, arithmetic and copies ran while one was open for 10% of the time, Pallas kernels for 4%

profile of v1, /device:TPU:0, one launch (start us, length us, event | category | flops | bytes accessed | tf_op | source)
XLA Modules:
  0.0 116.9 jit_solution(12579057180693169481)
XLA Ops:
  4.8 1.4 %copy-done.1 = f32[448,896]{1,0:T(8,128)S(1)} copy-done((f32[448,896]{1,0:T(8,128)S(1)}, f32[448,896]{1,0:T(8,128)}, u32[]{:S(2)}) %copy-start.1) | copy-done | bytes 1605656
  6.2 1.7 %shard_map.59.refs_8_ = f32[2016,128]{1,0:T(8,128)S(1)} custom-call(s32[1,576]{1,0:T(1,128)S(1)} %broadcast_in_dim.45.cols_ref, f32[448,896]{1,0:T(8,128)S(1)} %copy-done.1), custom_call_target="tpu_custom_call" | custom-call | tf_op jit(solution)/shard_map/pallas_call | solution.py:139
  7.9 3.0 %collective-permute-start.8 = (f32[2016,128]{1,0:T(8,128)S(1)}, f32[2016,128]{1,0:T(8,128)S(1)}, u32[]{:S(2)}, u32[]{:S(2)}) collective-permute-start(f32[2016,128]{1,0:T(8,128)S(1)} %shard_map.59.refs_8_), channel_id=1, source_target_pairs={{0,16},{8,24},{16,0},{24,8},{1,17},{9,25},{17,1},{25,9},{2,18},{10... | collective-permute-start | bytes 3096584 | tf_op jit(solution)/shard_map/ppermute | solution.py:153
  11.0 1.6 %collective-permute-start.1 = (f32[224,256]{1,0:T(8,128)S(1)}, f32[224,256]{1,0:T(8,128)}, u32[]{:S(2)}, u32[]{:S(2)}) collective-permute-start(f32[224,256]{1,0:T(8,128)S(1)} %copy-done.2), channel_id=1, source_target_pairs={{0,2},{1,3},{2,4},{3,5},{4,6},{5,7},{6,0},{7,1},{8,10},{9,11},{10,... | collective-permute-start | bytes 688136 | tf_op jit(solution)/shard_map/ppermute | solution.py:153
  12.5 2.6 %collective-permute-start.3 = (f32[224,256]{1,0:T(8,128)S(1)}, f32[224,256]{1,0:T(8,128)}, u32[]{:S(2)}, u32[]{:S(2)}) collective-permute-start(f32[224,256]{1,0:T(8,128)S(1)} %copy-done.2), channel_id=1, source_target_pairs={{0,4},{1,5},{2,6},{3,7},{4,0},{5,1},{6,2},{7,3},{8,12},{9,13},{10,... | collective-permute-start | bytes 688136 | tf_op jit(solution)/shard_map/ppermute | solution.py:153
  16.5 17.3 %collective-permute-done.8.refs_0_ = f32[2016,128]{1,0:T(8,128)S(1)} collective-permute-done((f32[2016,128]{1,0:T(8,128)S(1)}, f32[2016,128]{1,0:T(8,128)S(1)}, u32[]{:S(2)}, u32[]{:S(2)}) %collective-permute-start.8) | collective-permute-done | bytes 1032224 | tf_op jit(solution)/shard_map/ppermute | solution.py:153
  36.5 1.7 %collective-permute-start = (f32[224,256]{1,0:T(8,128)S(1)}, f32[224,256]{1,0:T(8,128)S(1)}, u32[]{:S(2)}, u32[]{:S(2)}) collective-permute-start(f32[224,256]{1,0:T(8,128)S(1)} %copy-done.2), channel_id=1, source_target_pairs={{0,1},{1,0},{2,3},{3,2},{4,5},{5,4},{6,7},{7,6},{8,9},{9,8},{10,11... | collective-permute-start | bytes 688136 | tf_op jit(solution)/shard_map/ppermute | solution.py:157
  40.2 1.9 %select_reduce_fusion = s32[448]{0:T(512)} fusion(s32[1792]{0:T(1024)} %fusion.10, s32[1792]{0:T(1024)} %param.5, s32[448]{0:T(512)} %iota_add_fusion), kind=kLoop, calls=%fused_computation | loop fusion | flops 2408000 | bytes 17920 | tf_op jit(solution)/shard_map/reduce_max | solution.py:214
  42.4 1.7 %collective-permute-start.4 = (f32[224,256]{1,0:T(8,128)}, f32[224,256]{1,0:T(8,128)}, u32[]{:S(2)}, u32[]{:S(2)}) collective-permute-start(f32[224,256]{1,0:T(8,128)} %collective-permute-done.3.refs_4_), channel_id=1, source_target_pairs={{0,1},{1,0},{2,3},{3,2},{4,5},{5,4},{6,7},{7,6},{8,9},{9,8},{10,11... | collective-permute-start | bytes 688136 | tf_op jit(solution)/shard_map/ppermute | solution.py:157
  44.5 2.1 %collective-permute-start.6 = (f32[224,256]{1,0:T(8,128)}, f32[224,256]{1,0:T(8,128)}, u32[]{:S(2)}, u32[]{:S(2)}) collective-permute-start(f32[224,256]{1,0:T(8,128)} %collective-permute-done.5.refs_6_), channel_id=1, source_target_pairs={{0,1},{1,0},{2,3},{3,2},{4,5},{5,4},{6,7},{7,6},{8,9},{9,8},{10,11... | collective-permute-start | bytes 688136 | tf_op jit(solution)/shard_map/ppermute | solution.py:157
  46.6 1.9 %pad_add_fusion.info_ref = s32[2]{0:T(128)} fusion(s32[1]{0:T(128)} %get-tuple-element.13, s32[1]{0:T(128)} %get-tuple-element.14), kind=kLoop, calls=%fused_computation.43 | loop fusion | flops 2 | bytes 16 | tf_op jit(solution)/shard_map/stack | solution.py:220
  48.5 1.8 %stack.54.info_ref = s32[10]{0:T(128)} concatenate(s32[1]{0:T(128)} %get-tuple-element.12, s32[1]{0:T(128)} %get-tuple-element.11, s32[1]{0:T(128)} %bitcast.3, s32[1]{0:T(128)} %bitcast.4, s32[1]{0:T(128)} %bitcast.5, s32[1]{0:T(128)} %bitcast.6, s32[1]{0:T(128)} %bitcast.7, s32[1]{0:T(128)} %bitcast.8, s32[1]{0:T(128)} %bitcast.9, s32[1]{0:T(128)} %bitcast.10), dimensions={0} | concatenate | bytes 80 | tf_op jit(solution)/shard_map/stack | solution.py:203
  51.6 4.1 %collective-permute-done.4.refs_5_ = f32[224,256]{1,0:T(8,128)} collective-permute-done((f32[224,256]{1,0:T(8,128)}, f32[224,256]{1,0:T(8,128)}, u32[]{:S(2)}, u32[]{:S(2)}) %collective-permute-start.4) | collective-permute-done | bytes 229408 | tf_op jit(solution)/shard_map/ppermute | solution.py:157
  55.8 4.2 %collective-permute-done.6.refs_7_ = f32[224,256]{1,0:T(8,128)} collective-permute-done((f32[224,256]{1,0:T(8,128)}, f32[224,256]{1,0:T(8,128)}, u32[]{:S(2)}, u32[]{:S(2)}) %collective-permute-start.6) | collective-permute-done | bytes 229408 | tf_op jit(solution)/shard_map/ppermute | solution.py:157
  60.6 3.9 %shard_map.60 = (f32[2,2376,128]{2,1,0:T(8,128)}, f32[448,256]{1,0:T(8,128)S(1)}) custom-call(s32[10]{0:T(128)S(1)} %copy-done.5, f32[224,256]{1,0:T(8,128)S(1)} %copy-done.2, f32[224,256]{1,0:T(8,128)S(1)} %collective-permute-done.refs_1_, f32[224,256]{1,0:T(8,128)} %collective-permute-done.1.refs_2_, f32[224,256]{1,0:T(8,128)} %collective-permute-done.2.refs_3_, ...), custom_call_target="tpu_custom_call" | custom-call | tf_op jit(solution)/shard_map/pallas_call | solution.py:139
  64.6 1.7 %copy-done = f32[2,2376,128]{2,1,0:T(8,128)S(1)} copy-done((f32[2,2376,128]{2,1,0:T(8,128)S(1)}, f32[2,2376,128]{2,1,0:T(8,128)}, u32[]{:S(2)}) %copy-start) | copy-done | bytes 2433048
  66.2 4.8 %shard_map.61 = f32[448,256]{1,0:T(8,128)} custom-call(s32[2]{0:T(128)S(1)} %copy-done.6, s32[1,448]{1,0:T(1,128)S(1)} %bitcast.18, f32[2,2376,128]{2,1,0:T(8,128)S(1)} %copy-done, f32[448,256]{1,0:T(8,128)S(1)} %get-tuple-element.5.part_ref, f32[2016,128]{1,0:T(8,128)S(1)} %collective-permute-done.8.refs_0_, f32[2016,128]{1,0:T(8,128)} %collective-permute-done.9.refs_1_), custom_call_target="tpu_custom_call" | custom-call | tf_op jit(solution)/shard_map/pallas_call | solution.py:139
  71.0 5.6 %all-to-all-start = ((f32[8,56,256]{2,1,0:T(8,128)}), f32[8,56,256]{2,1,0:T(8,128)S(1)}, u32[]{:S(2)}, u32[]{:S(2)}) async-start(f32[8,56,256]{2,1,0:T(8,128)} %bitcast.11), calls=%async_computation | async-start | bytes 917504 | tf_op jit(solution)/shard_map/all_to_all | solution.py:226
  77.2 1.6 %collective-permute-start.12 = (f32[448,128]{1,0:T(8,128)S(1)}, f32[448,128]{1,0:T(8,128)S(1)}, u32[]{:S(2)}, u32[]{:S(2)}) collective-permute-start(f32[448,128]{1,0:T(8,128)S(1)} %slice_select_fusion.refs_0_), channel_id=1, source_target_pairs={{0,16},{8,24},{16,0},{24,8},{1,17},{9,25},{17,1},{25,9},{2,18},{10... | collective-permute-start | bytes 688136 | tf_op jit(solution)/shard_map/ppermute | solution.py:153
  78.9 5.3 %collective-permute-done.12.refs_2_ = f32[448,128]{1,0:T(8,128)S(1)} collective-permute-done((f32[448,128]{1,0:T(8,128)S(1)}, f32[448,128]{1,0:T(8,128)S(1)}, u32[]{:S(2)}, u32[]{:S(2)}) %collective-permute-start.12) | collective-permute-done | bytes 229408 | tf_op jit(solution)/shard_map/ppermute | solution.py:153
  84.2 5.4 %all-to-all-done = f32[8,56,256]{2,1,0:T(8,128)S(1)} async-done(((f32[8,56,256]{2,1,0:T(8,128)}), f32[8,56,256]{2,1,0:T(8,128)S(1)}, u32[]{:S(2)}, u32[]{:S(2)}) %all-to-all-start) | async-done | bytes 458784 | tf_op jit(solution)/shard_map/all_to_all | solution.py:226
  90.7 1.4 %collective-permute-start.10 = (f32[224,256]{1,0:T(8,128)}, f32[224,256]{1,0:T(8,128)S(1)}, u32[]{:S(2)}, u32[]{:S(2)}) collective-permute-start(f32[224,256]{1,0:T(8,128)} %shard_map.62.mine_ref), channel_id=1, source_target_pairs={{0,1},{1,0},{2,3},{3,2},{4,5},{5,4},{6,7},{7,6},{8,9},{9,8},{10,11... | collective-permute-start | bytes 688136 | tf_op jit(solution)/shard_map/ppermute | solution.py:157
  92.2 4.9 %collective-permute-done.10.other_ref = f32[224,256]{1,0:T(8,128)S(1)} collective-permute-done((f32[224,256]{1,0:T(8,128)}, f32[224,256]{1,0:T(8,128)S(1)}, u32[]{:S(2)}, u32[]{:S(2)}) %collective-permute-start.10) | collective-permute-done | bytes 229408 | tf_op jit(solution)/shard_map/ppermute | solution.py:157
  99.2 16.9 %all_to_all.16 = f32[4,128,256]{2,1,0:T(8,128)S(1)} all-to-all(f32[4,128,256]{2,1,0:T(8,128)S(1)} %shard_map.63), channel_id=1, replica_groups={{0,2,4,6},{1,3,5,7},{8,10,12,14},{9,11,13,15},{16,18,20,22},{17,19,21,2..., dimensions={0} | all-to-all | bytes 1048576 | tf_op jit(solution)/shard_map/all_to_all | solution.py:252
  (61 shorter events, 15.6 us)
Async XLA Ops:
  0.6 33.1 %copy-start.7 = (s32[1792]{0:T(1024)S(1)}, s32[1792]{0:T(1024)}, u32[]{:S(2)}) copy-start(s32[1792]{0:T(1024)} %param.5) | copy-start | bytes 21508
  6.2 4.8 %copy-start.2 = (f32[224,256]{1,0:T(8,128)S(1)}, f32[224,256]{1,0:T(8,128)}, u32[]{:S(2)}) copy-start(f32[224,256]{1,0:T(8,128)} %refs_0_.1) | copy-start | bytes 688132
  7.9 25.8 %collective-permute-start.8 = (f32[2016,128]{1,0:T(8,128)S(1)}, f32[2016,128]{1,0:T(8,128)S(1)}, u32[]{:S(2)}, u32[]{:S(2)}) collective-permute-start(f32[2016,128]{1,0:T(8,128)S(1)} %shard_map.59.refs_8_), channel_id=1, source_target_pairs={{0,16},{8,24},{16,0},{24,8},{1,17},{9,25},{17,1},{25,9},{2,18},{10... | collective-permute-start | bytes 3096584 | tf_op jit(solution)/shard_map/ppermute | solution.py:153
  10.9 49.0 %collective-permute-start.7 = (f32[2016,128]{1,0:T(8,128)S(1)}, f32[2016,128]{1,0:T(8,128)S(1)}, u32[]{:S(2)}, u32[]{:S(2)}) collective-permute-start(f32[2016,128]{1,0:T(8,128)S(1)} %shard_map.59.refs_8_), channel_id=1, source_target_pairs={{0,8},{8,0},{16,24},{24,16},{1,9},{9,1},{17,25},{25,17},{2,10},{10... | collective-permute-start | bytes 3096584 | tf_op jit(solution)/shard_map/ppermute | solution.py:157
  11.0 25.6 %collective-permute-start.1 = (f32[224,256]{1,0:T(8,128)S(1)}, f32[224,256]{1,0:T(8,128)}, u32[]{:S(2)}, u32[]{:S(2)}) collective-permute-start(f32[224,256]{1,0:T(8,128)S(1)} %copy-done.2), channel_id=1, source_target_pairs={{0,2},{1,3},{2,4},{3,5},{4,6},{5,7},{6,0},{7,1},{8,10},{9,11},{10,... | collective-permute-start | bytes 688136 | tf_op jit(solution)/shard_map/ppermute | solution.py:153
  12.5 29.6 %collective-permute-start.3 = (f32[224,256]{1,0:T(8,128)S(1)}, f32[224,256]{1,0:T(8,128)}, u32[]{:S(2)}, u32[]{:S(2)}) collective-permute-start(f32[224,256]{1,0:T(8,128)S(1)} %copy-done.2), channel_id=1, source_target_pairs={{0,4},{1,5},{2,6},{3,7},{4,0},{5,1},{6,2},{7,3},{8,12},{9,13},{10,... | collective-permute-start | bytes 688136 | tf_op jit(solution)/shard_map/ppermute | solution.py:153
  15.1 27.3 %collective-permute-start.5 = (f32[224,256]{1,0:T(8,128)S(1)}, f32[224,256]{1,0:T(8,128)}, u32[]{:S(2)}, u32[]{:S(2)}) collective-permute-start(f32[224,256]{1,0:T(8,128)S(1)} %copy-done.2), channel_id=1, source_target_pairs={{0,6},{1,7},{2,0},{3,1},{4,2},{5,3},{6,4},{7,5},{8,14},{9,15},{10,... | collective-permute-start | bytes 688136 | tf_op jit(solution)/shard_map/ppermute | solution.py:153
  33.7 30.8 %collective-permute-start.9 = (f32[2016,128]{1,0:T(8,128)S(1)}, f32[2016,128]{1,0:T(8,128)}, u32[]{:S(2)}, u32[]{:S(2)}) collective-permute-start(f32[2016,128]{1,0:T(8,128)S(1)} %collective-permute-done.8.refs_0_), channel_id=1, source_target_pairs={{0,8},{8,0},{16,24},{24,16},{1,9},{9,1},{17,25},{25,17},{2,10},{10... | collective-permute-start | bytes 3096584 | tf_op jit(solution)/shard_map/ppermute | solution.py:157
  36.5 8.0 %collective-permute-start = (f32[224,256]{1,0:T(8,128)S(1)}, f32[224,256]{1,0:T(8,128)S(1)}, u32[]{:S(2)}, u32[]{:S(2)}) collective-permute-start(f32[224,256]{1,0:T(8,128)S(1)} %copy-done.2), channel_id=1, source_target_pairs={{0,1},{1,0},{2,3},{3,2},{4,5},{5,4},{6,7},{7,6},{8,9},{9,8},{10,11... | collective-permute-start | bytes 688136 | tf_op jit(solution)/shard_map/ppermute | solution.py:157
  42.1 9.5 %collective-permute-start.2 = (f32[224,256]{1,0:T(8,128)}, f32[224,256]{1,0:T(8,128)}, u32[]{:S(2)}, u32[]{:S(2)}) collective-permute-start(f32[224,256]{1,0:T(8,128)} %collective-permute-done.1.refs_2_), channel_id=1, source_target_pairs={{0,1},{1,0},{2,3},{3,2},{4,5},{5,4},{6,7},{7,6},{8,9},{9,8},{10,11... | collective-permute-start | bytes 688136 | tf_op jit(solution)/shard_map/ppermute | solution.py:157
  42.4 13.4 %collective-permute-start.4 = (f32[224,256]{1,0:T(8,128)}, f32[224,256]{1,0:T(8,128)}, u32[]{:S(2)}, u32[]{:S(2)}) collective-permute-start(f32[224,256]{1,0:T(8,128)} %collective-permute-done.3.refs_4_), channel_id=1, source_target_pairs={{0,1},{1,0},{2,3},{3,2},{4,5},{5,4},{6,7},{7,6},{8,9},{9,8},{10,11... | collective-permute-start | bytes 688136 | tf_op jit(solution)/shard_map/ppermute | solution.py:157
  44.5 15.5 %collective-permute-start.6 = (f32[224,256]{1,0:T(8,128)}, f32[224,256]{1,0:T(8,128)}, u32[]{:S(2)}, u32[]{:S(2)}) collective-permute-start(f32[224,256]{1,0:T(8,128)} %collective-permute-done.5.refs_6_), channel_id=1, source_target_pairs={{0,1},{1,0},{2,3},{3,2},{4,5},{5,4},{6,7},{7,6},{8,9},{9,8},{10,11... | collective-permute-start | bytes 688136 | tf_op jit(solution)/shard_map/ppermute | solution.py:157
  50.4 14.2 %copy-start.4 = (s32[448]{0:T(512)S(1)}, s32[448]{0:T(512)}, u32[]{:S(2)}) copy-start(s32[448]{0:T(512)} %select_reduce_fusion) | copy-start | bytes 5380
  50.4 14.2 %copy-start.6 = (s32[2]{0:T(128)S(1)}, s32[2]{0:T(128)}, u32[]{:S(2)}) copy-start(s32[2]{0:T(128)} %pad_add_fusion.info_ref) | copy-start | bytes 28
  64.6 1.7 %copy-start = (f32[2,2376,128]{2,1,0:T(8,128)S(1)}, f32[2,2376,128]{2,1,0:T(8,128)}, u32[]{:S(2)}) copy-start(f32[2,2376,128]{2,1,0:T(8,128)} %get-tuple-element.4.us_ref) | copy-start | bytes 7299076
  66.2 10.3 %copy-start.9 = (s32[224]{0:T(256)S(1)}, s32[224]{0:T(256)}, u32[]{:S(2)}) copy-start(s32[224]{0:T(256)} %get-tuple-element.8) | copy-start | bytes 2692
  66.2 10.7 %copy-start.10 = (s32[224]{0:T(256)S(1)}, s32[224]{0:T(256)}, u32[]{:S(2)}) copy-start(s32[224]{0:T(256)} %get-tuple-element.9) | copy-start | bytes 2692
  71.0 7.7 %copy-start.11 = (pred[224]{0:T(512)(128)(4,1)S(1)}, pred[224]{0:T(512)(128)(4,1)}, u32[]{:S(2)}) copy-start(pred[224]{0:T(512)(128)(4,1)} %get-tuple-element.10) | copy-start | bytes 676
  71.0 18.6 %all-to-all-start = ((f32[8,56,256]{2,1,0:T(8,128)}), f32[8,56,256]{2,1,0:T(8,128)S(1)}, u32[]{:S(2)}, u32[]{:S(2)}) async-start(f32[8,56,256]{2,1,0:T(8,128)} %bitcast.11), calls=%async_computation | async-start | bytes 917504 | tf_op jit(solution)/shard_map/all_to_all | solution.py:226
  77.1 39.0 %copy-start.8 = (f32[128,256]{1,0:T(8,128)S(1)}, f32[128,256]{1,0:T(8,128)}, u32[]{:S(2)}) copy-start(f32[128,256]{1,0:T(8,128)} %param.7) | copy-start | bytes 393220
  77.2 7.0 %collective-permute-start.12 = (f32[448,128]{1,0:T(8,128)S(1)}, f32[448,128]{1,0:T(8,128)S(1)}, u32[]{:S(2)}, u32[]{:S(2)}) collective-permute-start(f32[448,128]{1,0:T(8,128)S(1)} %slice_select_fusion.refs_0_), channel_id=1, source_target_pairs={{0,16},{8,24},{16,0},{24,8},{1,17},{9,25},{17,1},{25,9},{2,18},{10... | collective-permute-start | bytes 688136 | tf_op jit(solution)/shard_map/ppermute | solution.py:153
  78.8 13.3 %collective-permute-start.11 = (f32[448,128]{1,0:T(8,128)S(1)}, f32[448,128]{1,0:T(8,128)S(1)}, u32[]{:S(2)}, u32[]{:S(2)}) collective-permute-start(f32[448,128]{1,0:T(8,128)S(1)} %slice_select_fusion.refs_0_), channel_id=1, source_target_pairs={{0,8},{8,0},{16,24},{24,16},{1,9},{9,1},{17,25},{25,17},{2,10},{10... | collective-permute-start | bytes 688136 | tf_op jit(solution)/shard_map/ppermute | solution.py:157
  84.2 8.0 %collective-permute-start.13 = (f32[448,128]{1,0:T(8,128)S(1)}, f32[448,128]{1,0:T(8,128)S(1)}, u32[]{:S(2)}, u32[]{:S(2)}) collective-permute-start(f32[448,128]{1,0:T(8,128)S(1)} %collective-permute-done.12.refs_2_), channel_id=1, source_target_pairs={{0,8},{8,0},{16,24},{24,16},{1,9},{9,1},{17,25},{25,17},{2,10},{10... | collective-permute-start | bytes 688136 | tf_op jit(solution)/shard_map/ppermute | solution.py:157
  90.7 6.5 %collective-permute-start.10 = (f32[224,256]{1,0:T(8,128)}, f32[224,256]{1,0:T(8,128)S(1)}, u32[]{:S(2)}, u32[]{:S(2)}) collective-permute-start(f32[224,256]{1,0:T(8,128)} %shard_map.62.mine_ref), channel_id=1, source_target_pairs={{0,1},{1,0},{2,3},{3,2},{4,5},{5,4},{6,7},{7,6},{8,9},{9,8},{10,11... | collective-permute-start | bytes 688136 | tf_op jit(solution)/shard_map/ppermute | solution.py:157
  (3 other events, 3.0 us)

commit v2 on v0

v2 whole, which is shorter than its diff:
```python
import functools

import jax
import jax.numpy as jnp
from jax import lax
from jax.experimental import pallas as pl
from jax.experimental.pallas import tpu as pltpu
from jax.sharding import PartitionSpec as P

LANES = 128
BLOCK_CAP = 560
CAP = -(-BLOCK_CAP // 64) * 64
FULL = CAP // LANES
WIDE = (FULL + 1) * LANES
BF16 = jnp.bfloat16
VMEM = pl.BlockSpec(memory_space=pltpu.VMEM)


def f32(*shape):
    return jax.ShapeDtypeStruct(shape, jnp.float32)


def bf16(*shape):
    return jax.ShapeDtypeStruct(shape, BF16)


def split(v):
    high = v.astype(BF16)
    return high, (v - high.astype(jnp.float32)).astype(BF16)


def split3(v):
    high = v.astype(BF16)
    mid, low = split(v - high.astype(jnp.float32))
    return high, mid, low


def dot(a, b):
    return jnp.dot(a, b, preferred_element_type=jnp.float32)


def pick_rows(place, v):
    high, mid, low = split3(v)
    return dot(place, high) + (dot(place, mid) + dot(place, low))


def one_hot(mask):
    return jnp.where(mask, 1.0, 0.0)


def count(mask):
    return jnp.sum(jnp.where(mask, 1.0, 0.0)).astype(jnp.int32)


def log2(size):
    return size.bit_length() - 1


def each(refs, owners, fn):
    if owners is None:
        pl.loop(0, refs[0].shape[0])(lambda i: fn(i, refs[0].at[i]))
    else:
        for owner, ref in zip(owners, refs):
            fn(owner, ref)


def select_kernel(structure_ref, sigma_ref, out_ref, place_ref):
    step, steps = pl.program_id(0), pl.num_programs(0)
    part, cols = sigma_ref.shape
    n = structure_ref.shape[1]
    rows = out_ref.shape[0] * LANES // CAP

    @pl.when(step == 0)
    def _():
        first = lax.axis_index("prow") * cols
        names = jnp.broadcast_to(structure_ref[...], (8, n))
        shift = lax.rem(n - count(structure_ref[...] < first), n)
        named = pltpu.roll(names, shift, 1)[:1, :CAP] - first
        named = jnp.concatenate([named, named[:, FULL * LANES :]], axis=1)
        at = lax.broadcasted_iota(jnp.int32, (cols, WIDE), 0)
        place_ref[...] = one_hot(at == named).astype(BF16)

    high, low = split(sigma_ref[...])
    place = place_ref[...]
    picked = dot(high, place) + dot(low, place)
    start = step * part
    for i in range(FULL):
        where = pl.multiple_of(rows * i + start, 8)
        out_ref[pl.ds(where, part), :] = picked[:, LANES * i : LANES * (i + 1)]

    @pl.when(step < steps // 2)
    def _():
        where = pl.multiple_of(rows * FULL + start, 8)
        out_ref[pl.ds(where, part), : LANES // 2] = picked[:, FULL * LANES : CAP]

    @pl.when(step >= steps // 2)
    def _():
        where = pl.multiple_of(rows * FULL + start - rows // 2, 8)
        out_ref[pl.ds(where, part), LANES // 2 :] = picked[:, CAP:]


def block_term(block_ref, uh, ul, rows):
    parts = [block_ref[rows * i : rows * (i + 1), :] for i in range(FULL)]
    tail = block_ref[rows * FULL : rows * FULL + rows // 2, :]
    parts.append(jnp.concatenate([tail, pltpu.roll(tail, LANES // 2, 1)], axis=0))
    halves = [split(p) for p in parts]
    highs, lows = [h for h, _ in halves], [l for _, l in halves]
    left = jnp.concatenate(highs + highs + lows, axis=1)
    return dot(left, jnp.concatenate([uh, ul, uh], axis=0))


def prepare_kernel(direct, slots, nr, offsets, n_first, owners, structure_ref, turned_ref, *refs):
    uh_ref, ul_ref, part_ref, to_ref, from_ref, us_ref = refs[-6:]
    m, nc = turned_ref.shape
    w = uh_ref.shape[2]
    n = m * nc
    c = lax.axis_index("pcol")
    r = lax.axis_index("prow")
    z = c // 2
    u_refs = refs[: -6 - n_first] if n_first else refs[:-6]
    first_refs = refs[-6 - n_first : -6]
    rows = part_ref.shape[0]
    names = structure_ref[...]

    def place(owner, u_ref):
        u = u_ref[...]
        if w % LANES:
            u = jnp.concatenate([u, jnp.zeros((m, LANES - w % LANES), jnp.float32)], axis=1)
        for i in range(us_ref.shape[0]):
            us_ref[i, pl.ds(owner, m, stride=nc), :] = u[:, LANES * i : LANES * (i + 1)]

    if direct:
        for (dz, flip), u_ref in zip(offsets, u_refs):
            pl.when((z + dz >= 0) & (z + dz < nc // 2))(
                functools.partial(place, jnp.bitwise_xor(c + 2 * dz, flip), u_ref)
            )
    else:
        each(u_refs, None, place)
    us_ref[:, n:, :] = jnp.zeros((us_ref.shape[0], us_ref.shape[1] - n, LANES), jnp.float32)

    width = rows * 2

    def cut(owner):
        start = count(names < owner * width)
        base = pl.multiple_of((start // 8) * 8, 8)
        size = CAP + 8
        lanes = [
            pltpu.roll(us_ref[k, pl.ds(base, size), :], size - (start - base), 0)[:CAP]
            for k in range(us_ref.shape[0])
        ]
        u = jnp.concatenate(lanes, axis=1)[:, :w]
        u = jnp.concatenate([u, jnp.zeros((WIDE - CAP, w), jnp.float32)], axis=0)
        uh_ref[owner], ul_ref[owner] = split(u)

    if direct:
        for b in range(nr):
            cut(b)
    else:
        pl.loop(0, nr)(cut)
    image = jnp.zeros((rows, w), jnp.float32)
    for owner, block_ref in zip(owners(r), first_refs):
        image = image + block_term(block_ref, uh_ref[owner], ul_ref[owner], rows)
    part_ref[...] = image

    lg = log2(nc)
    row = c * rows + lax.broadcasted_iota(jnp.int32, (rows, n), 0)
    rank = jnp.sum(one_hot(names < row), axis=1, keepdims=True).astype(jnp.int32)
    member = jnp.sum(one_hot(names == row), axis=1, keepdims=True)
    turn = rank & (nc - 1)
    ahead = (count(names < c * rows) - turn + nc - 1) >> lg
    block = turn
    if direct:
        block = 2 * (((turn >> 1) - z) & (nc // 2 - 1)) + ((turn ^ c) & 1)
    slot = jnp.where(member > 0.5, block * slots + (rank >> lg) - ahead, -1)
    at = lax.broadcasted_iota(jnp.int32, (rows, nc * slots), 1)
    to_ref[...] = one_hot(at == slot).T.astype(BF16)

    lane = lax.broadcasted_iota(jnp.int32, (m, nc), 1)
    mine = jnp.sum(jnp.where(lane == c, turned_ref[...], 0).astype(jnp.float32), axis=1, keepdims=True)
    source = jnp.zeros((m, 1), jnp.int32)
    before = jnp.zeros((m, 1), jnp.int32)
    for k in range(1, nc):
        less = mine < float(k * rows)
        source = source + jnp.where(less, 0, 1)
        before = jnp.where(less, before, count(less))
    block = source
    if direct:
        block = 2 * ((z - (source >> 1)) & (nc // 2 - 1)) + ((source ^ c) & 1)
    slot = block * slots + lax.broadcasted_iota(jnp.int32, (m, 1), 0) - before
    at = lax.broadcasted_iota(jnp.int32, (m, nc * slots), 1)
    from_ref[...] = one_hot(at == slot).astype(BF16)


def image_kernel(n_out, owners, uh_ref, ul_ref, part_ref, to_ref, *refs):
    block_refs, out_refs = refs[:-n_out], refs[-n_out:]
    rows = part_ref.shape[0]
    if owners is None:
        stack = block_refs[0]
        add = lambda b, v: v + block_term(stack.at[b], uh_ref[b], ul_ref[b], rows)
        image = lax.fori_loop(0, stack.shape[0], add, part_ref[...])
    else:
        image = part_ref[...]
        for owner, block_ref in zip(owners(lax.axis_index("prow")), block_refs):
            image = image + block_term(block_ref, uh_ref[owner], ul_ref[owner], rows)
    image = pick_rows(to_ref[...], image)
    size = image.shape[0] // n_out
    for k, out_ref in enumerate(out_refs):
        out_ref[...] = image[size * k : size * (k + 1)]


def pick_kernel(from_ref, *refs):
    got = [ref[...] for ref in refs[:-1]]
    got = jnp.concatenate(got, axis=0) if len(got) > 1 else got[0]
    refs[-1][...] = -pick_rows(from_ref[...], got)


def turn_kernel(direct, owners, *refs):
    high_ref, low_ref = refs[-2:]
    z = lax.axis_index("pcol") // 2

    def put(owner, u_ref):
        where = ((owner - z) & (high_ref.shape[0] - 1)) if direct else owner
        high_ref[where], low_ref[where] = split(u_ref[...].T)

    each(refs[:-2], owners(lax.axis_index("prow")) if direct else None, put)


def correction_kernel(high_ref, low_ref, mine_ref, other_ref, *out_refs):
    sh, sl = split(jnp.concatenate([mine_ref[...], other_ref[...]], axis=0))
    nz = high_ref.shape[0]

    def term(t):
        return dot(high_ref[t], sh) + (dot(high_ref[t], sl) + dot(low_ref[t], sh))

    if len(out_refs) > 1:
        for t, out_ref in enumerate(out_refs):
            out_ref[...] = term(t)
    else:

        @pl.loop(0, nz)
        def _(t):
            out_refs[0][t] = term(t)


def call(kernel, out_shape, *args, **kw):
    many = isinstance(out_shape, (list, tuple))
    kw = {"in_specs": [VMEM] * len(args)} | kw
    return pl.pallas_call(
        kernel,
        out_shape=out_shape,
        out_specs=[VMEM] * len(out_shape) if many else VMEM,
        compiler_params=pltpu.CompilerParams(vmem_limit_bytes=20 * 2**20),
        **kw,
    )(*args)


def swap(v, axis, size):
    return lax.ppermute(v, axis, [(k, k ^ 1) for k in range(size)])


def spread(v, size):
    blocks = [v, swap(v, "prow", size)]
    for t in range(1, size // 2):
        far = lax.ppermute(v, "prow", [(k, (k + 2 * t) % size) for k in range(size)])
        blocks += [far, swap(far, "prow", size)]
    return blocks


def relative_owners(size, r):
    out = []
    for t in range(size // 2):
        owner = (r - 2 * t) & (size - 1)
        out += [owner, owner ^ 1]
    return out


def line_gather(u, nc):
    nz = nc // 2
    across = lambda v, ks: lax.ppermute(v, "pcol", [(2 * k + x, 2 * k + 1 - x) for k in ks for x in range(2)])
    along = lambda v, ks, by: lax.ppermute(v, "pcol", [(2 * k + x, 2 * (k + by) + x) for k in ks for x in range(2)])
    offsets, blocks = [(0, 0), (0, 1)], [u, across(u, range(nz))]
    up = down = u
    for t in range(1, nz):
        up = along(up, range(t - 1, nz - 1), 1)
        down = along(down, range(1, nz - t + 1), -1)
        offsets += [(-t, 0), (t, 0), (-t, 1), (t, 1)]
        blocks += [up, down, across(up, range(t, nz)), across(down, range(0, nz - t))]
    return offsets, blocks


def per_device(sigma_top, structure, u_panel, d_term):
    nc, nr = lax.axis_size("pcol"), lax.axis_size("prow")
    c = lax.axis_index("pcol")
    nz = nc // 2
    rows, cols = sigma_top.shape
    m, w = u_panel.shape
    n = structure.shape[0]
    slots = -(-rows // nc)
    direct = nc <= 8
    n_first = 2 if direct else 0
    names = structure.reshape(1, n)
    steps = 4
    part = rows // steps

    if direct:
        offsets, u_blocks = line_gather(u_panel, nc)
        partner = u_blocks[1]
    else:
        offsets, u_blocks = None, [lax.all_gather(u_panel, "pcol")]
        partner = swap(u_panel, "pcol", nc)

    chosen = call(
        select_kernel,
        f32(rows * CAP // LANES, LANES),
        names,
        sigma_top,
        grid=(steps,),
        in_specs=[pl.BlockSpec((1, n), lambda i: (0, 0)), pl.BlockSpec((part, cols), lambda i: (i, 0))],
        scratch_shapes=[pltpu.VMEM((cols, WIDE), BF16)],
    )
    near = [chosen, swap(chosen, "prow", nr)] if direct else []
    owners = functools.partial(relative_owners, nr)
    uh, ul, image, to, source = call(
        functools.partial(
            prepare_kernel, direct, slots, nr, offsets, n_first, lambda r: owners(r)[:2]
        ),
        [bf16(nr, WIDE, w), bf16(nr, WIDE, w), f32(rows, w), bf16(nc * slots, rows), bf16(m, nc * slots)],
        names,
        structure.reshape(m, nc),
        *u_blocks,
        *near,
        scratch_shapes=[pltpu.VMEM((-(-w // LANES), n + CAP + 8, LANES), jnp.float32)],
    )

    if direct:
        later = []
        for t in range(1, nr // 2):
            far = lax.ppermute(chosen, "prow", [(k, (k + 2 * t) % nr) for k in range(nr)])
            far, image = lax.optimization_barrier((far, image))
            later += [far, swap(far, "prow", nr)]
    else:
        later = [lax.all_gather(chosen, "prow")]
    n_out = nc if direct else 1
    sent = call(
        functools.partial(image_kernel, n_out, (lambda r: owners(r)[2:]) if direct else None),
        [f32(nc * slots // n_out, w)] * n_out,
        uh,
        ul,
        image,
        to,
        *later,
    )
    if direct:
        got = [sent[0]]
        for k in range(1, nc):
            got.append(lax.ppermute(sent[k], "pcol", [(i, ((i + 2 * (k // 2)) % nc) ^ (k % 2)) for i in range(nc)]))
    else:
        got = [lax.all_to_all(sent[0], "pcol", split_axis=0, concat_axis=0, tiled=True)]
    sigma_sj = call(pick_kernel, f32(m, w), source, *got)

    wd = w // 2
    pair = jnp.concatenate([u_panel, partner], axis=0)
    pair = jnp.where(jnp.bitwise_and(c, 1) == 0, pair[:, :wd], pair[:, wd:])
    if direct:
        pair, later[0] = lax.optimization_barrier((pair, later[0]))
        pairs = spread(pair, nr)
    else:
        pairs = [lax.all_gather(pair, "prow")]
    turned = call(
        functools.partial(turn_kernel, direct, owners), [bf16(nz, wd, 2 * m), bf16(nz, wd, 2 * m)], *pairs
    )
    other = swap(sigma_sj, "pcol", nc)
    if direct:
        terms = call(correction_kernel, [f32(wd, w)] * nz, *turned, sigma_sj, other)
        total = terms[0]
        for t in range(1, nz):
            total = total + lax.ppermute(terms[t], "pcol", [(k, (k + 2 * t) % nc) for k in range(nc)])
    else:
        terms = call(correction_kernel, f32(nz, wd, w), *turned, sigma_sj, other)
        groups = [[2 * k + x for k in range(nz)] for x in range(2)]
        terms = lax.all_to_all(terms, "pcol", split_axis=0, concat_axis=0, axis_index_groups=groups, tiled=True)
        total = jnp.sum(terms, axis=0)
    return sigma_sj, d_term - total


def solution(mesh):
    placed = (P("pcol", "prow"), P(), P("pcol", "prow"), P("pcol", "prow"))
    return jax.shard_map(
        per_device,
        mesh=mesh,
        in_specs=placed,
        out_specs=(P("pcol", "prow"), P("pcol", "prow")),
        check_vma=False,
    )
```

time: 304 us -> 120 us (0.39)
  waiting for transfers between devices: 201 us -> 28.3 us
  blocking collectives: 55.2 us -> 0 us
  starting transfers between devices: 0.16 us -> 44.3 us
  local copies, waits for them, and re-layouts: 9.46 us -> 31 us
  Pallas kernels: 0 us -> 13.6 us
  other arithmetic: 14.1 us -> 0.73 us
  between operations: 13.9 us -> 0.95 us
  matrix products: 9.24 us -> 0 us
    all_gather x2 -> x0, waiting for transfers between devices: 110 us -> none  [the longest x1 60.1 us: per_device(): piece = lax.all_gather(image_t, 'pcol', axis=1, tiled=True)]
    reduce_scatter x2 -> x0, waiting for transfers between devices: 90.4 us -> none  [the longest x1 62.4 us: per_device(): lax.psum_scatter(lax.dot_general(u_full, sigma_sj, (((0,), (0,)), ((), ()...]
    all_to_all x1 -> x0, blocking collectives: 46.3 us -> none  [per_device(): lax.all_to_all(placed_cols, 'prow', split_axis=0, concat_axis=1, tiled=True)]
    ppermute x0 -> x30, starting transfers between devices: none -> 44.3 us  [the longest x7 14.6 us: line_gather(): lax.ppermute(v, 'pcol', [(2 * k + x, 2 * k + 1 - x) for k in ks for x in...]
    unnamed x10 -> x77, local copies, waits for them, and re-layouts: 0.87 us -> 29.2 us
    ppermute x0 -> x30, waiting for transfers between devices: none -> 28.3 us  [the longest x6 9.18 us: line_gather(): lax.ppermute(v, 'pcol', [(2 * k + x, 2 * (k + by) + x) for k in ks for x...]
    pallas_call x0 -> x6, Pallas kernels: none -> 13.6 us  [call(): pl.pallas_call(kernel, out_shape=out_shape, out_specs=[VMEM] * len(out_sh...]
    scatter-add x1 -> x0, other arithmetic: 12.9 us -> none  [per_device(): placed_cols = jnp.zeros((order, cols_blk), jnp.float32).at[mapped].add(la...]
  transfers between devices with their start and end apart: 4 -> 30, of which waited for: 4 -> 13; matrix products, arithmetic and copies ran while one was open for 0% -> 2% of each run, Pallas kernels for 0% -> 11%
where the time goes in v2:
time: 120 us; the launch traced here: 119 us
  starting transfers between devices  44.3 us (37%)
  local copies, waits for them, and re-layouts  31 us (26%)
  waiting for transfers between devices  28.3 us (24%)
  Pallas kernels  13.6 us (11%)
    unnamed x77, local copies, waits for them, and re-layouts  29.2 us
    ppermute x7, starting transfers between devices, line_gather(): lax.ppermute(v, 'pcol', [(2 * k + x, 2 * k + 1 - x) for k in ks for x in...  14.6 us
    pallas_call x6, Pallas kernels, call(): pl.pallas_call(kernel, out_shape=out_shape, out_specs=[VMEM] * len(out_sh...  13.6 us
    ppermute x7, starting transfers between devices, per_device(): lax.ppermute(sent[k], 'pcol', [(i, (i + 2 * (k // 2)) % nc ^ k % 2) for i...  11.3 us
    ppermute x6, starting transfers between devices, line_gather(): lax.ppermute(v, 'pcol', [(2 * k + x, 2 * (k + by) + x) for k in ks for x...  10.1 us
    ppermute x6, waiting for transfers between devices, line_gather(): lax.ppermute(v, 'pcol', [(2 * k + x, 2 * (k + by) + x) for k in ks for x...  9.18 us
    ppermute x3, waiting for transfers between devices, per_device(): lax.ppermute(terms[t], 'pcol', [(k, (k + 2 * t) % nc) for k in range(nc)])  7.03 us
    ppermute x5, waiting for transfers between devices, swap(): return lax.ppermute(v, axis, [(k, k ^ 1) for k in range(size)])  5.74 us
  transfers between devices with their start and end apart: 30, of which 13 were waited for; matrix products, arithmetic and copies ran while one was open for 2% of the time, Pallas kernels for 11%

profile of v2, /device:TPU:0, one launch (start us, length us, event | category | flops | bytes accessed | tf_op | source)
XLA Modules:
  0.0 118.8 jit_solution(721821792157042862)
XLA Ops:
  0.6 4.9 %collective-permute-start.1 = (f32[224,256]{1,0:T(8,128)}, f32[224,256]{1,0:T(8,128)S(1)}, u32[]{:S(2)}, u32[]{:S(2)}) collective-permute-start(f32[224,256]{1,0:T(8,128)} %refs_0_.1), channel_id=1, source_target_pairs={{0,2},{1,3},{2,4},{3,5},{4,6},{5,7},{8,10},{9,11},{10,12},{11,13},... | collective-permute-start | bytes 688136 | tf_op jit(solution)/shard_map/ppermute | solution.py:280
  6.3 1.4 %copy-done = f32[448,896]{1,0:T(8,128)S(1)} copy-done((f32[448,896]{1,0:T(8,128)S(1)}, f32[448,896]{1,0:T(8,128)}, u32[]{:S(2)}) %copy-start) | copy-done | bytes 1605656
  7.7 3.1 %shard_map.59.refs_14_ = f32[2016,128]{1,0:T(8,128)S(1)} custom-call(s32[1,1792]{1,0:T(1,128)S(1)} %reshape.10.structure_ref, f32[448,896]{1,0:T(8,128)S(1)} %copy-done), custom_call_target="tpu_custom_call" | custom-call | tf_op jit(solution)/shard_map/pallas_call | solution.py:248
  10.9 1.6 %collective-permute-start.14 = (f32[2016,128]{1,0:T(8,128)S(1)}, f32[2016,128]{1,0:T(8,128)}, u32[]{:S(2)}, u32[]{:S(2)}) collective-permute-start(f32[2016,128]{1,0:T(8,128)S(1)} %shard_map.59.refs_14_), channel_id=1, source_target_pairs={{0,16},{8,24},{16,0},{24,8},{1,17},{9,25},{17,1},{25,9},{2,18},{10... | collective-permute-start | bytes 3096584 | tf_op jit(solution)/shard_map/ppermute | solution.py:338
  13.7 1.6 %collective-permute-start = (f32[224,256]{1,0:T(8,128)S(1)}, f32[224,256]{1,0:T(8,128)S(1)}, u32[]{:S(2)}, u32[]{:S(2)}) collective-permute-start(f32[224,256]{1,0:T(8,128)S(1)} %copy-done.4), channel_id=1, source_target_pairs={{0,1},{1,0},{2,3},{3,2},{4,5},{5,4},{6,7},{7,6},{8,9},{9,8},{10,11... | collective-permute-start | bytes 688136 | tf_op jit(solution)/shard_map/ppermute | solution.py:279
  16.0 6.0 %collective-permute-done.2.refs_3_ = f32[224,256]{1,0:T(8,128)S(1)} collective-permute-done((f32[224,256]{1,0:T(8,128)S(1)}, f32[224,256]{1,0:T(8,128)S(1)}, u32[]{:S(2)}, u32[]{:S(2)}) %collective-permute-start.2) | collective-permute-done | bytes 229408 | tf_op jit(solution)/shard_map/ppermute | solution.py:280
  25.4 3.4 %collective-permute-start.4 = (f32[224,256]{1,0:T(8,128)S(1)}, f32[224,256]{1,0:T(8,128)S(1)}, u32[]{:S(2)}, u32[]{:S(2)}) collective-permute-start(f32[224,256]{1,0:T(8,128)S(1)} %collective-permute-done.2.refs_3_), channel_id=1, source_target_pairs={{0,1},{1,0},{2,3},{3,2},{4,5},{5,4},{8,9},{9,8},{10,11},{11,10},{1... | collective-permute-start | bytes 688136 | tf_op jit(solution)/shard_map/ppermute | solution.py:279
  36.3 3.4 %collective-permute-start.8 = (f32[224,256]{1,0:T(8,128)S(1)}, f32[224,256]{1,0:T(8,128)S(1)}, u32[]{:S(2)}, u32[]{:S(2)}) collective-permute-start(f32[224,256]{1,0:T(8,128)S(1)} %collective-permute-done.6.refs_7_), channel_id=1, source_target_pairs={{0,1},{1,0},{2,3},{3,2},{8,9},{9,8},{10,11},{11,10},{16,17},{17,16... | collective-permute-start | bytes 688136 | tf_op jit(solution)/shard_map/ppermute | solution.py:279
  40.4 1.8 %collective-permute-done.10.refs_11_ = f32[224,256]{1,0:T(8,128)S(1)} collective-permute-done((f32[224,256]{1,0:T(8,128)S(1)}, f32[224,256]{1,0:T(8,128)S(1)}, u32[]{:S(2)}, u32[]{:S(2)}) %collective-permute-start.10) | collective-permute-done | bytes 229408 | tf_op jit(solution)/shard_map/ppermute | solution.py:280
  44.2 4.2 %collective-permute-start.12 = (f32[224,256]{1,0:T(8,128)S(1)}, f32[224,256]{1,0:T(8,128)}, u32[]{:S(2)}, u32[]{:S(2)}) collective-permute-start(f32[224,256]{1,0:T(8,128)S(1)} %collective-permute-done.10.refs_11_), channel_id=1, source_target_pairs={{0,1},{1,0},{8,9},{9,8},{16,17},{17,16},{24,25},{25,24}} | collective-permute-start | bytes 688136 | tf_op jit(solution)/shard_map/ppermute | solution.py:279
  50.7 1.9 %collective-permute-done.12.refs_13_ = f32[224,256]{1,0:T(8,128)} collective-permute-done((f32[224,256]{1,0:T(8,128)S(1)}, f32[224,256]{1,0:T(8,128)}, u32[]{:S(2)}, u32[]{:S(2)}) %collective-permute-start.12) | collective-permute-done | bytes 229408 | tf_op jit(solution)/shard_map/ppermute | solution.py:279
  64.8 5.0 %shard_map.60 = (bf16[4,640,256]{2,1,0:T(8,128)(2,1)S(1)}, bf16[4,640,256]{2,1,0:T(8,128)(2,1)S(1)}, f32[448,256]{1,0:T(8,128)S(1)}, bf16[448,448]{1,0:T(8,128)(2,1)S(1)}, bf16[224,448]{1,0:T(8,128)(2,1)S(1)}) custom-call(s32[1,1792]{1,0:T(1,128)S(1)} %reshape.10.structure_ref, s32[224,8]{1,0:T(8,128)S(1)} %reshape.11.turned_ref, f32[224,256]{1,0:T(8,128)S(1)} %copy-done.5, ...), custom_call_target="tpu_custom_call" | custom-call | tf_op jit(solution)/shard_map/pallas_call | solution.py:248
  78.0 3.5 %shard_map.61 = (f32[56,256]{1,0:T(8,128)S(1)}, f32[56,256]{1,0:T(8,128)S(1)}, f32[56,256]{1,0:T(8,128)S(1)}, f32[56,256]{1,0:T(8,128)S(1)}, f32[56,256]{1,0:T(8...) custom-call(bf16[4,640,256]{2,1,0:T(8,128)(2,1)S(1)} %get-tuple-element.25.uh_ref, ...), custom_call_target="tpu_custom_call" | custom-call | tf_op jit(solution)/shard_map/pallas_call | solution.py:248
  81.5 2.1 %collective-permute-start.16 = (f32[56,256]{1,0:T(8,128)S(1)}, f32[56,256]{1,0:T(8,128)S(1)}, u32[]{:S(2)}, u32[]{:S(2)}) collective-permute-start(f32[56,256]{1,0:T(8,128)S(1)} %get-tuple-element.32), channel_id=1, source_target_pairs={{0,1},{1,0},{2,3},{3,2},{4,5},{5,4},{6,7},{7,6},{8,9},{9,8},{10,11... | collective-permute-start | bytes 172040 | tf_op jit(solution)/shard_map/ppermute | solution.py:356
  83.6 1.9 %collective-permute-start.18 = (f32[56,256]{1,0:T(8,128)S(1)}, f32[56,256]{1,0:T(8,128)S(1)}, u32[]{:S(2)}, u32[]{:S(2)}) collective-permute-start(f32[56,256]{1,0:T(8,128)S(1)} %get-tuple-element.34), channel_id=1, source_target_pairs={{0,3},{1,2},{2,5},{3,4},{4,7},{5,6},{6,1},{7,0},{8,11},{9,10},{10,... | collective-permute-start | bytes 172040 | tf_op jit(solution)/shard_map/ppermute | solution.py:356
  85.5 2.0 %collective-permute-start.19 = (f32[56,256]{1,0:T(8,128)S(1)}, f32[56,256]{1,0:T(8,128)S(1)}, u32[]{:S(2)}, u32[]{:S(2)}) collective-permute-start(f32[56,256]{1,0:T(8,128)S(1)} %get-tuple-element.35), channel_id=1, source_target_pairs={{0,4},{1,5},{2,6},{3,7},{4,0},{5,1},{6,2},{7,3},{8,12},{9,13},{10,... | collective-permute-start | bytes 172040 | tf_op jit(solution)/shard_map/ppermute | solution.py:356
  88.9 2.4 %collective-permute-start.21 = (f32[56,256]{1,0:T(8,128)S(1)}, f32[56,256]{1,0:T(8,128)S(1)}, u32[]{:S(2)}, u32[]{:S(2)}) collective-permute-start(f32[56,256]{1,0:T(8,128)S(1)} %get-tuple-element.37), channel_id=1, source_target_pairs={{0,6},{1,7},{2,0},{3,1},{4,2},{5,3},{6,4},{7,5},{8,14},{9,15},{10,... | collective-permute-start | bytes 172040 | tf_op jit(solution)/shard_map/ppermute | solution.py:356
  91.2 1.5 %collective-permute-start.22 = (f32[56,256]{1,0:T(8,128)S(1)}, f32[56,256]{1,0:T(8,128)S(1)}, u32[]{:S(2)}, u32[]{:S(2)}) collective-permute-start(f32[56,256]{1,0:T(8,128)S(1)} %get-tuple-element.38), channel_id=1, source_target_pairs={{0,7},{1,6},{2,1},{3,0},{4,3},{5,2},{6,5},{7,4},{8,15},{9,14},{10,... | collective-permute-start | bytes 172040 | tf_op jit(solution)/shard_map/ppermute | solution.py:356
  97.5 1.4 %collective-permute-start.26 = (f32[224,256]{1,0:T(8,128)}, f32[224,256]{1,0:T(8,128)S(1)}, u32[]{:S(2)}, u32[]{:S(2)}) collective-permute-start(f32[224,256]{1,0:T(8,128)} %shard_map.62.mine_ref), channel_id=1, source_target_pairs={{0,1},{1,0},{2,3},{3,2},{4,5},{5,4},{6,7},{7,6},{8,9},{9,8},{10,11... | collective-permute-start | bytes 688136 | tf_op jit(solution)/shard_map/ppermute | solution.py:258
  99.3 5.5 %collective-permute-done.26.other_ref = f32[224,256]{1,0:T(8,128)S(1)} collective-permute-done((f32[224,256]{1,0:T(8,128)}, f32[224,256]{1,0:T(8,128)S(1)}, u32[]{:S(2)}, u32[]{:S(2)}) %collective-permute-start.26) | collective-permute-done | bytes 229408 | tf_op jit(solution)/shard_map/ppermute | solution.py:258
  106.3 2.3 %collective-permute-start.27 = (f32[128,256]{1,0:T(8,128)S(1)}, f32[128,256]{1,0:T(8,128)S(1)}, u32[]{:S(2)}, u32[]{:S(2)}) collective-permute-start(f32[128,256]{1,0:T(8,128)S(1)} %get-tuple-element.43), channel_id=1, source_target_pairs={{0,2},{1,3},{2,4},{3,5},{4,6},{5,7},{6,0},{7,1},{8,10},{9,11},{10,... | collective-permute-start | bytes 393224 | tf_op jit(solution)/shard_map/ppermute | solution.py:377
  109.6 1.5 %collective-permute-start.29 = (f32[128,256]{1,0:T(8,128)S(1)}, f32[128,256]{1,0:T(8,128)S(1)}, u32[]{:S(2)}, u32[]{:S(2)}) collective-permute-start(f32[128,256]{1,0:T(8,128)S(1)} %get-tuple-element.45), channel_id=1, source_target_pairs={{0,6},{1,7},{2,0},{3,1},{4,2},{5,3},{6,4},{7,5},{8,14},{9,15},{10,... | collective-permute-start | bytes 393224 | tf_op jit(solution)/shard_map/ppermute | solution.py:377
  111.0 3.7 %collective-permute-done.27 = f32[128,256]{1,0:T(8,128)S(1)} collective-permute-done((f32[128,256]{1,0:T(8,128)S(1)}, f32[128,256]{1,0:T(8,128)S(1)}, u32[]{:S(2)}, u32[]{:S(2)}) %collective-permute-start.27) | collective-permute-done | bytes 131104 | tf_op jit(solution)/shard_map/ppermute | solution.py:377
  114.7 3.4 %collective-permute-done.28 = f32[128,256]{1,0:T(8,128)S(1)} collective-permute-done((f32[128,256]{1,0:T(8,128)S(1)}, f32[128,256]{1,0:T(8,128)S(1)}, u32[]{:S(2)}, u32[]{:S(2)}) %collective-permute-start.28) | collective-permute-done | bytes 131104 | tf_op jit(solution)/shard_map/ppermute | solution.py:377
  (124 shorter events, 48.5 us)
Async XLA Ops:
  0.6 14.7 %collective-permute-start.1 = (f32[224,256]{1,0:T(8,128)}, f32[224,256]{1,0:T(8,128)S(1)}, u32[]{:S(2)}, u32[]{:S(2)}) collective-permute-start(f32[224,256]{1,0:T(8,128)} %refs_0_.1), channel_id=1, source_target_pairs={{0,2},{1,3},{2,4},{3,5},{4,6},{5,7},{8,10},{9,11},{10,12},{11,13},... | collective-permute-start | bytes 688136 | tf_op jit(solution)/shard_map/ppermute | solution.py:280
  10.8 41.8 %collective-permute-start.13 = (f32[2016,128]{1,0:T(8,128)S(1)}, f32[2016,128]{1,0:T(8,128)S(1)}, u32[]{:S(2)}, u32[]{:S(2)}) collective-permute-start(f32[2016,128]{1,0:T(8,128)S(1)} %shard_map.59.refs_14_), channel_id=1, source_target_pairs={{0,8},{8,0},{16,24},{24,16},{1,9},{9,1},{17,25},{25,17},{2,10},{10... | collective-permute-start | bytes 3096584 | tf_op jit(solution)/shard_map/ppermute | solution.py:258
  10.9 62.2 %collective-permute-start.14 = (f32[2016,128]{1,0:T(8,128)S(1)}, f32[2016,128]{1,0:T(8,128)}, u32[]{:S(2)}, u32[]{:S(2)}) collective-permute-start(f32[2016,128]{1,0:T(8,128)S(1)} %shard_map.59.refs_14_), channel_id=1, source_target_pairs={{0,16},{8,24},{16,0},{24,8},{1,17},{9,25},{17,1},{25,9},{2,18},{10... | collective-permute-start | bytes 3096584 | tf_op jit(solution)/shard_map/ppermute | solution.py:338
  12.5 9.6 %collective-permute-start.2 = (f32[224,256]{1,0:T(8,128)S(1)}, f32[224,256]{1,0:T(8,128)S(1)}, u32[]{:S(2)}, u32[]{:S(2)}) collective-permute-start(f32[224,256]{1,0:T(8,128)S(1)} %copy-done.4), channel_id=1, source_target_pairs={{2,0},{3,1},{4,2},{5,3},{6,4},{7,5},{10,8},{11,9},{12,10},{13,11},... | collective-permute-start | bytes 688136 | tf_op jit(solution)/shard_map/ppermute | solution.py:280
  13.7 9.6 %collective-permute-start = (f32[224,256]{1,0:T(8,128)S(1)}, f32[224,256]{1,0:T(8,128)S(1)}, u32[]{:S(2)}, u32[]{:S(2)}) collective-permute-start(f32[224,256]{1,0:T(8,128)S(1)} %copy-done.4), channel_id=1, source_target_pairs={{0,1},{1,0},{2,3},{3,2},{4,5},{5,4},{6,7},{7,6},{8,9},{9,8},{10,11... | collective-permute-start | bytes 688136 | tf_op jit(solution)/shard_map/ppermute | solution.py:279
  15.3 10.1 %collective-permute-start.5 = (f32[224,256]{1,0:T(8,128)S(1)}, f32[224,256]{1,0:T(8,128)S(1)}, u32[]{:S(2)}, u32[]{:S(2)}) collective-permute-start(f32[224,256]{1,0:T(8,128)S(1)} %collective-permute-done.1.refs_2_), channel_id=1, source_target_pairs={{2,4},{3,5},{4,6},{5,7},{10,12},{11,13},{12,14},{13,15},{18,20},{1... | collective-permute-start | bytes 688136 | tf_op jit(solution)/shard_map/ppermute | solution.py:280
  22.0 8.8 %collective-permute-start.6 = (f32[224,256]{1,0:T(8,128)S(1)}, f32[224,256]{1,0:T(8,128)S(1)}, u32[]{:S(2)}, u32[]{:S(2)}) collective-permute-start(f32[224,256]{1,0:T(8,128)S(1)} %collective-permute-done.2.refs_3_), channel_id=1, source_target_pairs={{2,0},{3,1},{4,2},{5,3},{10,8},{11,9},{12,10},{13,11},{18,16},{19,... | collective-permute-start | bytes 688136 | tf_op jit(solution)/shard_map/ppermute | solution.py:280
  24.0 7.5 %collective-permute-start.3 = (f32[224,256]{1,0:T(8,128)S(1)}, f32[224,256]{1,0:T(8,128)S(1)}, u32[]{:S(2)}, u32[]{:S(2)}) collective-permute-start(f32[224,256]{1,0:T(8,128)S(1)} %collective-permute-done.1.refs_2_), channel_id=1, source_target_pairs={{2,3},{3,2},{4,5},{5,4},{6,7},{7,6},{10,11},{11,10},{12,13},{13,12... | collective-permute-start | bytes 688136 | tf_op jit(solution)/shard_map/ppermute | solution.py:279
  25.4 8.8 %collective-permute-start.4 = (f32[224,256]{1,0:T(8,128)S(1)}, f32[224,256]{1,0:T(8,128)S(1)}, u32[]{:S(2)}, u32[]{:S(2)}) collective-permute-start(f32[224,256]{1,0:T(8,128)S(1)} %collective-permute-done.2.refs_3_), channel_id=1, source_target_pairs={{0,1},{1,0},{2,3},{3,2},{4,5},{5,4},{8,9},{9,8},{10,11},{11,10},{1... | collective-permute-start | bytes 688136 | tf_op jit(solution)/shard_map/ppermute | solution.py:279
  32.2 9.9 %collective-permute-start.10 = (f32[224,256]{1,0:T(8,128)S(1)}, f32[224,256]{1,0:T(8,128)S(1)}, u32[]{:S(2)}, u32[]{:S(2)}) collective-permute-start(f32[224,256]{1,0:T(8,128)S(1)} %collective-permute-done.6.refs_7_), channel_id=1, source_target_pairs={{2,0},{3,1},{10,8},{11,9},{18,16},{19,17},{26,24},{27,25}} | collective-permute-start | bytes 688136 | tf_op jit(solution)/shard_map/ppermute | solution.py:280
  34.9 8.6 %collective-permute-start.7 = (f32[224,256]{1,0:T(8,128)S(1)}, f32[224,256]{1,0:T(8,128)S(1)}, u32[]{:S(2)}, u32[]{:S(2)}) collective-permute-start(f32[224,256]{1,0:T(8,128)S(1)} %collective-permute-done.5.refs_6_), channel_id=1, source_target_pairs={{4,5},{5,4},{6,7},{7,6},{12,13},{13,12},{14,15},{15,14},{20,21},{2... | collective-permute-start | bytes 688136 | tf_op jit(solution)/shard_map/ppermute | solution.py:279
  36.3 13.0 %collective-permute-start.8 = (f32[224,256]{1,0:T(8,128)S(1)}, f32[224,256]{1,0:T(8,128)S(1)}, u32[]{:S(2)}, u32[]{:S(2)}) collective-permute-start(f32[224,256]{1,0:T(8,128)S(1)} %collective-permute-done.6.refs_7_), channel_id=1, source_target_pairs={{0,1},{1,0},{2,3},{3,2},{8,9},{9,8},{10,11},{11,10},{16,17},{17,16... | collective-permute-start | bytes 688136 | tf_op jit(solution)/shard_map/ppermute | solution.py:279
  42.2 7.8 %collective-permute-start.11 = (f32[224,256]{1,0:T(8,128)S(1)}, f32[224,256]{1,0:T(8,128)S(1)}, u32[]{:S(2)}, u32[]{:S(2)}) collective-permute-start(f32[224,256]{1,0:T(8,128)S(1)} %collective-permute-done.9.refs_10_), channel_id=1, source_target_pairs={{6,7},{7,6},{14,15},{15,14},{22,23},{23,22},{30,31},{31,30}} | collective-permute-start | bytes 688136 | tf_op jit(solution)/shard_map/ppermute | solution.py:279
  44.2 8.3 %collective-permute-start.12 = (f32[224,256]{1,0:T(8,128)S(1)}, f32[224,256]{1,0:T(8,128)}, u32[]{:S(2)}, u32[]{:S(2)}) collective-permute-start(f32[224,256]{1,0:T(8,128)S(1)} %collective-permute-done.10.refs_11_), channel_id=1, source_target_pairs={{0,1},{1,0},{8,9},{9,8},{16,17},{17,16},{24,25},{25,24}} | collective-permute-start | bytes 688136 | tf_op jit(solution)/shard_map/ppermute | solution.py:279
  75.1 12.3 %collective-permute-start.24 = (f32[448,128]{1,0:T(8,128)S(1)}, f32[448,128]{1,0:T(8,128)S(1)}, u32[]{:S(2)}, u32[]{:S(2)}) collective-permute-start(f32[448,128]{1,0:T(8,128)S(1)} %slice_select_fusion.refs_0_), channel_id=1, source_target_pairs={{0,16},{8,24},{16,0},{24,8},{1,17},{9,25},{17,1},{25,9},{2,18},{10... | collective-permute-start | bytes 688136 | tf_op jit(solution)/shard_map/ppermute | solution.py:264
  81.5 7.4 %collective-permute-start.16 = (f32[56,256]{1,0:T(8,128)S(1)}, f32[56,256]{1,0:T(8,128)S(1)}, u32[]{:S(2)}, u32[]{:S(2)}) collective-permute-start(f32[56,256]{1,0:T(8,128)S(1)} %get-tuple-element.32), channel_id=1, source_target_pairs={{0,1},{1,0},{2,3},{3,2},{4,5},{5,4},{6,7},{7,6},{8,9},{9,8},{10,11... | collective-permute-start | bytes 172040 | tf_op jit(solution)/shard_map/ppermute | solution.py:356
  83.6 7.7 %collective-permute-start.17 = (f32[56,256]{1,0:T(8,128)S(1)}, f32[56,256]{1,0:T(8,128)S(1)}, u32[]{:S(2)}, u32[]{:S(2)}) collective-permute-start(f32[56,256]{1,0:T(8,128)S(1)} %get-tuple-element.33), channel_id=1, source_target_pairs={{0,2},{1,3},{2,4},{3,5},{4,6},{5,7},{6,0},{7,1},{8,10},{9,11},{10,... | collective-permute-start | bytes 172040 | tf_op jit(solution)/shard_map/ppermute | solution.py:356
  83.6 9.2 %collective-permute-start.18 = (f32[56,256]{1,0:T(8,128)S(1)}, f32[56,256]{1,0:T(8,128)S(1)}, u32[]{:S(2)}, u32[]{:S(2)}) collective-permute-start(f32[56,256]{1,0:T(8,128)S(1)} %get-tuple-element.34), channel_id=1, source_target_pairs={{0,3},{1,2},{2,5},{3,4},{4,7},{5,6},{6,1},{7,0},{8,11},{9,10},{10,... | collective-permute-start | bytes 172040 | tf_op jit(solution)/shard_map/ppermute | solution.py:356
  85.5 8.5 %collective-permute-start.19 = (f32[56,256]{1,0:T(8,128)S(1)}, f32[56,256]{1,0:T(8,128)S(1)}, u32[]{:S(2)}, u32[]{:S(2)}) collective-permute-start(f32[56,256]{1,0:T(8,128)S(1)} %get-tuple-element.35), channel_id=1, source_target_pairs={{0,4},{1,5},{2,6},{3,7},{4,0},{5,1},{6,2},{7,3},{8,12},{9,13},{10,... | collective-permute-start | bytes 172040 | tf_op jit(solution)/shard_map/ppermute | solution.py:356
  87.5 7.8 %collective-permute-start.20 = (f32[56,256]{1,0:T(8,128)S(1)}, f32[56,256]{1,0:T(8,128)S(1)}, u32[]{:S(2)}, u32[]{:S(2)}) collective-permute-start(f32[56,256]{1,0:T(8,128)S(1)} %get-tuple-element.36), channel_id=1, source_target_pairs={{0,5},{1,4},{2,7},{3,6},{4,1},{5,0},{6,3},{7,2},{8,13},{9,12},{10,... | collective-permute-start | bytes 172040 | tf_op jit(solution)/shard_map/ppermute | solution.py:356
  97.5 7.3 %collective-permute-start.26 = (f32[224,256]{1,0:T(8,128)}, f32[224,256]{1,0:T(8,128)S(1)}, u32[]{:S(2)}, u32[]{:S(2)}) collective-permute-start(f32[224,256]{1,0:T(8,128)} %shard_map.62.mine_ref), channel_id=1, source_target_pairs={{0,1},{1,0},{2,3},{3,2},{4,5},{5,4},{6,7},{7,6},{8,9},{9,8},{10,11... | collective-permute-start | bytes 688136 | tf_op jit(solution)/shard_map/ppermute | solution.py:258
  106.3 8.4 %collective-permute-start.27 = (f32[128,256]{1,0:T(8,128)S(1)}, f32[128,256]{1,0:T(8,128)S(1)}, u32[]{:S(2)}, u32[]{:S(2)}) collective-permute-start(f32[128,256]{1,0:T(8,128)S(1)} %get-tuple-element.43), channel_id=1, source_target_pairs={{0,2},{1,3},{2,4},{3,5},{4,6},{5,7},{6,0},{7,1},{8,10},{9,11},{10,... | collective-permute-start | bytes 393224 | tf_op jit(solution)/shard_map/ppermute | solution.py:377
  108.6 9.5 %collective-permute-start.28 = (f32[128,256]{1,0:T(8,128)S(1)}, f32[128,256]{1,0:T(8,128)S(1)}, u32[]{:S(2)}, u32[]{:S(2)}) collective-permute-start(f32[128,256]{1,0:T(8,128)S(1)} %get-tuple-element.44), channel_id=1, source_target_pairs={{0,4},{1,5},{2,6},{3,7},{4,0},{5,1},{6,2},{7,3},{8,12},{9,13},{10,... | collective-permute-start | bytes 393224 | tf_op jit(solution)/shard_map/ppermute | solution.py:377
  109.6 8.5 %collective-permute-start.29 = (f32[128,256]{1,0:T(8,128)S(1)}, f32[128,256]{1,0:T(8,128)S(1)}, u32[]{:S(2)}, u32[]{:S(2)}) collective-permute-start(f32[128,256]{1,0:T(8,128)S(1)} %get-tuple-element.45), channel_id=1, source_target_pairs={{0,6},{1,7},{2,0},{3,1},{4,2},{5,3},{6,4},{7,5},{8,14},{9,15},{10,... | collective-permute-start | bytes 393224 | tf_op jit(solution)/shard_map/ppermute | solution.py:377
  (44 other events, 147.9 us)

commit v3 on v2

--- a/solution.py
+++ b/solution.py
@@ -109,33 +109,41 @@
     return dot(left, jnp.concatenate([uh, ul, uh], axis=0))
 
 
-def prepare_kernel(direct, slots, nr, offsets, n_first, owners, structure_ref, turned_ref, *refs):
-    uh_ref, ul_ref, part_ref, to_ref, from_ref, us_ref = refs[-6:]
-    m, nc = turned_ref.shape
-    w = uh_ref.shape[2]
-    n = m * nc
+def prepare_kernel(direct, slots, owners, structure_ref, *refs):
+    pair_ref = None
+    if direct:
+        pair_ref, refs = refs[-2], refs[:-2] + refs[-1:]
+    uh_ref, ul_ref, part_ref, to_ref, us_ref = refs[-5:]
+    nr, _, w = uh_ref.shape
+    nc = to_ref.shape[0] // slots
+    n_u = nc if direct else 1
+    u_refs, first_refs = refs[:n_u], refs[n_u:-5]
+    n = structure_ref.shape[1]
+    m = n // nc
     c = lax.axis_index("pcol")
     r = lax.axis_index("prow")
     z = c // 2
-    u_refs = refs[: -6 - n_first] if n_first else refs[:-6]
-    first_refs = refs[-6 - n_first : -6]
     rows = part_ref.shape[0]
     names = structure_ref[...]
 
-    def place(owner, u_ref):
-        u = u_ref[...]
+    def place(owner, u):
         if w % LANES:
             u = jnp.concatenate([u, jnp.zeros((m, LANES - w % LANES), jnp.float32)], axis=1)
         for i in range(us_ref.shape[0]):
-            us_ref[i, pl.ds(owner, m, stride=nc), :] = u[:, LANES * i : LANES * (i + 1)]
-
-    if direct:
-        for (dz, flip), u_ref in zip(offsets, u_refs):
-            pl.when((z + dz >= 0) & (z + dz < nc // 2))(
-                functools.partial(place, jnp.bitwise_xor(c + 2 * dz, flip), u_ref)
-            )
-    else:
-        each(u_refs, None, place)
+            us_ref[i, pl.ds(owner, u.shape[0], stride=nc), :] = u[:, LANES * i : LANES * (i + 1)]
+
+    if direct:
+        lane = pl.multiple_of((c & 1) * (w // 2), LANES)
+        pair_ref[:m, :] = u_refs[0][:, pl.ds(lane, w // 2)]
+        for owner, u_ref in zip(ring_owners(nc, c), u_refs):
+            place(owner, u_ref[...])
+
+            @pl.when(owner == jnp.bitwise_xor(c, 1))
+            def _():
+                pair_ref[m:, :] = u_ref[:, pl.ds(lane, w // 2)]
+
+    else:
+        pl.loop(0, nc)(lambda k: place(k, u_refs[0][k]))
     us_ref[:, n:, :] = jnp.zeros((us_ref.shape[0], us_ref.shape[1] - n, LANES), jnp.float32)
 
     width = rows * 2
@@ -168,27 +176,13 @@
     member = jnp.sum(one_hot(names == row), axis=1, keepdims=True)
     turn = rank & (nc - 1)
     ahead = (count(names < c * rows) - turn + nc - 1) >> lg
-    block = turn
-    if direct:
-        block = 2 * (((turn >> 1) - z) & (nc // 2 - 1)) + ((turn ^ c) & 1)
+    block = turn >> 1
+    if direct:
+        block = (block - z) & (nc // 2 - 1)
+    block = 2 * block + (turn & 1)
     slot = jnp.where(member > 0.5, block * slots + (rank >> lg) - ahead, -1)
     at = lax.broadcasted_iota(jnp.int32, (rows, nc * slots), 1)
     to_ref[...] = one_hot(at == slot).T.astype(BF16)
-
-    lane = lax.broadcasted_iota(jnp.int32, (m, nc), 1)
-    mine = jnp.sum(jnp.where(lane == c, turned_ref[...], 0).astype(jnp.float32), axis=1, keepdims=True)
-    source = jnp.zeros((m, 1), jnp.int32)
-    before = jnp.zeros((m, 1), jnp.int32)
-    for k in range(1, nc):
-        less = mine < float(k * rows)
-        source = source + jnp.where(less, 0, 1)
-        before = jnp.where(less, before, count(less))
-    block = source
-    if direct:
-        block = 2 * ((z - (source >> 1)) & (nc // 2 - 1)) + ((source ^ c) & 1)
-    slot = block * slots + lax.broadcasted_iota(jnp.int32, (m, 1), 0) - before
-    at = lax.broadcasted_iota(jnp.int32, (m, nc * slots), 1)
-    from_ref[...] = one_hot(at == slot).astype(BF16)
 
 
 def image_kernel(n_out, owners, uh_ref, ul_ref, part_ref, to_ref, *refs):
@@ -208,26 +202,50 @@
         out_ref[...] = image[size * k : size * (k + 1)]
 
 
-def pick_kernel(from_ref, *refs):
-    got = [ref[...] for ref in refs[:-1]]
-    got = jnp.concatenate(got, axis=0) if len(got) > 1 else got[0]
-    refs[-1][...] = -pick_rows(from_ref[...], got)
-
-
-def turn_kernel(direct, owners, *refs):
-    high_ref, low_ref = refs[-2:]
-    z = lax.axis_index("pcol") // 2
+def turn_kernel(direct, slots, owners, structure_ref, *refs):
+    from_ref, high_ref, low_ref = refs[-3:]
+    nz = high_ref.shape[0]
+    nc = 2 * nz
+    rows = slots * nc
+    n = structure_ref.shape[1]
+    m = n // nc
+    names = structure_ref[...]
+    c = lax.axis_index("pcol")
+    z = c // 2
 
     def put(owner, u_ref):
-        where = ((owner - z) & (high_ref.shape[0] - 1)) if direct else owner
+        where = ((owner - z) & (nz - 1)) if direct else owner
         high_ref[where], low_ref[where] = split(u_ref[...].T)
 
-    each(refs[:-2], owners(lax.axis_index("prow")) if direct else None, put)
-
-
-def correction_kernel(high_ref, low_ref, mine_ref, other_ref, *out_refs):
-    sh, sl = split(jnp.concatenate([mine_ref[...], other_ref[...]], axis=0))
+    each(refs[:-3], owners(lax.axis_index("prow")) if direct else None, put)
+
+    own = lax.broadcasted_iota(jnp.int32, (m, n), 1) - nc * lax.broadcasted_iota(jnp.int32, (m, n), 0)
+    at = lax.broadcasted_iota(jnp.int32, (m, 2 * rows), 1)
+    for half, column in enumerate((c, jnp.bitwise_xor(c, 1))):
+        mine = jnp.where(own == column, names, 0).astype(jnp.float32)
+        mine = jnp.sum(mine, axis=1, keepdims=True)
+        source = jnp.zeros((m, 1), jnp.int32)
+        before = jnp.zeros((m, 1), jnp.int32)
+        for k in range(1, nc):
+            less = mine < float(k * rows)
+            source = source + jnp.where(less, 0, 1)
+            before = jnp.where(less, before, count(less))
+        block = source >> 1
+        if direct:
+            block = (z - block) & (nz - 1)
+        block = 2 * (block + nz * ((source ^ c) & 1)) + (column & 1)
+        slot = block * slots + lax.broadcasted_iota(jnp.int32, (m, 1), 0) - before
+        from_ref[m * half : m * (half + 1), :] = one_hot(at == slot).astype(BF16)
+
+
+def correction_kernel(from_ref, high_ref, low_ref, *refs):
     nz = high_ref.shape[0]
+    n_in = 2 if len(refs) == 4 else 2 * nz
+    got = jnp.concatenate([ref[...] for ref in refs[:n_in]], axis=0)
+    sj_ref, out_refs = refs[n_in], refs[n_in + 1 :]
+    both = -pick_rows(from_ref[...], got)
+    sj_ref[...] = both[: sj_ref.shape[0]]
+    sh, sl = split(both)
 
     def term(t):
         return dot(high_ref[t], sh) + (dot(high_ref[t], sl) + dot(low_ref[t], sh))
@@ -274,18 +292,26 @@
     return out
 
 
-def line_gather(u, nc):
-    nz = nc // 2
-    across = lambda v, ks: lax.ppermute(v, "pcol", [(2 * k + x, 2 * k + 1 - x) for k in ks for x in range(2)])
-    along = lambda v, ks, by: lax.ppermute(v, "pcol", [(2 * k + x, 2 * (k + by) + x) for k in ks for x in range(2)])
-    offsets, blocks = [(0, 0), (0, 1)], [u, across(u, range(nz))]
+def ring_gather(u, nc):
+    ring = [2 * z for z in range(nc // 2)] + [2 * z + 1 for z in reversed(range(nc // 2))]
+    pairs = [(ring[q - 1], ring[q]) for q in range(nc)]
+    back = [(b, a) for a, b in pairs]
+    blocks = [u]
     up = down = u
-    for t in range(1, nz):
-        up = along(up, range(t - 1, nz - 1), 1)
-        down = along(down, range(1, nz - t + 1), -1)
-        offsets += [(-t, 0), (t, 0), (-t, 1), (t, 1)]
-        blocks += [up, down, across(up, range(t, nz)), across(down, range(0, nz - t))]
-    return offsets, blocks
+    for step in range(1, nc // 2):
+        up, down = lax.ppermute(up, "pcol", pairs), lax.ppermute(down, "pcol", back)
+        blocks += [up, down]
+    return blocks + [lax.ppermute(up, "pcol", pairs)]
+
+
+def ring_owners(nc, c):
+    q = jnp.where((c & 1) == 0, c >> 1, nc - 1 - (c >> 1))
+    out = []
+    for k in range(nc):
+        step = (k + 1) // 2
+        at = (q - step if k % 2 else q + step) & (nc - 1)
+        out.append(jnp.where(at < nc // 2, 2 * at, 2 * (nc - 1 - at) + 1))
+    return out
 
 
 def per_device(sigma_top, structure, u_panel, d_term):
@@ -294,20 +320,15 @@
     nz = nc // 2
     rows, cols = sigma_top.shape
     m, w = u_panel.shape
+    wd = w // 2
     n = structure.shape[0]
     slots = -(-rows // nc)
     direct = nc <= 8
-    n_first = 2 if direct else 0
     names = structure.reshape(1, n)
     steps = 4
     part = rows // steps
-
-    if direct:
-        offsets, u_blocks = line_gather(u_panel, nc)
-        partner = u_blocks[1]
-    else:
-        offsets, u_blocks = None, [lax.all_gather(u_panel, "pcol")]
-        partner = swap(u_panel, "pcol", nc)
+    groups = [[2 * k + x for k in range(nz)] for x in range(2)]
+    owners = functools.partial(relative_owners, nr)
 
     chosen = call(
         select_kernel,
@@ -319,15 +340,18 @@
         scratch_shapes=[pltpu.VMEM((cols, WIDE), BF16)],
     )
     near = [chosen, swap(chosen, "prow", nr)] if direct else []
-    owners = functools.partial(relative_owners, nr)
-    uh, ul, image, to, source = call(
-        functools.partial(
-            prepare_kernel, direct, slots, nr, offsets, n_first, lambda r: owners(r)[:2]
-        ),
-        [bf16(nr, WIDE, w), bf16(nr, WIDE, w), f32(rows, w), bf16(nc * slots, rows), bf16(m, nc * slots)],
+    if direct:
+        u_all = ring_gather(u_panel, nc)
+    else:
+        u_all = [lax.all_gather(u_panel, "pcol")]
+    out = [bf16(nr, WIDE, w), bf16(nr, WIDE, w), f32(rows, w), bf16(nc * slots, rows)]
+    if direct:
+        out.append(f32(2 * m, wd))
+    uh, ul, image, to, *pair = call(
+        functools.partial(prepare_kernel, direct, slots, lambda r: owners(r)[:2]),
+        out,
         names,
-        structure.reshape(m, nc),
-        *u_blocks,
+        *u_all,
         *near,
         scratch_shapes=[pltpu.VMEM((-(-w // LANES), n + CAP + 8, LANES), jnp.float32)],
     )
@@ -338,9 +362,14 @@
             far = lax.ppermute(chosen, "prow", [(k, (k + 2 * t) % nr) for k in range(nr)])
             far, image = lax.optimization_barrier((far, image))
             later += [far, swap(far, "prow", nr)]
+        pair, later[0] = lax.optimization_barrier((pair[0], later[0]))
+        pairs = spread(pair, nr)
     else:
         later = [lax.all_gather(chosen, "prow")]
-    n_out = nc if direct else 1
+        pair = jnp.concatenate([u_panel, swap(u_panel, "pcol", nc)], axis=0)
+        pair = jnp.where(jnp.bitwise_and(c, 1) == 0, pair[:, :wd], pair[:, wd:])
+        pairs = [lax.all_gather(pair, "prow")]
+    n_out = nz if direct else 1
     sent = call(
         functools.partial(image_kernel, n_out, (lambda r: owners(r)[2:]) if direct else None),
         [f32(nc * slots // n_out, w)] * n_out,
@@ -352,33 +381,28 @@
     )
     if direct:
         got = [sent[0]]
-        for k in range(1, nc):
-            got.append(lax.ppermute(sent[k], "pcol", [(i, ((i + 2 * (k // 2)) % nc) ^ (k % 2)) for i in range(nc)]))
-    else:
-        got = [lax.all_to_all(sent[0], "pcol", split_axis=0, concat_axis=0, tiled=True)]
-    sigma_sj = call(pick_kernel, f32(m, w), source, *got)
-
-    wd = w // 2
-    pair = jnp.concatenate([u_panel, partner], axis=0)
-    pair = jnp.where(jnp.bitwise_and(c, 1) == 0, pair[:, :wd], pair[:, wd:])
-    if direct:
-        pair, later[0] = lax.optimization_barrier((pair, later[0]))
-        pairs = spread(pair, nr)
-    else:
-        pairs = [lax.all_gather(pair, "prow")]
-    turned = call(
-        functools.partial(turn_kernel, direct, owners), [bf16(nz, wd, 2 * m), bf16(nz, wd, 2 * m)], *pairs
+        for t in range(1, nz):
+            got.append(lax.ppermute(sent[t], "pcol", [(k, (k + 2 * t) % nc) for k in range(nc)]))
+    else:
+        blocks = sent[0].reshape(nz, 2 * slots, w)
+        blocks = lax.all_to_all(blocks, "pcol", split_axis=0, concat_axis=0, axis_index_groups=groups, tiled=True)
+        got = [blocks.reshape(nc * slots, w)]
+    got = got + [swap(v, "pcol", nc) for v in got]
+
+    source, high, low = call(
+        functools.partial(turn_kernel, direct, slots, owners),
+        [bf16(2 * m, 2 * nc * slots), bf16(nz, wd, 2 * m), bf16(nz, wd, 2 * m)],
+        names,
+        *pairs,
     )
-    other = swap(sigma_sj, "pcol", nc)
-    if direct:
-        terms = call(correction_kernel, [f32(wd, w)] * nz, *turned, sigma_sj, other)
+    parts = [f32(wd, w)] * nz if direct else [f32(nz, wd, w)]
+    sigma_sj, *terms = call(correction_kernel, [f32(m, w)] + parts, source, high, low, *got)
+    if direct:
         total = terms[0]
         for t in range(1, nz):
             total = total + lax.ppermute(terms[t], "pcol", [(k, (k + 2 * t) % nc) for k in range(nc)])
     else:
-        terms = call(correction_kernel, f32(nz, wd, w), *turned, sigma_sj, other)
-        groups = [[2 * k + x for k in range(nz)] for x in range(2)]
-        terms = lax.all_to_all(terms, "pcol", split_axis=0, concat_axis=0, axis_index_groups=groups, tiled=True)
+        terms = lax.all_to_all(terms[0], "pcol", split_axis=0, concat_axis=0, axis_index_groups=groups, tiled=True)
         total = jnp.sum(terms, axis=0)
     return sigma_sj, d_term - total
 

time: 120 us -> 85.8 us (0.71)
  local copies, waits for them, and re-layouts: 31 us -> 2.13 us
  starting transfers between devices: 44.3 us -> 27.2 us
  waiting for transfers between devices: 28.3 us -> 41.1 us
    unnamed x77 -> x6, local copies, waits for them, and re-layouts: 29.2 us -> 1.43 us
    ppermute x20 -> x10, starting transfers between devices: 35.9 us -> 13.2 us  [the longest x3 5.57 us: per_device(): lax.ppermute(sent[t], 'pcol', [(k, (k + 2 * t) % nc) for k in range(nc)])]
    ppermute x20 -> x10, waiting for transfers between devices: 15.5 us -> 22.8 us  [the longest x3 14.5 us: ring_gather(): lax.ppermute(up, 'pcol', pairs)]
    ppermute x1, waiting for transfers between devices: 0.01 us -> 7.19 us  [spread(): lax.ppermute(v, 'prow', [(k, (k + 2 * t) % size) for k in range(size)])]
    ppermute x5 -> x8, starting transfers between devices: 1.5 us -> 5.77 us  [swap(): return lax.ppermute(v, axis, [(k, k ^ 1) for k in range(size)])]
    ppermute x5 -> x8, waiting for transfers between devices: 5.74 us -> 3.93 us  [swap(): return lax.ppermute(v, axis, [(k, k ^ 1) for k in range(size)])]
    pallas_call x6 -> x5, Pallas kernels: 13.6 us -> 13.4 us  [call(): pl.pallas_call(kernel, out_shape=out_shape, out_specs=[VMEM] * len(out_sh...]
  transfers between devices with their start and end apart: 30 -> 23, of which waited for: 13 -> 11; matrix products, arithmetic and copies ran while one was open for 2% -> 0% of each run, Pallas kernels for 11% -> 9%
where the time goes in v3:
time: 85.8 us; the launch traced here: 85.2 us
  waiting for transfers between devices  41.1 us (48%)
  starting transfers between devices  27.2 us (32%)
  Pallas kernels  13.4 us (16%)
  local copies, waits for them, and re-layouts  2.13 us (2%)
    ppermute x3, waiting for transfers between devices, ring_gather(): lax.ppermute(up, 'pcol', pairs)  14.5 us
    pallas_call x5, Pallas kernels, call(): pl.pallas_call(kernel, out_shape=out_shape, out_specs=[VMEM] * len(out_sh...  13.4 us
    ppermute x3, waiting for transfers between devices, per_device(): lax.ppermute(terms[t], 'pcol', [(k, (k + 2 * t) % nc) for k in range(nc)])  7.21 us
    ppermute x1, waiting for transfers between devices, spread(): lax.ppermute(v, 'prow', [(k, (k + 2 * t) % size) for k in range(size)])  7.19 us
    ppermute x8, starting transfers between devices, swap(): return lax.ppermute(v, axis, [(k, k ^ 1) for k in range(size)])  5.77 us
    ppermute x3, starting transfers between devices, per_device(): lax.ppermute(sent[t], 'pcol', [(k, (k + 2 * t) % nc) for k in range(nc)])  5.57 us
    ppermute x3, starting transfers between devices, per_device(): lax.ppermute(terms[t], 'pcol', [(k, (k + 2 * t) % nc) for k in range(nc)])  4.93 us
    ppermute x3, starting transfers between devices, ring_gather(): lax.ppermute(up, 'pcol', pairs)  4.73 us
  transfers between devices with their start and end apart: 23, of which 11 were waited for; matrix products, arithmetic and copies ran while one was open for 0% of the time, Pallas kernels for 9%

profile of v3, /device:TPU:0, one launch (start us, length us, event | category | flops | bytes accessed | tf_op | source)
XLA Modules:
  0.0 85.2 jit_solution(10172969343643714315)
XLA Ops:
  2.8 3.1 %shard_map.59.refs_8_ = f32[2016,128]{1,0:T(8,128)S(1)} custom-call(s32[1,1792]{1,0:T(1,128)S(1)} %reshape.7.structure_ref, f32[448,896]{1,0:T(8,128)S(1)} %copy-done), custom_call_target="tpu_custom_call" | custom-call | tf_op jit(solution)/shard_map/pallas_call | solution.py:266
  6.4 2.6 %collective-permute-start.8 = (f32[2016,128]{1,0:T(8,128)S(1)}, f32[2016,128]{1,0:T(8,128)S(1)}, u32[]{:S(2)}, u32[]{:S(2)}) collective-permute-start(f32[2016,128]{1,0:T(8,128)S(1)} %shard_map.59.refs_8_), channel_id=1, source_target_pairs={{0,16},{8,24},{16,0},{24,8},{1,17},{9,25},{17,1},{25,9},{2,18},{10... | collective-permute-start | bytes 3096584 | tf_op jit(solution)/shard_map/ppermute | solution.py:362
  8.9 1.6 %collective-permute-start = (f32[224,256]{1,0:T(8,128)S(1)}, f32[224,256]{1,0:T(8,128)S(1)}, u32[]{:S(2)}, u32[]{:S(2)}) collective-permute-start(f32[224,256]{1,0:T(8,128)S(1)} %copy-done.1), channel_id=1, source_target_pairs={{1,0},{0,2},{2,4},{4,6},{6,7},{7,5},{5,3},{3,1},{9,8},{8,10},{10,1... | collective-permute-start | bytes 688136 | tf_op jit(solution)/shard_map/ppermute | solution.py:302
  11.0 5.6 %collective-permute-done.refs_1_ = f32[224,256]{1,0:T(8,128)S(1)} collective-permute-done((f32[224,256]{1,0:T(8,128)S(1)}, f32[224,256]{1,0:T(8,128)S(1)}, u32[]{:S(2)}, u32[]{:S(2)}) %collective-permute-start) | collective-permute-done | bytes 229408 | tf_op jit(solution)/shard_map/ppermute | solution.py:302
  16.6 1.6 %collective-permute-start.2 = (f32[224,256]{1,0:T(8,128)S(1)}, f32[224,256]{1,0:T(8,128)S(1)}, u32[]{:S(2)}, u32[]{:S(2)}) collective-permute-start(f32[224,256]{1,0:T(8,128)S(1)} %collective-permute-done.refs_1_), channel_id=1, source_target_pairs={{1,0},{0,2},{2,4},{4,6},{6,7},{7,5},{5,3},{3,1},{9,8},{8,10},{10,1... | collective-permute-start | bytes 688136 | tf_op jit(solution)/shard_map/ppermute | solution.py:302
  18.7 4.8 %collective-permute-done.2.refs_3_ = f32[224,256]{1,0:T(8,128)S(1)} collective-permute-done((f32[224,256]{1,0:T(8,128)S(1)}, f32[224,256]{1,0:T(8,128)S(1)}, u32[]{:S(2)}, u32[]{:S(2)}) %collective-permute-start.2) | collective-permute-done | bytes 229408 | tf_op jit(solution)/shard_map/ppermute | solution.py:302
  23.5 1.6 %collective-permute-start.4 = (f32[224,256]{1,0:T(8,128)S(1)}, f32[224,256]{1,0:T(8,128)S(1)}, u32[]{:S(2)}, u32[]{:S(2)}) collective-permute-start(f32[224,256]{1,0:T(8,128)S(1)} %collective-permute-done.2.refs_3_), channel_id=1, source_target_pairs={{1,0},{0,2},{2,4},{4,6},{6,7},{7,5},{5,3},{3,1},{9,8},{8,10},{10,1... | collective-permute-start | bytes 688136 | tf_op jit(solution)/shard_map/ppermute | solution.py:302
  25.5 4.0 %collective-permute-done.4.refs_5_ = f32[224,256]{1,0:T(8,128)S(1)} collective-permute-done((f32[224,256]{1,0:T(8,128)S(1)}, f32[224,256]{1,0:T(8,128)S(1)}, u32[]{:S(2)}, u32[]{:S(2)}) %collective-permute-start.4) | collective-permute-done | bytes 229408 | tf_op jit(solution)/shard_map/ppermute | solution.py:302
  29.5 1.6 %collective-permute-start.6 = (f32[224,256]{1,0:T(8,128)S(1)}, f32[224,256]{1,0:T(8,128)S(1)}, u32[]{:S(2)}, u32[]{:S(2)}) collective-permute-start(f32[224,256]{1,0:T(8,128)S(1)} %collective-permute-done.4.refs_5_), channel_id=1, source_target_pairs={{1,0},{0,2},{2,4},{4,6},{6,7},{7,5},{5,3},{3,1},{9,8},{8,10},{10,1... | collective-permute-start | bytes 688136 | tf_op jit(solution)/shard_map/ppermute | solution.py:304
  31.1 4.4 %collective-permute-done.6.refs_7_ = f32[224,256]{1,0:T(8,128)S(1)} collective-permute-done((f32[224,256]{1,0:T(8,128)S(1)}, f32[224,256]{1,0:T(8,128)S(1)}, u32[]{:S(2)}, u32[]{:S(2)}) %collective-permute-start.6) | collective-permute-done | bytes 229408 | tf_op jit(solution)/shard_map/ppermute | solution.py:304
  35.5 3.8 %shard_map.60 = (bf16[4,640,256]{2,1,0:T(8,128)(2,1)S(1)}, bf16[4,640,256]{2,1,0:T(8,128)(2,1)S(1)}, f32[448,256]{1,0:T(8,128)S(1)}, bf16[448,448]{1,0:T(8,128)(2,1)S(1)}, f32[448,128]{1,0:T(8,128)S(1)}) custom-call(s32[1,1792]{1,0:T(1,128)S(1)} %reshape.7.structure_ref, f32[224,256]{1,0:T(8,128)S(1)} %copy-done.1, ...), custom_call_target="tpu_custom_call" | custom-call | tf_op jit(solution)/shard_map/pallas_call | solution.py:266
  40.3 7.2 %collective-permute-done.10.refs_2_ = f32[448,128]{1,0:T(8,128)S(1)} collective-permute-done((f32[448,128]{1,0:T(8,128)S(1)}, f32[448,128]{1,0:T(8,128)S(1)}, u32[]{:S(2)}, u32[]{:S(2)}) %collective-permute-start.10) | collective-permute-done | bytes 229408 | tf_op jit(solution)/shard_map/ppermute | solution.py:282
  47.5 2.3 %shard_map.62 = (f32[112,256]{1,0:T(8,128)S(1)}, f32[112,256]{1,0:T(8,128)S(1)}, f32[112,256]{1,0:T(8,128)S(1)}, f32[112,256]{1,0:T(8,128)S(1)}) custom-call(bf16[4,640,256]{2,1,0:T(8,128)(2,1)S(1)} %get-tuple-element.30.uh_ref, bf16[4,640,256]{2,1,0:T(8,128)(2,1)S(1)} %get-tuple-element.31.ul_ref, f32[448,256]{1,0:T(8,128)S(1)} %get-tuple-element.32.part_ref, ...), custom_call_target="tpu_custom_call" | custom-call | tf_op jit(solution)/shard_map/pallas_call | solution.py:266
  49.7 1.6 %collective-permute-start.13 = (f32[112,256]{1,0:T(8,128)S(1)}, f32[112,256]{1,0:T(8,128)S(1)}, u32[]{:S(2)}, u32[]{:S(2)}) collective-permute-start(f32[112,256]{1,0:T(8,128)S(1)} %get-tuple-element.36), channel_id=1, source_target_pairs={{0,2},{1,3},{2,4},{3,5},{4,6},{5,7},{6,0},{7,1},{8,10},{9,11},{10,... | collective-permute-start | bytes 344072 | tf_op jit(solution)/shard_map/ppermute | solution.py:385
  51.4 2.6 %collective-permute-start.14 = (f32[112,256]{1,0:T(8,128)S(1)}, f32[112,256]{1,0:T(8,128)S(1)}, u32[]{:S(2)}, u32[]{:S(2)}) collective-permute-start(f32[112,256]{1,0:T(8,128)S(1)} %get-tuple-element.37), channel_id=1, source_target_pairs={{0,4},{1,5},{2,6},{3,7},{4,0},{5,1},{6,2},{7,3},{8,12},{9,13},{10,... | collective-permute-start | bytes 344072 | tf_op jit(solution)/shard_map/ppermute | solution.py:385
  55.3 1.5 %collective-permute-start.16 = (f32[112,256]{1,0:T(8,128)S(1)}, f32[112,256]{1,0:T(8,128)S(1)}, u32[]{:S(2)}, u32[]{:S(2)}) collective-permute-start(f32[112,256]{1,0:T(8,128)S(1)} %get-tuple-element.35.refs_0_), channel_id=1, source_target_pairs={{0,1},{1,0},{2,3},{3,2},{4,5},{5,4},{6,7},{7,6},{8,9},{9,8},{10,11... | collective-permute-start | bytes 344072 | tf_op jit(solution)/shard_map/ppermute | solution.py:276
  57.6 1.5 %collective-permute-start.17 = (f32[112,256]{1,0:T(8,128)S(1)}, f32[112,256]{1,0:T(8,128)S(1)}, u32[]{:S(2)}, u32[]{:S(2)}) collective-permute-start(f32[112,256]{1,0:T(8,128)S(1)} %collective-permute-done.13.refs_1_), channel_id=1, source_target_pairs={{0,1},{1,0},{2,3},{3,2},{4,5},{5,4},{6,7},{7,6},{8,9},{9,8},{10,11... | collective-permute-start | bytes 344072 | tf_op jit(solution)/shard_map/ppermute | solution.py:276
  59.1 3.1 %collective-permute-done.14.refs_2_ = f32[112,256]{1,0:T(8,128)S(1)} collective-permute-done((f32[112,256]{1,0:T(8,128)S(1)}, f32[112,256]{1,0:T(8,128)S(1)}, u32[]{:S(2)}, u32[]{:S(2)}) %collective-permute-start.14) | collective-permute-done | bytes 114720 | tf_op jit(solution)/shard_map/ppermute | solution.py:385
  64.2 1.5 %shard_map.61 = (bf16[448,896]{1,0:T(8,128)(2,1)S(1)}, bf16[4,128,448]{2,1,0:T(8,128)(2,1)S(1)}, bf16[4,128,448]{2,1,0:T(8,128)(2,1)S(1)}) custom-call(s32[1,1792]{1,0:T(1,128)S(1)} %reshape.7.structure_ref, f32[448,128]{1,0:T(8,128)S(1)} %get-tuple-element.26.refs_0_, f32[448,128]{1,0:T(8,128)S(1)} %collective-permute-done.9.refs_1_, ...), custom_call_target="tpu_custom_call" | custom-call | tf_op jit(solution)/shard_map/pallas_call | solution.py:266
  65.8 2.4 %collective-permute-done.18.refs_6_ = f32[112,256]{1,0:T(8,128)S(1)} collective-permute-done((f32[112,256]{1,0:T(8,128)S(1)}, f32[112,256]{1,0:T(8,128)S(1)}, u32[]{:S(2)}, u32[]{:S(2)}) %collective-permute-start.18) | collective-permute-done | bytes 114720 | tf_op jit(solution)/shard_map/ppermute | solution.py:276
  69.7 2.7 %shard_map.63 = (f32[224,256]{1,0:T(8,128)}, f32[128,256]{1,0:T(8,128)S(1)}, f32[128,256]{1,0:T(8,128)S(1)}, f32[128,256]{1,0:T(8,128)S(1)}, f32[128,256]{1,0:T(8,128)S(1)}) custom-call(bf16[448,896]{1,0:T(8,128)(2,1)S(1)} %get-tuple-element.27.from_ref, bf16[4,128,448]{2,1,0:T(8,128)(2,1)S(1)} %get-tuple-element.28.high_ref, ...), custom_call_target="tpu_custom_call" | custom-call | tf_op jit(solution)/shard_map/pallas_call | solution.py:266
  73.6 3.1 %collective-permute-start.21 = (f32[128,256]{1,0:T(8,128)S(1)}, f32[128,256]{1,0:T(8,128)S(1)}, u32[]{:S(2)}, u32[]{:S(2)}) collective-permute-start(f32[128,256]{1,0:T(8,128)S(1)} %get-tuple-element.42), channel_id=1, source_target_pairs={{0,4},{1,5},{2,6},{3,7},{4,0},{5,1},{6,2},{7,3},{8,12},{9,13},{10,... | collective-permute-start | bytes 393224 | tf_op jit(solution)/shard_map/ppermute | solution.py:403
  77.3 3.4 %collective-permute-done.20 = f32[128,256]{1,0:T(8,128)S(1)} collective-permute-done((f32[128,256]{1,0:T(8,128)S(1)}, f32[128,256]{1,0:T(8,128)S(1)}, u32[]{:S(2)}, u32[]{:S(2)}) %collective-permute-start.20) | collective-permute-done | bytes 131104 | tf_op jit(solution)/shard_map/ppermute | solution.py:403
  80.7 3.7 %collective-permute-done.21 = f32[128,256]{1,0:T(8,128)S(1)} collective-permute-done((f32[128,256]{1,0:T(8,128)S(1)}, f32[128,256]{1,0:T(8,128)S(1)}, u32[]{:S(2)}, u32[]{:S(2)}) %collective-permute-start.21) | collective-permute-done | bytes 131104 | tf_op jit(solution)/shard_map/ppermute | solution.py:403
  (35 shorter events, 13.1 us)
Async XLA Ops:
  5.8 29.7 %collective-permute-start.7 = (f32[2016,128]{1,0:T(8,128)S(1)}, f32[2016,128]{1,0:T(8,128)S(1)}, u32[]{:S(2)}, u32[]{:S(2)}) collective-permute-start(f32[2016,128]{1,0:T(8,128)S(1)} %shard_map.59.refs_8_), channel_id=1, source_target_pairs={{0,8},{8,0},{16,24},{24,16},{1,9},{9,1},{17,25},{25,17},{2,10},{10... | collective-permute-start | bytes 3096584 | tf_op jit(solution)/shard_map/ppermute | solution.py:276
  6.4 33.0 %collective-permute-start.8 = (f32[2016,128]{1,0:T(8,128)S(1)}, f32[2016,128]{1,0:T(8,128)S(1)}, u32[]{:S(2)}, u32[]{:S(2)}) collective-permute-start(f32[2016,128]{1,0:T(8,128)S(1)} %shard_map.59.refs_8_), channel_id=1, source_target_pairs={{0,16},{8,24},{16,0},{24,8},{1,17},{9,25},{17,1},{25,9},{2,18},{10... | collective-permute-start | bytes 3096584 | tf_op jit(solution)/shard_map/ppermute | solution.py:362
  8.9 7.7 %collective-permute-start = (f32[224,256]{1,0:T(8,128)S(1)}, f32[224,256]{1,0:T(8,128)S(1)}, u32[]{:S(2)}, u32[]{:S(2)}) collective-permute-start(f32[224,256]{1,0:T(8,128)S(1)} %copy-done.1), channel_id=1, source_target_pairs={{1,0},{0,2},{2,4},{4,6},{6,7},{7,5},{5,3},{3,1},{9,8},{8,10},{10,1... | collective-permute-start | bytes 688136 | tf_op jit(solution)/shard_map/ppermute | solution.py:302
  10.5 7.7 %collective-permute-start.1 = (f32[224,256]{1,0:T(8,128)S(1)}, f32[224,256]{1,0:T(8,128)S(1)}, u32[]{:S(2)}, u32[]{:S(2)}) collective-permute-start(f32[224,256]{1,0:T(8,128)S(1)} %copy-done.1), channel_id=1, source_target_pairs={{0,1},{2,0},{4,2},{6,4},{7,6},{5,7},{3,5},{1,3},{8,9},{10,8},{12,1... | collective-permute-start | bytes 688136 | tf_op jit(solution)/shard_map/ppermute | solution.py:302
  16.6 6.8 %collective-permute-start.2 = (f32[224,256]{1,0:T(8,128)S(1)}, f32[224,256]{1,0:T(8,128)S(1)}, u32[]{:S(2)}, u32[]{:S(2)}) collective-permute-start(f32[224,256]{1,0:T(8,128)S(1)} %collective-permute-done.refs_1_), channel_id=1, source_target_pairs={{1,0},{0,2},{2,4},{4,6},{6,7},{7,5},{5,3},{3,1},{9,8},{8,10},{10,1... | collective-permute-start | bytes 688136 | tf_op jit(solution)/shard_map/ppermute | solution.py:302
  18.2 6.8 %collective-permute-start.3 = (f32[224,256]{1,0:T(8,128)S(1)}, f32[224,256]{1,0:T(8,128)S(1)}, u32[]{:S(2)}, u32[]{:S(2)}) collective-permute-start(f32[224,256]{1,0:T(8,128)S(1)} %collective-permute-done.1.refs_2_), channel_id=1, source_target_pairs={{0,1},{2,0},{4,2},{6,4},{7,6},{5,7},{3,5},{1,3},{8,9},{10,8},{12,1... | collective-permute-start | bytes 688136 | tf_op jit(solution)/shard_map/ppermute | solution.py:302
  23.5 6.0 %collective-permute-start.4 = (f32[224,256]{1,0:T(8,128)S(1)}, f32[224,256]{1,0:T(8,128)S(1)}, u32[]{:S(2)}, u32[]{:S(2)}) collective-permute-start(f32[224,256]{1,0:T(8,128)S(1)} %collective-permute-done.2.refs_3_), channel_id=1, source_target_pairs={{1,0},{0,2},{2,4},{4,6},{6,7},{7,5},{5,3},{3,1},{9,8},{8,10},{10,1... | collective-permute-start | bytes 688136 | tf_op jit(solution)/shard_map/ppermute | solution.py:302
  25.0 6.0 %collective-permute-start.5 = (f32[224,256]{1,0:T(8,128)S(1)}, f32[224,256]{1,0:T(8,128)S(1)}, u32[]{:S(2)}, u32[]{:S(2)}) collective-permute-start(f32[224,256]{1,0:T(8,128)S(1)} %collective-permute-done.3.refs_4_), channel_id=1, source_target_pairs={{0,1},{2,0},{4,2},{6,4},{7,6},{5,7},{3,5},{1,3},{8,9},{10,8},{12,1... | collective-permute-start | bytes 688136 | tf_op jit(solution)/shard_map/ppermute | solution.py:302
  29.5 6.0 %collective-permute-start.6 = (f32[224,256]{1,0:T(8,128)S(1)}, f32[224,256]{1,0:T(8,128)S(1)}, u32[]{:S(2)}, u32[]{:S(2)}) collective-permute-start(f32[224,256]{1,0:T(8,128)S(1)} %collective-permute-done.4.refs_5_), channel_id=1, source_target_pairs={{1,0},{0,2},{2,4},{4,6},{6,7},{7,5},{5,3},{3,1},{9,8},{8,10},{10,1... | collective-permute-start | bytes 688136 | tf_op jit(solution)/shard_map/ppermute | solution.py:304
  39.3 8.1 %collective-permute-start.12 = (f32[2016,128]{1,0:T(8,128)S(1)}, f32[2016,128]{1,0:T(8,128)S(1)}, u32[]{:S(2)}, u32[]{:S(2)}) collective-permute-start(f32[2016,128]{1,0:T(8,128)S(1)} %collective-permute-done.8.refs_0_), channel_id=1, source_target_pairs={{0,8},{8,0},{16,24},{24,16},{1,9},{9,1},{17,25},{25,17},{2,10},{10... | collective-permute-start | bytes 3096584 | tf_op jit(solution)/shard_map/ppermute | solution.py:276
  39.4 8.0 %collective-permute-start.10 = (f32[448,128]{1,0:T(8,128)S(1)}, f32[448,128]{1,0:T(8,128)S(1)}, u32[]{:S(2)}, u32[]{:S(2)}) collective-permute-start(f32[448,128]{1,0:T(8,128)S(1)} %get-tuple-element.26.refs_0_), channel_id=1, source_target_pairs={{0,16},{8,24},{16,0},{24,8},{1,17},{9,25},{17,1},{25,9},{2,18},{10... | collective-permute-start | bytes 688136 | tf_op jit(solution)/shard_map/ppermute | solution.py:282
  40.1 15.2 %collective-permute-start.9 = (f32[448,128]{1,0:T(8,128)S(1)}, f32[448,128]{1,0:T(8,128)S(1)}, u32[]{:S(2)}, u32[]{:S(2)}) collective-permute-start(f32[448,128]{1,0:T(8,128)S(1)} %get-tuple-element.26.refs_0_), channel_id=1, source_target_pairs={{0,8},{8,0},{16,24},{24,16},{1,9},{9,1},{17,25},{25,17},{2,10},{10... | collective-permute-start | bytes 688136 | tf_op jit(solution)/shard_map/ppermute | solution.py:276
  47.4 16.8 %collective-permute-start.11 = (f32[448,128]{1,0:T(8,128)S(1)}, f32[448,128]{1,0:T(8,128)S(1)}, u32[]{:S(2)}, u32[]{:S(2)}) collective-permute-start(f32[448,128]{1,0:T(8,128)S(1)} %collective-permute-done.10.refs_2_), channel_id=1, source_target_pairs={{0,8},{8,0},{16,24},{24,16},{1,9},{9,1},{17,25},{25,17},{2,10},{10... | collective-permute-start | bytes 688136 | tf_op jit(solution)/shard_map/ppermute | solution.py:276
  49.7 7.9 %collective-permute-start.13 = (f32[112,256]{1,0:T(8,128)S(1)}, f32[112,256]{1,0:T(8,128)S(1)}, u32[]{:S(2)}, u32[]{:S(2)}) collective-permute-start(f32[112,256]{1,0:T(8,128)S(1)} %get-tuple-element.36), channel_id=1, source_target_pairs={{0,2},{1,3},{2,4},{3,5},{4,6},{5,7},{6,0},{7,1},{8,10},{9,11},{10,... | collective-permute-start | bytes 344072 | tf_op jit(solution)/shard_map/ppermute | solution.py:385
  51.4 10.8 %collective-permute-start.14 = (f32[112,256]{1,0:T(8,128)S(1)}, f32[112,256]{1,0:T(8,128)S(1)}, u32[]{:S(2)}, u32[]{:S(2)}) collective-permute-start(f32[112,256]{1,0:T(8,128)S(1)} %get-tuple-element.37), channel_id=1, source_target_pairs={{0,4},{1,5},{2,6},{3,7},{4,0},{5,1},{6,2},{7,3},{8,12},{9,13},{10,... | collective-permute-start | bytes 344072 | tf_op jit(solution)/shard_map/ppermute | solution.py:385
  53.9 9.7 %collective-permute-start.15 = (f32[112,256]{1,0:T(8,128)S(1)}, f32[112,256]{1,0:T(8,128)S(1)}, u32[]{:S(2)}, u32[]{:S(2)}) collective-permute-start(f32[112,256]{1,0:T(8,128)S(1)} %get-tuple-element.38), channel_id=1, source_target_pairs={{0,6},{1,7},{2,0},{3,1},{4,2},{5,3},{6,4},{7,5},{8,14},{9,15},{10,... | collective-permute-start | bytes 344072 | tf_op jit(solution)/shard_map/ppermute | solution.py:385
  55.3 10.4 %collective-permute-start.16 = (f32[112,256]{1,0:T(8,128)S(1)}, f32[112,256]{1,0:T(8,128)S(1)}, u32[]{:S(2)}, u32[]{:S(2)}) collective-permute-start(f32[112,256]{1,0:T(8,128)S(1)} %get-tuple-element.35.refs_0_), channel_id=1, source_target_pairs={{0,1},{1,0},{2,3},{3,2},{4,5},{5,4},{6,7},{7,6},{8,9},{9,8},{10,11... | collective-permute-start | bytes 344072 | tf_op jit(solution)/shard_map/ppermute | solution.py:276
  57.6 8.1 %collective-permute-start.17 = (f32[112,256]{1,0:T(8,128)S(1)}, f32[112,256]{1,0:T(8,128)S(1)}, u32[]{:S(2)}, u32[]{:S(2)}) collective-permute-start(f32[112,256]{1,0:T(8,128)S(1)} %collective-permute-done.13.refs_1_), channel_id=1, source_target_pairs={{0,1},{1,0},{2,3},{3,2},{4,5},{5,4},{6,7},{7,6},{8,9},{9,8},{10,11... | collective-permute-start | bytes 344072 | tf_op jit(solution)/shard_map/ppermute | solution.py:276
  62.2 6.0 %collective-permute-start.18 = (f32[112,256]{1,0:T(8,128)S(1)}, f32[112,256]{1,0:T(8,128)S(1)}, u32[]{:S(2)}, u32[]{:S(2)}) collective-permute-start(f32[112,256]{1,0:T(8,128)S(1)} %collective-permute-done.14.refs_2_), channel_id=1, source_target_pairs={{0,1},{1,0},{2,3},{3,2},{4,5},{5,4},{6,7},{7,6},{8,9},{9,8},{10,11... | collective-permute-start | bytes 344072 | tf_op jit(solution)/shard_map/ppermute | solution.py:276
  63.7 6.0 %collective-permute-start.19 = (f32[112,256]{1,0:T(8,128)S(1)}, f32[112,256]{1,0:T(8,128)S(1)}, u32[]{:S(2)}, u32[]{:S(2)}) collective-permute-start(f32[112,256]{1,0:T(8,128)S(1)} %collective-permute-done.15.refs_3_), channel_id=1, source_target_pairs={{0,1},{1,0},{2,3},{3,2},{4,5},{5,4},{6,7},{7,6},{8,9},{9,8},{10,11... | collective-permute-start | bytes 344072 | tf_op jit(solution)/shard_map/ppermute | solution.py:276
  69.7 14.8 %copy-start.2 = (f32[128,256]{1,0:T(8,128)S(1)}, f32[128,256]{1,0:T(8,128)}, u32[]{:S(2)}) copy-start(f32[128,256]{1,0:T(8,128)} %param.7) | copy-start | bytes 393220
  72.4 8.4 %collective-permute-start.20 = (f32[128,256]{1,0:T(8,128)S(1)}, f32[128,256]{1,0:T(8,128)S(1)}, u32[]{:S(2)}, u32[]{:S(2)}) collective-permute-start(f32[128,256]{1,0:T(8,128)S(1)} %get-tuple-element.41), channel_id=1, source_target_pairs={{0,2},{1,3},{2,4},{3,5},{4,6},{5,7},{6,0},{7,1},{8,10},{9,11},{10,... | collective-permute-start | bytes 393224 | tf_op jit(solution)/shard_map/ppermute | solution.py:403
  73.6 10.9 %collective-permute-start.21 = (f32[128,256]{1,0:T(8,128)S(1)}, f32[128,256]{1,0:T(8,128)S(1)}, u32[]{:S(2)}, u32[]{:S(2)}) collective-permute-start(f32[128,256]{1,0:T(8,128)S(1)} %get-tuple-element.42), channel_id=1, source_target_pairs={{0,4},{1,5},{2,6},{3,7},{4,0},{5,1},{6,2},{7,3},{8,12},{9,13},{10,... | collective-permute-start | bytes 393224 | tf_op jit(solution)/shard_map/ppermute | solution.py:403
  76.7 7.8 %collective-permute-start.22 = (f32[128,256]{1,0:T(8,128)S(1)}, f32[128,256]{1,0:T(8,128)S(1)}, u32[]{:S(2)}, u32[]{:S(2)}) collective-permute-start(f32[128,256]{1,0:T(8,128)S(1)} %get-tuple-element.43), channel_id=1, source_target_pairs={{0,6},{1,7},{2,0},{3,1},{4,2},{5,3},{6,4},{7,5},{8,14},{9,15},{10,... | collective-permute-start | bytes 393224 | tf_op jit(solution)/shard_map/ppermute | solution.py:403
  (2 other events, 7.6 us)

commit v4 on v3

--- a/solution.py
+++ b/solution.py
@@ -14,6 +14,7 @@
 WIDE = (FULL + 1) * LANES
 BF16 = jnp.bfloat16
 VMEM = pl.BlockSpec(memory_space=pltpu.VMEM)
+HBM = pl.BlockSpec(memory_space=pltpu.HBM)
 
 
 def f32(*shape):
@@ -64,39 +65,42 @@
             fn(owner, ref)
 
 
-def select_kernel(structure_ref, sigma_ref, out_ref, place_ref):
-    step, steps = pl.program_id(0), pl.num_programs(0)
-    part, cols = sigma_ref.shape
+def select_kernel(structure_ref, sigma_ref, u_ref, out_ref, top_ref, low_ref, held_ref, sems):
+    rows, cols = held_ref.shape
     n = structure_ref.shape[1]
-    rows = out_ref.shape[0] * LANES // CAP
-
-    @pl.when(step == 0)
-    def _():
-        first = lax.axis_index("prow") * cols
-        names = jnp.broadcast_to(structure_ref[...], (8, n))
-        shift = lax.rem(n - count(structure_ref[...] < first), n)
-        named = pltpu.roll(names, shift, 1)[:1, :CAP] - first
-        named = jnp.concatenate([named, named[:, FULL * LANES :]], axis=1)
-        at = lax.broadcasted_iota(jnp.int32, (cols, WIDE), 0)
-        place_ref[...] = one_hot(at == named).astype(BF16)
-
-    high, low = split(sigma_ref[...])
-    place = place_ref[...]
-    picked = dot(high, place) + dot(low, place)
-    start = step * part
-    for i in range(FULL):
-        where = pl.multiple_of(rows * i + start, 8)
-        out_ref[pl.ds(where, part), :] = picked[:, LANES * i : LANES * (i + 1)]
-
-    @pl.when(step < steps // 2)
-    def _():
-        where = pl.multiple_of(rows * FULL + start, 8)
-        out_ref[pl.ds(where, part), : LANES // 2] = picked[:, FULL * LANES : CAP]
-
-    @pl.when(step >= steps // 2)
-    def _():
-        where = pl.multiple_of(rows * FULL + start - rows // 2, 8)
-        out_ref[pl.ds(where, part), LANES // 2 :] = picked[:, CAP:]
+    parts = sems.shape[0] - 2
+    part = rows // parts
+    copies = []
+    for k in range(parts):
+        at = pl.ds(part * k, part)
+        copies.append(pltpu.make_async_copy(sigma_ref.at[at, :], held_ref.at[at, :], sems.at[k]))
+        copies[-1].start()
+    half = top_ref.shape[0]
+    halves = []
+    for k, ref in enumerate((top_ref, low_ref)):
+        halves.append(pltpu.make_async_copy(u_ref.at[pl.ds(half * k, half), :], ref, sems.at[parts + k]))
+        halves[-1].start()
+    first = lax.axis_index("prow") * cols
+    names = jnp.broadcast_to(structure_ref[...], (8, n))
+    shift = lax.rem(n - count(structure_ref[...] < first), n)
+    named = pltpu.roll(names, shift, 1)[:1, :CAP] - first
+    named = jnp.concatenate([named, named[:, FULL * LANES :]], axis=1)
+    at = lax.broadcasted_iota(jnp.int32, (cols, WIDE), 0)
+    place = one_hot(at == named).astype(BF16)
+    for k in range(parts):
+        copies[k].wait()
+        high, low = split(held_ref[part * k : part * (k + 1), :])
+        picked = dot(high, place) + dot(low, place)
+        for i in range(FULL):
+            at = rows * i + part * k
+            out_ref[at : at + part, :] = picked[:, LANES * i : LANES * (i + 1)]
+        at = rows * FULL + part * (k % (parts // 2))
+        if k < parts // 2:
+            out_ref[at : at + part, : LANES // 2] = picked[:, FULL * LANES : CAP]
+        else:
+            out_ref[at : at + part, LANES // 2 :] = picked[:, CAP:]
+    for copy in halves:
+        copy.wait()
 
 
 def block_term(block_ref, uh, ul, rows):
@@ -109,20 +113,18 @@
     return dot(left, jnp.concatenate([uh, ul, uh], axis=0))
 
 
-def prepare_kernel(direct, slots, owners, structure_ref, *refs):
+def prepare_kernel(direct, nc, owners, structure_ref, *refs):
     pair_ref = None
     if direct:
         pair_ref, refs = refs[-2], refs[:-2] + refs[-1:]
-    uh_ref, ul_ref, part_ref, to_ref, us_ref = refs[-5:]
+    uh_ref, ul_ref, part_ref, us_ref = refs[-4:]
     nr, _, w = uh_ref.shape
-    nc = to_ref.shape[0] // slots
-    n_u = nc if direct else 1
-    u_refs, first_refs = refs[:n_u], refs[n_u:-5]
+    n_u = 2 * nc if direct else 1
+    u_refs, first_refs = refs[:n_u], refs[n_u:-4]
     n = structure_ref.shape[1]
     m = n // nc
     c = lax.axis_index("pcol")
     r = lax.axis_index("prow")
-    z = c // 2
     rows = part_ref.shape[0]
     names = structure_ref[...]
 
@@ -134,13 +136,16 @@
 
     if direct:
         lane = pl.multiple_of((c & 1) * (w // 2), LANES)
-        pair_ref[:m, :] = u_refs[0][:, pl.ds(lane, w // 2)]
-        for owner, u_ref in zip(ring_owners(nc, c), u_refs):
-            place(owner, u_ref[...])
+        size = m // 2
+        for h in range(2):
+            pair_ref[size * h : size * (h + 1), :] = u_refs[h][:, pl.ds(lane, w // 2)]
+        for (owner, h), u_ref in zip(ring_owners(nc, c), u_refs):
+            place(nc * size * h + owner, u_ref[...])
+            at = m + size * h
 
             @pl.when(owner == jnp.bitwise_xor(c, 1))
             def _():
-                pair_ref[m:, :] = u_ref[:, pl.ds(lane, w // 2)]
+                pair_ref[at : at + size, :] = u_ref[:, pl.ds(lane, w // 2)]
 
     else:
         pl.loop(0, nc)(lambda k: place(k, u_refs[0][k]))
@@ -170,6 +175,10 @@
         image = image + block_term(block_ref, uh_ref[owner], ul_ref[owner], rows)
     part_ref[...] = image
 
+
+def row_order(names, c, rows, nc, slots, direct):
+    n = names.shape[1]
+    z = c // 2
     lg = log2(nc)
     row = c * rows + lax.broadcasted_iota(jnp.int32, (rows, n), 0)
     rank = jnp.sum(one_hot(names < row), axis=1, keepdims=True).astype(jnp.int32)
@@ -182,18 +191,29 @@
     block = 2 * block + (turn & 1)
     slot = jnp.where(member > 0.5, block * slots + (rank >> lg) - ahead, -1)
     at = lax.broadcasted_iota(jnp.int32, (rows, nc * slots), 1)
-    to_ref[...] = one_hot(at == slot).T.astype(BF16)
+    return one_hot(at == slot).T.astype(BF16)
+
+
+def near_kernel(direct, slots, owners, structure_ref, uh_ref, ul_ref, part_ref, *refs):
+    block_refs, (image_ref, to_ref) = refs[:-2], refs[-2:]
+    rows = part_ref.shape[0]
+    image = part_ref[...]
+    for owner, block_ref in zip(owners(lax.axis_index("prow")), block_refs):
+        image = image + block_term(block_ref, uh_ref[owner], ul_ref[owner], rows)
+    image_ref[...] = image
+    nc = to_ref.shape[0] // slots
+    to_ref[...] = row_order(structure_ref[...], lax.axis_index("pcol"), rows, nc, slots, direct)
 
 
 def image_kernel(n_out, owners, uh_ref, ul_ref, part_ref, to_ref, *refs):
     block_refs, out_refs = refs[:-n_out], refs[-n_out:]
     rows = part_ref.shape[0]
+    image = part_ref[...]
     if owners is None:
         stack = block_refs[0]
         add = lambda b, v: v + block_term(stack.at[b], uh_ref[b], ul_ref[b], rows)
-        image = lax.fori_loop(0, stack.shape[0], add, part_ref[...])
-    else:
-        image = part_ref[...]
+        image = lax.fori_loop(0, stack.shape[0], add, image)
+    else:
         for owner, block_ref in zip(owners(lax.axis_index("prow")), block_refs):
             image = image + block_term(block_ref, uh_ref[owner], ul_ref[owner], rows)
     image = pick_rows(to_ref[...], image)
@@ -260,14 +280,16 @@
             out_refs[0][t] = term(t)
 
 
-def call(kernel, out_shape, *args, **kw):
+def call(kernel, out_shape, *args, flops=0, vmem=20, **kw):
     many = isinstance(out_shape, (list, tuple))
+    size = sum(v.size * v.dtype.itemsize for v in jax.tree.leaves((out_shape, args)))
     kw = {"in_specs": [VMEM] * len(args)} | kw
     return pl.pallas_call(
         kernel,
         out_shape=out_shape,
         out_specs=[VMEM] * len(out_shape) if many else VMEM,
-        compiler_params=pltpu.CompilerParams(vmem_limit_bytes=20 * 2**20),
+        cost_estimate=pl.CostEstimate(flops=flops, bytes_accessed=size, transcendentals=0),
+        compiler_params=pltpu.CompilerParams(vmem_limit_bytes=vmem * 2**20),
         **kw,
     )(*args)
 
@@ -276,10 +298,11 @@
     return lax.ppermute(v, axis, [(k, k ^ 1) for k in range(size)])
 
 
-def spread(v, size):
+def spread(v, size, after):
     blocks = [v, swap(v, "prow", size)]
     for t in range(1, size // 2):
         far = lax.ppermute(v, "prow", [(k, (k + 2 * t) % size) for k in range(size)])
+        far, _ = lax.optimization_barrier((far, after))
         blocks += [far, swap(far, "prow", size)]
     return blocks
 
@@ -292,25 +315,27 @@
     return out
 
 
-def ring_gather(u, nc):
+def ring_gather(halves, nc):
     ring = [2 * z for z in range(nc // 2)] + [2 * z + 1 for z in reversed(range(nc // 2))]
     pairs = [(ring[q - 1], ring[q]) for q in range(nc)]
     back = [(b, a) for a, b in pairs]
-    blocks = [u]
-    up = down = u
+    held = [(v, v) for v in halves]
+    blocks = list(halves)
     for step in range(1, nc // 2):
-        up, down = lax.ppermute(up, "pcol", pairs), lax.ppermute(down, "pcol", back)
-        blocks += [up, down]
-    return blocks + [lax.ppermute(up, "pcol", pairs)]
+        for h in range(2):
+            held[h] = lax.ppermute(held[h][0], "pcol", pairs), lax.ppermute(held[h][1], "pcol", back)
+            blocks += held[h]
+    return blocks + [lax.ppermute(held[0][0], "pcol", pairs), lax.ppermute(held[1][1], "pcol", back)]
 
 
 def ring_owners(nc, c):
     q = jnp.where((c & 1) == 0, c >> 1, nc - 1 - (c >> 1))
-    out = []
-    for k in range(nc):
-        step = (k + 1) // 2
-        at = (q - step if k % 2 else q + step) & (nc - 1)
-        out.append(jnp.where(at < nc // 2, 2 * at, 2 * (nc - 1 - at) + 1))
+    out = [(c, 0), (c, 1)]
+    for step in range(1, nc // 2 + 1):
+        for h in range(2):
+            for sign in (-1, 1) if step < nc // 2 else (-1,):
+                at = (q + sign * step) & (nc - 1)
+                out.append((jnp.where(at < nc // 2, 2 * at, 2 * (nc - 1 - at) + 1), h))
     return out
 
 
@@ -325,60 +350,72 @@
     slots = -(-rows // nc)
     direct = nc <= 8
     names = structure.reshape(1, n)
-    steps = 4
-    part = rows // steps
     groups = [[2 * k + x for k in range(nz)] for x in range(2)]
     owners = functools.partial(relative_owners, nr)
 
-    chosen = call(
+    chosen, *halves = call(
         select_kernel,
-        f32(rows * CAP // LANES, LANES),
+        [f32(rows * CAP // LANES, LANES), f32(m // 2, w), f32(m // 2, w)],
         names,
         sigma_top,
-        grid=(steps,),
-        in_specs=[pl.BlockSpec((1, n), lambda i: (0, 0)), pl.BlockSpec((part, cols), lambda i: (i, 0))],
-        scratch_shapes=[pltpu.VMEM((cols, WIDE), BF16)],
+        u_panel,
+        in_specs=[VMEM, HBM, HBM],
+        scratch_shapes=[pltpu.VMEM((rows, cols), jnp.float32), pltpu.SemaphoreType.DMA((6,))],
+        flops=4 * rows * cols * WIDE,
+        vmem=52,
     )
     near = [chosen, swap(chosen, "prow", nr)] if direct else []
     if direct:
-        u_all = ring_gather(u_panel, nc)
+        u_all = ring_gather(halves, nc)
     else:
         u_all = [lax.all_gather(u_panel, "pcol")]
-    out = [bf16(nr, WIDE, w), bf16(nr, WIDE, w), f32(rows, w), bf16(nc * slots, rows)]
-    if direct:
-        out.append(f32(2 * m, wd))
-    uh, ul, image, to, *pair = call(
-        functools.partial(prepare_kernel, direct, slots, lambda r: owners(r)[:2]),
-        out,
+    term = 6 * rows * WIDE * w
+    uh, ul, image, *pair = call(
+        functools.partial(prepare_kernel, direct, nc, lambda r: owners(r)[:2]),
+        [bf16(nr, WIDE, w), bf16(nr, WIDE, w), f32(rows, w)] + [f32(2 * m, wd)] * direct,
         names,
         *u_all,
         *near,
         scratch_shapes=[pltpu.VMEM((-(-w // LANES), n + CAP + 8, LANES), jnp.float32)],
-    )
-
-    if direct:
-        later = []
+        flops=2 * term,
+    )
+    beside, later = [], []
+    if direct:
         for t in range(1, nr // 2):
             far = lax.ppermute(chosen, "prow", [(k, (k + 2 * t) % nr) for k in range(nr)])
-            far, image = lax.optimization_barrier((far, image))
-            later += [far, swap(far, "prow", nr)]
-        pair, later[0] = lax.optimization_barrier((pair[0], later[0]))
-        pairs = spread(pair, nr)
+            far, _ = lax.optimization_barrier((far, image))
+            beside.append(far)
+            later.append(swap(far, "prow", nr))
     else:
         later = [lax.all_gather(chosen, "prow")]
-        pair = jnp.concatenate([u_panel, swap(u_panel, "pcol", nc)], axis=0)
-        pair = jnp.where(jnp.bitwise_and(c, 1) == 0, pair[:, :wd], pair[:, wd:])
-        pairs = [lax.all_gather(pair, "prow")]
+    image, to = call(
+        functools.partial(near_kernel, direct, slots, lambda r: owners(r)[2::2]),
+        [f32(rows, w), bf16(nc * slots, rows)],
+        names,
+        uh,
+        ul,
+        image,
+        *beside,
+        flops=term,
+    )
     n_out = nz if direct else 1
     sent = call(
-        functools.partial(image_kernel, n_out, (lambda r: owners(r)[2:]) if direct else None),
+        functools.partial(image_kernel, n_out, (lambda r: owners(r)[3::2]) if direct else None),
         [f32(nc * slots // n_out, w)] * n_out,
         uh,
         ul,
         image,
         to,
         *later,
-    )
+        flops=term,
+    )
+    if direct:
+        pair, _ = lax.optimization_barrier((pair[0], beside[0]))
+        pairs = spread(pair, nr, sent[0])
+    else:
+        pair = jnp.concatenate([u_panel, swap(u_panel, "pcol", nc)], axis=0)
+        pair = jnp.where(jnp.bitwise_and(c, 1) == 0, pair[:, :wd], pair[:, wd:])
+        pairs = [lax.all_gather(pair, "prow")]
     if direct:
         got = [sent[0]]
         for t in range(1, nz):
@@ -396,7 +433,7 @@
         *pairs,
     )
     parts = [f32(wd, w)] * nz if direct else [f32(nz, wd, w)]
-    sigma_sj, *terms = call(correction_kernel, [f32(m, w)] + parts, source, high, low, *got)
+    sigma_sj, *terms = call(correction_kernel, [f32(m, w)] + parts, source, high, low, *got, flops=term)
     if direct:
         total = terms[0]
         for t in range(1, nz):

time: 85.8 us -> 84.6 us (0.986)
  waiting for transfers between devices: 41.1 us -> 30.2 us
  starting transfers between devices: 27.2 us -> 37 us
    ppermute x7 -> x14, starting transfers between devices: 7.66 us -> 18 us  [the longest x6 7.7 us: ring_gather(): lax.ppermute(held[h][1], 'pcol', back)]
    ppermute x7 -> x14, waiting for transfers between devices: 18.9 us -> 10.4 us  [the longest x6 4.03 us: ring_gather(): lax.ppermute(held[h][0], 'pcol', pairs)]
    ppermute x1, waiting for transfers between devices: 7.19 us -> 3.63 us  [spread(): lax.ppermute(v, 'prow', [(k, (k + 2 * t) % size) for k in range(size)])]
    pallas_call x5 -> x6, Pallas kernels: 13.4 us -> 13.8 us  [call(): pl.pallas_call(kernel, out_shape=out_shape, out_specs=[VMEM] * len(out_sh...]
  transfers between devices with their start and end apart: 23 -> 30, of which waited for: 11 -> 14; matrix products, arithmetic and copies ran while one was open for 0% -> 0% of each run, Pallas kernels for 9% -> 9%
where the time goes in v4:
time: 84.6 us; the launch traced here: 84.2 us
  starting transfers between devices  37 us (44%)
  waiting for transfers between devices  30.2 us (36%)
  Pallas kernels  13.8 us (16%)
  local copies, waits for them, and re-layouts  1.64 us (2%)
    pallas_call x6, Pallas kernels, call(): pl.pallas_call(kernel, out_shape=out_shape, out_specs=[VMEM] * len(out_sh...  13.8 us
    ppermute x6, starting transfers between devices, ring_gather(): lax.ppermute(held[h][1], 'pcol', back)  7.7 us
    ppermute x3, waiting for transfers between devices, per_device(): lax.ppermute(terms[t], 'pcol', [(k, (k + 2 * t) % nc) for k in range(nc)])  7.42 us
    ppermute x6, starting transfers between devices, ring_gather(): lax.ppermute(held[h][0], 'pcol', pairs)  7.28 us
    ppermute x8, starting transfers between devices, swap(): return lax.ppermute(v, axis, [(k, k ^ 1) for k in range(size)])  5.68 us
    ppermute x3, starting transfers between devices, per_device(): lax.ppermute(sent[t], 'pcol', [(k, (k + 2 * t) % nc) for k in range(nc)])  5.52 us
    ppermute x3, starting transfers between devices, per_device(): lax.ppermute(terms[t], 'pcol', [(k, (k + 2 * t) % nc) for k in range(nc)])  4.67 us
    ppermute x8, waiting for transfers between devices, swap(): return lax.ppermute(v, axis, [(k, k ^ 1) for k in range(size)])  4.57 us
  transfers between devices with their start and end apart: 30, of which 14 were waited for; matrix products, arithmetic and copies ran while one was open for 0% of the time, Pallas kernels for 9%

profile of v4, /device:TPU:0, one launch (start us, length us, event | category | flops | bytes accessed | tf_op | source)
XLA Modules:
  0.0 84.2 jit_solution(9071867766270783276)
XLA Ops:
  2.3 3.3 %shard_map.59 = (f32[2016,128]{1,0:T(8,128)S(1)}, f32[112,256]{1,0:T(8,128)S(1)}, f32[112,256]{1,0:T(8,128)S(1)}) custom-call(s32[1,1792]{1,0:T(1,128)S(1)} %reshape.7.structure_ref, f32[448,896]{1,0:T(8,128)} %sigma_ref.1, f32[224,256]{1,0:T(8,128)S(1)} %copy-done), custom_call_target="tpu_custom_call" | custom-call | flops 1027604480 | bytes 3103744 | tf_op jit(solution)/shard_map/pallas_call | solution.py:287
  6.2 2.6 %collective-permute-start.15 = (f32[2016,128]{1,0:T(8,128)S(1)}, f32[2016,128]{1,0:T(8,128)S(1)}, u32[]{:S(2)}, u32[]{:S(2)}) collective-permute-start(f32[2016,128]{1,0:T(8,128)S(1)} %get-tuple-element.28.refs_16_), channel_id=1, source_target_pairs={{0,16},{8,24},{16,0},{24,8},{1,17},{9,25},{17,1},{25,9},{2,18},{10... | collective-permute-start | bytes 3096584 | tf_op jit(solution)/shard_map/ppermute | solution.py:385
  8.7 1.6 %collective-permute-start = (f32[112,256]{1,0:T(8,128)S(1)}, f32[112,256]{1,0:T(8,128)S(1)}, u32[]{:S(2)}, u32[]{:S(2)}) collective-permute-start(f32[112,256]{1,0:T(8,128)S(1)} %get-tuple-element.26.refs_0_), channel_id=1, source_target_pairs={{1,0},{0,2},{2,4},{4,6},{6,7},{7,5},{5,3},{3,1},{9,8},{8,10},{10,1... | collective-permute-start | bytes 344072 | tf_op jit(solution)/shard_map/ppermute | solution.py:326
  10.7 1.6 %collective-permute-start.2 = (f32[112,256]{1,0:T(8,128)S(1)}, f32[112,256]{1,0:T(8,128)S(1)}, u32[]{:S(2)}, u32[]{:S(2)}) collective-permute-start(f32[112,256]{1,0:T(8,128)S(1)} %get-tuple-element.27.refs_1_), channel_id=1, source_target_pairs={{1,0},{0,2},{2,4},{4,6},{6,7},{7,5},{5,3},{3,1},{9,8},{8,10},{10,1... | collective-permute-start | bytes 344072 | tf_op jit(solution)/shard_map/ppermute | solution.py:326
  12.3 2.4 %collective-permute-done.refs_2_ = f32[112,256]{1,0:T(8,128)S(1)} collective-permute-done((f32[112,256]{1,0:T(8,128)S(1)}, f32[112,256]{1,0:T(8,128)S(1)}, u32[]{:S(2)}, u32[]{:S(2)}) %collective-permute-start) | collective-permute-done | bytes 114720 | tf_op jit(solution)/shard_map/ppermute | solution.py:326
  18.2 2.4 %collective-permute-done.1.refs_3_ = f32[112,256]{1,0:T(8,128)S(1)} collective-permute-done((f32[112,256]{1,0:T(8,128)S(1)}, f32[112,256]{1,0:T(8,128)S(1)}, u32[]{:S(2)}, u32[]{:S(2)}) %collective-permute-start.1) | collective-permute-done | bytes 114720 | tf_op jit(solution)/shard_map/ppermute | solution.py:326
  20.7 1.6 %collective-permute-start.6 = (f32[112,256]{1,0:T(8,128)S(1)}, f32[112,256]{1,0:T(8,128)S(1)}, u32[]{:S(2)}, u32[]{:S(2)}) collective-permute-start(f32[112,256]{1,0:T(8,128)S(1)} %collective-permute-done.2.refs_4_), channel_id=1, source_target_pairs={{1,0},{0,2},{2,4},{4,6},{6,7},{7,5},{5,3},{3,1},{9,8},{8,10},{10,1... | collective-permute-start | bytes 344072 | tf_op jit(solution)/shard_map/ppermute | solution.py:326
  24.3 1.6 %collective-permute-done.6.refs_8_ = f32[112,256]{1,0:T(8,128)S(1)} collective-permute-done((f32[112,256]{1,0:T(8,128)S(1)}, f32[112,256]{1,0:T(8,128)S(1)}, u32[]{:S(2)}, u32[]{:S(2)}) %collective-permute-start.6) | collective-permute-done | bytes 114720 | tf_op jit(solution)/shard_map/ppermute | solution.py:326
  30.8 1.5 %collective-permute-start.12 = (f32[112,256]{1,0:T(8,128)S(1)}, f32[112,256]{1,0:T(8,128)S(1)}, u32[]{:S(2)}, u32[]{:S(2)}) collective-permute-start(f32[112,256]{1,0:T(8,128)S(1)} %collective-permute-done.8.refs_10_), channel_id=1, source_target_pairs={{1,0},{0,2},{2,4},{4,6},{6,7},{7,5},{5,3},{3,1},{9,8},{8,10},{10,1... | collective-permute-start | bytes 344072 | tf_op jit(solution)/shard_map/ppermute | solution.py:328
  33.8 1.8 %collective-permute-done.12.refs_14_ = f32[112,256]{1,0:T(8,128)S(1)} collective-permute-done((f32[112,256]{1,0:T(8,128)S(1)}, f32[112,256]{1,0:T(8,128)S(1)}, u32[]{:S(2)}, u32[]{:S(2)}) %collective-permute-start.12) | collective-permute-done | bytes 114720 | tf_op jit(solution)/shard_map/ppermute | solution.py:328
  35.6 1.5 %collective-permute-done.13.refs_15_ = f32[112,256]{1,0:T(8,128)S(1)} collective-permute-done((f32[112,256]{1,0:T(8,128)S(1)}, f32[112,256]{1,0:T(8,128)S(1)}, u32[]{:S(2)}, u32[]{:S(2)}) %collective-permute-start.13) | collective-permute-done | bytes 114720 | tf_op jit(solution)/shard_map/ppermute | solution.py:328
  37.1 3.3 %shard_map.60 = (bf16[4,640,256]{2,1,0:T(8,128)(2,1)S(1)}, bf16[4,640,256]{2,1,0:T(8,128)(2,1)S(1)}, f32[448,256]{1,0:T(8,128)S(1)}, f32[448,128]{1,0:T(8,128)S(1)}) custom-call(s32[1,1792]{1,0:T(1,128)S(1)} %reshape.7.structure_ref, f32[112,256]{1,0:T(8,128)S(1)} %get-tuple-element.26.refs_0_, f32[112,256]{1,0:T(8,128)S(1)} %get-tuple-element.27.refs_1_, ...), custom_call_target="tpu_custom_call" | custom-call | flops 880803840 | bytes 7216128 | tf_op jit(solution)/shard_map/pallas_call | solution.py:287
  43.1 1.8 %shard_map.62 = (f32[112,256]{1,0:T(8,128)S(1)}, f32[112,256]{1,0:T(8,128)S(1)}, f32[112,256]{1,0:T(8,128)S(1)}, f32[112,256]{1,0:T(8,128)S(1)}) custom-call(bf16[4,640,256]{2,1,0:T(8,128)(2,1)S(1)} %get-tuple-element.33.uh_ref, bf16[4,640,256]{2,1,0:T(8,128)(2,1)S(1)} %get-tuple-element.34.ul_ref, f32[448,256]{1,0:T(8,128)S(1)} %get-tuple-element.35.part_ref, ...), custom_call_target="tpu_custom_call" | custom-call | flops 440401920 | bytes 4972544 | tf_op jit(solution)/shard_map/pallas_call | solution.py:287
  44.9 3.6 %collective-permute-done.17.refs_2_ = f32[448,128]{1,0:T(8,128)S(1)} collective-permute-done((f32[448,128]{1,0:T(8,128)S(1)}, f32[448,128]{1,0:T(8,128)S(1)}, u32[]{:S(2)}, u32[]{:S(2)}) %collective-permute-start.17) | collective-permute-done | bytes 229408 | tf_op jit(solution)/shard_map/ppermute | solution.py:304
  48.5 1.6 %collective-permute-start.20 = (f32[112,256]{1,0:T(8,128)S(1)}, f32[112,256]{1,0:T(8,128)S(1)}, u32[]{:S(2)}, u32[]{:S(2)}) collective-permute-start(f32[112,256]{1,0:T(8,128)S(1)} %get-tuple-element.42), channel_id=1, source_target_pairs={{0,2},{1,3},{2,4},{3,5},{4,6},{5,7},{6,0},{7,1},{8,10},{9,11},{10,... | collective-permute-start | bytes 344072 | tf_op jit(solution)/shard_map/ppermute | solution.py:422
  50.1 2.9 %collective-permute-start.21 = (f32[112,256]{1,0:T(8,128)S(1)}, f32[112,256]{1,0:T(8,128)S(1)}, u32[]{:S(2)}, u32[]{:S(2)}) collective-permute-start(f32[112,256]{1,0:T(8,128)S(1)} %get-tuple-element.43), channel_id=1, source_target_pairs={{0,4},{1,5},{2,6},{3,7},{4,0},{5,1},{6,2},{7,3},{8,12},{9,13},{10,... | collective-permute-start | bytes 344072 | tf_op jit(solution)/shard_map/ppermute | solution.py:422
  57.8 3.3 %collective-permute-done.21.refs_2_ = f32[112,256]{1,0:T(8,128)S(1)} collective-permute-done((f32[112,256]{1,0:T(8,128)S(1)}, f32[112,256]{1,0:T(8,128)S(1)}, u32[]{:S(2)}, u32[]{:S(2)}) %collective-permute-start.21) | collective-permute-done | bytes 114720 | tf_op jit(solution)/shard_map/ppermute | solution.py:422
  63.2 1.5 %shard_map.63 = (bf16[448,896]{1,0:T(8,128)(2,1)S(1)}, bf16[4,128,448]{2,1,0:T(8,128)(2,1)S(1)}, bf16[4,128,448]{2,1,0:T(8,128)(2,1)S(1)}) custom-call(s32[1,1792]{1,0:T(1,128)S(1)} %reshape.7.structure_ref, f32[448,128]{1,0:T(8,128)S(1)} %get-tuple-element.32.refs_0_, f32[448,128]{1,0:T(8,128)S(1)} %collective-permute-done.16.refs_1_, ...), custom_call_target="tpu_custom_call" | custom-call | bytes 2644992 | tf_op jit(solution)/shard_map/pallas_call | solution.py:287
  64.7 2.4 %collective-permute-done.25.refs_6_ = f32[112,256]{1,0:T(8,128)S(1)} collective-permute-done((f32[112,256]{1,0:T(8,128)S(1)}, f32[112,256]{1,0:T(8,128)S(1)}, u32[]{:S(2)}, u32[]{:S(2)}) %collective-permute-start.25) | collective-permute-done | bytes 114720 | tf_op jit(solution)/shard_map/ppermute | solution.py:298
  67.2 1.5 %collective-permute-done.26.refs_7_ = f32[112,256]{1,0:T(8,128)S(1)} collective-permute-done((f32[112,256]{1,0:T(8,128)S(1)}, f32[112,256]{1,0:T(8,128)S(1)}, u32[]{:S(2)}, u32[]{:S(2)}) %collective-permute-start.26) | collective-permute-done | bytes 114720 | tf_op jit(solution)/shard_map/ppermute | solution.py:298
  68.7 2.7 %shard_map.64 = (f32[224,256]{1,0:T(8,128)}, f32[128,256]{1,0:T(8,128)S(1)}, f32[128,256]{1,0:T(8,128)S(1)}, f32[128,256]{1,0:T(8,128)S(1)}, f32[128,256]{1,0:T(8,128)S(1)}) custom-call(bf16[448,896]{1,0:T(8,128)(2,1)S(1)} %get-tuple-element.39.from_ref, bf16[4,128,448]{2,1,0:T(8,128)(2,1)S(1)} %get-tuple-element.40.high_ref, ...), custom_call_target="tpu_custom_call" | custom-call | flops 440401920 | bytes 3391488 | tf_op jit(solution)/shard_map/pallas_call | solution.py:287
  72.1 3.4 %collective-permute-start.28 = (f32[128,256]{1,0:T(8,128)S(1)}, f32[128,256]{1,0:T(8,128)S(1)}, u32[]{:S(2)}, u32[]{:S(2)}) collective-permute-start(f32[128,256]{1,0:T(8,128)S(1)} %get-tuple-element.48), channel_id=1, source_target_pairs={{0,4},{1,5},{2,6},{3,7},{4,0},{5,1},{6,2},{7,3},{8,12},{9,13},{10,... | collective-permute-start | bytes 393224 | tf_op jit(solution)/shard_map/ppermute | solution.py:440
  76.0 3.6 %collective-permute-done.27 = f32[128,256]{1,0:T(8,128)S(1)} collective-permute-done((f32[128,256]{1,0:T(8,128)S(1)}, f32[128,256]{1,0:T(8,128)S(1)}, u32[]{:S(2)}, u32[]{:S(2)}) %collective-permute-start.27) | collective-permute-done | bytes 131104 | tf_op jit(solution)/shard_map/ppermute | solution.py:440
  79.7 3.8 %collective-permute-done.28 = f32[128,256]{1,0:T(8,128)S(1)} collective-permute-done((f32[128,256]{1,0:T(8,128)S(1)}, f32[128,256]{1,0:T(8,128)S(1)}, u32[]{:S(2)}, u32[]{:S(2)}) %collective-permute-start.28) | collective-permute-done | bytes 131104 | tf_op jit(solution)/shard_map/ppermute | solution.py:440
  (48 shorter events, 26.2 us)
Async XLA Ops:
  5.6 31.5 %collective-permute-start.14 = (f32[2016,128]{1,0:T(8,128)S(1)}, f32[2016,128]{1,0:T(8,128)S(1)}, u32[]{:S(2)}, u32[]{:S(2)}) collective-permute-start(f32[2016,128]{1,0:T(8,128)S(1)} %get-tuple-element.28.refs_16_), channel_id=1, source_target_pairs={{0,8},{8,0},{16,24},{24,16},{1,9},{9,1},{17,25},{25,17},{2,10},{10... | collective-permute-start | bytes 3096584 | tf_op jit(solution)/shard_map/ppermute | solution.py:298
  6.2 34.2 %collective-permute-start.15 = (f32[2016,128]{1,0:T(8,128)S(1)}, f32[2016,128]{1,0:T(8,128)S(1)}, u32[]{:S(2)}, u32[]{:S(2)}) collective-permute-start(f32[2016,128]{1,0:T(8,128)S(1)} %get-tuple-element.28.refs_16_), channel_id=1, source_target_pairs={{0,16},{8,24},{16,0},{24,8},{1,17},{9,25},{17,1},{25,9},{2,18},{10... | collective-permute-start | bytes 3096584 | tf_op jit(solution)/shard_map/ppermute | solution.py:385
  8.7 6.0 %collective-permute-start = (f32[112,256]{1,0:T(8,128)S(1)}, f32[112,256]{1,0:T(8,128)S(1)}, u32[]{:S(2)}, u32[]{:S(2)}) collective-permute-start(f32[112,256]{1,0:T(8,128)S(1)} %get-tuple-element.26.refs_0_), channel_id=1, source_target_pairs={{1,0},{0,2},{2,4},{4,6},{6,7},{7,5},{5,3},{3,1},{9,8},{8,10},{10,1... | collective-permute-start | bytes 344072 | tf_op jit(solution)/shard_map/ppermute | solution.py:326
  10.3 5.9 %collective-permute-start.3 = (f32[112,256]{1,0:T(8,128)S(1)}, f32[112,256]{1,0:T(8,128)S(1)}, u32[]{:S(2)}, u32[]{:S(2)}) collective-permute-start(f32[112,256]{1,0:T(8,128)S(1)} %get-tuple-element.27.refs_1_), channel_id=1, source_target_pairs={{0,1},{2,0},{4,2},{6,4},{7,6},{5,7},{3,5},{1,3},{8,9},{10,8},{12,1... | collective-permute-start | bytes 344072 | tf_op jit(solution)/shard_map/ppermute | solution.py:326
  10.7 6.1 %collective-permute-start.2 = (f32[112,256]{1,0:T(8,128)S(1)}, f32[112,256]{1,0:T(8,128)S(1)}, u32[]{:S(2)}, u32[]{:S(2)}) collective-permute-start(f32[112,256]{1,0:T(8,128)S(1)} %get-tuple-element.27.refs_1_), channel_id=1, source_target_pairs={{1,0},{0,2},{2,4},{4,6},{6,7},{7,5},{5,3},{3,1},{9,8},{8,10},{10,1... | collective-permute-start | bytes 344072 | tf_op jit(solution)/shard_map/ppermute | solution.py:326
  14.7 6.0 %collective-permute-start.1 = (f32[112,256]{1,0:T(8,128)S(1)}, f32[112,256]{1,0:T(8,128)S(1)}, u32[]{:S(2)}, u32[]{:S(2)}) collective-permute-start(f32[112,256]{1,0:T(8,128)S(1)} %get-tuple-element.26.refs_0_), channel_id=1, source_target_pairs={{0,1},{2,0},{4,2},{6,4},{7,6},{5,7},{3,5},{1,3},{8,9},{10,8},{12,1... | collective-permute-start | bytes 344072 | tf_op jit(solution)/shard_map/ppermute | solution.py:326
  16.2 6.0 %collective-permute-start.4 = (f32[112,256]{1,0:T(8,128)S(1)}, f32[112,256]{1,0:T(8,128)S(1)}, u32[]{:S(2)}, u32[]{:S(2)}) collective-permute-start(f32[112,256]{1,0:T(8,128)S(1)} %collective-permute-done.refs_2_), channel_id=1, source_target_pairs={{1,0},{0,2},{2,4},{4,6},{6,7},{7,5},{5,3},{3,1},{9,8},{8,10},{10,1... | collective-permute-start | bytes 344072 | tf_op jit(solution)/shard_map/ppermute | solution.py:326
  16.8 6.9 %collective-permute-start.7 = (f32[112,256]{1,0:T(8,128)S(1)}, f32[112,256]{1,0:T(8,128)S(1)}, u32[]{:S(2)}, u32[]{:S(2)}) collective-permute-start(f32[112,256]{1,0:T(8,128)S(1)} %collective-permute-done.3.refs_5_), channel_id=1, source_target_pairs={{0,1},{2,0},{4,2},{6,4},{7,6},{5,7},{3,5},{1,3},{8,9},{10,8},{12,1... | collective-permute-start | bytes 344072 | tf_op jit(solution)/shard_map/ppermute | solution.py:326
  20.7 5.3 %collective-permute-start.6 = (f32[112,256]{1,0:T(8,128)S(1)}, f32[112,256]{1,0:T(8,128)S(1)}, u32[]{:S(2)}, u32[]{:S(2)}) collective-permute-start(f32[112,256]{1,0:T(8,128)S(1)} %collective-permute-done.2.refs_4_), channel_id=1, source_target_pairs={{1,0},{0,2},{2,4},{4,6},{6,7},{7,5},{5,3},{3,1},{9,8},{8,10},{10,1... | collective-permute-start | bytes 344072 | tf_op jit(solution)/shard_map/ppermute | solution.py:326
  22.3 5.2 %collective-permute-start.5 = (f32[112,256]{1,0:T(8,128)S(1)}, f32[112,256]{1,0:T(8,128)S(1)}, u32[]{:S(2)}, u32[]{:S(2)}) collective-permute-start(f32[112,256]{1,0:T(8,128)S(1)} %collective-permute-done.1.refs_3_), channel_id=1, source_target_pairs={{0,1},{2,0},{4,2},{6,4},{7,6},{5,7},{3,5},{1,3},{8,9},{10,8},{12,1... | collective-permute-start | bytes 344072 | tf_op jit(solution)/shard_map/ppermute | solution.py:326
  23.8 5.1 %collective-permute-start.8 = (f32[112,256]{1,0:T(8,128)S(1)}, f32[112,256]{1,0:T(8,128)S(1)}, u32[]{:S(2)}, u32[]{:S(2)}) collective-permute-start(f32[112,256]{1,0:T(8,128)S(1)} %collective-permute-done.4.refs_6_), channel_id=1, source_target_pairs={{1,0},{0,2},{2,4},{4,6},{6,7},{7,5},{5,3},{3,1},{9,8},{8,10},{10,1... | collective-permute-start | bytes 344072 | tf_op jit(solution)/shard_map/ppermute | solution.py:326
  40.5 8.0 %collective-permute-start.17 = (f32[448,128]{1,0:T(8,128)S(1)}, f32[448,128]{1,0:T(8,128)S(1)}, u32[]{:S(2)}, u32[]{:S(2)}) collective-permute-start(f32[448,128]{1,0:T(8,128)S(1)} %get-tuple-element.32.refs_0_), channel_id=1, source_target_pairs={{0,16},{8,24},{16,0},{24,8},{1,17},{9,25},{17,1},{25,9},{2,18},{10... | collective-permute-start | bytes 688136 | tf_op jit(solution)/shard_map/ppermute | solution.py:304
  41.1 13.0 %collective-permute-start.16 = (f32[448,128]{1,0:T(8,128)S(1)}, f32[448,128]{1,0:T(8,128)S(1)}, u32[]{:S(2)}, u32[]{:S(2)}) collective-permute-start(f32[448,128]{1,0:T(8,128)S(1)} %get-tuple-element.32.refs_0_), channel_id=1, source_target_pairs={{0,8},{8,0},{16,24},{24,16},{1,9},{9,1},{17,25},{25,17},{2,10},{10... | collective-permute-start | bytes 688136 | tf_op jit(solution)/shard_map/ppermute | solution.py:298
  48.5 14.7 %collective-permute-start.19 = (f32[448,128]{1,0:T(8,128)S(1)}, f32[448,128]{1,0:T(8,128)S(1)}, u32[]{:S(2)}, u32[]{:S(2)}) collective-permute-start(f32[448,128]{1,0:T(8,128)S(1)} %collective-permute-done.17.refs_2_), channel_id=1, source_target_pairs={{0,8},{8,0},{16,24},{24,16},{1,9},{9,1},{17,25},{25,17},{2,10},{10... | collective-permute-start | bytes 688136 | tf_op jit(solution)/shard_map/ppermute | solution.py:298
  48.5 8.0 %collective-permute-start.20 = (f32[112,256]{1,0:T(8,128)S(1)}, f32[112,256]{1,0:T(8,128)S(1)}, u32[]{:S(2)}, u32[]{:S(2)}) collective-permute-start(f32[112,256]{1,0:T(8,128)S(1)} %get-tuple-element.42), channel_id=1, source_target_pairs={{0,2},{1,3},{2,4},{3,5},{4,6},{5,7},{6,0},{7,1},{8,10},{9,11},{10,... | collective-permute-start | bytes 344072 | tf_op jit(solution)/shard_map/ppermute | solution.py:422
  50.1 11.1 %collective-permute-start.21 = (f32[112,256]{1,0:T(8,128)S(1)}, f32[112,256]{1,0:T(8,128)S(1)}, u32[]{:S(2)}, u32[]{:S(2)}) collective-permute-start(f32[112,256]{1,0:T(8,128)S(1)} %get-tuple-element.43), channel_id=1, source_target_pairs={{0,4},{1,5},{2,6},{3,7},{4,0},{5,1},{6,2},{7,3},{8,12},{9,13},{10,... | collective-permute-start | bytes 344072 | tf_op jit(solution)/shard_map/ppermute | solution.py:422
  52.9 9.4 %collective-permute-start.22 = (f32[112,256]{1,0:T(8,128)S(1)}, f32[112,256]{1,0:T(8,128)S(1)}, u32[]{:S(2)}, u32[]{:S(2)}) collective-permute-start(f32[112,256]{1,0:T(8,128)S(1)} %get-tuple-element.44), channel_id=1, source_target_pairs={{0,6},{1,7},{2,0},{3,1},{4,2},{5,3},{6,4},{7,5},{8,14},{9,15},{10,... | collective-permute-start | bytes 344072 | tf_op jit(solution)/shard_map/ppermute | solution.py:422
  54.0 10.7 %collective-permute-start.23 = (f32[112,256]{1,0:T(8,128)S(1)}, f32[112,256]{1,0:T(8,128)S(1)}, u32[]{:S(2)}, u32[]{:S(2)}) collective-permute-start(f32[112,256]{1,0:T(8,128)S(1)} %get-tuple-element.37.refs_0_), channel_id=1, source_target_pairs={{0,1},{1,0},{2,3},{3,2},{4,5},{5,4},{6,7},{7,6},{8,9},{9,8},{10,11... | collective-permute-start | bytes 344072 | tf_op jit(solution)/shard_map/ppermute | solution.py:298
  56.5 8.2 %collective-permute-start.24 = (f32[112,256]{1,0:T(8,128)S(1)}, f32[112,256]{1,0:T(8,128)S(1)}, u32[]{:S(2)}, u32[]{:S(2)}) collective-permute-start(f32[112,256]{1,0:T(8,128)S(1)} %collective-permute-done.20.refs_1_), channel_id=1, source_target_pairs={{0,1},{1,0},{2,3},{3,2},{4,5},{5,4},{6,7},{7,6},{8,9},{9,8},{10,11... | collective-permute-start | bytes 344072 | tf_op jit(solution)/shard_map/ppermute | solution.py:298
  61.1 6.0 %collective-permute-start.25 = (f32[112,256]{1,0:T(8,128)S(1)}, f32[112,256]{1,0:T(8,128)S(1)}, u32[]{:S(2)}, u32[]{:S(2)}) collective-permute-start(f32[112,256]{1,0:T(8,128)S(1)} %collective-permute-done.21.refs_2_), channel_id=1, source_target_pairs={{0,1},{1,0},{2,3},{3,2},{4,5},{5,4},{6,7},{7,6},{8,9},{9,8},{10,11... | collective-permute-start | bytes 344072 | tf_op jit(solution)/shard_map/ppermute | solution.py:298
  62.3 6.3 %collective-permute-start.26 = (f32[112,256]{1,0:T(8,128)S(1)}, f32[112,256]{1,0:T(8,128)S(1)}, u32[]{:S(2)}, u32[]{:S(2)}) collective-permute-start(f32[112,256]{1,0:T(8,128)S(1)} %collective-permute-done.22.refs_3_), channel_id=1, source_target_pairs={{0,1},{1,0},{2,3},{3,2},{4,5},{5,4},{6,7},{7,6},{8,9},{9,8},{10,11... | collective-permute-start | bytes 344072 | tf_op jit(solution)/shard_map/ppermute | solution.py:298
  71.4 8.3 %collective-permute-start.27 = (f32[128,256]{1,0:T(8,128)S(1)}, f32[128,256]{1,0:T(8,128)S(1)}, u32[]{:S(2)}, u32[]{:S(2)}) collective-permute-start(f32[128,256]{1,0:T(8,128)S(1)} %get-tuple-element.47), channel_id=1, source_target_pairs={{0,2},{1,3},{2,4},{3,5},{4,6},{5,7},{6,0},{7,1},{8,10},{9,11},{10,... | collective-permute-start | bytes 393224 | tf_op jit(solution)/shard_map/ppermute | solution.py:440
  72.1 11.4 %collective-permute-start.28 = (f32[128,256]{1,0:T(8,128)S(1)}, f32[128,256]{1,0:T(8,128)S(1)}, u32[]{:S(2)}, u32[]{:S(2)}) collective-permute-start(f32[128,256]{1,0:T(8,128)S(1)} %get-tuple-element.48), channel_id=1, source_target_pairs={{0,4},{1,5},{2,6},{3,7},{4,0},{5,1},{6,2},{7,3},{8,12},{9,13},{10,... | collective-permute-start | bytes 393224 | tf_op jit(solution)/shard_map/ppermute | solution.py:440
  75.4 8.1 %collective-permute-start.29 = (f32[128,256]{1,0:T(8,128)S(1)}, f32[128,256]{1,0:T(8,128)S(1)}, u32[]{:S(2)}, u32[]{:S(2)}) collective-permute-start(f32[128,256]{1,0:T(8,128)S(1)} %get-tuple-element.49), channel_id=1, source_target_pairs={{0,6},{1,7},{2,0},{3,1},{4,2},{5,3},{6,4},{7,5},{8,14},{9,15},{10,... | collective-permute-start | bytes 393224 | tf_op jit(solution)/shard_map/ppermute | solution.py:440
  (8 other events, 42.7 us)

commit v5 on v4

--- a/solution.py
+++ b/solution.py
@@ -65,24 +65,20 @@
             fn(owner, ref)
 
 
-def select_kernel(structure_ref, sigma_ref, u_ref, out_ref, top_ref, low_ref, held_ref, sems):
+def select_kernel(structure_ref, sigma_ref, out_ref, held_ref, sems):
     rows, cols = held_ref.shape
-    n = structure_ref.shape[1]
-    parts = sems.shape[0] - 2
+    n = structure_ref.shape[0]
+    parts = sems.shape[0]
     part = rows // parts
     copies = []
     for k in range(parts):
         at = pl.ds(part * k, part)
         copies.append(pltpu.make_async_copy(sigma_ref.at[at, :], held_ref.at[at, :], sems.at[k]))
         copies[-1].start()
-    half = top_ref.shape[0]
-    halves = []
-    for k, ref in enumerate((top_ref, low_ref)):
-        halves.append(pltpu.make_async_copy(u_ref.at[pl.ds(half * k, half), :], ref, sems.at[parts + k]))
-        halves[-1].start()
     first = lax.axis_index("prow") * cols
-    names = jnp.broadcast_to(structure_ref[...], (8, n))
-    shift = lax.rem(n - count(structure_ref[...] < first), n)
+    listed = structure_ref[...].reshape(1, -1)
+    names = jnp.broadcast_to(listed, (8, n))
+    shift = lax.rem(n - count(listed < first), n)
     named = pltpu.roll(names, shift, 1)[:1, :CAP] - first
     named = jnp.concatenate([named, named[:, FULL * LANES :]], axis=1)
     at = lax.broadcasted_iota(jnp.int32, (cols, WIDE), 0)
@@ -99,8 +95,6 @@
             out_ref[at : at + part, : LANES // 2] = picked[:, FULL * LANES : CAP]
         else:
             out_ref[at : at + part, LANES // 2 :] = picked[:, CAP:]
-    for copy in halves:
-        copy.wait()
 
 
 def block_term(block_ref, uh, ul, rows):
@@ -119,14 +113,14 @@
         pair_ref, refs = refs[-2], refs[:-2] + refs[-1:]
     uh_ref, ul_ref, part_ref, us_ref = refs[-4:]
     nr, _, w = uh_ref.shape
-    n_u = 2 * nc if direct else 1
+    n_u = nc if direct else 1
     u_refs, first_refs = refs[:n_u], refs[n_u:-4]
-    n = structure_ref.shape[1]
+    n = structure_ref.shape[0]
     m = n // nc
     c = lax.axis_index("pcol")
     r = lax.axis_index("prow")
     rows = part_ref.shape[0]
-    names = structure_ref[...]
+    names = structure_ref[...].reshape(1, -1)
 
     def place(owner, u):
         if w % LANES:
@@ -136,16 +130,13 @@
 
     if direct:
         lane = pl.multiple_of((c & 1) * (w // 2), LANES)
-        size = m // 2
-        for h in range(2):
-            pair_ref[size * h : size * (h + 1), :] = u_refs[h][:, pl.ds(lane, w // 2)]
-        for (owner, h), u_ref in zip(ring_owners(nc, c), u_refs):
-            place(nc * size * h + owner, u_ref[...])
-            at = m + size * h
+        pair_ref[:m, :] = u_refs[0][:, pl.ds(lane, w // 2)]
+        for owner, u_ref in zip(ring_owners(nc, c), u_refs):
+            place(owner, u_ref[...])
 
             @pl.when(owner == jnp.bitwise_xor(c, 1))
             def _():
-                pair_ref[at : at + size, :] = u_ref[:, pl.ds(lane, w // 2)]
+                pair_ref[m:, :] = u_ref[:, pl.ds(lane, w // 2)]
 
     else:
         pl.loop(0, nc)(lambda k: place(k, u_refs[0][k]))
@@ -202,7 +193,7 @@
         image = image + block_term(block_ref, uh_ref[owner], ul_ref[owner], rows)
     image_ref[...] = image
     nc = to_ref.shape[0] // slots
-    to_ref[...] = row_order(structure_ref[...], lax.axis_index("pcol"), rows, nc, slots, direct)
+    to_ref[...] = row_order(structure_ref[...].reshape(1, -1), lax.axis_index("pcol"), rows, nc, slots, direct)
 
 
 def image_kernel(n_out, owners, uh_ref, ul_ref, part_ref, to_ref, *refs):
@@ -227,9 +218,9 @@
     nz = high_ref.shape[0]
     nc = 2 * nz
     rows = slots * nc
-    n = structure_ref.shape[1]
+    n = structure_ref.shape[0]
     m = n // nc
-    names = structure_ref[...]
+    names = structure_ref[...].reshape(1, -1)
     c = lax.axis_index("pcol")
     z = c // 2
 
@@ -298,12 +289,11 @@
     return lax.ppermute(v, axis, [(k, k ^ 1) for k in range(size)])
 
 
-def spread(v, size, after):
+def spread(v, size):
     blocks = [v, swap(v, "prow", size)]
     for t in range(1, size // 2):
-        far = lax.ppermute(v, "prow", [(k, (k + 2 * t) % size) for k in range(size)])
-        far, _ = lax.optimization_barrier((far, after))
-        blocks += [far, swap(far, "prow", size)]
+        for flip in range(2):
+            blocks.append(lax.ppermute(v, "prow", [(k, ((k + 2 * t) % size) ^ flip) for k in range(size)]))
     return blocks
 
 
@@ -315,27 +305,25 @@
     return out
 
 
-def ring_gather(halves, nc):
+def ring_gather(u, nc):
     ring = [2 * z for z in range(nc // 2)] + [2 * z + 1 for z in reversed(range(nc // 2))]
     pairs = [(ring[q - 1], ring[q]) for q in range(nc)]
     back = [(b, a) for a, b in pairs]
-    held = [(v, v) for v in halves]
-    blocks = list(halves)
+    blocks = [u]
+    up = down = u
     for step in range(1, nc // 2):
-        for h in range(2):
-            held[h] = lax.ppermute(held[h][0], "pcol", pairs), lax.ppermute(held[h][1], "pcol", back)
-            blocks += held[h]
-    return blocks + [lax.ppermute(held[0][0], "pcol", pairs), lax.ppermute(held[1][1], "pcol", back)]
+        up, down = lax.ppermute(up, "pcol", pairs), lax.ppermute(down, "pcol", back)
+        blocks += [up, down]
+    return blocks + [lax.ppermute(up, "pcol", pairs)]
 
 
 def ring_owners(nc, c):
     q = jnp.where((c & 1) == 0, c >> 1, nc - 1 - (c >> 1))
-    out = [(c, 0), (c, 1)]
-    for step in range(1, nc // 2 + 1):
-        for h in range(2):
-            for sign in (-1, 1) if step < nc // 2 else (-1,):
-                at = (q + sign * step) & (nc - 1)
-                out.append((jnp.where(at < nc // 2, 2 * at, 2 * (nc - 1 - at) + 1), h))
+    out = []
+    for k in range(nc):
+        step = (k + 1) // 2
+        at = (q - step if k % 2 else q + step) & (nc - 1)
+        out.append(jnp.where(at < nc // 2, 2 * at, 2 * (nc - 1 - at) + 1))
     return out
 
 
@@ -349,38 +337,38 @@
     n = structure.shape[0]
     slots = -(-rows // nc)
     direct = nc <= 8
-    names = structure.reshape(1, n)
+    names = structure
     groups = [[2 * k + x for k in range(nz)] for x in range(2)]
     owners = functools.partial(relative_owners, nr)
 
-    chosen, *halves = call(
+    chosen = call(
         select_kernel,
-        [f32(rows * CAP // LANES, LANES), f32(m // 2, w), f32(m // 2, w)],
+        f32(rows * CAP // LANES, LANES),
         names,
         sigma_top,
-        u_panel,
-        in_specs=[VMEM, HBM, HBM],
-        scratch_shapes=[pltpu.VMEM((rows, cols), jnp.float32), pltpu.SemaphoreType.DMA((6,))],
+        in_specs=[VMEM, HBM],
+        scratch_shapes=[pltpu.VMEM((rows, cols), jnp.float32), pltpu.SemaphoreType.DMA((4,))],
         flops=4 * rows * cols * WIDE,
         vmem=52,
     )
-    near = [chosen, swap(chosen, "prow", nr)] if direct else []
-    if direct:
-        u_all = ring_gather(halves, nc)
+    near = [chosen] if direct else []
+    if direct:
+        u_all = ring_gather(u_panel, nc)
     else:
         u_all = [lax.all_gather(u_panel, "pcol")]
     term = 6 * rows * WIDE * w
     uh, ul, image, *pair = call(
-        functools.partial(prepare_kernel, direct, nc, lambda r: owners(r)[:2]),
+        functools.partial(prepare_kernel, direct, nc, lambda r: owners(r)[:1]),
         [bf16(nr, WIDE, w), bf16(nr, WIDE, w), f32(rows, w)] + [f32(2 * m, wd)] * direct,
         names,
         *u_all,
         *near,
         scratch_shapes=[pltpu.VMEM((-(-w // LANES), n + CAP + 8, LANES), jnp.float32)],
-        flops=2 * term,
+        flops=term,
     )
     beside, later = [], []
     if direct:
+        beside.append(swap(chosen, "prow", nr))
         for t in range(1, nr // 2):
             far = lax.ppermute(chosen, "prow", [(k, (k + 2 * t) % nr) for k in range(nr)])
             far, _ = lax.optimization_barrier((far, image))
@@ -389,7 +377,7 @@
     else:
         later = [lax.all_gather(chosen, "prow")]
     image, to = call(
-        functools.partial(near_kernel, direct, slots, lambda r: owners(r)[2::2]),
+        functools.partial(near_kernel, direct, slots, lambda r: owners(r)[1:2] + owners(r)[2::2]),
         [f32(rows, w), bf16(nc * slots, rows)],
         names,
         uh,
@@ -398,6 +386,14 @@
         *beside,
         flops=term,
     )
+    if direct:
+        pair, _ = lax.optimization_barrier((pair[0], beside[1]))
+        pairs = spread(pair, nr)
+        pairs[1], to = lax.optimization_barrier((pairs[1], to))
+    else:
+        pair = jnp.concatenate([u_panel, swap(u_panel, "pcol", nc)], axis=0)
+        pair = jnp.where(jnp.bitwise_and(c, 1) == 0, pair[:, :wd], pair[:, wd:])
+        pairs = [lax.all_gather(pair, "prow")]
     n_out = nz if direct else 1
     sent = call(
         functools.partial(image_kernel, n_out, (lambda r: owners(r)[3::2]) if direct else None),
@@ -410,13 +406,6 @@
         flops=term,
     )
     if direct:
-        pair, _ = lax.optimization_barrier((pair[0], beside[0]))
-        pairs = spread(pair, nr, sent[0])
-    else:
-        pair = jnp.concatenate([u_panel, swap(u_panel, "pcol", nc)], axis=0)
-        pair = jnp.where(jnp.bitwise_and(c, 1) == 0, pair[:, :wd], pair[:, wd:])
-        pairs = [lax.all_gather(pair, "prow")]
-    if direct:
         got = [sent[0]]
         for t in range(1, nz):
             got.append(lax.ppermute(sent[t], "pcol", [(k, (k + 2 * t) % nc) for k in range(nc)]))
@@ -425,7 +414,6 @@
         blocks = lax.all_to_all(blocks, "pcol", split_axis=0, concat_axis=0, axis_index_groups=groups, tiled=True)
         got = [blocks.reshape(nc * slots, w)]
     got = got + [swap(v, "pcol", nc) for v in got]
-
     source, high, low = call(
         functools.partial(turn_kernel, direct, slots, owners),
         [bf16(2 * m, 2 * nc * slots), bf16(nz, wd, 2 * m), bf16(nz, wd, 2 * m)],

time: 84.6 us -> 78.7 us (0.930)
  starting transfers between devices: 37 us -> 28.1 us
  waiting for transfers between devices: 30.2 us -> 33.6 us
  local copies, waits for them, and re-layouts: 1.64 us -> 0.74 us
    ppermute x15 -> x9, starting transfers between devices: 18.6 us -> 9.12 us  [the longest x3 4.85 us: ring_gather(): lax.ppermute(up, 'pcol', pairs)]
    ppermute x15 -> x9, waiting for transfers between devices: 14 us -> 18 us  [the longest x3 13.6 us: ring_gather(): lax.ppermute(up, 'pcol', pairs)]
    ppermute x8 -> x7, waiting for transfers between devices: 4.57 us -> 3.98 us  [swap(): return lax.ppermute(v, axis, [(k, k ^ 1) for k in range(size)])]
    ppermute x8 -> x7, starting transfers between devices: 5.68 us -> 5.61 us  [swap(): return lax.ppermute(v, axis, [(k, k ^ 1) for k in range(size)])]
  transfers between devices with their start and end apart: 30 -> 23, of which waited for: 14 -> 11; matrix products, arithmetic and copies ran while one was open for 0% -> 0% of each run, Pallas kernels for 9% -> 10%
where the time goes in v5:
time: 78.7 us; the launch traced here: 78.2 us
  waiting for transfers between devices  33.6 us (43%)
  starting transfers between devices  28.1 us (36%)
  Pallas kernels  14.2 us (18%)
    pallas_call x6, Pallas kernels, call(): pl.pallas_call(kernel, out_shape=out_shape, out_specs=[VMEM] * len(out_sh...  14.2 us
    ppermute x3, waiting for transfers between devices, ring_gather(): lax.ppermute(up, 'pcol', pairs)  13.6 us
    ppermute x3, waiting for transfers between devices, per_device(): lax.ppermute(terms[t], 'pcol', [(k, (k + 2 * t) % nc) for k in range(nc)])  7.56 us
    ppermute x7, starting transfers between devices, swap(): return lax.ppermute(v, axis, [(k, k ^ 1) for k in range(size)])  5.61 us
    ppermute x3, starting transfers between devices, per_device(): lax.ppermute(sent[t], 'pcol', [(k, (k + 2 * t) % nc) for k in range(nc)])  5.57 us
    ppermute x3, starting transfers between devices, ring_gather(): lax.ppermute(up, 'pcol', pairs)  4.85 us
    ppermute x3, starting transfers between devices, per_device(): lax.ppermute(terms[t], 'pcol', [(k, (k + 2 * t) % nc) for k in range(nc)])  4.81 us
    ppermute x1, waiting for transfers between devices, ring_gather(): return blocks + [lax.ppermute(up, 'pcol', pairs)]  4.4 us
  transfers between devices with their start and end apart: 23, of which 11 were waited for; matrix products, arithmetic and copies ran while one was open for 0% of the time, Pallas kernels for 10%

profile of v5, /device:TPU:0, one launch (start us, length us, event | category | flops | bytes accessed | tf_op | source)
XLA Modules:
  0.0 78.2 jit_solution(1290110981314795470)
XLA Ops:
  1.4 3.5 %shard_map.59.refs_8_ = f32[2016,128]{1,0:T(8,128)S(1)} custom-call(s32[1792]{0:T(1024)S(1)} %copy-done.1, f32[448,896]{1,0:T(8,128)} %sigma_ref.1), custom_call_target="tpu_custom_call" | custom-call | flops 1027604480 | bytes 2644992 | tf_op jit(solution)/shard_map/pallas_call | solution.py:278
  4.9 3.0 %collective-permute-start.7 = (f32[2016,128]{1,0:T(8,128)S(1)}, f32[2016,128]{1,0:T(8,128)S(1)}, u32[]{:S(2)}, u32[]{:S(2)}) collective-permute-start(f32[2016,128]{1,0:T(8,128)S(1)} %shard_map.59.refs_8_), channel_id=1, source_target_pairs={{0,16},{8,24},{16,0},{24,8},{1,17},{9,25},{17,1},{25,9},{2,18},{10... | collective-permute-start | bytes 3096584 | tf_op jit(solution)/shard_map/ppermute | solution.py:373
  7.9 1.6 %collective-permute-start = (f32[224,256]{1,0:T(8,128)S(1)}, f32[224,256]{1,0:T(8,128)S(1)}, u32[]{:S(2)}, u32[]{:S(2)}) collective-permute-start(f32[224,256]{1,0:T(8,128)S(1)} %copy-done), channel_id=1, source_target_pairs={{1,0},{0,2},{2,4},{4,6},{6,7},{7,5},{5,3},{3,1},{9,8},{8,10},{10,1... | collective-permute-start | bytes 688136 | tf_op jit(solution)/shard_map/ppermute | solution.py:315
  9.9 5.0 %collective-permute-done.refs_1_ = f32[224,256]{1,0:T(8,128)S(1)} collective-permute-done((f32[224,256]{1,0:T(8,128)S(1)}, f32[224,256]{1,0:T(8,128)S(1)}, u32[]{:S(2)}, u32[]{:S(2)}) %collective-permute-start) | collective-permute-done | bytes 229408 | tf_op jit(solution)/shard_map/ppermute | solution.py:315
  15.0 1.6 %collective-permute-start.2 = (f32[224,256]{1,0:T(8,128)S(1)}, f32[224,256]{1,0:T(8,128)S(1)}, u32[]{:S(2)}, u32[]{:S(2)}) collective-permute-start(f32[224,256]{1,0:T(8,128)S(1)} %collective-permute-done.refs_1_), channel_id=1, source_target_pairs={{1,0},{0,2},{2,4},{4,6},{6,7},{7,5},{5,3},{3,1},{9,8},{8,10},{10,1... | collective-permute-start | bytes 688136 | tf_op jit(solution)/shard_map/ppermute | solution.py:315
  17.0 4.1 %collective-permute-done.2.refs_3_ = f32[224,256]{1,0:T(8,128)S(1)} collective-permute-done((f32[224,256]{1,0:T(8,128)S(1)}, f32[224,256]{1,0:T(8,128)S(1)}, u32[]{:S(2)}, u32[]{:S(2)}) %collective-permute-start.2) | collective-permute-done | bytes 229408 | tf_op jit(solution)/shard_map/ppermute | solution.py:315
  21.1 1.7 %collective-permute-start.4 = (f32[224,256]{1,0:T(8,128)S(1)}, f32[224,256]{1,0:T(8,128)S(1)}, u32[]{:S(2)}, u32[]{:S(2)}) collective-permute-start(f32[224,256]{1,0:T(8,128)S(1)} %collective-permute-done.2.refs_3_), channel_id=1, source_target_pairs={{1,0},{0,2},{2,4},{4,6},{6,7},{7,5},{5,3},{3,1},{9,8},{8,10},{10,1... | collective-permute-start | bytes 688136 | tf_op jit(solution)/shard_map/ppermute | solution.py:315
  23.1 4.5 %collective-permute-done.4.refs_5_ = f32[224,256]{1,0:T(8,128)S(1)} collective-permute-done((f32[224,256]{1,0:T(8,128)S(1)}, f32[224,256]{1,0:T(8,128)S(1)}, u32[]{:S(2)}, u32[]{:S(2)}) %collective-permute-start.4) | collective-permute-done | bytes 229408 | tf_op jit(solution)/shard_map/ppermute | solution.py:315
  27.6 1.6 %collective-permute-start.6 = (f32[224,256]{1,0:T(8,128)S(1)}, f32[224,256]{1,0:T(8,128)S(1)}, u32[]{:S(2)}, u32[]{:S(2)}) collective-permute-start(f32[224,256]{1,0:T(8,128)S(1)} %collective-permute-done.4.refs_5_), channel_id=1, source_target_pairs={{1,0},{0,2},{2,4},{4,6},{6,7},{7,5},{5,3},{3,1},{9,8},{8,10},{10,1... | collective-permute-start | bytes 688136 | tf_op jit(solution)/shard_map/ppermute | solution.py:317
  29.2 4.4 %collective-permute-done.6.refs_7_ = f32[224,256]{1,0:T(8,128)S(1)} collective-permute-done((f32[224,256]{1,0:T(8,128)S(1)}, f32[224,256]{1,0:T(8,128)S(1)}, u32[]{:S(2)}, u32[]{:S(2)}) %collective-permute-start.6) | collective-permute-done | bytes 229408 | tf_op jit(solution)/shard_map/ppermute | solution.py:317
  33.6 3.1 %shard_map.60 = (bf16[4,640,256]{2,1,0:T(8,128)(2,1)S(1)}, bf16[4,640,256]{2,1,0:T(8,128)(2,1)S(1)}, f32[448,256]{1,0:T(8,128)S(1)}, f32[448,128]{1,0:T(8,128)S(1)}) custom-call(s32[1792]{0:T(1024)S(1)} %copy-done.1, f32[224,256]{1,0:T(8,128)S(1)} %copy-done, f32[224,256]{1,0:T(8,128)S(1)} %collective-permute-done.refs_1_, ...), custom_call_target="tpu_custom_call" | custom-call | flops 440401920 | bytes 6183936 | tf_op jit(solution)/shard_map/pallas_call | solution.py:278
  38.8 1.7 %shard_map.61 = (f32[448,256]{1,0:T(8,128)S(1)}, bf16[448,448]{1,0:T(8,128)(2,1)S(1)}) custom-call(s32[1792]{0:T(1024)S(1)} %copy-done.1, bf16[4,640,256]{2,1,0:T(8,128)(2,1)S(1)} %get-tuple-element.28.uh_ref, bf16[4,640,256]{2,1,0:T(8,128)(2,1)S(1)} %get-tuple-element.29.ul_ref, f32[448,256]{1,0:T(8,128)S(1)} %get-tuple-element.25.part_ref, ...), custom_call_target="tpu_custom_call" | custom-call | flops 440401920 | bytes 6011904 | tf_op jit(solution)/shard_map/pallas_call | solution.py:278
  40.5 1.8 %shard_map.63 = (f32[112,256]{1,0:T(8,128)S(1)}, f32[112,256]{1,0:T(8,128)S(1)}, f32[112,256]{1,0:T(8,128)S(1)}, f32[112,256]{1,0:T(8,128)S(1)}) custom-call(bf16[4,640,256]{2,1,0:T(8,128)(2,1)S(1)} %get-tuple-element.28.uh_ref, bf16[4,640,256]{2,1,0:T(8,128)(2,1)S(1)} %get-tuple-element.29.ul_ref, f32[448,256]{1,0:T(8,128)S(1)} %get-tuple-element.35.part_ref, ...), custom_call_target="tpu_custom_call" | custom-call | flops 440401920 | bytes 4972544 | tf_op jit(solution)/shard_map/pallas_call | solution.py:278
  42.2 1.7 %collective-permute-start.13 = (f32[112,256]{1,0:T(8,128)S(1)}, f32[112,256]{1,0:T(8,128)S(1)}, u32[]{:S(2)}, u32[]{:S(2)}) collective-permute-start(f32[112,256]{1,0:T(8,128)S(1)} %get-tuple-element.38), channel_id=1, source_target_pairs={{0,2},{1,3},{2,4},{3,5},{4,6},{5,7},{6,0},{7,1},{8,10},{9,11},{10,... | collective-permute-start | bytes 344072 | tf_op jit(solution)/shard_map/ppermute | solution.py:411
  43.9 2.6 %collective-permute-start.14 = (f32[112,256]{1,0:T(8,128)S(1)}, f32[112,256]{1,0:T(8,128)S(1)}, u32[]{:S(2)}, u32[]{:S(2)}) collective-permute-start(f32[112,256]{1,0:T(8,128)S(1)} %get-tuple-element.39), channel_id=1, source_target_pairs={{0,4},{1,5},{2,6},{3,7},{4,0},{5,1},{6,2},{7,3},{8,12},{9,13},{10,... | collective-permute-start | bytes 344072 | tf_op jit(solution)/shard_map/ppermute | solution.py:411
  50.2 1.5 %collective-permute-start.17 = (f32[112,256]{1,0:T(8,128)S(1)}, f32[112,256]{1,0:T(8,128)S(1)}, u32[]{:S(2)}, u32[]{:S(2)}) collective-permute-start(f32[112,256]{1,0:T(8,128)S(1)} %collective-permute-done.13.refs_1_), channel_id=1, source_target_pairs={{0,1},{1,0},{2,3},{3,2},{4,5},{5,4},{6,7},{7,6},{8,9},{9,8},{10,11... | collective-permute-start | bytes 344072 | tf_op jit(solution)/shard_map/ppermute | solution.py:289
  51.7 3.1 %collective-permute-done.14.refs_2_ = f32[112,256]{1,0:T(8,128)S(1)} collective-permute-done((f32[112,256]{1,0:T(8,128)S(1)}, f32[112,256]{1,0:T(8,128)S(1)}, u32[]{:S(2)}, u32[]{:S(2)}) %collective-permute-start.14) | collective-permute-done | bytes 114720 | tf_op jit(solution)/shard_map/ppermute | solution.py:411
  54.9 1.5 %collective-permute-start.18 = (f32[112,256]{1,0:T(8,128)S(1)}, f32[112,256]{1,0:T(8,128)S(1)}, u32[]{:S(2)}, u32[]{:S(2)}) collective-permute-start(f32[112,256]{1,0:T(8,128)S(1)} %collective-permute-done.14.refs_2_), channel_id=1, source_target_pairs={{0,1},{1,0},{2,3},{3,2},{4,5},{5,4},{6,7},{7,6},{8,9},{9,8},{10,11... | collective-permute-start | bytes 344072 | tf_op jit(solution)/shard_map/ppermute | solution.py:289
  58.4 2.4 %collective-permute-done.18.refs_6_ = f32[112,256]{1,0:T(8,128)S(1)} collective-permute-done((f32[112,256]{1,0:T(8,128)S(1)}, f32[112,256]{1,0:T(8,128)S(1)}, u32[]{:S(2)}, u32[]{:S(2)}) %collective-permute-start.18) | collective-permute-done | bytes 114720 | tf_op jit(solution)/shard_map/ppermute | solution.py:289
  60.9 1.5 %collective-permute-done.19.refs_7_ = f32[112,256]{1,0:T(8,128)S(1)} collective-permute-done((f32[112,256]{1,0:T(8,128)S(1)}, f32[112,256]{1,0:T(8,128)S(1)}, u32[]{:S(2)}, u32[]{:S(2)}) %collective-permute-start.19) | collective-permute-done | bytes 114720 | tf_op jit(solution)/shard_map/ppermute | solution.py:289
  62.4 2.7 %shard_map.64 = (f32[224,256]{1,0:T(8,128)}, f32[128,256]{1,0:T(8,128)S(1)}, f32[128,256]{1,0:T(8,128)S(1)}, f32[128,256]{1,0:T(8,128)S(1)}, f32[128,256]{1,0:T(8,128)S(1)}) custom-call(bf16[448,896]{1,0:T(8,128)(2,1)S(1)} %get-tuple-element.32.from_ref, bf16[4,128,448]{2,1,0:T(8,128)(2,1)S(1)} %get-tuple-element.33.high_ref, ...), custom_call_target="tpu_custom_call" | custom-call | flops 440401920 | bytes 3391488 | tf_op jit(solution)/shard_map/pallas_call | solution.py:278
  66.2 3.4 %collective-permute-start.21 = (f32[128,256]{1,0:T(8,128)S(1)}, f32[128,256]{1,0:T(8,128)S(1)}, u32[]{:S(2)}, u32[]{:S(2)}) collective-permute-start(f32[128,256]{1,0:T(8,128)S(1)} %get-tuple-element.44), channel_id=1, source_target_pairs={{0,4},{1,5},{2,6},{3,7},{4,0},{5,1},{6,2},{7,3},{8,12},{9,13},{10,... | collective-permute-start | bytes 393224 | tf_op jit(solution)/shard_map/ppermute | solution.py:428
  69.9 3.6 %collective-permute-done.20 = f32[128,256]{1,0:T(8,128)S(1)} collective-permute-done((f32[128,256]{1,0:T(8,128)S(1)}, f32[128,256]{1,0:T(8,128)S(1)}, u32[]{:S(2)}, u32[]{:S(2)}) %collective-permute-start.20) | collective-permute-done | bytes 131104 | tf_op jit(solution)/shard_map/ppermute | solution.py:428
  73.5 3.8 %collective-permute-done.21 = f32[128,256]{1,0:T(8,128)S(1)} collective-permute-done((f32[128,256]{1,0:T(8,128)S(1)}, f32[128,256]{1,0:T(8,128)S(1)}, u32[]{:S(2)}, u32[]{:S(2)}) %collective-permute-start.21) | collective-permute-done | bytes 131104 | tf_op jit(solution)/shard_map/ppermute | solution.py:428
  (35 shorter events, 12.0 us)
Async XLA Ops:
  4.9 31.9 %collective-permute-start.7 = (f32[2016,128]{1,0:T(8,128)S(1)}, f32[2016,128]{1,0:T(8,128)S(1)}, u32[]{:S(2)}, u32[]{:S(2)}) collective-permute-start(f32[2016,128]{1,0:T(8,128)S(1)} %shard_map.59.refs_8_), channel_id=1, source_target_pairs={{0,16},{8,24},{16,0},{24,8},{1,17},{9,25},{17,1},{25,9},{2,18},{10... | collective-permute-start | bytes 3096584 | tf_op jit(solution)/shard_map/ppermute | solution.py:373
  7.9 7.1 %collective-permute-start = (f32[224,256]{1,0:T(8,128)S(1)}, f32[224,256]{1,0:T(8,128)S(1)}, u32[]{:S(2)}, u32[]{:S(2)}) collective-permute-start(f32[224,256]{1,0:T(8,128)S(1)} %copy-done), channel_id=1, source_target_pairs={{1,0},{0,2},{2,4},{4,6},{6,7},{7,5},{5,3},{3,1},{9,8},{8,10},{10,1... | collective-permute-start | bytes 688136 | tf_op jit(solution)/shard_map/ppermute | solution.py:315
  9.5 7.1 %collective-permute-start.1 = (f32[224,256]{1,0:T(8,128)S(1)}, f32[224,256]{1,0:T(8,128)S(1)}, u32[]{:S(2)}, u32[]{:S(2)}) collective-permute-start(f32[224,256]{1,0:T(8,128)S(1)} %copy-done), channel_id=1, source_target_pairs={{0,1},{2,0},{4,2},{6,4},{7,6},{5,7},{3,5},{1,3},{8,9},{10,8},{12,1... | collective-permute-start | bytes 688136 | tf_op jit(solution)/shard_map/ppermute | solution.py:315
  15.0 6.1 %collective-permute-start.2 = (f32[224,256]{1,0:T(8,128)S(1)}, f32[224,256]{1,0:T(8,128)S(1)}, u32[]{:S(2)}, u32[]{:S(2)}) collective-permute-start(f32[224,256]{1,0:T(8,128)S(1)} %collective-permute-done.refs_1_), channel_id=1, source_target_pairs={{1,0},{0,2},{2,4},{4,6},{6,7},{7,5},{5,3},{3,1},{9,8},{8,10},{10,1... | collective-permute-start | bytes 688136 | tf_op jit(solution)/shard_map/ppermute | solution.py:315
  16.6 6.2 %collective-permute-start.3 = (f32[224,256]{1,0:T(8,128)S(1)}, f32[224,256]{1,0:T(8,128)S(1)}, u32[]{:S(2)}, u32[]{:S(2)}) collective-permute-start(f32[224,256]{1,0:T(8,128)S(1)} %collective-permute-done.1.refs_2_), channel_id=1, source_target_pairs={{0,1},{2,0},{4,2},{6,4},{7,6},{5,7},{3,5},{1,3},{8,9},{10,8},{12,1... | collective-permute-start | bytes 688136 | tf_op jit(solution)/shard_map/ppermute | solution.py:315
  21.1 6.5 %collective-permute-start.4 = (f32[224,256]{1,0:T(8,128)S(1)}, f32[224,256]{1,0:T(8,128)S(1)}, u32[]{:S(2)}, u32[]{:S(2)}) collective-permute-start(f32[224,256]{1,0:T(8,128)S(1)} %collective-permute-done.2.refs_3_), channel_id=1, source_target_pairs={{1,0},{0,2},{2,4},{4,6},{6,7},{7,5},{5,3},{3,1},{9,8},{8,10},{10,1... | collective-permute-start | bytes 688136 | tf_op jit(solution)/shard_map/ppermute | solution.py:315
  22.8 6.4 %collective-permute-start.5 = (f32[224,256]{1,0:T(8,128)S(1)}, f32[224,256]{1,0:T(8,128)S(1)}, u32[]{:S(2)}, u32[]{:S(2)}) collective-permute-start(f32[224,256]{1,0:T(8,128)S(1)} %collective-permute-done.3.refs_4_), channel_id=1, source_target_pairs={{0,1},{2,0},{4,2},{6,4},{7,6},{5,7},{3,5},{1,3},{8,9},{10,8},{12,1... | collective-permute-start | bytes 688136 | tf_op jit(solution)/shard_map/ppermute | solution.py:315
  27.6 6.0 %collective-permute-start.6 = (f32[224,256]{1,0:T(8,128)S(1)}, f32[224,256]{1,0:T(8,128)S(1)}, u32[]{:S(2)}, u32[]{:S(2)}) collective-permute-start(f32[224,256]{1,0:T(8,128)S(1)} %collective-permute-done.4.refs_5_), channel_id=1, source_target_pairs={{1,0},{0,2},{2,4},{4,6},{6,7},{7,5},{5,3},{3,1},{9,8},{8,10},{10,1... | collective-permute-start | bytes 688136 | tf_op jit(solution)/shard_map/ppermute | solution.py:317
  29.2 9.5 %collective-permute-start.9 = (f32[2016,128]{1,0:T(8,128)S(1)}, f32[2016,128]{1,0:T(8,128)S(1)}, u32[]{:S(2)}, u32[]{:S(2)}) collective-permute-start(f32[2016,128]{1,0:T(8,128)S(1)} %shard_map.59.refs_8_), channel_id=1, source_target_pairs={{0,8},{8,0},{16,24},{24,16},{1,9},{9,1},{17,25},{25,17},{2,10},{10... | collective-permute-start | bytes 3096584 | tf_op jit(solution)/shard_map/ppermute | solution.py:289
  36.8 3.7 %collective-permute-start.12 = (f32[2016,128]{1,0:T(8,128)S(1)}, f32[2016,128]{1,0:T(8,128)S(1)}, u32[]{:S(2)}, u32[]{:S(2)}) collective-permute-start(f32[2016,128]{1,0:T(8,128)S(1)} %collective-permute-done.7.refs_1_), channel_id=1, source_target_pairs={{0,8},{8,0},{16,24},{24,16},{1,9},{9,1},{17,25},{25,17},{2,10},{10... | collective-permute-start | bytes 3096584 | tf_op jit(solution)/shard_map/ppermute | solution.py:289
  36.8 3.6 %collective-permute-start.8 = (f32[448,128]{1,0:T(8,128)S(1)}, f32[448,128]{1,0:T(8,128)S(1)}, u32[]{:S(2)}, u32[]{:S(2)}) collective-permute-start(f32[448,128]{1,0:T(8,128)S(1)} %get-tuple-element.27.refs_0_), channel_id=1, source_target_pairs={{0,8},{8,0},{16,24},{24,16},{1,9},{9,1},{17,25},{25,17},{2,10},{10... | collective-permute-start | bytes 688136 | tf_op jit(solution)/shard_map/ppermute | solution.py:289
  37.3 10.5 %collective-permute-start.10 = (f32[448,128]{1,0:T(8,128)S(1)}, f32[448,128]{1,0:T(8,128)S(1)}, u32[]{:S(2)}, u32[]{:S(2)}) collective-permute-start(f32[448,128]{1,0:T(8,128)S(1)} %get-tuple-element.27.refs_0_), channel_id=1, source_target_pairs={{0,16},{8,24},{16,0},{24,8},{1,17},{9,25},{17,1},{25,9},{2,18},{10... | collective-permute-start | bytes 688136 | tf_op jit(solution)/shard_map/ppermute | solution.py:296
  37.7 19.2 %collective-permute-start.11 = (f32[448,128]{1,0:T(8,128)S(1)}, f32[448,128]{1,0:T(8,128)S(1)}, u32[]{:S(2)}, u32[]{:S(2)}) collective-permute-start(f32[448,128]{1,0:T(8,128)S(1)} %get-tuple-element.27.refs_0_), channel_id=1, source_target_pairs={{0,24},{8,16},{16,8},{24,0},{1,25},{9,17},{17,9},{25,1},{2,26},{10... | collective-permute-start | bytes 688136 | tf_op jit(solution)/shard_map/ppermute | solution.py:296
  42.2 8.0 %collective-permute-start.13 = (f32[112,256]{1,0:T(8,128)S(1)}, f32[112,256]{1,0:T(8,128)S(1)}, u32[]{:S(2)}, u32[]{:S(2)}) collective-permute-start(f32[112,256]{1,0:T(8,128)S(1)} %get-tuple-element.38), channel_id=1, source_target_pairs={{0,2},{1,3},{2,4},{3,5},{4,6},{5,7},{6,0},{7,1},{8,10},{9,11},{10,... | collective-permute-start | bytes 344072 | tf_op jit(solution)/shard_map/ppermute | solution.py:411
  43.9 11.0 %collective-permute-start.14 = (f32[112,256]{1,0:T(8,128)S(1)}, f32[112,256]{1,0:T(8,128)S(1)}, u32[]{:S(2)}, u32[]{:S(2)}) collective-permute-start(f32[112,256]{1,0:T(8,128)S(1)} %get-tuple-element.39), channel_id=1, source_target_pairs={{0,4},{1,5},{2,6},{3,7},{4,0},{5,1},{6,2},{7,3},{8,12},{9,13},{10,... | collective-permute-start | bytes 344072 | tf_op jit(solution)/shard_map/ppermute | solution.py:411
  46.5 9.9 %collective-permute-start.15 = (f32[112,256]{1,0:T(8,128)S(1)}, f32[112,256]{1,0:T(8,128)S(1)}, u32[]{:S(2)}, u32[]{:S(2)}) collective-permute-start(f32[112,256]{1,0:T(8,128)S(1)} %get-tuple-element.40), channel_id=1, source_target_pairs={{0,6},{1,7},{2,0},{3,1},{4,2},{5,3},{6,4},{7,5},{8,14},{9,15},{10,... | collective-permute-start | bytes 344072 | tf_op jit(solution)/shard_map/ppermute | solution.py:411
  47.8 10.6 %collective-permute-start.16 = (f32[112,256]{1,0:T(8,128)S(1)}, f32[112,256]{1,0:T(8,128)S(1)}, u32[]{:S(2)}, u32[]{:S(2)}) collective-permute-start(f32[112,256]{1,0:T(8,128)S(1)} %get-tuple-element.37.refs_0_), channel_id=1, source_target_pairs={{0,1},{1,0},{2,3},{3,2},{4,5},{5,4},{6,7},{7,6},{8,9},{9,8},{10,11... | collective-permute-start | bytes 344072 | tf_op jit(solution)/shard_map/ppermute | solution.py:289
  50.2 8.2 %collective-permute-start.17 = (f32[112,256]{1,0:T(8,128)S(1)}, f32[112,256]{1,0:T(8,128)S(1)}, u32[]{:S(2)}, u32[]{:S(2)}) collective-permute-start(f32[112,256]{1,0:T(8,128)S(1)} %collective-permute-done.13.refs_1_), channel_id=1, source_target_pairs={{0,1},{1,0},{2,3},{3,2},{4,5},{5,4},{6,7},{7,6},{8,9},{9,8},{10,11... | collective-permute-start | bytes 344072 | tf_op jit(solution)/shard_map/ppermute | solution.py:289
  54.9 6.0 %collective-permute-start.18 = (f32[112,256]{1,0:T(8,128)S(1)}, f32[112,256]{1,0:T(8,128)S(1)}, u32[]{:S(2)}, u32[]{:S(2)}) collective-permute-start(f32[112,256]{1,0:T(8,128)S(1)} %collective-permute-done.14.refs_2_), channel_id=1, source_target_pairs={{0,1},{1,0},{2,3},{3,2},{4,5},{5,4},{6,7},{7,6},{8,9},{9,8},{10,11... | collective-permute-start | bytes 344072 | tf_op jit(solution)/shard_map/ppermute | solution.py:289
  56.4 6.0 %collective-permute-start.19 = (f32[112,256]{1,0:T(8,128)S(1)}, f32[112,256]{1,0:T(8,128)S(1)}, u32[]{:S(2)}, u32[]{:S(2)}) collective-permute-start(f32[112,256]{1,0:T(8,128)S(1)} %collective-permute-done.15.refs_3_), channel_id=1, source_target_pairs={{0,1},{1,0},{2,3},{3,2},{4,5},{5,4},{6,7},{7,6},{8,9},{9,8},{10,11... | collective-permute-start | bytes 344072 | tf_op jit(solution)/shard_map/ppermute | solution.py:289
  62.4 15.1 %copy-start.2 = (f32[128,256]{1,0:T(8,128)S(1)}, f32[128,256]{1,0:T(8,128)}, u32[]{:S(2)}) copy-start(f32[128,256]{1,0:T(8,128)} %param.7) | copy-start | bytes 393220
  65.1 8.4 %collective-permute-start.20 = (f32[128,256]{1,0:T(8,128)S(1)}, f32[128,256]{1,0:T(8,128)S(1)}, u32[]{:S(2)}, u32[]{:S(2)}) collective-permute-start(f32[128,256]{1,0:T(8,128)S(1)} %get-tuple-element.43), channel_id=1, source_target_pairs={{0,2},{1,3},{2,4},{3,5},{4,6},{5,7},{6,0},{7,1},{8,10},{9,11},{10,... | collective-permute-start | bytes 393224 | tf_op jit(solution)/shard_map/ppermute | solution.py:428
  66.2 11.2 %collective-permute-start.21 = (f32[128,256]{1,0:T(8,128)S(1)}, f32[128,256]{1,0:T(8,128)S(1)}, u32[]{:S(2)}, u32[]{:S(2)}) collective-permute-start(f32[128,256]{1,0:T(8,128)S(1)} %get-tuple-element.44), channel_id=1, source_target_pairs={{0,4},{1,5},{2,6},{3,7},{4,0},{5,1},{6,2},{7,3},{8,12},{9,13},{10,... | collective-permute-start | bytes 393224 | tf_op jit(solution)/shard_map/ppermute | solution.py:428
  69.5 7.9 %collective-permute-start.22 = (f32[128,256]{1,0:T(8,128)S(1)}, f32[128,256]{1,0:T(8,128)S(1)}, u32[]{:S(2)}, u32[]{:S(2)}) collective-permute-start(f32[128,256]{1,0:T(8,128)S(1)} %get-tuple-element.45), channel_id=1, source_target_pairs={{0,6},{1,7},{2,0},{3,1},{4,2},{5,3},{6,4},{7,5},{8,14},{9,15},{10,... | collective-permute-start | bytes 393224 | tf_op jit(solution)/shard_map/ppermute | solution.py:428
  (2 other events, 8.0 us)

commit v6 on v5

--- a/solution.py
+++ b/solution.py
@@ -108,13 +108,10 @@
 
 
 def prepare_kernel(direct, nc, owners, structure_ref, *refs):
-    pair_ref = None
-    if direct:
-        pair_ref, refs = refs[-2], refs[:-2] + refs[-1:]
-    uh_ref, ul_ref, part_ref, us_ref = refs[-4:]
+    uh_ref, ul_ref, part_ref, own_ref, us_ref = refs[-5:]
     nr, _, w = uh_ref.shape
     n_u = nc if direct else 1
-    u_refs, first_refs = refs[:n_u], refs[n_u:-4]
+    u_refs, first_refs = refs[:n_u], refs[n_u:-5]
     n = structure_ref.shape[0]
     m = n // nc
     c = lax.axis_index("pcol")
@@ -129,32 +126,27 @@
             us_ref[i, pl.ds(owner, u.shape[0], stride=nc), :] = u[:, LANES * i : LANES * (i + 1)]
 
     if direct:
-        lane = pl.multiple_of((c & 1) * (w // 2), LANES)
-        pair_ref[:m, :] = u_refs[0][:, pl.ds(lane, w // 2)]
         for owner, u_ref in zip(ring_owners(nc, c), u_refs):
             place(owner, u_ref[...])
-
-            @pl.when(owner == jnp.bitwise_xor(c, 1))
-            def _():
-                pair_ref[m:, :] = u_ref[:, pl.ds(lane, w // 2)]
-
     else:
         pl.loop(0, nc)(lambda k: place(k, u_refs[0][k]))
     us_ref[:, n:, :] = jnp.zeros((us_ref.shape[0], us_ref.shape[1] - n, LANES), jnp.float32)
 
     width = rows * 2
 
-    def cut(owner):
+    def rows_of(owner, lane_blocks):
         start = count(names < owner * width)
         base = pl.multiple_of((start // 8) * 8, 8)
         size = CAP + 8
-        lanes = [
-            pltpu.roll(us_ref[k, pl.ds(base, size), :], size - (start - base), 0)[:CAP]
-            for k in range(us_ref.shape[0])
-        ]
-        u = jnp.concatenate(lanes, axis=1)[:, :w]
+        lanes = [pltpu.roll(us_ref[k, pl.ds(base, size), :], size - (start - base), 0)[:CAP] for k in lane_blocks]
+        return jnp.concatenate(lanes, axis=1)
+
+    def cut(owner):
+        u = rows_of(owner, range(us_ref.shape[0]))[:, :w]
         u = jnp.concatenate([u, jnp.zeros((WIDE - CAP, w), jnp.float32)], axis=0)
         uh_ref[owner], ul_ref[owner] = split(u)
+
+    own_ref[...] = rows_of(c // 2, [c & 1]) if direct else rows_of(c // 2, [0])[:, :w]
 
     if direct:
         for b in range(nr):
@@ -196,67 +188,79 @@
     to_ref[...] = row_order(structure_ref[...].reshape(1, -1), lax.axis_index("pcol"), rows, nc, slots, direct)
 
 
-def image_kernel(n_out, owners, uh_ref, ul_ref, part_ref, to_ref, *refs):
+def image_kernel(direct, owners, uh_ref, ul_ref, part_ref, to_ref, *refs):
+    n_out = len(refs) - (1 if not direct else len(owners(0)))
     block_refs, out_refs = refs[:-n_out], refs[-n_out:]
     rows = part_ref.shape[0]
     image = part_ref[...]
-    if owners is None:
+    if direct:
+        for owner, block_ref in zip(owners(lax.axis_index("prow")), block_refs):
+            image = image + block_term(block_ref, uh_ref[owner], ul_ref[owner], rows)
+    else:
         stack = block_refs[0]
         add = lambda b, v: v + block_term(stack.at[b], uh_ref[b], ul_ref[b], rows)
         image = lax.fori_loop(0, stack.shape[0], add, image)
-    else:
-        for owner, block_ref in zip(owners(lax.axis_index("prow")), block_refs):
-            image = image + block_term(block_ref, uh_ref[owner], ul_ref[owner], rows)
     image = pick_rows(to_ref[...], image)
+    out_refs[0][...] = image
     size = image.shape[0] // n_out
-    for k, out_ref in enumerate(out_refs):
-        out_ref[...] = image[size * k : size * (k + 1)]
+    for k in range(1, n_out):
+        out_refs[k][...] = image[size * k : size * (k + 1)]
 
 
 def turn_kernel(direct, slots, owners, structure_ref, *refs):
     from_ref, high_ref, low_ref = refs[-3:]
     nz = high_ref.shape[0]
     nc = 2 * nz
+    lg = log2(nc)
     rows = slots * nc
     n = structure_ref.shape[0]
     m = n // nc
     names = structure_ref[...].reshape(1, -1)
     c = lax.axis_index("pcol")
-    z = c // 2
+    z, x = c // 2, c & 1
+
+    start, middle = count(names < 2 * z * rows), count(names < (2 * z + 1) * rows)
+    named = pltpu.roll(jnp.broadcast_to(names, (8, n)), lax.rem(n - start, n), 1)[:1, :CAP]
+    index = start + lax.broadcasted_iota(jnp.int32, (1, CAP), 1)
+    half = jnp.where(named >= (2 * z + 1) * rows, 1, 0)
+    turn = index & (nc - 1)
+    ahead = (jnp.where(half == 1, middle, start) - turn + nc - 1) >> lg
+    block = turn >> 1
+    if direct:
+        block = (block - z) & (nz - 1)
+    slot = (2 * block + (turn & 1)) * slots + (index >> lg) - ahead + (half ^ x) * rows
+    slot = jnp.where((named >= 2 * z * rows) & (named < (2 * z + 2) * rows), slot, -1)
+    at = lax.broadcasted_iota(jnp.int32, (2 * rows, CAP), 0)
+    place = one_hot(at == slot).astype(BF16)
 
     def put(owner, u_ref):
         where = ((owner - z) & (nz - 1)) if direct else owner
-        high_ref[where], low_ref[where] = split(u_ref[...].T)
+        for out_ref, part in zip((high_ref, low_ref), split(u_ref[...].T)):
+            turned = lax.dot_general(part, place, (((1,), (1,)), ((), ())), preferred_element_type=jnp.float32)
+            out_ref[where] = turned.astype(BF16)
 
     each(refs[:-3], owners(lax.axis_index("prow")) if direct else None, put)
 
     own = lax.broadcasted_iota(jnp.int32, (m, n), 1) - nc * lax.broadcasted_iota(jnp.int32, (m, n), 0)
-    at = lax.broadcasted_iota(jnp.int32, (m, 2 * rows), 1)
-    for half, column in enumerate((c, jnp.bitwise_xor(c, 1))):
-        mine = jnp.where(own == column, names, 0).astype(jnp.float32)
-        mine = jnp.sum(mine, axis=1, keepdims=True)
-        source = jnp.zeros((m, 1), jnp.int32)
-        before = jnp.zeros((m, 1), jnp.int32)
-        for k in range(1, nc):
-            less = mine < float(k * rows)
-            source = source + jnp.where(less, 0, 1)
-            before = jnp.where(less, before, count(less))
-        block = source >> 1
-        if direct:
-            block = (z - block) & (nz - 1)
-        block = 2 * (block + nz * ((source ^ c) & 1)) + (column & 1)
-        slot = block * slots + lax.broadcasted_iota(jnp.int32, (m, 1), 0) - before
-        from_ref[m * half : m * (half + 1), :] = one_hot(at == slot).astype(BF16)
-
-
-def correction_kernel(from_ref, high_ref, low_ref, *refs):
-    nz = high_ref.shape[0]
-    n_in = 2 if len(refs) == 4 else 2 * nz
-    got = jnp.concatenate([ref[...] for ref in refs[:n_in]], axis=0)
-    sj_ref, out_refs = refs[n_in], refs[n_in + 1 :]
-    both = -pick_rows(from_ref[...], got)
-    sj_ref[...] = both[: sj_ref.shape[0]]
-    sh, sl = split(both)
+    mine = jnp.sum(jnp.where(own == c, names, 0).astype(jnp.float32), axis=1, keepdims=True)
+    source = jnp.zeros((m, 1), jnp.int32)
+    before = jnp.zeros((m, 1), jnp.int32)
+    for k in range(1, nc):
+        less = mine < float(k * rows)
+        source = source + jnp.where(less, 0, 1)
+        before = jnp.where(less, before, count(less))
+    block = source >> 1
+    if direct:
+        block = (z - block) & (nz - 1)
+    block = block + nz * ((source ^ c) & 1)
+    slot = block * slots + lax.broadcasted_iota(jnp.int32, (m, 1), 0) - before
+    at = lax.broadcasted_iota(jnp.int32, (m, rows), 1)
+    from_ref[...] = one_hot(at == slot).astype(BF16)
+
+
+def correction_kernel(slots, n_got, high_ref, low_ref, whole_ref, other_ref, *refs):
+    got_refs, (mine_ref, theirs_ref), out_refs = refs[:n_got], refs[n_got : n_got + 2], refs[n_got + 2 :]
+    sh, sl = split(jnp.concatenate([whole_ref[...], other_ref[...]], axis=0))
 
     def term(t):
         return dot(high_ref[t], sh) + (dot(high_ref[t], sl) + dot(low_ref[t], sh))
@@ -266,9 +270,23 @@
             out_ref[...] = term(t)
     else:
 
-        @pl.loop(0, nz)
+        @pl.loop(0, out_refs[0].shape[0])
         def _(t):
             out_refs[0][t] = term(t)
+
+    first = (lax.axis_index("pcol") & 1) == 0
+    mine, theirs = [], []
+    for ref, k in [(whole_ref, 0)] * (n_got > 1) + [(ref, k) for ref in got_refs for k in range(ref.shape[0] // (2 * slots))]:
+        low = ref[2 * slots * k : 2 * slots * k + slots, :]
+        high = ref[2 * slots * k + slots : 2 * slots * (k + 1), :]
+        mine.append(jnp.where(first, low, high))
+        theirs.append(jnp.where(first, high, low))
+    mine_ref[...] = jnp.concatenate(mine, axis=0)
+    theirs_ref[...] = jnp.concatenate(theirs, axis=0)
+
+
+def pick_kernel(from_ref, mine_ref, other_ref, out_ref):
+    out_ref[...] = -pick_rows(from_ref[...], jnp.concatenate([mine_ref[...], other_ref[...]], axis=0))
 
 
 def call(kernel, out_shape, *args, flops=0, vmem=20, **kw):
@@ -289,11 +307,12 @@
     return lax.ppermute(v, axis, [(k, k ^ 1) for k in range(size)])
 
 
-def spread(v, size):
-    blocks = [v, swap(v, "prow", size)]
+def spread(v, near, size, after):
+    blocks = [v, near]
     for t in range(1, size // 2):
-        for flip in range(2):
-            blocks.append(lax.ppermute(v, "prow", [(k, ((k + 2 * t) % size) ^ flip) for k in range(size)]))
+        far = lax.ppermute(v, "prow", [(k, (k + 2 * t) % size) for k in range(size)])
+        far, _ = lax.optimization_barrier((far, after))
+        blocks += [far, swap(far, "prow", size)]
     return blocks
 
 
@@ -313,6 +332,7 @@
     up = down = u
     for step in range(1, nc // 2):
         up, down = lax.ppermute(up, "pcol", pairs), lax.ppermute(down, "pcol", back)
+        up, down = lax.optimization_barrier((up, down))
         blocks += [up, down]
     return blocks + [lax.ppermute(up, "pcol", pairs)]
 
@@ -357,14 +377,14 @@
     else:
         u_all = [lax.all_gather(u_panel, "pcol")]
     term = 6 * rows * WIDE * w
-    uh, ul, image, *pair = call(
+    uh, ul, image, own = call(
         functools.partial(prepare_kernel, direct, nc, lambda r: owners(r)[:1]),
-        [bf16(nr, WIDE, w), bf16(nr, WIDE, w), f32(rows, w)] + [f32(2 * m, wd)] * direct,
+        [bf16(nr, WIDE, w), bf16(nr, WIDE, w), f32(rows, w), f32(CAP, wd if direct else w)],
         names,
         *u_all,
         *near,
         scratch_shapes=[pltpu.VMEM((-(-w // LANES), n + CAP + 8, LANES), jnp.float32)],
-        flops=term,
+        flops=15 * term // 2,
     )
     beside, later = [], []
     if direct:
@@ -387,17 +407,12 @@
         flops=term,
     )
     if direct:
-        pair, _ = lax.optimization_barrier((pair[0], beside[1]))
-        pairs = spread(pair, nr)
-        pairs[1], to = lax.optimization_barrier((pairs[1], to))
-    else:
-        pair = jnp.concatenate([u_panel, swap(u_panel, "pcol", nc)], axis=0)
-        pair = jnp.where(jnp.bitwise_and(c, 1) == 0, pair[:, :wd], pair[:, wd:])
-        pairs = [lax.all_gather(pair, "prow")]
-    n_out = nz if direct else 1
+        own, _ = lax.optimization_barrier((own, beside[1]))
+        near = swap(own, "prow", nr)
+        near, to = lax.optimization_barrier((near, to))
     sent = call(
-        functools.partial(image_kernel, n_out, (lambda r: owners(r)[3::2]) if direct else None),
-        [f32(nc * slots // n_out, w)] * n_out,
+        functools.partial(image_kernel, direct, lambda r: owners(r)[3::2]),
+        [f32(nc * slots, w)] + [f32(2 * slots, w)] * ((nz - 1) * direct),
         uh,
         ul,
         image,
@@ -405,23 +420,40 @@
         *later,
         flops=term,
     )
-    if direct:
-        got = [sent[0]]
+    whole = sent[0]
+    other = swap(whole, "pcol", nc)
+    if direct:
+        got = []
         for t in range(1, nz):
             got.append(lax.ppermute(sent[t], "pcol", [(k, (k + 2 * t) % nc) for k in range(nc)]))
-    else:
-        blocks = sent[0].reshape(nz, 2 * slots, w)
+        owned = spread(own, near, nr, whole)
+    else:
+        blocks = whole.reshape(nz, 2 * slots, w)
         blocks = lax.all_to_all(blocks, "pcol", split_axis=0, concat_axis=0, axis_index_groups=groups, tiled=True)
         got = [blocks.reshape(nc * slots, w)]
-    got = got + [swap(v, "pcol", nc) for v in got]
+        own = jnp.where(jnp.bitwise_and(c, 1) == 0, own[:, :wd], own[:, wd:])
+        owned = [lax.all_gather(own, "prow")]
+
+    turned = bf16(nz, wd, 2 * nc * slots)
     source, high, low = call(
         functools.partial(turn_kernel, direct, slots, owners),
-        [bf16(2 * m, 2 * nc * slots), bf16(nz, wd, 2 * m), bf16(nz, wd, 2 * m)],
+        [bf16(m, nc * slots), turned, turned],
         names,
-        *pairs,
+        *owned,
+        flops=8 * nz * wd * nc * slots * CAP,
     )
     parts = [f32(wd, w)] * nz if direct else [f32(nz, wd, w)]
-    sigma_sj, *terms = call(correction_kernel, [f32(m, w)] + parts, source, high, low, *got, flops=term)
+    mine, theirs, *terms = call(
+        functools.partial(correction_kernel, slots, len(got)),
+        [f32(nz * slots, w)] * 2 + parts,
+        high,
+        low,
+        whole,
+        other,
+        *got,
+        flops=term,
+    )
+    sigma_sj = call(pick_kernel, f32(m, w), source, mine, swap(theirs, "pcol", nc), flops=term // 4)
     if direct:
         total = terms[0]
         for t in range(1, nz):
@@ -429,7 +461,8 @@
     else:
         terms = lax.all_to_all(terms[0], "pcol", split_axis=0, concat_axis=0, axis_index_groups=groups, tiled=True)
         total = jnp.sum(terms, axis=0)
-    return sigma_sj, d_term - total
+    sigma_sj, d_term = lax.optimization_barrier((sigma_sj, d_term))
+    return sigma_sj, d_term + total
 
 
 def solution(mesh):

time: 78.7 us -> 72.9 us (0.926)
  starting transfers between devices: 28.1 us -> 23.4 us
  waiting for transfers between devices: 33.6 us -> 30.9 us
  Pallas kernels: 14.2 us -> 15.6 us
    ppermute x3, waiting for transfers between devices: 13.6 us -> 8.12 us  [ring_gather(): lax.ppermute(up, 'pcol', pairs)]
    ppermute x7 -> x6, starting transfers between devices: 5.61 us -> 1.5 us  [swap(): return lax.ppermute(v, axis, [(k, k ^ 1) for k in range(size)])]
    ppermute x3, waiting for transfers between devices: 0.01 us -> 4.07 us  [ring_gather(): lax.ppermute(down, 'pcol', back)]
    ppermute x2 -> x1, waiting for transfers between devices: 0.01 us -> 3.48 us  [spread(): lax.ppermute(v, 'prow', [(k, (k + 2 * t) % size) for k in range(size)])]
    ppermute x3, waiting for transfers between devices: 7.56 us -> 4.39 us  [per_device(): lax.ppermute(terms[t], 'pcol', [(k, (k + 2 * t) % nc) for k in range(nc)])]
    ppermute x7 -> x6, waiting for transfers between devices: 3.98 us -> 2.05 us  [swap(): return lax.ppermute(v, axis, [(k, k ^ 1) for k in range(size)])]
    pallas_call x6 -> x7, Pallas kernels: 14.2 us -> 15.6 us  [call(): pl.pallas_call(kernel, out_shape=out_shape, out_specs=[VMEM] * len(out_sh...]
    ppermute x3, starting transfers between devices: 4.85 us -> 6.23 us  [ring_gather(): lax.ppermute(up, 'pcol', pairs)]
  transfers between devices with their start and end apart: 23 -> 21, of which waited for: 11 -> 10; matrix products, arithmetic and copies ran while one was open for 0% -> 0% of each run, Pallas kernels for 10% -> 20%
where the time goes in v6:
time: 72.9 us; the launch traced here: 72.1 us
  waiting for transfers between devices  30.9 us (42%)
  starting transfers between devices  23.4 us (32%)
  Pallas kernels  15.6 us (21%)
  between operations  0.73 us (1%)
    pallas_call x7, Pallas kernels, call(): pl.pallas_call(kernel, out_shape=out_shape, out_specs=[VMEM] * len(out_sh...  15.6 us
    ppermute x3, waiting for transfers between devices, ring_gather(): lax.ppermute(up, 'pcol', pairs)  8.12 us
    ppermute x3, starting transfers between devices, ring_gather(): lax.ppermute(up, 'pcol', pairs)  6.23 us
    ppermute x3, starting transfers between devices, per_device(): lax.ppermute(terms[t], 'pcol', [(k, (k + 2 * t) % nc) for k in range(nc)])  5.1 us
    ppermute x3, starting transfers between devices, per_device(): lax.ppermute(sent[t], 'pcol', [(k, (k + 2 * t) % nc) for k in range(nc)])  4.59 us
    ppermute x1, waiting for transfers between devices, ring_gather(): return blocks + [lax.ppermute(up, 'pcol', pairs)]  4.53 us
    ppermute x3, waiting for transfers between devices, per_device(): lax.ppermute(terms[t], 'pcol', [(k, (k + 2 * t) % nc) for k in range(nc)])  4.39 us
    ppermute x3, waiting for transfers between devices, per_device(): lax.ppermute(sent[t], 'pcol', [(k, (k + 2 * t) % nc) for k in range(nc)])  4.31 us
  transfers between devices with their start and end apart: 21, of which 10 were waited for; matrix products, arithmetic and copies ran while one was open for 0% of the time, Pallas kernels for 20%

profile of v6, /device:TPU:0, one launch (start us, length us, event | category | flops | bytes accessed | tf_op | source)
XLA Modules:
  0.0 72.1 jit_solution(1535826642027665648)
XLA Ops:
  0.6 3.1 %collective-permute-start = (f32[224,256]{1,0:T(8,128)}, f32[224,256]{1,0:T(8,128)S(1)}, u32[]{:S(2)}, u32[]{:S(2)}) collective-permute-start(f32[224,256]{1,0:T(8,128)} %refs_0_.1), channel_id=1, source_target_pairs={{1,0},{0,2},{2,4},{4,6},{6,7},{7,5},{5,3},{3,1},{9,8},{8,10},{10,1... | collective-permute-start | bytes 688136 | tf_op jit(solution)/shard_map/ppermute | solution.py:334
  4.4 3.5 %shard_map.59.refs_8_ = f32[2016,128]{1,0:T(8,128)S(1)} custom-call(s32[1792]{0:T(1024)S(1)} %copy-done, f32[448,896]{1,0:T(8,128)} %sigma_ref.1), custom_call_target="tpu_custom_call" | custom-call | flops 1027604480 | bytes 2644992 | tf_op jit(solution)/shard_map/pallas_call | solution.py:296
  7.9 2.0 %collective-permute-start.7 = (f32[2016,128]{1,0:T(8,128)S(1)}, f32[2016,128]{1,0:T(8,128)S(1)}, u32[]{:S(2)}, u32[]{:S(2)}) collective-permute-start(f32[2016,128]{1,0:T(8,128)S(1)} %shard_map.59.refs_8_), channel_id=1, source_target_pairs={{0,16},{8,24},{16,0},{24,8},{1,17},{9,25},{17,1},{25,9},{2,18},{10... | collective-permute-start | bytes 3096584 | tf_op jit(solution)/shard_map/ppermute | solution.py:393
  11.0 1.6 %collective-permute-start.2 = (f32[224,256]{1,0:T(8,128)S(1)}, f32[224,256]{1,0:T(8,128)S(1)}, u32[]{:S(2)}, u32[]{:S(2)}) collective-permute-start(f32[224,256]{1,0:T(8,128)S(1)} %collective-permute-done.refs_1_), channel_id=1, source_target_pairs={{1,0},{0,2},{2,4},{4,6},{6,7},{7,5},{5,3},{3,1},{9,8},{8,10},{10,1... | collective-permute-start | bytes 688136 | tf_op jit(solution)/shard_map/ppermute | solution.py:334
  13.0 4.1 %collective-permute-done.2.refs_3_ = f32[224,256]{1,0:T(8,128)S(1)} collective-permute-done((f32[224,256]{1,0:T(8,128)S(1)}, f32[224,256]{1,0:T(8,128)S(1)}, u32[]{:S(2)}, u32[]{:S(2)}) %collective-permute-start.2) | collective-permute-done | bytes 229408 | tf_op jit(solution)/shard_map/ppermute | solution.py:334
  17.1 1.4 %collective-permute-done.3.refs_4_ = f32[224,256]{1,0:T(8,128)S(1)} collective-permute-done((f32[224,256]{1,0:T(8,128)S(1)}, f32[224,256]{1,0:T(8,128)S(1)}, u32[]{:S(2)}, u32[]{:S(2)}) %collective-permute-start.3) | collective-permute-done | bytes 229408 | tf_op jit(solution)/shard_map/ppermute | solution.py:334
  18.6 1.6 %collective-permute-start.4 = (f32[224,256]{1,0:T(8,128)S(1)}, f32[224,256]{1,0:T(8,128)S(1)}, u32[]{:S(2)}, u32[]{:S(2)}) collective-permute-start(f32[224,256]{1,0:T(8,128)S(1)} %collective-permute-done.2.refs_3_), channel_id=1, source_target_pairs={{1,0},{0,2},{2,4},{4,6},{6,7},{7,5},{5,3},{3,1},{9,8},{8,10},{10,1... | collective-permute-start | bytes 688136 | tf_op jit(solution)/shard_map/ppermute | solution.py:334
  20.6 4.0 %collective-permute-done.4.refs_5_ = f32[224,256]{1,0:T(8,128)S(1)} collective-permute-done((f32[224,256]{1,0:T(8,128)S(1)}, f32[224,256]{1,0:T(8,128)S(1)}, u32[]{:S(2)}, u32[]{:S(2)}) %collective-permute-start.4) | collective-permute-done | bytes 229408 | tf_op jit(solution)/shard_map/ppermute | solution.py:334
  24.6 1.6 %collective-permute-done.5.refs_6_ = f32[224,256]{1,0:T(8,128)S(1)} collective-permute-done((f32[224,256]{1,0:T(8,128)S(1)}, f32[224,256]{1,0:T(8,128)S(1)}, u32[]{:S(2)}, u32[]{:S(2)}) %collective-permute-start.5) | collective-permute-done | bytes 229408 | tf_op jit(solution)/shard_map/ppermute | solution.py:334
  26.2 1.5 %collective-permute-start.6 = (f32[224,256]{1,0:T(8,128)S(1)}, f32[224,256]{1,0:T(8,128)S(1)}, u32[]{:S(2)}, u32[]{:S(2)}) collective-permute-start(f32[224,256]{1,0:T(8,128)S(1)} %collective-permute-done.4.refs_5_), channel_id=1, source_target_pairs={{1,0},{0,2},{2,4},{4,6},{6,7},{7,5},{5,3},{3,1},{9,8},{8,10},{10,1... | collective-permute-start | bytes 688136 | tf_op jit(solution)/shard_map/ppermute | solution.py:337
  27.7 4.5 %collective-permute-done.6.refs_7_ = f32[224,256]{1,0:T(8,128)S(1)} collective-permute-done((f32[224,256]{1,0:T(8,128)S(1)}, f32[224,256]{1,0:T(8,128)S(1)}, u32[]{:S(2)}, u32[]{:S(2)}) %collective-permute-start.6) | collective-permute-done | bytes 229408 | tf_op jit(solution)/shard_map/ppermute | solution.py:337
  32.2 3.1 %shard_map.60 = (bf16[4,640,256]{2,1,0:T(8,128)(2,1)S(1)}, bf16[4,640,256]{2,1,0:T(8,128)(2,1)S(1)}, f32[448,256]{1,0:T(8,128)S(1)}, f32[576,128]{1,0:T(8,128)S(1)}) custom-call(s32[1792]{0:T(1024)S(1)} %copy-done, f32[224,256]{1,0:T(8,128)S(1)} %copy-done.1, f32[224,256]{1,0:T(8,128)S(1)} %collective-permute-done.refs_1_, ...), custom_call_target="tpu_custom_call" | custom-call | flops 3303014400 | bytes 6249472 | tf_op jit(solution)/shard_map/pallas_call | solution.py:296
  35.9 1.5 %collective-permute-start.10 = (f32[576,128]{1,0:T(8,128)S(1)}, f32[576,128]{1,0:T(8,128)S(1)}, u32[]{:S(2)}, u32[]{:S(2)}) collective-permute-start(f32[576,128]{1,0:T(8,128)S(1)} %get-tuple-element.43.refs_0_), channel_id=1, source_target_pairs={{0,16},{8,24},{16,0},{24,8},{1,17},{9,25},{17,1},{25,9},{2,18},{10... | collective-permute-start | bytes 884744 | tf_op jit(solution)/shard_map/ppermute | solution.py:313
  37.5 1.7 %shard_map.61 = (f32[448,256]{1,0:T(8,128)S(1)}, bf16[448,448]{1,0:T(8,128)(2,1)S(1)}) custom-call(s32[1792]{0:T(1024)S(1)} %copy-done, bf16[4,640,256]{2,1,0:T(8,128)(2,1)S(1)} %get-tuple-element.44.uh_ref, bf16[4,640,256]{2,1,0:T(8,128)(2,1)S(1)} %get-tuple-element.45.ul_ref, f32[448,256]{1,0:T(8,128)S(1)} %get-tuple-element.41.part_ref, ...), custom_call_target="tpu_custom_call" | custom-call | flops 440401920 | bytes 6011904 | tf_op jit(solution)/shard_map/pallas_call | solution.py:296
  39.2 1.8 %shard_map.62 = (f32[448,256]{1,0:T(8,128)S(1)}, f32[112,256]{1,0:T(8,128)S(1)}, f32[112,256]{1,0:T(8,128)S(1)}, f32[112,256]{1,0:T(8,128)S(1)}) custom-call(bf16[4,640,256]{2,1,0:T(8,128)(2,1)S(1)} %get-tuple-element.44.uh_ref, bf16[4,640,256]{2,1,0:T(8,128)(2,1)S(1)} %get-tuple-element.45.ul_ref, f32[448,256]{1,0:T(8,128)S(1)} %get-tuple-element.48.part_ref, ...), custom_call_target="tpu_custom_call" | custom-call | flops 440401920 | bytes 5316608 | tf_op jit(solution)/shard_map/pallas_call | solution.py:296
  41.5 3.5 %collective-permute-done.10.refs_2_ = f32[576,128]{1,0:T(8,128)S(1)} collective-permute-done((f32[576,128]{1,0:T(8,128)S(1)}, f32[576,128]{1,0:T(8,128)S(1)}, u32[]{:S(2)}, u32[]{:S(2)}) %collective-permute-start.10) | collective-permute-done | bytes 294944 | tf_op jit(solution)/shard_map/ppermute | solution.py:313
  44.9 1.5 %collective-permute-start.14 = (f32[112,256]{1,0:T(8,128)S(1)}, f32[112,256]{1,0:T(8,128)S(1)}, u32[]{:S(2)}, u32[]{:S(2)}) collective-permute-start(f32[112,256]{1,0:T(8,128)S(1)} %get-tuple-element.55), channel_id=1, source_target_pairs={{0,2},{1,3},{2,4},{3,5},{4,6},{5,7},{6,0},{7,1},{8,10},{9,11},{10,... | collective-permute-start | bytes 344072 | tf_op jit(solution)/shard_map/ppermute | solution.py:428
  47.0 2.5 %collective-permute-start.16 = (f32[112,256]{1,0:T(8,128)S(1)}, f32[112,256]{1,0:T(8,128)S(1)}, u32[]{:S(2)}, u32[]{:S(2)}) collective-permute-start(f32[112,256]{1,0:T(8,128)S(1)} %get-tuple-element.57), channel_id=1, source_target_pairs={{0,6},{1,7},{2,0},{3,1},{4,2},{5,3},{6,4},{7,5},{8,14},{9,15},{10,... | collective-permute-start | bytes 344072 | tf_op jit(solution)/shard_map/ppermute | solution.py:428
  49.5 3.5 %shard_map.63 = (bf16[224,448]{1,0:T(8,128)(2,1)S(1)}, bf16[4,128,896]{2,1,0:T(8,128)(2,1)S(1)}, bf16[4,128,896]{2,1,0:T(8,128)(2,1)S(1)}) custom-call(s32[1792]{0:T(1024)S(1)} %copy-done, f32[576,128]{1,0:T(8,128)S(1)} %get-tuple-element.43.refs_0_, f32[576,128]{1,0:T(8,128)S(1)} %collective-permute-done.8.refs_1_, ...), custom_call_target="tpu_custom_call" | custom-call | flops 1056964608 | bytes 3222528 | tf_op jit(solution)/shard_map/pallas_call | solution.py:296
  53.0 4.3 %collective-permute-done.15.refs_1_ = f32[112,256]{1,0:T(8,128)S(1)} collective-permute-done((f32[112,256]{1,0:T(8,128)S(1)}, f32[112,256]{1,0:T(8,128)S(1)}, u32[]{:S(2)}, u32[]{:S(2)}) %collective-permute-start.15) | collective-permute-done | bytes 114720 | tf_op jit(solution)/shard_map/ppermute | solution.py:428
  58.8 2.7 %collective-permute-start.18 = (f32[128,256]{1,0:T(8,128)S(1)}, f32[128,256]{1,0:T(8,128)S(1)}, u32[]{:S(2)}, u32[]{:S(2)}) collective-permute-start(f32[128,256]{1,0:T(8,128)S(1)} %get-tuple-element.63), channel_id=1, source_target_pairs={{0,2},{1,3},{2,4},{3,5},{4,6},{5,7},{6,0},{7,1},{8,10},{9,11},{10,... | collective-permute-start | bytes 393224 | tf_op jit(solution)/shard_map/ppermute | solution.py:460
  62.2 1.7 %collective-permute-start.20 = (f32[128,256]{1,0:T(8,128)S(1)}, f32[128,256]{1,0:T(8,128)S(1)}, u32[]{:S(2)}, u32[]{:S(2)}) collective-permute-start(f32[128,256]{1,0:T(8,128)S(1)} %get-tuple-element.65), channel_id=1, source_target_pairs={{0,6},{1,7},{2,0},{3,1},{4,2},{5,3},{6,4},{7,5},{8,14},{9,15},{10,... | collective-permute-start | bytes 393224 | tf_op jit(solution)/shard_map/ppermute | solution.py:460
  63.9 2.0 %collective-permute-done.17.other_ref = f32[224,256]{1,0:T(8,128)S(1)} collective-permute-done((f32[224,256]{1,0:T(8,128)S(1)}, f32[224,256]{1,0:T(8,128)S(1)}, u32[]{:S(2)}, u32[]{:S(2)}) %collective-permute-start.17) | collective-permute-done | bytes 229408 | tf_op jit(solution)/shard_map/ppermute | solution.py:307
  67.0 4.4 %collective-permute-done.19 = f32[128,256]{1,0:T(8,128)S(1)} collective-permute-done((f32[128,256]{1,0:T(8,128)S(1)}, f32[128,256]{1,0:T(8,128)S(1)}, u32[]{:S(2)}, u32[]{:S(2)}) %collective-permute-start.19) | collective-permute-done | bytes 131104 | tf_op jit(solution)/shard_map/ppermute | solution.py:460
  (32 shorter events, 8.3 us)
Async XLA Ops:
  0.6 9.3 %collective-permute-start = (f32[224,256]{1,0:T(8,128)}, f32[224,256]{1,0:T(8,128)S(1)}, u32[]{:S(2)}, u32[]{:S(2)}) collective-permute-start(f32[224,256]{1,0:T(8,128)} %refs_0_.1), channel_id=1, source_target_pairs={{1,0},{0,2},{2,4},{4,6},{6,7},{7,5},{5,3},{3,1},{9,8},{8,10},{10,1... | collective-permute-start | bytes 688136 | tf_op jit(solution)/shard_map/ppermute | solution.py:334
  3.7 7.3 %collective-permute-start.1 = (f32[224,256]{1,0:T(8,128)}, f32[224,256]{1,0:T(8,128)S(1)}, u32[]{:S(2)}, u32[]{:S(2)}) collective-permute-start(f32[224,256]{1,0:T(8,128)} %refs_0_.1), channel_id=1, source_target_pairs={{0,1},{2,0},{4,2},{6,4},{7,6},{5,7},{3,5},{1,3},{8,9},{10,8},{12,1... | collective-permute-start | bytes 688136 | tf_op jit(solution)/shard_map/ppermute | solution.py:334
  3.7 0.7 copy-start
  4.4 27.8 %copy-start.1 = (f32[224,256]{1,0:T(8,128)S(1)}, f32[224,256]{1,0:T(8,128)}, u32[]{:S(2)}) copy-start(f32[224,256]{1,0:T(8,128)} %refs_0_.1) | copy-start | bytes 688132
  7.9 27.5 %collective-permute-start.7 = (f32[2016,128]{1,0:T(8,128)S(1)}, f32[2016,128]{1,0:T(8,128)S(1)}, u32[]{:S(2)}, u32[]{:S(2)}) collective-permute-start(f32[2016,128]{1,0:T(8,128)S(1)} %shard_map.59.refs_8_), channel_id=1, source_target_pairs={{0,16},{8,24},{16,0},{24,8},{1,17},{9,25},{17,1},{25,9},{2,18},{10... | collective-permute-start | bytes 3096584 | tf_op jit(solution)/shard_map/ppermute | solution.py:393
  11.0 6.2 %collective-permute-start.2 = (f32[224,256]{1,0:T(8,128)S(1)}, f32[224,256]{1,0:T(8,128)S(1)}, u32[]{:S(2)}, u32[]{:S(2)}) collective-permute-start(f32[224,256]{1,0:T(8,128)S(1)} %collective-permute-done.refs_1_), channel_id=1, source_target_pairs={{1,0},{0,2},{2,4},{4,6},{6,7},{7,5},{5,3},{3,1},{9,8},{8,10},{10,1... | collective-permute-start | bytes 688136 | tf_op jit(solution)/shard_map/ppermute | solution.py:334
  12.6 6.0 %collective-permute-start.3 = (f32[224,256]{1,0:T(8,128)S(1)}, f32[224,256]{1,0:T(8,128)S(1)}, u32[]{:S(2)}, u32[]{:S(2)}) collective-permute-start(f32[224,256]{1,0:T(8,128)S(1)} %collective-permute-done.1.refs_2_), channel_id=1, source_target_pairs={{0,1},{2,0},{4,2},{6,4},{7,6},{5,7},{3,5},{1,3},{8,9},{10,8},{12,1... | collective-permute-start | bytes 688136 | tf_op jit(solution)/shard_map/ppermute | solution.py:334
  18.6 6.0 %collective-permute-start.4 = (f32[224,256]{1,0:T(8,128)S(1)}, f32[224,256]{1,0:T(8,128)S(1)}, u32[]{:S(2)}, u32[]{:S(2)}) collective-permute-start(f32[224,256]{1,0:T(8,128)S(1)} %collective-permute-done.2.refs_3_), channel_id=1, source_target_pairs={{1,0},{0,2},{2,4},{4,6},{6,7},{7,5},{5,3},{3,1},{9,8},{8,10},{10,1... | collective-permute-start | bytes 688136 | tf_op jit(solution)/shard_map/ppermute | solution.py:334
  20.2 6.0 %collective-permute-start.5 = (f32[224,256]{1,0:T(8,128)S(1)}, f32[224,256]{1,0:T(8,128)S(1)}, u32[]{:S(2)}, u32[]{:S(2)}) collective-permute-start(f32[224,256]{1,0:T(8,128)S(1)} %collective-permute-done.3.refs_4_), channel_id=1, source_target_pairs={{0,1},{2,0},{4,2},{6,4},{7,6},{5,7},{3,5},{1,3},{8,9},{10,8},{12,1... | collective-permute-start | bytes 688136 | tf_op jit(solution)/shard_map/ppermute | solution.py:334
  26.2 6.0 %collective-permute-start.6 = (f32[224,256]{1,0:T(8,128)S(1)}, f32[224,256]{1,0:T(8,128)S(1)}, u32[]{:S(2)}, u32[]{:S(2)}) collective-permute-start(f32[224,256]{1,0:T(8,128)S(1)} %collective-permute-done.4.refs_5_), channel_id=1, source_target_pairs={{1,0},{0,2},{2,4},{4,6},{6,7},{7,5},{5,3},{3,1},{9,8},{8,10},{10,1... | collective-permute-start | bytes 688136 | tf_op jit(solution)/shard_map/ppermute | solution.py:337
  27.7 9.8 %collective-permute-start.9 = (f32[2016,128]{1,0:T(8,128)S(1)}, f32[2016,128]{1,0:T(8,128)S(1)}, u32[]{:S(2)}, u32[]{:S(2)}) collective-permute-start(f32[2016,128]{1,0:T(8,128)S(1)} %shard_map.59.refs_8_), channel_id=1, source_target_pairs={{0,8},{8,0},{16,24},{24,16},{1,9},{9,1},{17,25},{25,17},{2,10},{10... | collective-permute-start | bytes 3096584 | tf_op jit(solution)/shard_map/ppermute | solution.py:307
  35.4 3.8 %collective-permute-start.11 = (f32[2016,128]{1,0:T(8,128)S(1)}, f32[2016,128]{1,0:T(8,128)S(1)}, u32[]{:S(2)}, u32[]{:S(2)}) collective-permute-start(f32[2016,128]{1,0:T(8,128)S(1)} %collective-permute-done.7.refs_1_), channel_id=1, source_target_pairs={{0,8},{8,0},{16,24},{24,16},{1,9},{9,1},{17,25},{25,17},{2,10},{10... | collective-permute-start | bytes 3096584 | tf_op jit(solution)/shard_map/ppermute | solution.py:307
  35.4 3.7 %collective-permute-start.8 = (f32[576,128]{1,0:T(8,128)S(1)}, f32[576,128]{1,0:T(8,128)S(1)}, u32[]{:S(2)}, u32[]{:S(2)}) collective-permute-start(f32[576,128]{1,0:T(8,128)S(1)} %get-tuple-element.43.refs_0_), channel_id=1, source_target_pairs={{0,8},{8,0},{16,24},{24,16},{1,9},{9,1},{17,25},{25,17},{2,10},{10... | collective-permute-start | bytes 884744 | tf_op jit(solution)/shard_map/ppermute | solution.py:307
  35.9 9.0 %collective-permute-start.10 = (f32[576,128]{1,0:T(8,128)S(1)}, f32[576,128]{1,0:T(8,128)S(1)}, u32[]{:S(2)}, u32[]{:S(2)}) collective-permute-start(f32[576,128]{1,0:T(8,128)S(1)} %get-tuple-element.43.refs_0_), channel_id=1, source_target_pairs={{0,16},{8,24},{16,0},{24,8},{1,17},{9,25},{17,1},{25,9},{2,18},{10... | collective-permute-start | bytes 884744 | tf_op jit(solution)/shard_map/ppermute | solution.py:313
  40.9 16.4 %collective-permute-start.13 = (f32[448,256]{1,0:T(8,128)S(1)}, f32[448,256]{1,0:T(8,128)S(1)}, u32[]{:S(2)}, u32[]{:S(2)}) collective-permute-start(f32[448,256]{1,0:T(8,128)S(1)} %get-tuple-element.50.whole_ref), channel_id=1, source_target_pairs={{0,1},{1,0},{2,3},{3,2},{4,5},{5,4},{6,7},{7,6},{8,9},{9,8},{10,11... | collective-permute-start | bytes 1376264 | tf_op jit(solution)/shard_map/ppermute | solution.py:307
  44.9 4.6 %collective-permute-start.12 = (f32[576,128]{1,0:T(8,128)S(1)}, f32[576,128]{1,0:T(8,128)S(1)}, u32[]{:S(2)}, u32[]{:S(2)}) collective-permute-start(f32[576,128]{1,0:T(8,128)S(1)} %collective-permute-done.10.refs_2_), channel_id=1, source_target_pairs={{0,8},{8,0},{16,24},{24,16},{1,9},{9,1},{17,25},{25,17},{2,10},{10... | collective-permute-start | bytes 884744 | tf_op jit(solution)/shard_map/ppermute | solution.py:307
  44.9 8.1 %collective-permute-start.14 = (f32[112,256]{1,0:T(8,128)S(1)}, f32[112,256]{1,0:T(8,128)S(1)}, u32[]{:S(2)}, u32[]{:S(2)}) collective-permute-start(f32[112,256]{1,0:T(8,128)S(1)} %get-tuple-element.55), channel_id=1, source_target_pairs={{0,2},{1,3},{2,4},{3,5},{4,6},{5,7},{6,0},{7,1},{8,10},{9,11},{10,... | collective-permute-start | bytes 344072 | tf_op jit(solution)/shard_map/ppermute | solution.py:428
  46.4 10.9 %collective-permute-start.15 = (f32[112,256]{1,0:T(8,128)S(1)}, f32[112,256]{1,0:T(8,128)S(1)}, u32[]{:S(2)}, u32[]{:S(2)}) collective-permute-start(f32[112,256]{1,0:T(8,128)S(1)} %get-tuple-element.56), channel_id=1, source_target_pairs={{0,4},{1,5},{2,6},{3,7},{4,0},{5,1},{6,2},{7,3},{8,12},{9,13},{10,... | collective-permute-start | bytes 344072 | tf_op jit(solution)/shard_map/ppermute | solution.py:428
  47.0 10.3 %collective-permute-start.16 = (f32[112,256]{1,0:T(8,128)S(1)}, f32[112,256]{1,0:T(8,128)S(1)}, u32[]{:S(2)}, u32[]{:S(2)}) collective-permute-start(f32[112,256]{1,0:T(8,128)S(1)} %get-tuple-element.57), channel_id=1, source_target_pairs={{0,6},{1,7},{2,0},{3,1},{4,2},{5,3},{6,4},{7,5},{8,14},{9,15},{10,... | collective-permute-start | bytes 344072 | tf_op jit(solution)/shard_map/ppermute | solution.py:428
  57.3 14.1 %copy-start.2 = (f32[128,256]{1,0:T(8,128)S(1)}, f32[128,256]{1,0:T(8,128)}, u32[]{:S(2)}) copy-start(f32[128,256]{1,0:T(8,128)} %param.7) | copy-start | bytes 393220
  58.4 7.6 %collective-permute-start.17 = (f32[224,256]{1,0:T(8,128)S(1)}, f32[224,256]{1,0:T(8,128)S(1)}, u32[]{:S(2)}, u32[]{:S(2)}) collective-permute-start(f32[224,256]{1,0:T(8,128)S(1)} %get-tuple-element.59), channel_id=1, source_target_pairs={{0,1},{1,0},{2,3},{3,2},{4,5},{5,4},{6,7},{7,6},{8,9},{9,8},{10,11... | collective-permute-start | bytes 688136 | tf_op jit(solution)/shard_map/ppermute | solution.py:307
  58.8 8.2 %collective-permute-start.18 = (f32[128,256]{1,0:T(8,128)S(1)}, f32[128,256]{1,0:T(8,128)S(1)}, u32[]{:S(2)}, u32[]{:S(2)}) collective-permute-start(f32[128,256]{1,0:T(8,128)S(1)} %get-tuple-element.63), channel_id=1, source_target_pairs={{0,2},{1,3},{2,4},{3,5},{4,6},{5,7},{6,0},{7,1},{8,10},{9,11},{10,... | collective-permute-start | bytes 393224 | tf_op jit(solution)/shard_map/ppermute | solution.py:460
  61.4 9.9 %collective-permute-start.19 = (f32[128,256]{1,0:T(8,128)S(1)}, f32[128,256]{1,0:T(8,128)S(1)}, u32[]{:S(2)}, u32[]{:S(2)}) collective-permute-start(f32[128,256]{1,0:T(8,128)S(1)} %get-tuple-element.64), channel_id=1, source_target_pairs={{0,4},{1,5},{2,6},{3,7},{4,0},{5,1},{6,2},{7,3},{8,12},{9,13},{10,... | collective-permute-start | bytes 393224 | tf_op jit(solution)/shard_map/ppermute | solution.py:460
  62.2 9.2 %collective-permute-start.20 = (f32[128,256]{1,0:T(8,128)S(1)}, f32[128,256]{1,0:T(8,128)S(1)}, u32[]{:S(2)}, u32[]{:S(2)}) collective-permute-start(f32[128,256]{1,0:T(8,128)S(1)} %get-tuple-element.65), channel_id=1, source_target_pairs={{0,6},{1,7},{2,0},{3,1},{4,2},{5,3},{6,4},{7,5},{8,14},{9,15},{10,... | collective-permute-start | bytes 393224 | tf_op jit(solution)/shard_map/ppermute | solution.py:460

commit v7 on v6

--- a/solution.py
+++ b/solution.py
@@ -85,8 +85,8 @@
     place = one_hot(at == named).astype(BF16)
     for k in range(parts):
         copies[k].wait()
-        high, low = split(held_ref[part * k : part * (k + 1), :])
-        picked = dot(high, place) + dot(low, place)
+        picked = dot(jnp.concatenate(split(held_ref[part * k : part * (k + 1), :]), axis=0), place)
+        picked = picked[:part] + picked[part:]
         for i in range(FULL):
             at = rows * i + part * k
             out_ref[at : at + part, :] = picked[:, LANES * i : LANES * (i + 1)]
@@ -177,15 +177,20 @@
     return one_hot(at == slot).T.astype(BF16)
 
 
-def near_kernel(direct, slots, owners, structure_ref, uh_ref, ul_ref, part_ref, *refs):
-    block_refs, (image_ref, to_ref) = refs[:-2], refs[-2:]
+def order_kernel(direct, slots, structure_ref, to_ref):
+    nc = to_ref.shape[0] // slots
+    rows = to_ref.shape[1]
+    names = structure_ref[...].reshape(1, -1)
+    to_ref[...] = row_order(names, lax.axis_index("pcol"), rows, nc, slots, direct)
+
+
+def near_kernel(owners, uh_ref, ul_ref, part_ref, *refs):
+    block_refs, image_ref = refs[:-1], refs[-1]
     rows = part_ref.shape[0]
     image = part_ref[...]
     for owner, block_ref in zip(owners(lax.axis_index("prow")), block_refs):
         image = image + block_term(block_ref, uh_ref[owner], ul_ref[owner], rows)
     image_ref[...] = image
-    nc = to_ref.shape[0] // slots
-    to_ref[...] = row_order(structure_ref[...].reshape(1, -1), lax.axis_index("pcol"), rows, nc, slots, direct)
 
 
 def image_kernel(direct, owners, uh_ref, ul_ref, part_ref, to_ref, *refs):
@@ -208,8 +213,8 @@
 
 
 def turn_kernel(direct, slots, owners, structure_ref, *refs):
-    from_ref, high_ref, low_ref = refs[-3:]
-    nz = high_ref.shape[0]
+    from_ref, high_ref, low_ref, held_ref = refs[-4:]
+    nz, wd = high_ref.shape[:2]
     nc = 2 * nz
     lg = log2(nc)
     rows = slots * nc
@@ -235,11 +240,15 @@
 
     def put(owner, u_ref):
         where = ((owner - z) & (nz - 1)) if direct else owner
-        for out_ref, part in zip((high_ref, low_ref), split(u_ref[...].T)):
-            turned = lax.dot_general(part, place, (((1,), (1,)), ((), ())), preferred_element_type=jnp.float32)
-            out_ref[where] = turned.astype(BF16)
-
-    each(refs[:-3], owners(lax.axis_index("prow")) if direct else None, put)
+        high, low = split(u_ref[...].T)
+        held_ref[pl.ds(pl.multiple_of(where * wd, wd), wd), :] = high
+        held_ref[pl.ds(pl.multiple_of((where + nz) * wd, wd), wd), :] = low
+
+    each(refs[:-4], owners(lax.axis_index("prow")) if direct else None, put)
+    turned = lax.dot_general(held_ref[...], place, (((1,), (1,)), ((), ())), preferred_element_type=jnp.float32)
+    turned = turned.astype(BF16).reshape(2, nz, wd, 2 * rows)
+    high_ref[...] = turned[0]
+    low_ref[...] = turned[1]
 
     own = lax.broadcasted_iota(jnp.int32, (m, n), 1) - nc * lax.broadcasted_iota(jnp.int32, (m, n), 0)
     mine = jnp.sum(jnp.where(own == c, names, 0).astype(jnp.float32), axis=1, keepdims=True)
@@ -258,9 +267,8 @@
     from_ref[...] = one_hot(at == slot).astype(BF16)
 
 
-def correction_kernel(slots, n_got, high_ref, low_ref, whole_ref, other_ref, *refs):
-    got_refs, (mine_ref, theirs_ref), out_refs = refs[:n_got], refs[n_got : n_got + 2], refs[n_got + 2 :]
-    sh, sl = split(jnp.concatenate([whole_ref[...], other_ref[...]], axis=0))
+def correction_kernel(high_ref, low_ref, mine_ref, other_ref, *out_refs):
+    sh, sl = split(jnp.concatenate([mine_ref[...], other_ref[...]], axis=0))
 
     def term(t):
         return dot(high_ref[t], sh) + (dot(high_ref[t], sl) + dot(low_ref[t], sh))
@@ -274,13 +282,18 @@
         def _(t):
             out_refs[0][t] = term(t)
 
+
+def part_kernel(slots, *refs):
+    mine_ref, theirs_ref = refs[-2:]
     first = (lax.axis_index("pcol") & 1) == 0
+    blocks = mine_ref.shape[0] // slots
     mine, theirs = [], []
-    for ref, k in [(whole_ref, 0)] * (n_got > 1) + [(ref, k) for ref in got_refs for k in range(ref.shape[0] // (2 * slots))]:
-        low = ref[2 * slots * k : 2 * slots * k + slots, :]
-        high = ref[2 * slots * k + slots : 2 * slots * (k + 1), :]
-        mine.append(jnp.where(first, low, high))
-        theirs.append(jnp.where(first, high, low))
+    for ref in refs[:-2]:
+        for k in range(blocks // len(refs[:-2])):
+            low = ref[2 * slots * k : 2 * slots * k + slots, :]
+            high = ref[2 * slots * k + slots : 2 * slots * (k + 1), :]
+            mine.append(jnp.where(first, low, high))
+            theirs.append(jnp.where(first, high, low))
     mine_ref[...] = jnp.concatenate(mine, axis=0)
     theirs_ref[...] = jnp.concatenate(theirs, axis=0)
 
@@ -307,12 +320,11 @@
     return lax.ppermute(v, axis, [(k, k ^ 1) for k in range(size)])
 
 
-def spread(v, near, size, after):
-    blocks = [v, near]
+def spread(v, size):
+    blocks = [v, swap(v, "prow", size)]
     for t in range(1, size // 2):
-        far = lax.ppermute(v, "prow", [(k, (k + 2 * t) % size) for k in range(size)])
-        far, _ = lax.optimization_barrier((far, after))
-        blocks += [far, swap(far, "prow", size)]
+        for flip in range(2):
+            blocks.append(lax.ppermute(v, "prow", [(k, ((k + 2 * t) % size) ^ flip) for k in range(size)]))
     return blocks
 
 
@@ -324,7 +336,7 @@
     return out
 
 
-def ring_gather(u, nc):
+def ring_gather(u, nc, aside):
     ring = [2 * z for z in range(nc // 2)] + [2 * z + 1 for z in reversed(range(nc // 2))]
     pairs = [(ring[q - 1], ring[q]) for q in range(nc)]
     back = [(b, a) for a, b in pairs]
@@ -332,9 +344,11 @@
     up = down = u
     for step in range(1, nc // 2):
         up, down = lax.ppermute(up, "pcol", pairs), lax.ppermute(down, "pcol", back)
-        up, down = lax.optimization_barrier((up, down))
+        if step == 1:
+            up, down = lax.optimization_barrier((up, down))
         blocks += [up, down]
-    return blocks + [lax.ppermute(up, "pcol", pairs)]
+    last, aside = lax.optimization_barrier((lax.ppermute(up, "pcol", pairs), aside))
+    return blocks + [last], aside
 
 
 def ring_owners(nc, c):
@@ -367,13 +381,14 @@
         names,
         sigma_top,
         in_specs=[VMEM, HBM],
-        scratch_shapes=[pltpu.VMEM((rows, cols), jnp.float32), pltpu.SemaphoreType.DMA((4,))],
+        scratch_shapes=[pltpu.VMEM((rows, cols), jnp.float32), pltpu.SemaphoreType.DMA((2,))],
         flops=4 * rows * cols * WIDE,
         vmem=52,
     )
     near = [chosen] if direct else []
-    if direct:
-        u_all = ring_gather(u_panel, nc)
+    to = call(functools.partial(order_kernel, direct, slots), bf16(nc * slots, rows), names)
+    if direct:
+        u_all, to = ring_gather(u_panel, nc, to)
     else:
         u_all = [lax.all_gather(u_panel, "pcol")]
     term = 6 * rows * WIDE * w
@@ -396,20 +411,20 @@
             later.append(swap(far, "prow", nr))
     else:
         later = [lax.all_gather(chosen, "prow")]
-    image, to = call(
-        functools.partial(near_kernel, direct, slots, lambda r: owners(r)[1:2] + owners(r)[2::2]),
-        [f32(rows, w), bf16(nc * slots, rows)],
-        names,
-        uh,
-        ul,
-        image,
-        *beside,
-        flops=term,
-    )
+    if direct:
+        image = call(
+            functools.partial(near_kernel, lambda r: owners(r)[1:2] + owners(r)[2::2]),
+            f32(rows, w),
+            uh,
+            ul,
+            image,
+            *beside,
+            flops=term,
+        )
     if direct:
         own, _ = lax.optimization_barrier((own, beside[1]))
-        near = swap(own, "prow", nr)
-        near, to = lax.optimization_barrier((near, to))
+        owned = spread(own, nr)
+        owned[1], to = lax.optimization_barrier((owned[1], to))
     sent = call(
         functools.partial(image_kernel, direct, lambda r: owners(r)[3::2]),
         [f32(nc * slots, w)] + [f32(2 * slots, w)] * ((nz - 1) * direct),
@@ -423,10 +438,9 @@
     whole = sent[0]
     other = swap(whole, "pcol", nc)
     if direct:
-        got = []
+        got = [whole]
         for t in range(1, nz):
             got.append(lax.ppermute(sent[t], "pcol", [(k, (k + 2 * t) % nc) for k in range(nc)]))
-        owned = spread(own, near, nr, whole)
     else:
         blocks = whole.reshape(nz, 2 * slots, w)
         blocks = lax.all_to_all(blocks, "pcol", split_axis=0, concat_axis=0, axis_index_groups=groups, tiled=True)
@@ -440,19 +454,15 @@
         [bf16(m, nc * slots), turned, turned],
         names,
         *owned,
+        scratch_shapes=[pltpu.VMEM((2 * nz * wd, CAP), BF16)],
         flops=8 * nz * wd * nc * slots * CAP,
     )
     parts = [f32(wd, w)] * nz if direct else [f32(nz, wd, w)]
-    mine, theirs, *terms = call(
-        functools.partial(correction_kernel, slots, len(got)),
-        [f32(nz * slots, w)] * 2 + parts,
-        high,
-        low,
-        whole,
-        other,
-        *got,
-        flops=term,
-    )
+    got, _ = lax.optimization_barrier((got, source))
+    mine, theirs = call(functools.partial(part_kernel, slots), [f32(nz * slots, w)] * 2, *got, flops=2 * term)
+    other, _ = lax.optimization_barrier((other, mine))
+    terms = call(correction_kernel, parts, high, low, whole, other, flops=term)
+    theirs, _ = lax.optimization_barrier((theirs, terms[0]))
     sigma_sj = call(pick_kernel, f32(m, w), source, mine, swap(theirs, "pcol", nc), flops=term // 4)
     if direct:
         total = terms[0]

time: 72.9 us -> 68.9 us (0.945)
  waiting for transfers between devices: 30.9 us -> 26.4 us
  starting transfers between devices: 23.4 us -> 24.6 us
    ppermute x3, waiting for transfers between devices: 4.31 us -> 0.01 us  [per_device(): lax.ppermute(sent[t], 'pcol', [(k, (k + 2 * t) % nc) for k in range(nc)])]
    ppermute x3 -> x4, waiting for transfers between devices: 8.12 us -> 11.7 us  [ring_gather(): lax.ppermute(up, 'pcol', pairs)]
    ppermute x2, waiting for transfers between devices: 8 us -> 5.09 us  [spread(): lax.ppermute(v, 'prow', [(k, (k + 2 * t) % size ^ flip) for k in range(si...]
    ppermute x3 -> x4, starting transfers between devices: 6.23 us -> 7.81 us  [ring_gather(): lax.ppermute(up, 'pcol', pairs)]
    ppermute x2, starting transfers between devices: 3.01 us -> 1.71 us  [spread(): lax.ppermute(v, 'prow', [(k, (k + 2 * t) % size ^ flip) for k in range(si...]
    ppermute x3, starting transfers between devices: 4.59 us -> 5.35 us  [per_device(): lax.ppermute(sent[t], 'pcol', [(k, (k + 2 * t) % nc) for k in range(nc)])]
    pallas_call x7 -> x9, Pallas kernels: 15.6 us -> 15 us  [call(): pl.pallas_call(kernel, out_shape=out_shape, out_specs=[VMEM] * len(out_sh...]
    ppermute x6 -> x5, waiting for transfers between devices: 2.05 us -> 1.7 us  [swap(): return lax.ppermute(v, axis, [(k, k ^ 1) for k in range(size)])]
  transfers between devices with their start and end apart: 21 -> 21, of which waited for: 10 -> 11; matrix products, arithmetic and copies ran while one was open for 0% -> 0% of each run, Pallas kernels for 20% -> 21%
where the time goes in v7:
time: 68.9 us; the launch traced here: 68.2 us
  waiting for transfers between devices  26.4 us (38%)
  starting transfers between devices  24.6 us (36%)
  Pallas kernels  15 us (22%)
  between operations  0.78 us (1%)
  local copies, waits for them, and re-layouts  0.71 us (1%)
  other arithmetic  0.7 us (1%)
    pallas_call x9, Pallas kernels, call(): pl.pallas_call(kernel, out_shape=out_shape, out_specs=[VMEM] * len(out_sh...  15 us
    ppermute x4, waiting for transfers between devices, ring_gather(): lax.ppermute(up, 'pcol', pairs)  11.7 us
    ppermute x4, starting transfers between devices, ring_gather(): lax.ppermute(up, 'pcol', pairs)  7.81 us
    ppermute x3, starting transfers between devices, per_device(): lax.ppermute(sent[t], 'pcol', [(k, (k + 2 * t) % nc) for k in range(nc)])  5.35 us
    ppermute x3, starting transfers between devices, per_device(): lax.ppermute(terms[t], 'pcol', [(k, (k + 2 * t) % nc) for k in range(nc)])  5.22 us
    ppermute x2, waiting for transfers between devices, spread(): lax.ppermute(v, 'prow', [(k, (k + 2 * t) % size ^ flip) for k in range(si...  5.09 us
    ppermute x3, waiting for transfers between devices, per_device(): lax.ppermute(terms[t], 'pcol', [(k, (k + 2 * t) % nc) for k in range(nc)])  4.52 us
    ppermute x3, waiting for transfers between devices, ring_gather(): lax.ppermute(down, 'pcol', back)  3.36 us
  transfers between devices with their start and end apart: 21, of which 11 were waited for; matrix products, arithmetic and copies ran while one was open for 0% of the time, Pallas kernels for 21%

profile of v7, /device:TPU:0, one launch (start us, length us, event | category | flops | bytes accessed | tf_op | source)
XLA Modules:
  0.0 68.2 jit_solution(9271963130601698597)
XLA Ops:
  0.6 3.1 %collective-permute-start = (f32[224,256]{1,0:T(8,128)}, f32[224,256]{1,0:T(8,128)S(1)}, u32[]{:S(2)}, u32[]{:S(2)}) collective-permute-start(f32[224,256]{1,0:T(8,128)} %refs_0_.1), channel_id=1, source_target_pairs={{1,0},{0,2},{2,4},{4,6},{6,7},{7,5},{5,3},{3,1},{9,8},{8,10},{10,1... | collective-permute-start | bytes 688136 | tf_op jit(solution)/shard_map/ppermute | solution.py:346
  4.4 3.3 %shard_map.60.refs_8_ = f32[2016,128]{1,0:T(8,128)S(1)} custom-call(s32[1792]{0:T(1024)S(1)} %copy-done, f32[448,896]{1,0:T(8,128)} %sigma_ref.1), custom_call_target="tpu_custom_call" | custom-call | flops 1027604480 | bytes 2644992 | tf_op jit(solution)/shard_map/pallas_call | solution.py:309
  7.7 2.0 %collective-permute-start.7 = (f32[2016,128]{1,0:T(8,128)S(1)}, f32[2016,128]{1,0:T(8,128)S(1)}, u32[]{:S(2)}, u32[]{:S(2)}) collective-permute-start(f32[2016,128]{1,0:T(8,128)S(1)} %shard_map.60.refs_8_), channel_id=1, source_target_pairs={{0,16},{8,24},{16,0},{24,8},{1,17},{9,25},{17,1},{25,9},{2,18},{10... | collective-permute-start | bytes 3096584 | tf_op jit(solution)/shard_map/ppermute | solution.py:408
  9.7 1.2 %collective-permute-done.1.refs_2_ = f32[224,256]{1,0:T(8,128)S(1)} collective-permute-done((f32[224,256]{1,0:T(8,128)}, f32[224,256]{1,0:T(8,128)S(1)}, u32[]{:S(2)}, u32[]{:S(2)}) %collective-permute-start.1) | collective-permute-done | bytes 229408 | tf_op jit(solution)/shard_map/ppermute | solution.py:346
  11.0 1.6 %collective-permute-start.2 = (f32[224,256]{1,0:T(8,128)S(1)}, f32[224,256]{1,0:T(8,128)S(1)}, u32[]{:S(2)}, u32[]{:S(2)}) collective-permute-start(f32[224,256]{1,0:T(8,128)S(1)} %collective-permute-done.refs_1_), channel_id=1, source_target_pairs={{1,0},{0,2},{2,4},{4,6},{6,7},{7,5},{5,3},{3,1},{9,8},{8,10},{10,1... | collective-permute-start | bytes 688136 | tf_op jit(solution)/shard_map/ppermute | solution.py:346
  12.6 4.6 %collective-permute-done.2.refs_3_ = f32[224,256]{1,0:T(8,128)S(1)} collective-permute-done((f32[224,256]{1,0:T(8,128)S(1)}, f32[224,256]{1,0:T(8,128)S(1)}, u32[]{:S(2)}, u32[]{:S(2)}) %collective-permute-start.2) | collective-permute-done | bytes 229408 | tf_op jit(solution)/shard_map/ppermute | solution.py:346
  17.1 1.6 %collective-permute-start.4 = (f32[224,256]{1,0:T(8,128)S(1)}, f32[224,256]{1,0:T(8,128)S(1)}, u32[]{:S(2)}, u32[]{:S(2)}) collective-permute-start(f32[224,256]{1,0:T(8,128)S(1)} %collective-permute-done.2.refs_3_), channel_id=1, source_target_pairs={{1,0},{0,2},{2,4},{4,6},{6,7},{7,5},{5,3},{3,1},{9,8},{8,10},{10,1... | collective-permute-start | bytes 688136 | tf_op jit(solution)/shard_map/ppermute | solution.py:346
  19.2 4.5 %collective-permute-done.4.refs_5_ = f32[224,256]{1,0:T(8,128)S(1)} collective-permute-done((f32[224,256]{1,0:T(8,128)S(1)}, f32[224,256]{1,0:T(8,128)S(1)}, u32[]{:S(2)}, u32[]{:S(2)}) %collective-permute-start.4) | collective-permute-done | bytes 229408 | tf_op jit(solution)/shard_map/ppermute | solution.py:346
  23.6 1.6 %collective-permute-start.6 = (f32[224,256]{1,0:T(8,128)S(1)}, f32[224,256]{1,0:T(8,128)S(1)}, u32[]{:S(2)}, u32[]{:S(2)}) collective-permute-start(f32[224,256]{1,0:T(8,128)S(1)} %collective-permute-done.4.refs_5_), channel_id=1, source_target_pairs={{1,0},{0,2},{2,4},{4,6},{6,7},{7,5},{5,3},{3,1},{9,8},{8,10},{10,1... | collective-permute-start | bytes 688136 | tf_op jit(solution)/shard_map/ppermute | solution.py:350
  27.0 2.7 %collective-permute-done.6.refs_7_ = f32[224,256]{1,0:T(8,128)S(1)} collective-permute-done((f32[224,256]{1,0:T(8,128)S(1)}, f32[224,256]{1,0:T(8,128)S(1)}, u32[]{:S(2)}, u32[]{:S(2)}) %collective-permute-start.6) | collective-permute-done | bytes 229408 | tf_op jit(solution)/shard_map/ppermute | solution.py:350
  29.6 1.9 %collective-permute-done.5.refs_6_ = f32[224,256]{1,0:T(8,128)S(1)} collective-permute-done((f32[224,256]{1,0:T(8,128)S(1)}, f32[224,256]{1,0:T(8,128)S(1)}, u32[]{:S(2)}, u32[]{:S(2)}) %collective-permute-start.5) | collective-permute-done | bytes 229408 | tf_op jit(solution)/shard_map/ppermute | solution.py:346
  31.5 3.1 %shard_map.61 = (bf16[4,640,256]{2,1,0:T(8,128)(2,1)S(1)}, bf16[4,640,256]{2,1,0:T(8,128)(2,1)S(1)}, f32[448,256]{1,0:T(8,128)S(1)}, f32[576,128]{1,0:T(8,128)S(1)}) custom-call(s32[1792]{0:T(1024)S(1)} %copy-done, f32[224,256]{1,0:T(8,128)S(1)} %copy-done.1, f32[224,256]{1,0:T(8,128)S(1)} %collective-permute-done.refs_1_, ...), custom_call_target="tpu_custom_call" | custom-call | flops 3303014400 | bytes 6249472 | tf_op jit(solution)/shard_map/pallas_call | solution.py:309
  35.2 1.2 %collective-permute-start.10 = (f32[576,128]{1,0:T(8,128)S(1)}, f32[576,128]{1,0:T(8,128)S(1)}, u32[]{:S(2)}, u32[]{:S(2)}) collective-permute-start(f32[576,128]{1,0:T(8,128)S(1)} %get-tuple-element.41.refs_0_), channel_id=1, source_target_pairs={{0,24},{8,16},{16,8},{24,0},{1,25},{9,17},{17,9},{25,1},{2,26},{10... | collective-permute-start | bytes 884744 | tf_op jit(solution)/shard_map/ppermute | solution.py:327
  37.0 1.1 %shard_map.63.part_ref = f32[448,256]{1,0:T(8,128)S(1)} custom-call(bf16[4,640,256]{2,1,0:T(8,128)(2,1)S(1)} %get-tuple-element.45.uh_ref, bf16[4,640,256]{2,1,0:T(8,128)(2,1)S(1)} %get-tuple-element.46.ul_ref, f32[448,256]{1,0:T(8,128)S(1)} %get-tuple-element.39.part_ref, f32[2016,128]{1,0:T(8,128)S(1)} %collective-permute-done.11.refs_0_, ...), custom_call_target="tpu_custom_call" | custom-call | flops 440401920 | bytes 5603328 | tf_op jit(solution)/shard_map/pallas_call | solution.py:309
  38.1 1.8 %shard_map.64 = (f32[448,256]{1,0:T(8,128)S(1)}, f32[112,256]{1,0:T(8,128)S(1)}, f32[112,256]{1,0:T(8,128)S(1)}, f32[112,256]{1,0:T(8,128)S(1)}) custom-call(bf16[4,640,256]{2,1,0:T(8,128)(2,1)S(1)} %get-tuple-element.45.uh_ref, bf16[4,640,256]{2,1,0:T(8,128)(2,1)S(1)} %get-tuple-element.46.ul_ref, f32[448,256]{1,0:T(8,128)S(1)} %shard_map.63.part_ref, ...), custom_call_target="tpu_custom_call" | custom-call | flops 440401920 | bytes 5316608 | tf_op jit(solution)/shard_map/pallas_call | solution.py:309
  40.4 1.2 %collective-permute-start.13 = (f32[112,256]{1,0:T(8,128)S(1)}, f32[112,256]{1,0:T(8,128)S(1)}, u32[]{:S(2)}, u32[]{:S(2)}) collective-permute-start(f32[112,256]{1,0:T(8,128)S(1)} %get-tuple-element.49), channel_id=1, source_target_pairs={{0,2},{1,3},{2,4},{3,5},{4,6},{5,7},{6,0},{7,1},{8,10},{9,11},{10,... | collective-permute-start | bytes 344072 | tf_op jit(solution)/shard_map/ppermute | solution.py:443
  41.6 1.8 %collective-permute-start.14 = (f32[112,256]{1,0:T(8,128)S(1)}, f32[112,256]{1,0:T(8,128)S(1)}, u32[]{:S(2)}, u32[]{:S(2)}) collective-permute-start(f32[112,256]{1,0:T(8,128)S(1)} %get-tuple-element.50), channel_id=1, source_target_pairs={{0,4},{1,5},{2,6},{3,7},{4,0},{5,1},{6,2},{7,3},{8,12},{9,13},{10,... | collective-permute-start | bytes 344072 | tf_op jit(solution)/shard_map/ppermute | solution.py:443
  44.3 2.4 %collective-permute-start.15 = (f32[112,256]{1,0:T(8,128)S(1)}, f32[112,256]{1,0:T(8,128)S(1)}, u32[]{:S(2)}, u32[]{:S(2)}) collective-permute-start(f32[112,256]{1,0:T(8,128)S(1)} %get-tuple-element.51), channel_id=1, source_target_pairs={{0,6},{1,7},{2,0},{3,1},{4,2},{5,3},{6,4},{7,5},{8,14},{9,15},{10,... | collective-permute-start | bytes 344072 | tf_op jit(solution)/shard_map/ppermute | solution.py:443
  46.7 4.2 %collective-permute-done.9.refs_2_ = f32[576,128]{1,0:T(8,128)S(1)} collective-permute-done((f32[576,128]{1,0:T(8,128)S(1)}, f32[576,128]{1,0:T(8,128)S(1)}, u32[]{:S(2)}, u32[]{:S(2)}) %collective-permute-start.9) | collective-permute-done | bytes 294944 | tf_op jit(solution)/shard_map/ppermute | solution.py:327
  50.9 2.5 %shard_map.62 = (bf16[224,448]{1,0:T(8,128)(2,1)S(1)}, bf16[4,128,896]{2,1,0:T(8,128)(2,1)S(1)}, bf16[4,128,896]{2,1,0:T(8,128)(2,1)S(1)}) custom-call(s32[1792]{0:T(1024)S(1)} %copy-done, f32[576,128]{1,0:T(8,128)S(1)} %get-tuple-element.41.refs_0_, f32[576,128]{1,0:T(8,128)S(1)} %collective-permute-done.8.refs_1_, ...), custom_call_target="tpu_custom_call" | custom-call | flops 1056964608 | bytes 3222528 | tf_op jit(solution)/shard_map/pallas_call | solution.py:309
  55.0 2.9 %collective-permute-start.18 = (f32[128,256]{1,0:T(8,128)S(1)}, f32[128,256]{1,0:T(8,128)S(1)}, u32[]{:S(2)}, u32[]{:S(2)}) collective-permute-start(f32[128,256]{1,0:T(8,128)S(1)} %get-tuple-element.65), channel_id=1, source_target_pairs={{0,2},{1,3},{2,4},{3,5},{4,6},{5,7},{6,0},{7,1},{8,10},{9,11},{10,... | collective-permute-start | bytes 393224 | tf_op jit(solution)/shard_map/ppermute | solution.py:470
  57.9 1.6 %collective-permute-start.19 = (f32[128,256]{1,0:T(8,128)S(1)}, f32[128,256]{1,0:T(8,128)S(1)}, u32[]{:S(2)}, u32[]{:S(2)}) collective-permute-start(f32[128,256]{1,0:T(8,128)S(1)} %get-tuple-element.66), channel_id=1, source_target_pairs={{0,4},{1,5},{2,6},{3,7},{4,0},{5,1},{6,2},{7,3},{8,12},{9,13},{10,... | collective-permute-start | bytes 393224 | tf_op jit(solution)/shard_map/ppermute | solution.py:470
  60.2 1.7 %collective-permute-done.17.other_ref = f32[224,256]{1,0:T(8,128)S(1)} collective-permute-done((f32[224,256]{1,0:T(8,128)S(1)}, f32[224,256]{1,0:T(8,128)S(1)}, u32[]{:S(2)}, u32[]{:S(2)}) %collective-permute-start.17) | collective-permute-done | bytes 229408 | tf_op jit(solution)/shard_map/ppermute | solution.py:320
  63.2 4.3 %collective-permute-done.19 = f32[128,256]{1,0:T(8,128)S(1)} collective-permute-done((f32[128,256]{1,0:T(8,128)S(1)}, f32[128,256]{1,0:T(8,128)S(1)}, u32[]{:S(2)}, u32[]{:S(2)}) %collective-permute-start.19) | collective-permute-done | bytes 131104 | tf_op jit(solution)/shard_map/ppermute | solution.py:470
  (34 shorter events, 9.8 us)
Async XLA Ops:
  0.6 9.1 %collective-permute-start = (f32[224,256]{1,0:T(8,128)}, f32[224,256]{1,0:T(8,128)S(1)}, u32[]{:S(2)}, u32[]{:S(2)}) collective-permute-start(f32[224,256]{1,0:T(8,128)} %refs_0_.1), channel_id=1, source_target_pairs={{1,0},{0,2},{2,4},{4,6},{6,7},{7,5},{5,3},{3,1},{9,8},{8,10},{10,1... | collective-permute-start | bytes 688136 | tf_op jit(solution)/shard_map/ppermute | solution.py:346
  3.7 7.3 %collective-permute-start.1 = (f32[224,256]{1,0:T(8,128)}, f32[224,256]{1,0:T(8,128)S(1)}, u32[]{:S(2)}, u32[]{:S(2)}) collective-permute-start(f32[224,256]{1,0:T(8,128)} %refs_0_.1), channel_id=1, source_target_pairs={{0,1},{2,0},{4,2},{6,4},{7,6},{5,7},{3,5},{1,3},{8,9},{10,8},{12,1... | collective-permute-start | bytes 688136 | tf_op jit(solution)/shard_map/ppermute | solution.py:346
  3.7 0.7 %copy-start = (s32[1792]{0:T(1024)S(1)}, s32[1792]{0:T(1024)}, u32[]{:S(2)}) copy-start(s32[1792]{0:T(1024)} %structure_ref.7) | copy-start | bytes 21508
  4.4 27.1 %copy-start.1 = (f32[224,256]{1,0:T(8,128)S(1)}, f32[224,256]{1,0:T(8,128)}, u32[]{:S(2)}) copy-start(f32[224,256]{1,0:T(8,128)} %refs_0_.1) | copy-start | bytes 688132
  7.7 26.9 %collective-permute-start.7 = (f32[2016,128]{1,0:T(8,128)S(1)}, f32[2016,128]{1,0:T(8,128)S(1)}, u32[]{:S(2)}, u32[]{:S(2)}) collective-permute-start(f32[2016,128]{1,0:T(8,128)S(1)} %shard_map.60.refs_8_), channel_id=1, source_target_pairs={{0,16},{8,24},{16,0},{24,8},{1,17},{9,25},{17,1},{25,9},{2,18},{10... | collective-permute-start | bytes 3096584 | tf_op jit(solution)/shard_map/ppermute | solution.py:408
  11.0 6.2 %collective-permute-start.2 = (f32[224,256]{1,0:T(8,128)S(1)}, f32[224,256]{1,0:T(8,128)S(1)}, u32[]{:S(2)}, u32[]{:S(2)}) collective-permute-start(f32[224,256]{1,0:T(8,128)S(1)} %collective-permute-done.refs_1_), channel_id=1, source_target_pairs={{1,0},{0,2},{2,4},{4,6},{6,7},{7,5},{5,3},{3,1},{9,8},{8,10},{10,1... | collective-permute-start | bytes 688136 | tf_op jit(solution)/shard_map/ppermute | solution.py:346
  17.1 6.5 %collective-permute-start.4 = (f32[224,256]{1,0:T(8,128)S(1)}, f32[224,256]{1,0:T(8,128)S(1)}, u32[]{:S(2)}, u32[]{:S(2)}) collective-permute-start(f32[224,256]{1,0:T(8,128)S(1)} %collective-permute-done.2.refs_3_), channel_id=1, source_target_pairs={{1,0},{0,2},{2,4},{4,6},{6,7},{7,5},{5,3},{3,1},{9,8},{8,10},{10,1... | collective-permute-start | bytes 688136 | tf_op jit(solution)/shard_map/ppermute | solution.py:346
  18.7 6.8 %collective-permute-start.3 = (f32[224,256]{1,0:T(8,128)S(1)}, f32[224,256]{1,0:T(8,128)S(1)}, u32[]{:S(2)}, u32[]{:S(2)}) collective-permute-start(f32[224,256]{1,0:T(8,128)S(1)} %collective-permute-done.1.refs_2_), channel_id=1, source_target_pairs={{0,1},{2,0},{4,2},{6,4},{7,6},{5,7},{3,5},{1,3},{8,9},{10,8},{12,1... | collective-permute-start | bytes 688136 | tf_op jit(solution)/shard_map/ppermute | solution.py:346
  23.6 6.0 %collective-permute-start.6 = (f32[224,256]{1,0:T(8,128)S(1)}, f32[224,256]{1,0:T(8,128)S(1)}, u32[]{:S(2)}, u32[]{:S(2)}) collective-permute-start(f32[224,256]{1,0:T(8,128)S(1)} %collective-permute-done.4.refs_5_), channel_id=1, source_target_pairs={{1,0},{0,2},{2,4},{4,6},{6,7},{7,5},{5,3},{3,1},{9,8},{8,10},{10,1... | collective-permute-start | bytes 688136 | tf_op jit(solution)/shard_map/ppermute | solution.py:350
  25.5 6.0 %collective-permute-start.5 = (f32[224,256]{1,0:T(8,128)S(1)}, f32[224,256]{1,0:T(8,128)S(1)}, u32[]{:S(2)}, u32[]{:S(2)}) collective-permute-start(f32[224,256]{1,0:T(8,128)S(1)} %collective-permute-done.3.refs_4_), channel_id=1, source_target_pairs={{0,1},{2,0},{4,2},{6,4},{7,6},{5,7},{3,5},{1,3},{8,9},{10,8},{12,1... | collective-permute-start | bytes 688136 | tf_op jit(solution)/shard_map/ppermute | solution.py:346
  25.9 11.0 %collective-permute-start.11 = (f32[2016,128]{1,0:T(8,128)S(1)}, f32[2016,128]{1,0:T(8,128)S(1)}, u32[]{:S(2)}, u32[]{:S(2)}) collective-permute-start(f32[2016,128]{1,0:T(8,128)S(1)} %shard_map.60.refs_8_), channel_id=1, source_target_pairs={{0,8},{8,0},{16,24},{24,16},{1,9},{9,1},{17,25},{25,17},{2,10},{10... | collective-permute-start | bytes 3096584 | tf_op jit(solution)/shard_map/ppermute | solution.py:320
  34.7 3.5 %collective-permute-start.12 = (f32[2016,128]{1,0:T(8,128)S(1)}, f32[2016,128]{1,0:T(8,128)S(1)}, u32[]{:S(2)}, u32[]{:S(2)}) collective-permute-start(f32[2016,128]{1,0:T(8,128)S(1)} %collective-permute-done.7.refs_1_), channel_id=1, source_target_pairs={{0,8},{8,0},{16,24},{24,16},{1,9},{9,1},{17,25},{25,17},{2,10},{10... | collective-permute-start | bytes 3096584 | tf_op jit(solution)/shard_map/ppermute | solution.py:320
  34.7 3.4 %collective-permute-start.8 = (f32[576,128]{1,0:T(8,128)S(1)}, f32[576,128]{1,0:T(8,128)S(1)}, u32[]{:S(2)}, u32[]{:S(2)}) collective-permute-start(f32[576,128]{1,0:T(8,128)S(1)} %get-tuple-element.41.refs_0_), channel_id=1, source_target_pairs={{0,8},{8,0},{16,24},{24,16},{1,9},{9,1},{17,25},{25,17},{2,10},{10... | collective-permute-start | bytes 884744 | tf_op jit(solution)/shard_map/ppermute | solution.py:320
  35.2 9.0 %collective-permute-start.10 = (f32[576,128]{1,0:T(8,128)S(1)}, f32[576,128]{1,0:T(8,128)S(1)}, u32[]{:S(2)}, u32[]{:S(2)}) collective-permute-start(f32[576,128]{1,0:T(8,128)S(1)} %get-tuple-element.41.refs_0_), channel_id=1, source_target_pairs={{0,24},{8,16},{16,8},{24,0},{1,25},{9,17},{17,9},{25,1},{2,26},{10... | collective-permute-start | bytes 884744 | tf_op jit(solution)/shard_map/ppermute | solution.py:327
  36.4 14.4 %collective-permute-start.9 = (f32[576,128]{1,0:T(8,128)S(1)}, f32[576,128]{1,0:T(8,128)S(1)}, u32[]{:S(2)}, u32[]{:S(2)}) collective-permute-start(f32[576,128]{1,0:T(8,128)S(1)} %get-tuple-element.41.refs_0_), channel_id=1, source_target_pairs={{0,16},{8,24},{16,0},{24,8},{1,17},{9,25},{17,1},{25,9},{2,18},{10... | collective-permute-start | bytes 884744 | tf_op jit(solution)/shard_map/ppermute | solution.py:327
  39.9 13.6 %collective-permute-start.16 = (f32[448,256]{1,0:T(8,128)S(1)}, f32[448,256]{1,0:T(8,128)S(1)}, u32[]{:S(2)}, u32[]{:S(2)}) collective-permute-start(f32[448,256]{1,0:T(8,128)S(1)} %get-tuple-element.52.refs_0_.mine_ref), channel_id=1, source_target_pairs={{0,1},{1,0},{2,3},{3,2},{4,5},{5,4},{6,7},{7,6},{8,9},{9,8},{10,11... | collective-permute-start | bytes 1376264 | tf_op jit(solution)/shard_map/ppermute | solution.py:320
  40.4 13.0 %collective-permute-start.13 = (f32[112,256]{1,0:T(8,128)S(1)}, f32[112,256]{1,0:T(8,128)S(1)}, u32[]{:S(2)}, u32[]{:S(2)}) collective-permute-start(f32[112,256]{1,0:T(8,128)S(1)} %get-tuple-element.49), channel_id=1, source_target_pairs={{0,2},{1,3},{2,4},{3,5},{4,6},{5,7},{6,0},{7,1},{8,10},{9,11},{10,... | collective-permute-start | bytes 344072 | tf_op jit(solution)/shard_map/ppermute | solution.py:443
  41.6 11.8 %collective-permute-start.14 = (f32[112,256]{1,0:T(8,128)S(1)}, f32[112,256]{1,0:T(8,128)S(1)}, u32[]{:S(2)}, u32[]{:S(2)}) collective-permute-start(f32[112,256]{1,0:T(8,128)S(1)} %get-tuple-element.50), channel_id=1, source_target_pairs={{0,4},{1,5},{2,6},{3,7},{4,0},{5,1},{6,2},{7,3},{8,12},{9,13},{10,... | collective-permute-start | bytes 344072 | tf_op jit(solution)/shard_map/ppermute | solution.py:443
  44.3 9.1 %collective-permute-start.15 = (f32[112,256]{1,0:T(8,128)S(1)}, f32[112,256]{1,0:T(8,128)S(1)}, u32[]{:S(2)}, u32[]{:S(2)}) collective-permute-start(f32[112,256]{1,0:T(8,128)S(1)} %get-tuple-element.51), channel_id=1, source_target_pairs={{0,6},{1,7},{2,0},{3,1},{4,2},{5,3},{6,4},{7,5},{8,14},{9,15},{10,... | collective-permute-start | bytes 344072 | tf_op jit(solution)/shard_map/ppermute | solution.py:443
  53.5 14.1 %copy-start.2 = (f32[128,256]{1,0:T(8,128)S(1)}, f32[128,256]{1,0:T(8,128)}, u32[]{:S(2)}) copy-start(f32[128,256]{1,0:T(8,128)} %param.7) | copy-start | bytes 393220
  54.5 7.4 %collective-permute-start.17 = (f32[224,256]{1,0:T(8,128)S(1)}, f32[224,256]{1,0:T(8,128)S(1)}, u32[]{:S(2)}, u32[]{:S(2)}) collective-permute-start(f32[224,256]{1,0:T(8,128)S(1)} %get-tuple-element.62), channel_id=1, source_target_pairs={{0,1},{1,0},{2,3},{3,2},{4,5},{5,4},{6,7},{7,6},{8,9},{9,8},{10,11... | collective-permute-start | bytes 688136 | tf_op jit(solution)/shard_map/ppermute | solution.py:320
  55.0 8.2 %collective-permute-start.18 = (f32[128,256]{1,0:T(8,128)S(1)}, f32[128,256]{1,0:T(8,128)S(1)}, u32[]{:S(2)}, u32[]{:S(2)}) collective-permute-start(f32[128,256]{1,0:T(8,128)S(1)} %get-tuple-element.65), channel_id=1, source_target_pairs={{0,2},{1,3},{2,4},{3,5},{4,6},{5,7},{6,0},{7,1},{8,10},{9,11},{10,... | collective-permute-start | bytes 393224 | tf_op jit(solution)/shard_map/ppermute | solution.py:470
  57.9 9.7 %collective-permute-start.19 = (f32[128,256]{1,0:T(8,128)S(1)}, f32[128,256]{1,0:T(8,128)S(1)}, u32[]{:S(2)}, u32[]{:S(2)}) collective-permute-start(f32[128,256]{1,0:T(8,128)S(1)} %get-tuple-element.66), channel_id=1, source_target_pairs={{0,4},{1,5},{2,6},{3,7},{4,0},{5,1},{6,2},{7,3},{8,12},{9,13},{10,... | collective-permute-start | bytes 393224 | tf_op jit(solution)/shard_map/ppermute | solution.py:470
  59.4 8.1 %collective-permute-start.20 = (f32[128,256]{1,0:T(8,128)S(1)}, f32[128,256]{1,0:T(8,128)S(1)}, u32[]{:S(2)}, u32[]{:S(2)}) collective-permute-start(f32[128,256]{1,0:T(8,128)S(1)} %get-tuple-element.67), channel_id=1, source_target_pairs={{0,6},{1,7},{2,0},{3,1},{4,2},{5,3},{6,4},{7,5},{8,14},{9,15},{10,... | collective-permute-start | bytes 393224 | tf_op jit(solution)/shard_map/ppermute | solution.py:470

commit v8 on v7

--- a/solution.py
+++ b/solution.py
@@ -107,56 +107,48 @@
     return dot(left, jnp.concatenate([uh, ul, uh], axis=0))
 
 
-def prepare_kernel(direct, nc, owners, structure_ref, *refs):
-    uh_ref, ul_ref, part_ref, own_ref, us_ref = refs[-5:]
-    nr, _, w = uh_ref.shape
-    n_u = nc if direct else 1
-    u_refs, first_refs = refs[:n_u], refs[n_u:-5]
-    n = structure_ref.shape[0]
-    m = n // nc
+def place_rows(us_ref, u, owner):
+    m, w = u.shape
+    nc = (us_ref.shape[1] - CAP - 8) // m
+    if w % LANES:
+        u = jnp.concatenate([u, jnp.zeros((m, LANES - w % LANES), jnp.float32)], axis=1)
+    for i in range(us_ref.shape[0]):
+        us_ref[i, pl.ds(owner, m, stride=nc), :] = u[:, LANES * i : LANES * (i + 1)]
+
+
+def rows_of(us_ref, names, owner, width, lane_blocks):
+    start = count(names < owner * width)
+    base = pl.multiple_of((start // 8) * 8, 8)
+    size = CAP + 8
+    lanes = [pltpu.roll(us_ref[k, pl.ds(base, size), :], size - (start - base), 0)[:CAP] for k in lane_blocks]
+    return jnp.concatenate(lanes, axis=1)
+
+
+def cut(us_ref, names, owner, width, w):
+    u = rows_of(us_ref, names, owner, width, range(us_ref.shape[0]))[:, :w]
+    return split(jnp.concatenate([u, jnp.zeros((WIDE - CAP, w), jnp.float32)], axis=0))
+
+
+def place_kernel(direct, nc, *refs):
+    u_refs, us_ref = refs[:-1], refs[-1]
+    end = us_ref.shape[1] - CAP - 8
+    us_ref[:, end:, :] = jnp.zeros((us_ref.shape[0], CAP + 8, LANES), jnp.float32)
+    if direct:
+        for owner, u_ref in zip(ring_owners(nc, lax.axis_index("pcol")), u_refs):
+            place_rows(us_ref, u_ref[...], owner)
+    else:
+        pl.loop(0, nc)(lambda k: place_rows(us_ref, u_refs[0][k], k))
+
+
+def last_kernel(nc, width, structure_ref, before_ref, *refs):
+    us_ref, own_ref = refs[-2:]
     c = lax.axis_index("pcol")
-    r = lax.axis_index("prow")
-    rows = part_ref.shape[0]
+    us_ref[...] = before_ref[...]
+    if len(refs) > 2:
+        place_rows(us_ref, refs[0][...], ring_owners(nc, c)[-1])
     names = structure_ref[...].reshape(1, -1)
-
-    def place(owner, u):
-        if w % LANES:
-            u = jnp.concatenate([u, jnp.zeros((m, LANES - w % LANES), jnp.float32)], axis=1)
-        for i in range(us_ref.shape[0]):
-            us_ref[i, pl.ds(owner, u.shape[0], stride=nc), :] = u[:, LANES * i : LANES * (i + 1)]
-
-    if direct:
-        for owner, u_ref in zip(ring_owners(nc, c), u_refs):
-            place(owner, u_ref[...])
-    else:
-        pl.loop(0, nc)(lambda k: place(k, u_refs[0][k]))
-    us_ref[:, n:, :] = jnp.zeros((us_ref.shape[0], us_ref.shape[1] - n, LANES), jnp.float32)
-
-    width = rows * 2
-
-    def rows_of(owner, lane_blocks):
-        start = count(names < owner * width)
-        base = pl.multiple_of((start // 8) * 8, 8)
-        size = CAP + 8
-        lanes = [pltpu.roll(us_ref[k, pl.ds(base, size), :], size - (start - base), 0)[:CAP] for k in lane_blocks]
-        return jnp.concatenate(lanes, axis=1)
-
-    def cut(owner):
-        u = rows_of(owner, range(us_ref.shape[0]))[:, :w]
-        u = jnp.concatenate([u, jnp.zeros((WIDE - CAP, w), jnp.float32)], axis=0)
-        uh_ref[owner], ul_ref[owner] = split(u)
-
-    own_ref[...] = rows_of(c // 2, [c & 1]) if direct else rows_of(c // 2, [0])[:, :w]
-
-    if direct:
-        for b in range(nr):
-            cut(b)
-    else:
-        pl.loop(0, nr)(cut)
-    image = jnp.zeros((rows, w), jnp.float32)
-    for owner, block_ref in zip(owners(r), first_refs):
-        image = image + block_term(block_ref, uh_ref[owner], ul_ref[owner], rows)
-    part_ref[...] = image
+    w = own_ref.shape[1]
+    own_ref[...] = rows_of(us_ref, names, c // 2, width, [c & 1] if len(refs) > 2 else [0])[:, :w]
 
 
 def row_order(names, c, rows, nc, slots, direct):
@@ -184,23 +176,36 @@
     to_ref[...] = row_order(names, lax.axis_index("pcol"), rows, nc, slots, direct)
 
 
-def near_kernel(owners, uh_ref, ul_ref, part_ref, *refs):
-    block_refs, image_ref = refs[:-1], refs[-1]
+def near_kernel(owners, rest, structure_ref, us_ref, *refs):
+    block_refs, (image_ref, uh_ref, ul_ref) = refs[:-3], refs[-3:]
+    rows, w = image_ref.shape
+    width = rows * 2
+    names = structure_ref[...].reshape(1, -1)
+    r = lax.axis_index("prow")
+    image = jnp.zeros((rows, w), jnp.float32)
+    for owner, block_ref in zip(owners(r), block_refs):
+        image = image + block_term(block_ref, *cut(us_ref, names, owner, width, w), rows)
+    image_ref[...] = image
+    if rest is None:
+
+        @pl.loop(0, uh_ref.shape[0])
+        def _(k):
+            uh_ref[k], ul_ref[k] = cut(us_ref, names, k, width, w)
+
+    else:
+        for k, owner in enumerate(rest(r)):
+            uh_ref[k], ul_ref[k] = cut(us_ref, names, owner, width, w)
+
+
+def image_kernel(direct, uh_ref, ul_ref, part_ref, to_ref, *refs):
+    n_in = uh_ref.shape[0] if direct else 1
+    block_refs, out_refs = refs[:n_in], refs[n_in:]
+    n_out = len(out_refs)
     rows = part_ref.shape[0]
     image = part_ref[...]
-    for owner, block_ref in zip(owners(lax.axis_index("prow")), block_refs):
-        image = image + block_term(block_ref, uh_ref[owner], ul_ref[owner], rows)
-    image_ref[...] = image
-
-
-def image_kernel(direct, owners, uh_ref, ul_ref, part_ref, to_ref, *refs):
-    n_out = len(refs) - (1 if not direct else len(owners(0)))
-    block_refs, out_refs = refs[:-n_out], refs[-n_out:]
-    rows = part_ref.shape[0]
-    image = part_ref[...]
-    if direct:
-        for owner, block_ref in zip(owners(lax.axis_index("prow")), block_refs):
-            image = image + block_term(block_ref, uh_ref[owner], ul_ref[owner], rows)
+    if direct:
+        for k, block_ref in enumerate(block_refs):
+            image = image + block_term(block_ref, uh_ref[k], ul_ref[k], rows)
     else:
         stack = block_refs[0]
         add = lambda b, v: v + block_term(stack.at[b], uh_ref[b], ul_ref[b], rows)
@@ -385,48 +390,50 @@
         flops=4 * rows * cols * WIDE,
         vmem=52,
     )
-    near = [chosen] if direct else []
     to = call(functools.partial(order_kernel, direct, slots), bf16(nc * slots, rows), names)
     if direct:
         u_all, to = ring_gather(u_panel, nc, to)
     else:
         u_all = [lax.all_gather(u_panel, "pcol")]
     term = 6 * rows * WIDE * w
-    uh, ul, image, own = call(
-        functools.partial(prepare_kernel, direct, nc, lambda r: owners(r)[:1]),
-        [bf16(nr, WIDE, w), bf16(nr, WIDE, w), f32(rows, w), f32(CAP, wd if direct else w)],
+    placed = f32(-(-w // LANES), n + CAP + 8, LANES)
+    early, late = (u_all[:-1], u_all[-1:]) if direct else (u_all, [])
+    before = call(functools.partial(place_kernel, direct, nc), placed, *early, flops=8 * term)
+    us, own = call(
+        functools.partial(last_kernel, nc, cols),
+        [placed, f32(CAP, wd if direct else w)],
         names,
-        *u_all,
-        *near,
-        scratch_shapes=[pltpu.VMEM((-(-w // LANES), n + CAP + 8, LANES), jnp.float32)],
-        flops=15 * term // 2,
-    )
-    beside, later = [], []
-    if direct:
-        beside.append(swap(chosen, "prow", nr))
+        before,
+        *late,
+        flops=term,
+    )
+    near, later = [], []
+    if direct:
+        near = [chosen, swap(chosen, "prow", nr)]
         for t in range(1, nr // 2):
             far = lax.ppermute(chosen, "prow", [(k, (k + 2 * t) % nr) for k in range(nr)])
-            far, _ = lax.optimization_barrier((far, image))
-            beside.append(far)
+            far, _ = lax.optimization_barrier((far, own))
+            near.append(far)
             later.append(swap(far, "prow", nr))
     else:
         later = [lax.all_gather(chosen, "prow")]
-    if direct:
-        image = call(
-            functools.partial(near_kernel, lambda r: owners(r)[1:2] + owners(r)[2::2]),
-            f32(rows, w),
-            uh,
-            ul,
-            image,
-            *beside,
-            flops=term,
-        )
-    if direct:
-        own, _ = lax.optimization_barrier((own, beside[1]))
+    halves = bf16(len(later) if direct else nr, WIDE, w)
+    image, uh, ul = call(
+        functools.partial(
+            near_kernel, lambda r: owners(r)[:2] + owners(r)[2::2], (lambda r: owners(r)[3::2]) if direct else None
+        ),
+        [f32(rows, w), halves, halves],
+        names,
+        us,
+        *near,
+        flops=3 * term,
+    )
+    if direct:
+        own, _ = lax.optimization_barrier((own, near[2]))
         owned = spread(own, nr)
         owned[1], to = lax.optimization_barrier((owned[1], to))
     sent = call(
-        functools.partial(image_kernel, direct, lambda r: owners(r)[3::2]),
+        functools.partial(image_kernel, direct),
         [f32(nc * slots, w)] + [f32(2 * slots, w)] * ((nz - 1) * direct),
         uh,
         ul,

time: 68.9 us -> 68.1 us (0.988)
  waiting for transfers between devices: 26.4 us -> 24.4 us
  starting transfers between devices: 24.6 us -> 26.4 us
    ppermute x2, waiting for transfers between devices: 5.09 us -> 2.1 us  [spread(): lax.ppermute(v, 'prow', [(k, (k + 2 * t) % size ^ flip) for k in range(si...]
    ppermute x1, waiting for transfers between devices: 0.01 us -> 2.37 us  [per_device(): lax.ppermute(chosen, 'prow', [(k, (k + 2 * t) % nr) for k in range(nr)])]
    ppermute x3, waiting for transfers between devices: 3.36 us -> 1.23 us  [ring_gather(): lax.ppermute(down, 'pcol', back)]
    ppermute x3, waiting for transfers between devices: 0.01 us -> 1.76 us  [per_device(): lax.ppermute(sent[t], 'pcol', [(k, (k + 2 * t) % nc) for k in range(nc)])]
    ppermute x5, starting transfers between devices: 1.6 us -> 2.91 us  [swap(): return lax.ppermute(v, axis, [(k, k ^ 1) for k in range(size)])]
    ppermute x4, waiting for transfers between devices: 11.7 us -> 11 us  [ring_gather(): lax.ppermute(up, 'pcol', pairs)]
    pallas_call x9 -> x10, Pallas kernels: 15 us -> 14.5 us  [call(): pl.pallas_call(kernel, out_shape=out_shape, out_specs=[VMEM] * len(out_sh...]
  transfers between devices with their start and end apart: 21 -> 21, of which waited for: 11 -> 10; matrix products, arithmetic and copies ran while one was open for 0% -> 0% of each run, Pallas kernels for 21% -> 20%
where the time goes in v8:
time: 68.1 us; the launch traced here: 67.5 us
  starting transfers between devices  26.4 us (39%)
  waiting for transfers between devices  24.4 us (36%)
  Pallas kernels  14.5 us (21%)
  between operations  0.75 us (1%)
  local copies, waits for them, and re-layouts  0.71 us (1%)
  other arithmetic  0.7 us (1%)
    pallas_call x10, Pallas kernels, call(): pl.pallas_call(kernel, out_shape=out_shape, out_specs=[VMEM] * len(out_sh...  14.5 us
    ppermute x4, waiting for transfers between devices, ring_gather(): lax.ppermute(up, 'pcol', pairs)  11 us
    ppermute x4, starting transfers between devices, ring_gather(): lax.ppermute(up, 'pcol', pairs)  7.81 us
    ppermute x3, starting transfers between devices, per_device(): lax.ppermute(sent[t], 'pcol', [(k, (k + 2 * t) % nc) for k in range(nc)])  5.52 us
    ppermute x3, starting transfers between devices, per_device(): lax.ppermute(terms[t], 'pcol', [(k, (k + 2 * t) % nc) for k in range(nc)])  5.52 us
    ppermute x3, waiting for transfers between devices, per_device(): lax.ppermute(terms[t], 'pcol', [(k, (k + 2 * t) % nc) for k in range(nc)])  4.67 us
    ppermute x5, starting transfers between devices, swap(): return lax.ppermute(v, axis, [(k, k ^ 1) for k in range(size)])  2.91 us
    ppermute x1, waiting for transfers between devices, per_device(): lax.ppermute(chosen, 'prow', [(k, (k + 2 * t) % nr) for k in range(nr)])  2.37 us
  transfers between devices with their start and end apart: 21, of which 10 were waited for; matrix products, arithmetic and copies ran while one was open for 0% of the time, Pallas kernels for 20%

profile of v8, /device:TPU:0, one launch (start us, length us, event | category | flops | bytes accessed | tf_op | source)
XLA Modules:
  0.0 67.5 jit_solution(8718994219028993533)
XLA Ops:
  0.6 3.1 %collective-permute-start = (f32[224,256]{1,0:T(8,128)}, f32[224,256]{1,0:T(8,128)S(1)}, u32[]{:S(2)}, u32[]{:S(2)}) collective-permute-start(f32[224,256]{1,0:T(8,128)} %refs_0_.1), channel_id=1, source_target_pairs={{1,0},{0,2},{2,4},{4,6},{6,7},{7,5},{5,3},{3,1},{9,8},{8,10},{10,1... | collective-permute-start | bytes 688136 | tf_op jit(solution)/shard_map/ppermute | solution.py:351
  4.4 3.3 %shard_map.62.refs_0_ = f32[2016,128]{1,0:T(8,128)S(1)} custom-call(s32[1792]{0:T(1024)S(1)} %copy-done, f32[448,896]{1,0:T(8,128)} %sigma_ref.1), custom_call_target="tpu_custom_call" | custom-call | flops 1027604480 | bytes 2644992 | tf_op jit(solution)/shard_map/pallas_call | solution.py:314
  7.7 2.0 %collective-permute-start.7 = (f32[2016,128]{1,0:T(8,128)S(1)}, f32[2016,128]{1,0:T(8,128)S(1)}, u32[]{:S(2)}, u32[]{:S(2)}) collective-permute-start(f32[2016,128]{1,0:T(8,128)S(1)} %shard_map.62.refs_0_), channel_id=1, source_target_pairs={{0,16},{8,24},{16,0},{24,8},{1,17},{9,25},{17,1},{25,9},{2,18},{10... | collective-permute-start | bytes 3096584 | tf_op jit(solution)/shard_map/ppermute | solution.py:414
  9.8 1.2 %collective-permute-done.1.refs_2_ = f32[224,256]{1,0:T(8,128)S(1)} collective-permute-done((f32[224,256]{1,0:T(8,128)}, f32[224,256]{1,0:T(8,128)S(1)}, u32[]{:S(2)}, u32[]{:S(2)}) %collective-permute-start.1) | collective-permute-done | bytes 229408 | tf_op jit(solution)/shard_map/ppermute | solution.py:351
  11.0 1.6 %collective-permute-start.2 = (f32[224,256]{1,0:T(8,128)S(1)}, f32[224,256]{1,0:T(8,128)S(1)}, u32[]{:S(2)}, u32[]{:S(2)}) collective-permute-start(f32[224,256]{1,0:T(8,128)S(1)} %collective-permute-done.refs_1_), channel_id=1, source_target_pairs={{1,0},{0,2},{2,4},{4,6},{6,7},{7,5},{5,3},{3,1},{9,8},{8,10},{10,1... | collective-permute-start | bytes 688136 | tf_op jit(solution)/shard_map/ppermute | solution.py:351
  13.0 4.1 %collective-permute-done.2.refs_3_ = f32[224,256]{1,0:T(8,128)S(1)} collective-permute-done((f32[224,256]{1,0:T(8,128)S(1)}, f32[224,256]{1,0:T(8,128)S(1)}, u32[]{:S(2)}, u32[]{:S(2)}) %collective-permute-start.2) | collective-permute-done | bytes 229408 | tf_op jit(solution)/shard_map/ppermute | solution.py:351
  17.1 1.6 %collective-permute-start.4 = (f32[224,256]{1,0:T(8,128)S(1)}, f32[224,256]{1,0:T(8,128)S(1)}, u32[]{:S(2)}, u32[]{:S(2)}) collective-permute-start(f32[224,256]{1,0:T(8,128)S(1)} %collective-permute-done.2.refs_3_), channel_id=1, source_target_pairs={{1,0},{0,2},{2,4},{4,6},{6,7},{7,5},{5,3},{3,1},{9,8},{8,10},{10,1... | collective-permute-start | bytes 688136 | tf_op jit(solution)/shard_map/ppermute | solution.py:351
  20.2 3.0 %collective-permute-done.4.refs_5_ = f32[224,256]{1,0:T(8,128)S(1)} collective-permute-done((f32[224,256]{1,0:T(8,128)S(1)}, f32[224,256]{1,0:T(8,128)S(1)}, u32[]{:S(2)}, u32[]{:S(2)}) %collective-permute-start.4) | collective-permute-done | bytes 229408 | tf_op jit(solution)/shard_map/ppermute | solution.py:351
  23.2 1.6 %collective-permute-start.6 = (f32[224,256]{1,0:T(8,128)S(1)}, f32[224,256]{1,0:T(8,128)S(1)}, u32[]{:S(2)}, u32[]{:S(2)}) collective-permute-start(f32[224,256]{1,0:T(8,128)S(1)} %collective-permute-done.4.refs_5_), channel_id=1, source_target_pairs={{1,0},{0,2},{2,4},{4,6},{6,7},{7,5},{5,3},{3,1},{9,8},{8,10},{10,1... | collective-permute-start | bytes 688136 | tf_op jit(solution)/shard_map/ppermute | solution.py:355
  25.2 3.9 %collective-permute-done.6.refs_0_ = f32[224,256]{1,0:T(8,128)S(1)} collective-permute-done((f32[224,256]{1,0:T(8,128)S(1)}, f32[224,256]{1,0:T(8,128)S(1)}, u32[]{:S(2)}, u32[]{:S(2)}) %collective-permute-start.6) | collective-permute-done | bytes 229408 | tf_op jit(solution)/shard_map/ppermute | solution.py:355
  29.7 2.4 %collective-permute-done.7.refs_2_ = f32[2016,128]{1,0:T(8,128)S(1)} collective-permute-done((f32[2016,128]{1,0:T(8,128)S(1)}, f32[2016,128]{1,0:T(8,128)S(1)}, u32[]{:S(2)}, u32[]{:S(2)}) %collective-permute-start.7) | collective-permute-done | bytes 1032224 | tf_op jit(solution)/shard_map/ppermute | solution.py:414
  32.6 1.3 %collective-permute-start.10 = (f32[576,128]{1,0:T(8,128)S(1)}, f32[576,128]{1,0:T(8,128)S(1)}, u32[]{:S(2)}, u32[]{:S(2)}) collective-permute-start(f32[576,128]{1,0:T(8,128)S(1)} %get-tuple-element.41.refs_0_), channel_id=1, source_target_pairs={{0,24},{8,16},{16,8},{24,0},{1,25},{9,17},{17,9},{25,1},{2,26},{10... | collective-permute-start | bytes 884744 | tf_op jit(solution)/shard_map/ppermute | solution.py:332
  34.3 2.8 %shard_map.64 = (f32[448,256]{1,0:T(8,128)S(1)}, bf16[1,640,256]{2,1,0:T(8,128)(2,1)S(1)}, bf16[1,640,256]{2,1,0:T(8,128)(2,1)S(1)}) custom-call(s32[1792]{0:T(1024)S(1)} %copy-done, f32[2,2376,128]{2,1,0:T(8,128)S(1)} %get-tuple-element.45.us_ref, f32[2016,128]{1,0:T(8,128)S(1)} %shard_map.62.refs_0_, f32[2016,128]{1,0:T(8,128)S(1)} %collective-permute-done.11.refs_1_, ...), custom_call_target="tpu_custom_call" | custom-call | flops 1321205760 | bytes 6650880 | tf_op jit(solution)/shard_map/pallas_call | solution.py:314
  37.2 1.8 %shard_map.65 = (f32[448,256]{1,0:T(8,128)S(1)}, f32[112,256]{1,0:T(8,128)S(1)}, f32[112,256]{1,0:T(8,128)S(1)}, f32[112,256]{1,0:T(8,128)S(1)}) custom-call(bf16[1,640,256]{2,1,0:T(8,128)(2,1)S(1)} %get-tuple-element.46.uh_ref, bf16[1,640,256]{2,1,0:T(8,128)(2,1)S(1)} %get-tuple-element.47.ul_ref, f32[448,256]{1,0:T(8,128)S(1)} %get-tuple-element.48.part_ref, ...), custom_call_target="tpu_custom_call" | custom-call | flops 440401920 | bytes 3350528 | tf_op jit(solution)/shard_map/pallas_call | solution.py:314
  38.9 1.6 %collective-permute-start.16 = (f32[448,256]{1,0:T(8,128)S(1)}, f32[448,256]{1,0:T(8,128)S(1)}, u32[]{:S(2)}, u32[]{:S(2)}) collective-permute-start(f32[448,256]{1,0:T(8,128)S(1)} %get-tuple-element.54.refs_0_.mine_ref), channel_id=1, source_target_pairs={{0,1},{1,0},{2,3},{3,2},{4,5},{5,4},{6,7},{7,6},{8,9},{9,8},{10,11... | collective-permute-start | bytes 1376264 | tf_op jit(solution)/shard_map/ppermute | solution.py:325
  40.6 1.6 %collective-permute-start.13 = (f32[112,256]{1,0:T(8,128)S(1)}, f32[112,256]{1,0:T(8,128)S(1)}, u32[]{:S(2)}, u32[]{:S(2)}) collective-permute-start(f32[112,256]{1,0:T(8,128)S(1)} %get-tuple-element.51), channel_id=1, source_target_pairs={{0,2},{1,3},{2,4},{3,5},{4,6},{5,7},{6,0},{7,1},{8,10},{9,11},{10,... | collective-permute-start | bytes 344072 | tf_op jit(solution)/shard_map/ppermute | solution.py:450
  42.1 2.6 %collective-permute-start.14 = (f32[112,256]{1,0:T(8,128)S(1)}, f32[112,256]{1,0:T(8,128)S(1)}, u32[]{:S(2)}, u32[]{:S(2)}) collective-permute-start(f32[112,256]{1,0:T(8,128)S(1)} %get-tuple-element.52), channel_id=1, source_target_pairs={{0,4},{1,5},{2,6},{3,7},{4,0},{5,1},{6,2},{7,3},{8,12},{9,13},{10,... | collective-permute-start | bytes 344072 | tf_op jit(solution)/shard_map/ppermute | solution.py:450
  44.7 1.3 %collective-permute-start.15 = (f32[112,256]{1,0:T(8,128)S(1)}, f32[112,256]{1,0:T(8,128)S(1)}, u32[]{:S(2)}, u32[]{:S(2)}) collective-permute-start(f32[112,256]{1,0:T(8,128)S(1)} %get-tuple-element.53), channel_id=1, source_target_pairs={{0,6},{1,7},{2,0},{3,1},{4,2},{5,3},{6,4},{7,5},{8,14},{9,15},{10,... | collective-permute-start | bytes 344072 | tf_op jit(solution)/shard_map/ppermute | solution.py:450
  46.1 2.1 %collective-permute-done.9.refs_2_ = f32[576,128]{1,0:T(8,128)S(1)} collective-permute-done((f32[576,128]{1,0:T(8,128)S(1)}, f32[576,128]{1,0:T(8,128)S(1)}, u32[]{:S(2)}, u32[]{:S(2)}) %collective-permute-start.9) | collective-permute-done | bytes 294944 | tf_op jit(solution)/shard_map/ppermute | solution.py:332
  48.2 2.5 %shard_map.63 = (bf16[224,448]{1,0:T(8,128)(2,1)S(1)}, bf16[4,128,896]{2,1,0:T(8,128)(2,1)S(1)}, bf16[4,128,896]{2,1,0:T(8,128)(2,1)S(1)}) custom-call(s32[1792]{0:T(1024)S(1)} %copy-done, f32[576,128]{1,0:T(8,128)S(1)} %get-tuple-element.41.refs_0_, f32[576,128]{1,0:T(8,128)S(1)} %collective-permute-done.8.refs_1_, ...), custom_call_target="tpu_custom_call" | custom-call | flops 1056964608 | bytes 3222528 | tf_op jit(solution)/shard_map/pallas_call | solution.py:314
  50.7 1.8 %collective-permute-done.14.refs_2_ = f32[112,256]{1,0:T(8,128)S(1)} collective-permute-done((f32[112,256]{1,0:T(8,128)S(1)}, f32[112,256]{1,0:T(8,128)S(1)}, u32[]{:S(2)}, u32[]{:S(2)}) %collective-permute-start.14) | collective-permute-done | bytes 114720 | tf_op jit(solution)/shard_map/ppermute | solution.py:450
  54.3 2.7 %collective-permute-start.18 = (f32[128,256]{1,0:T(8,128)S(1)}, f32[128,256]{1,0:T(8,128)S(1)}, u32[]{:S(2)}, u32[]{:S(2)}) collective-permute-start(f32[128,256]{1,0:T(8,128)S(1)} %get-tuple-element.67), channel_id=1, source_target_pairs={{0,2},{1,3},{2,4},{3,5},{4,6},{5,7},{6,0},{7,1},{8,10},{9,11},{10,... | collective-permute-start | bytes 393224 | tf_op jit(solution)/shard_map/ppermute | solution.py:477
  57.1 1.6 %collective-permute-start.19 = (f32[128,256]{1,0:T(8,128)S(1)}, f32[128,256]{1,0:T(8,128)S(1)}, u32[]{:S(2)}, u32[]{:S(2)}) collective-permute-start(f32[128,256]{1,0:T(8,128)S(1)} %get-tuple-element.68), channel_id=1, source_target_pairs={{0,4},{1,5},{2,6},{3,7},{4,0},{5,1},{6,2},{7,3},{8,12},{9,13},{10,... | collective-permute-start | bytes 393224 | tf_op jit(solution)/shard_map/ppermute | solution.py:477
  62.5 4.3 %collective-permute-done.19 = f32[128,256]{1,0:T(8,128)S(1)} collective-permute-done((f32[128,256]{1,0:T(8,128)S(1)}, f32[128,256]{1,0:T(8,128)S(1)}, u32[]{:S(2)}, u32[]{:S(2)}) %collective-permute-start.19) | collective-permute-done | bytes 131104 | tf_op jit(solution)/shard_map/ppermute | solution.py:477
  (35 shorter events, 10.9 us)
Async XLA Ops:
  0.6 9.1 %collective-permute-start = (f32[224,256]{1,0:T(8,128)}, f32[224,256]{1,0:T(8,128)S(1)}, u32[]{:S(2)}, u32[]{:S(2)}) collective-permute-start(f32[224,256]{1,0:T(8,128)} %refs_0_.1), channel_id=1, source_target_pairs={{1,0},{0,2},{2,4},{4,6},{6,7},{7,5},{5,3},{3,1},{9,8},{8,10},{10,1... | collective-permute-start | bytes 688136 | tf_op jit(solution)/shard_map/ppermute | solution.py:351
  3.7 7.3 %collective-permute-start.1 = (f32[224,256]{1,0:T(8,128)}, f32[224,256]{1,0:T(8,128)S(1)}, u32[]{:S(2)}, u32[]{:S(2)}) collective-permute-start(f32[224,256]{1,0:T(8,128)} %refs_0_.1), channel_id=1, source_target_pairs={{0,1},{2,0},{4,2},{6,4},{7,6},{5,7},{3,5},{1,3},{8,9},{10,8},{12,1... | collective-permute-start | bytes 688136 | tf_op jit(solution)/shard_map/ppermute | solution.py:351
  3.7 0.7 %copy-start = (s32[1792]{0:T(1024)S(1)}, s32[1792]{0:T(1024)}, u32[]{:S(2)}) copy-start(s32[1792]{0:T(1024)} %structure_ref.9) | copy-start | bytes 21508
  4.4 20.3 %copy-start.1 = (f32[224,256]{1,0:T(8,128)S(1)}, f32[224,256]{1,0:T(8,128)}, u32[]{:S(2)}) copy-start(f32[224,256]{1,0:T(8,128)} %refs_0_.1) | copy-start | bytes 688132
  7.7 24.3 %collective-permute-start.7 = (f32[2016,128]{1,0:T(8,128)S(1)}, f32[2016,128]{1,0:T(8,128)S(1)}, u32[]{:S(2)}, u32[]{:S(2)}) collective-permute-start(f32[2016,128]{1,0:T(8,128)S(1)} %shard_map.62.refs_0_), channel_id=1, source_target_pairs={{0,16},{8,24},{16,0},{24,8},{1,17},{9,25},{17,1},{25,9},{2,18},{10... | collective-permute-start | bytes 3096584 | tf_op jit(solution)/shard_map/ppermute | solution.py:414
  11.0 6.2 %collective-permute-start.2 = (f32[224,256]{1,0:T(8,128)S(1)}, f32[224,256]{1,0:T(8,128)S(1)}, u32[]{:S(2)}, u32[]{:S(2)}) collective-permute-start(f32[224,256]{1,0:T(8,128)S(1)} %collective-permute-done.refs_1_), channel_id=1, source_target_pairs={{1,0},{0,2},{2,4},{4,6},{6,7},{7,5},{5,3},{3,1},{9,8},{8,10},{10,1... | collective-permute-start | bytes 688136 | tf_op jit(solution)/shard_map/ppermute | solution.py:351
  12.6 6.2 %collective-permute-start.3 = (f32[224,256]{1,0:T(8,128)S(1)}, f32[224,256]{1,0:T(8,128)S(1)}, u32[]{:S(2)}, u32[]{:S(2)}) collective-permute-start(f32[224,256]{1,0:T(8,128)S(1)} %collective-permute-done.1.refs_2_), channel_id=1, source_target_pairs={{0,1},{2,0},{4,2},{6,4},{7,6},{5,7},{3,5},{1,3},{8,9},{10,8},{12,1... | collective-permute-start | bytes 688136 | tf_op jit(solution)/shard_map/ppermute | solution.py:351
  17.1 6.0 %collective-permute-start.4 = (f32[224,256]{1,0:T(8,128)S(1)}, f32[224,256]{1,0:T(8,128)S(1)}, u32[]{:S(2)}, u32[]{:S(2)}) collective-permute-start(f32[224,256]{1,0:T(8,128)S(1)} %collective-permute-done.2.refs_3_), channel_id=1, source_target_pairs={{1,0},{0,2},{2,4},{4,6},{6,7},{7,5},{5,3},{3,1},{9,8},{8,10},{10,1... | collective-permute-start | bytes 688136 | tf_op jit(solution)/shard_map/ppermute | solution.py:351
  18.7 6.0 %collective-permute-start.5 = (f32[224,256]{1,0:T(8,128)S(1)}, f32[224,256]{1,0:T(8,128)S(1)}, u32[]{:S(2)}, u32[]{:S(2)}) collective-permute-start(f32[224,256]{1,0:T(8,128)S(1)} %collective-permute-done.3.refs_4_), channel_id=1, source_target_pairs={{0,1},{2,0},{4,2},{6,4},{7,6},{5,7},{3,5},{1,3},{8,9},{10,8},{12,1... | collective-permute-start | bytes 688136 | tf_op jit(solution)/shard_map/ppermute | solution.py:351
  19.2 15.1 %collective-permute-start.11 = (f32[2016,128]{1,0:T(8,128)S(1)}, f32[2016,128]{1,0:T(8,128)S(1)}, u32[]{:S(2)}, u32[]{:S(2)}) collective-permute-start(f32[2016,128]{1,0:T(8,128)S(1)} %shard_map.62.refs_0_), channel_id=1, source_target_pairs={{0,8},{8,0},{16,24},{24,16},{1,9},{9,1},{17,25},{25,17},{2,10},{10... | collective-permute-start | bytes 3096584 | tf_op jit(solution)/shard_map/ppermute | solution.py:325
  23.2 6.0 %collective-permute-start.6 = (f32[224,256]{1,0:T(8,128)S(1)}, f32[224,256]{1,0:T(8,128)S(1)}, u32[]{:S(2)}, u32[]{:S(2)}) collective-permute-start(f32[224,256]{1,0:T(8,128)S(1)} %collective-permute-done.4.refs_5_), channel_id=1, source_target_pairs={{1,0},{0,2},{2,4},{4,6},{6,7},{7,5},{5,3},{3,1},{9,8},{8,10},{10,1... | collective-permute-start | bytes 688136 | tf_op jit(solution)/shard_map/ppermute | solution.py:355
  32.0 5.1 %collective-permute-start.12 = (f32[2016,128]{1,0:T(8,128)S(1)}, f32[2016,128]{1,0:T(8,128)S(1)}, u32[]{:S(2)}, u32[]{:S(2)}) collective-permute-start(f32[2016,128]{1,0:T(8,128)S(1)} %collective-permute-done.7.refs_2_), channel_id=1, source_target_pairs={{0,8},{8,0},{16,24},{24,16},{1,9},{9,1},{17,25},{25,17},{2,10},{10... | collective-permute-start | bytes 3096584 | tf_op jit(solution)/shard_map/ppermute | solution.py:325
  32.0 5.1 %collective-permute-start.8 = (f32[576,128]{1,0:T(8,128)S(1)}, f32[576,128]{1,0:T(8,128)S(1)}, u32[]{:S(2)}, u32[]{:S(2)}) collective-permute-start(f32[576,128]{1,0:T(8,128)S(1)} %get-tuple-element.41.refs_0_), channel_id=1, source_target_pairs={{0,8},{8,0},{16,24},{24,16},{1,9},{9,1},{17,25},{25,17},{2,10},{10... | collective-permute-start | bytes 884744 | tf_op jit(solution)/shard_map/ppermute | solution.py:325
  32.6 12.2 %collective-permute-start.10 = (f32[576,128]{1,0:T(8,128)S(1)}, f32[576,128]{1,0:T(8,128)S(1)}, u32[]{:S(2)}, u32[]{:S(2)}) collective-permute-start(f32[576,128]{1,0:T(8,128)S(1)} %get-tuple-element.41.refs_0_), channel_id=1, source_target_pairs={{0,24},{8,16},{16,8},{24,0},{1,25},{9,17},{17,9},{25,1},{2,26},{10... | collective-permute-start | bytes 884744 | tf_op jit(solution)/shard_map/ppermute | solution.py:332
  33.9 14.3 %collective-permute-start.9 = (f32[576,128]{1,0:T(8,128)S(1)}, f32[576,128]{1,0:T(8,128)S(1)}, u32[]{:S(2)}, u32[]{:S(2)}) collective-permute-start(f32[576,128]{1,0:T(8,128)S(1)} %get-tuple-element.41.refs_0_), channel_id=1, source_target_pairs={{0,16},{8,24},{16,0},{24,8},{1,17},{9,25},{17,1},{25,9},{2,18},{10... | collective-permute-start | bytes 884744 | tf_op jit(solution)/shard_map/ppermute | solution.py:332
  38.9 13.6 %collective-permute-start.16 = (f32[448,256]{1,0:T(8,128)S(1)}, f32[448,256]{1,0:T(8,128)S(1)}, u32[]{:S(2)}, u32[]{:S(2)}) collective-permute-start(f32[448,256]{1,0:T(8,128)S(1)} %get-tuple-element.54.refs_0_.mine_ref), channel_id=1, source_target_pairs={{0,1},{1,0},{2,3},{3,2},{4,5},{5,4},{6,7},{7,6},{8,9},{9,8},{10,11... | collective-permute-start | bytes 1376264 | tf_op jit(solution)/shard_map/ppermute | solution.py:325
  40.6 10.1 %collective-permute-start.13 = (f32[112,256]{1,0:T(8,128)S(1)}, f32[112,256]{1,0:T(8,128)S(1)}, u32[]{:S(2)}, u32[]{:S(2)}) collective-permute-start(f32[112,256]{1,0:T(8,128)S(1)} %get-tuple-element.51), channel_id=1, source_target_pairs={{0,2},{1,3},{2,4},{3,5},{4,6},{5,7},{6,0},{7,1},{8,10},{9,11},{10,... | collective-permute-start | bytes 344072 | tf_op jit(solution)/shard_map/ppermute | solution.py:450
  42.1 10.3 %collective-permute-start.14 = (f32[112,256]{1,0:T(8,128)S(1)}, f32[112,256]{1,0:T(8,128)S(1)}, u32[]{:S(2)}, u32[]{:S(2)}) collective-permute-start(f32[112,256]{1,0:T(8,128)S(1)} %get-tuple-element.52), channel_id=1, source_target_pairs={{0,4},{1,5},{2,6},{3,7},{4,0},{5,1},{6,2},{7,3},{8,12},{9,13},{10,... | collective-permute-start | bytes 344072 | tf_op jit(solution)/shard_map/ppermute | solution.py:450
  44.7 7.7 %collective-permute-start.15 = (f32[112,256]{1,0:T(8,128)S(1)}, f32[112,256]{1,0:T(8,128)S(1)}, u32[]{:S(2)}, u32[]{:S(2)}) collective-permute-start(f32[112,256]{1,0:T(8,128)S(1)} %get-tuple-element.53), channel_id=1, source_target_pairs={{0,6},{1,7},{2,0},{3,1},{4,2},{5,3},{6,4},{7,5},{8,14},{9,15},{10,... | collective-permute-start | bytes 344072 | tf_op jit(solution)/shard_map/ppermute | solution.py:450
  52.5 14.3 %copy-start.2 = (f32[128,256]{1,0:T(8,128)S(1)}, f32[128,256]{1,0:T(8,128)}, u32[]{:S(2)}) copy-start(f32[128,256]{1,0:T(8,128)} %param.7) | copy-start | bytes 393220
  53.5 7.5 %collective-permute-start.17 = (f32[224,256]{1,0:T(8,128)S(1)}, f32[224,256]{1,0:T(8,128)S(1)}, u32[]{:S(2)}, u32[]{:S(2)}) collective-permute-start(f32[224,256]{1,0:T(8,128)S(1)} %get-tuple-element.64), channel_id=1, source_target_pairs={{0,1},{1,0},{2,3},{3,2},{4,5},{5,4},{6,7},{7,6},{8,9},{9,8},{10,11... | collective-permute-start | bytes 688136 | tf_op jit(solution)/shard_map/ppermute | solution.py:325
  54.3 8.2 %collective-permute-start.18 = (f32[128,256]{1,0:T(8,128)S(1)}, f32[128,256]{1,0:T(8,128)S(1)}, u32[]{:S(2)}, u32[]{:S(2)}) collective-permute-start(f32[128,256]{1,0:T(8,128)S(1)} %get-tuple-element.67), channel_id=1, source_target_pairs={{0,2},{1,3},{2,4},{3,5},{4,6},{5,7},{6,0},{7,1},{8,10},{9,11},{10,... | collective-permute-start | bytes 393224 | tf_op jit(solution)/shard_map/ppermute | solution.py:477
  57.1 9.7 %collective-permute-start.19 = (f32[128,256]{1,0:T(8,128)S(1)}, f32[128,256]{1,0:T(8,128)S(1)}, u32[]{:S(2)}, u32[]{:S(2)}) collective-permute-start(f32[128,256]{1,0:T(8,128)S(1)} %get-tuple-element.68), channel_id=1, source_target_pairs={{0,4},{1,5},{2,6},{3,7},{4,0},{5,1},{6,2},{7,3},{8,12},{9,13},{10,... | collective-permute-start | bytes 393224 | tf_op jit(solution)/shard_map/ppermute | solution.py:477
  58.7 8.1 %collective-permute-start.20 = (f32[128,256]{1,0:T(8,128)S(1)}, f32[128,256]{1,0:T(8,128)S(1)}, u32[]{:S(2)}, u32[]{:S(2)}) collective-permute-start(f32[128,256]{1,0:T(8,128)S(1)} %get-tuple-element.69), channel_id=1, source_target_pairs={{0,6},{1,7},{2,0},{3,1},{4,2},{5,3},{6,4},{7,5},{8,14},{9,15},{10,... | collective-permute-start | bytes 393224 | tf_op jit(solution)/shard_map/ppermute | solution.py:477

commit v9 on v8

--- a/solution.py
+++ b/solution.py
@@ -81,11 +81,16 @@
     shift = lax.rem(n - count(listed < first), n)
     named = pltpu.roll(names, shift, 1)[:1, :CAP] - first
     named = jnp.concatenate([named, named[:, FULL * LANES :]], axis=1)
-    at = lax.broadcasted_iota(jnp.int32, (cols, WIDE), 0)
-    place = one_hot(at == named).astype(BF16)
+    step = 2 * LANES
+    places = []
+    for k in range(0, WIDE, step):
+        at = lax.broadcasted_iota(jnp.int32, (cols - k, min(step, WIDE - k)), 0) + k
+        places.append(one_hot(at == named[:, k : k + step]).astype(BF16))
     for k in range(parts):
         copies[k].wait()
-        picked = dot(jnp.concatenate(split(held_ref[part * k : part * (k + 1), :]), axis=0), place)
+        both = jnp.concatenate(split(held_ref[part * k : part * (k + 1), :]), axis=0)
+        picked = [dot(both[:, step * i :], place) for i, place in enumerate(places)]
+        picked = jnp.concatenate(picked, axis=1)
         picked = picked[:part] + picked[part:]
         for i in range(FULL):
             at = rows * i + part * k
@@ -169,11 +174,47 @@
     return one_hot(at == slot).T.astype(BF16)
 
 
-def order_kernel(direct, slots, structure_ref, to_ref):
+def order_kernel(direct, slots, structure_ref, to_ref, place_ref, from_ref):
     nc = to_ref.shape[0] // slots
     rows = to_ref.shape[1]
+    nz = nc // 2
+    lg = log2(nc)
     names = structure_ref[...].reshape(1, -1)
-    to_ref[...] = row_order(names, lax.axis_index("pcol"), rows, nc, slots, direct)
+    n = names.shape[1]
+    m = n // nc
+    c = lax.axis_index("pcol")
+    z, x = c // 2, c & 1
+    to_ref[...] = row_order(names, c, rows, nc, slots, direct)
+
+    start, middle = count(names < 2 * z * rows), count(names < (2 * z + 1) * rows)
+    named = pltpu.roll(jnp.broadcast_to(names, (8, n)), lax.rem(n - start, n), 1)[:1, :CAP]
+    index = start + lax.broadcasted_iota(jnp.int32, (1, CAP), 1)
+    half = jnp.where(named >= (2 * z + 1) * rows, 1, 0)
+    turn = index & (nc - 1)
+    ahead = (jnp.where(half == 1, middle, start) - turn + nc - 1) >> lg
+    block = turn >> 1
+    if direct:
+        block = (block - z) & (nz - 1)
+    slot = (2 * block + (turn & 1)) * slots + (index >> lg) - ahead + (half ^ x) * rows
+    slot = jnp.where((named >= 2 * z * rows) & (named < (2 * z + 2) * rows), slot, -1)
+    at = lax.broadcasted_iota(jnp.int32, (2 * rows, CAP), 0)
+    place_ref[...] = one_hot(at == slot).T.astype(BF16)
+
+    own = lax.broadcasted_iota(jnp.int32, (m, n), 1) - nc * lax.broadcasted_iota(jnp.int32, (m, n), 0)
+    mine = jnp.sum(jnp.where(own == c, names, 0).astype(jnp.float32), axis=1, keepdims=True)
+    source = jnp.zeros((m, 1), jnp.int32)
+    before = jnp.zeros((m, 1), jnp.int32)
+    for k in range(1, nc):
+        less = mine < float(k * rows)
+        source = source + jnp.where(less, 0, 1)
+        before = jnp.where(less, before, count(less))
+    block = source >> 1
+    if direct:
+        block = (z - block) & (nz - 1)
+    block = block + nz * ((source ^ c) & 1)
+    slot = block * slots + lax.broadcasted_iota(jnp.int32, (m, 1), 0) - before
+    at = lax.broadcasted_iota(jnp.int32, (m, rows), 1)
+    from_ref[...] = one_hot(at == slot).astype(BF16)
 
 
 def near_kernel(owners, rest, structure_ref, us_ref, *refs):
@@ -197,15 +238,25 @@
             uh_ref[k], ul_ref[k] = cut(us_ref, names, owner, width, w)
 
 
+def far_terms(first, uh_ref, ul_ref, image, block_refs):
+    rows = image.shape[0]
+    for k, block_ref in enumerate(block_refs):
+        image = image + block_term(block_ref, uh_ref[first + 2 * k], ul_ref[first + 2 * k], rows)
+    return image
+
+
+def far_kernel(first, uh_ref, ul_ref, part_ref, *refs):
+    refs[-1][...] = far_terms(first, uh_ref, ul_ref, part_ref[...], refs[:-1])
+
+
 def image_kernel(direct, uh_ref, ul_ref, part_ref, to_ref, *refs):
-    n_in = uh_ref.shape[0] if direct else 1
+    n_in = uh_ref.shape[0] // 2 if direct else 1
     block_refs, out_refs = refs[:n_in], refs[n_in:]
     n_out = len(out_refs)
     rows = part_ref.shape[0]
     image = part_ref[...]
     if direct:
-        for k, block_ref in enumerate(block_refs):
-            image = image + block_term(block_ref, uh_ref[k], ul_ref[k], rows)
+        image = far_terms(1, uh_ref, ul_ref, image, block_refs)
     else:
         stack = block_refs[0]
         add = lambda b, v: v + block_term(stack.at[b], uh_ref[b], ul_ref[b], rows)
@@ -217,31 +268,10 @@
         out_refs[k][...] = image[size * k : size * (k + 1)]
 
 
-def turn_kernel(direct, slots, owners, structure_ref, *refs):
-    from_ref, high_ref, low_ref, held_ref = refs[-4:]
-    nz, wd = high_ref.shape[:2]
-    nc = 2 * nz
-    lg = log2(nc)
-    rows = slots * nc
-    n = structure_ref.shape[0]
-    m = n // nc
-    names = structure_ref[...].reshape(1, -1)
-    c = lax.axis_index("pcol")
-    z, x = c // 2, c & 1
-
-    start, middle = count(names < 2 * z * rows), count(names < (2 * z + 1) * rows)
-    named = pltpu.roll(jnp.broadcast_to(names, (8, n)), lax.rem(n - start, n), 1)[:1, :CAP]
-    index = start + lax.broadcasted_iota(jnp.int32, (1, CAP), 1)
-    half = jnp.where(named >= (2 * z + 1) * rows, 1, 0)
-    turn = index & (nc - 1)
-    ahead = (jnp.where(half == 1, middle, start) - turn + nc - 1) >> lg
-    block = turn >> 1
-    if direct:
-        block = (block - z) & (nz - 1)
-    slot = (2 * block + (turn & 1)) * slots + (index >> lg) - ahead + (half ^ x) * rows
-    slot = jnp.where((named >= 2 * z * rows) & (named < (2 * z + 2) * rows), slot, -1)
-    at = lax.broadcasted_iota(jnp.int32, (2 * rows, CAP), 0)
-    place = one_hot(at == slot).astype(BF16)
+def turn_kernel(direct, owners, place_ref, *refs):
+    high_ref, low_ref, held_ref = refs[-3:]
+    nz, wd, size = high_ref.shape
+    z = lax.axis_index("pcol") // 2
 
     def put(owner, u_ref):
         where = ((owner - z) & (nz - 1)) if direct else owner
@@ -249,27 +279,10 @@
         held_ref[pl.ds(pl.multiple_of(where * wd, wd), wd), :] = high
         held_ref[pl.ds(pl.multiple_of((where + nz) * wd, wd), wd), :] = low
 
-    each(refs[:-4], owners(lax.axis_index("prow")) if direct else None, put)
-    turned = lax.dot_general(held_ref[...], place, (((1,), (1,)), ((), ())), preferred_element_type=jnp.float32)
-    turned = turned.astype(BF16).reshape(2, nz, wd, 2 * rows)
+    each(refs[:-3], owners(lax.axis_index("prow")) if direct else None, put)
+    turned = dot(held_ref[...], place_ref[...]).astype(BF16).reshape(2, nz, wd, size)
     high_ref[...] = turned[0]
     low_ref[...] = turned[1]
-
-    own = lax.broadcasted_iota(jnp.int32, (m, n), 1) - nc * lax.broadcasted_iota(jnp.int32, (m, n), 0)
-    mine = jnp.sum(jnp.where(own == c, names, 0).astype(jnp.float32), axis=1, keepdims=True)
-    source = jnp.zeros((m, 1), jnp.int32)
-    before = jnp.zeros((m, 1), jnp.int32)
-    for k in range(1, nc):
-        less = mine < float(k * rows)
-        source = source + jnp.where(less, 0, 1)
-        before = jnp.where(less, before, count(less))
-    block = source >> 1
-    if direct:
-        block = (z - block) & (nz - 1)
-    block = block + nz * ((source ^ c) & 1)
-    slot = block * slots + lax.broadcasted_iota(jnp.int32, (m, 1), 0) - before
-    at = lax.broadcasted_iota(jnp.int32, (m, rows), 1)
-    from_ref[...] = one_hot(at == slot).astype(BF16)
 
 
 def correction_kernel(high_ref, low_ref, mine_ref, other_ref, *out_refs):
@@ -325,8 +338,9 @@
     return lax.ppermute(v, axis, [(k, k ^ 1) for k in range(size)])
 
 
-def spread(v, size):
+def spread(v, size, after):
     blocks = [v, swap(v, "prow", size)]
+    v, _ = lax.optimization_barrier((v, after))
     for t in range(1, size // 2):
         for flip in range(2):
             blocks.append(lax.ppermute(v, "prow", [(k, ((k + 2 * t) % size) ^ flip) for k in range(size)]))
@@ -390,7 +404,11 @@
         flops=4 * rows * cols * WIDE,
         vmem=52,
     )
-    to = call(functools.partial(order_kernel, direct, slots), bf16(nc * slots, rows), names)
+    to, place, source = call(
+        functools.partial(order_kernel, direct, slots),
+        [bf16(nc * slots, rows), bf16(CAP, 2 * nc * slots), bf16(m, nc * slots)],
+        names,
+    )
     if direct:
         u_all, to = ring_gather(u_panel, nc, to)
     else:
@@ -407,21 +425,13 @@
         *late,
         flops=term,
     )
-    near, later = [], []
-    if direct:
-        near = [chosen, swap(chosen, "prow", nr)]
-        for t in range(1, nr // 2):
-            far = lax.ppermute(chosen, "prow", [(k, (k + 2 * t) % nr) for k in range(nr)])
-            far, _ = lax.optimization_barrier((far, own))
-            near.append(far)
-            later.append(swap(far, "prow", nr))
-    else:
-        later = [lax.all_gather(chosen, "prow")]
-    halves = bf16(len(later) if direct else nr, WIDE, w)
+    halves = bf16(nr - 2 if direct else nr, WIDE, w)
+    near = []
+    if direct:
+        again, _ = lax.optimization_barrier((chosen, u_all[1]))
+        near = [chosen, swap(again, "prow", nr)]
     image, uh, ul = call(
-        functools.partial(
-            near_kernel, lambda r: owners(r)[:2] + owners(r)[2::2], (lambda r: owners(r)[3::2]) if direct else None
-        ),
+        functools.partial(near_kernel, lambda r: owners(r)[:2], (lambda r: owners(r)[2:]) if direct else None),
         [f32(rows, w), halves, halves],
         names,
         us,
@@ -429,8 +439,17 @@
         flops=3 * term,
     )
     if direct:
-        own, _ = lax.optimization_barrier((own, near[2]))
-        owned = spread(own, nr)
+        beside, later = [], []
+        for t in range(1, nr // 2):
+            far = lax.ppermute(chosen, "prow", [(k, (k + 2 * t) % nr) for k in range(nr)])
+            far, _ = lax.optimization_barrier((far, image))
+            beside.append(far)
+            later.append(swap(far, "prow", nr))
+        image = call(functools.partial(far_kernel, 0), f32(rows, w), uh, ul, image, *beside, flops=term)
+    else:
+        later = [lax.all_gather(chosen, "prow")]
+    if direct:
+        owned = spread(own, nr, beside[0])
         owned[1], to = lax.optimization_barrier((owned[1], to))
     sent = call(
         functools.partial(image_kernel, direct),
@@ -456,16 +475,16 @@
         owned = [lax.all_gather(own, "prow")]
 
     turned = bf16(nz, wd, 2 * nc * slots)
-    source, high, low = call(
-        functools.partial(turn_kernel, direct, slots, owners),
-        [bf16(m, nc * slots), turned, turned],
-        names,
+    high, low = call(
+        functools.partial(turn_kernel, direct, owners),
+        [turned, turned],
+        place,
         *owned,
         scratch_shapes=[pltpu.VMEM((2 * nz * wd, CAP), BF16)],
         flops=8 * nz * wd * nc * slots * CAP,
     )
     parts = [f32(wd, w)] * nz if direct else [f32(nz, wd, w)]
-    got, _ = lax.optimization_barrier((got, source))
+    got, _ = lax.optimization_barrier((got, high))
     mine, theirs = call(functools.partial(part_kernel, slots), [f32(nz * slots, w)] * 2, *got, flops=2 * term)
     other, _ = lax.optimization_barrier((other, mine))
     terms = call(correction_kernel, parts, high, low, whole, other, flops=term)

time: 68.1 us -> 72.7 us (1.068)
  waiting for transfers between devices: 24.4 us -> 28.2 us
    ppermute x4, waiting for transfers between devices: 11 us -> 14.8 us  [ring_gather(): lax.ppermute(up, 'pcol', pairs)]
    ppermute x5, waiting for transfers between devices: 1.23 us -> 4.06 us  [swap(): return lax.ppermute(v, axis, [(k, k ^ 1) for k in range(size)])]
    ppermute x1, waiting for transfers between devices: 2.37 us -> 0.01 us  [per_device(): lax.ppermute(chosen, 'prow', [(k, (k + 2 * t) % nr) for k in range(nr)])]
    ppermute x3, starting transfers between devices: 5.52 us -> 7.61 us  [per_device(): lax.ppermute(sent[t], 'pcol', [(k, (k + 2 * t) % nc) for k in range(nc)])]
    ppermute x3, waiting for transfers between devices: 1.76 us -> 0.42 us  [per_device(): lax.ppermute(sent[t], 'pcol', [(k, (k + 2 * t) % nc) for k in range(nc)])]
    pallas_call x10 -> x11, Pallas kernels: 14.5 us -> 14.8 us  [call(): pl.pallas_call(kernel, out_shape=out_shape, out_specs=[VMEM] * len(out_sh...]
  transfers between devices with their start and end apart: 21 -> 21, of which waited for: 10 -> 14; matrix products, arithmetic and copies ran while one was open for 0% -> 0% of each run, Pallas kernels for 20% -> 19%
where the time goes in v9:
time: 72.7 us; the launch traced here: 72.2 us
  waiting for transfers between devices  28.2 us (39%)
  starting transfers between devices  27 us (37%)
  Pallas kernels  14.8 us (20%)
  between operations  0.76 us (1%)
    pallas_call x11, Pallas kernels, call(): pl.pallas_call(kernel, out_shape=out_shape, out_specs=[VMEM] * len(out_sh...  14.8 us
    ppermute x4, waiting for transfers between devices, ring_gather(): lax.ppermute(up, 'pcol', pairs)  14.8 us
    ppermute x4, starting transfers between devices, ring_gather(): lax.ppermute(up, 'pcol', pairs)  7.81 us
    ppermute x3, starting transfers between devices, per_device(): lax.ppermute(sent[t], 'pcol', [(k, (k + 2 * t) % nc) for k in range(nc)])  7.61 us
    ppermute x3, starting transfers between devices, per_device(): lax.ppermute(terms[t], 'pcol', [(k, (k + 2 * t) % nc) for k in range(nc)])  5.29 us
    ppermute x3, waiting for transfers between devices, per_device(): lax.ppermute(terms[t], 'pcol', [(k, (k + 2 * t) % nc) for k in range(nc)])  4.89 us
    ppermute x5, waiting for transfers between devices, swap(): return lax.ppermute(v, axis, [(k, k ^ 1) for k in range(size)])  4.06 us
    ppermute x2, waiting for transfers between devices, spread(): lax.ppermute(v, 'prow', [(k, (k + 2 * t) % size ^ flip) for k in range(si...  2.51 us
  transfers between devices with their start and end apart: 21, of which 14 were waited for; matrix products, arithmetic and copies ran while one was open for 0% of the time, Pallas kernels for 19%

profile of v9, /device:TPU:0, one launch (start us, length us, event | category | flops | bytes accessed | tf_op | source)
XLA Modules:
  0.0 72.2 jit_solution(6469135250180365182)
XLA Ops:
  0.6 3.1 %collective-permute-start = (f32[224,256]{1,0:T(8,128)}, f32[224,256]{1,0:T(8,128)S(1)}, u32[]{:S(2)}, u32[]{:S(2)}) collective-permute-start(f32[224,256]{1,0:T(8,128)} %refs_0_.1), channel_id=1, source_target_pairs={{1,0},{0,2},{2,4},{4,6},{6,7},{7,5},{5,3},{3,1},{9,8},{8,10},{10,1... | collective-permute-start | bytes 688136 | tf_op jit(solution)/shard_map/ppermute | solution.py:365
  4.4 2.7 %shard_map.62.refs_0_ = f32[2016,128]{1,0:T(8,128)S(1)} custom-call(s32[1792]{0:T(1024)S(1)} %copy-done, f32[448,896]{1,0:T(8,128)} %sigma_ref.1), custom_call_target="tpu_custom_call" | custom-call | flops 1027604480 | bytes 2644992 | tf_op jit(solution)/shard_map/pallas_call | solution.py:327
  7.1 2.3 %collective-permute-done.refs_1_ = f32[224,256]{1,0:T(8,128)S(1)} collective-permute-done((f32[224,256]{1,0:T(8,128)}, f32[224,256]{1,0:T(8,128)S(1)}, u32[]{:S(2)}, u32[]{:S(2)}) %collective-permute-start) | collective-permute-done | bytes 229408 | tf_op jit(solution)/shard_map/ppermute | solution.py:365
  9.4 1.5 %collective-permute-done.1.refs_2_ = f32[224,256]{1,0:T(8,128)S(1)} collective-permute-done((f32[224,256]{1,0:T(8,128)}, f32[224,256]{1,0:T(8,128)S(1)}, u32[]{:S(2)}, u32[]{:S(2)}) %collective-permute-start.1) | collective-permute-done | bytes 229408 | tf_op jit(solution)/shard_map/ppermute | solution.py:365
  11.0 1.5 %collective-permute-start.8 = (f32[2016,128]{1,0:T(8,128)S(1)}, f32[2016,128]{1,0:T(8,128)S(1)}, u32[]{:S(2)}, u32[]{:S(2)}) collective-permute-start(f32[2016,128]{1,0:T(8,128)S(1)} %shard_map.62.refs_0_), channel_id=1, source_target_pairs={{0,16},{8,24},{16,0},{24,8},{1,17},{9,25},{17,1},{25,9},{2,18},{10... | collective-permute-start | bytes 3096584 | tf_op jit(solution)/shard_map/ppermute | solution.py:444
  12.5 1.6 %collective-permute-start.2 = (f32[224,256]{1,0:T(8,128)S(1)}, f32[224,256]{1,0:T(8,128)S(1)}, u32[]{:S(2)}, u32[]{:S(2)}) collective-permute-start(f32[224,256]{1,0:T(8,128)S(1)} %collective-permute-done.refs_1_), channel_id=1, source_target_pairs={{1,0},{0,2},{2,4},{4,6},{6,7},{7,5},{5,3},{3,1},{9,8},{8,10},{10,1... | collective-permute-start | bytes 688136 | tf_op jit(solution)/shard_map/ppermute | solution.py:365
  14.5 5.7 %collective-permute-done.2.refs_3_ = f32[224,256]{1,0:T(8,128)S(1)} collective-permute-done((f32[224,256]{1,0:T(8,128)S(1)}, f32[224,256]{1,0:T(8,128)S(1)}, u32[]{:S(2)}, u32[]{:S(2)}) %collective-permute-start.2) | collective-permute-done | bytes 229408 | tf_op jit(solution)/shard_map/ppermute | solution.py:365
  20.2 1.6 %collective-permute-start.4 = (f32[224,256]{1,0:T(8,128)S(1)}, f32[224,256]{1,0:T(8,128)S(1)}, u32[]{:S(2)}, u32[]{:S(2)}) collective-permute-start(f32[224,256]{1,0:T(8,128)S(1)} %collective-permute-done.2.refs_3_), channel_id=1, source_target_pairs={{1,0},{0,2},{2,4},{4,6},{6,7},{7,5},{5,3},{3,1},{9,8},{8,10},{10,1... | collective-permute-start | bytes 688136 | tf_op jit(solution)/shard_map/ppermute | solution.py:365
  22.3 2.1 %shard_map.59 = (bf16[448,448]{1,0:T(8,128)(2,1)S(1)}, bf16[576,896]{1,0:T(8,128)(2,1)S(1)}, bf16[224,448]{1,0:T(8,128)(2,1)S(1)}) custom-call(s32[1792]{0:T(1024)S(1)} %copy-done), custom_call_target="tpu_custom_call" | custom-call | bytes 1641472 | tf_op jit(solution)/shard_map/pallas_call | solution.py:327
  24.3 2.8 %collective-permute-done.4.refs_5_ = f32[224,256]{1,0:T(8,128)S(1)} collective-permute-done((f32[224,256]{1,0:T(8,128)S(1)}, f32[224,256]{1,0:T(8,128)S(1)}, u32[]{:S(2)}, u32[]{:S(2)}) %collective-permute-start.4) | collective-permute-done | bytes 229408 | tf_op jit(solution)/shard_map/ppermute | solution.py:365
  27.2 1.6 %collective-permute-start.6 = (f32[224,256]{1,0:T(8,128)S(1)}, f32[224,256]{1,0:T(8,128)S(1)}, u32[]{:S(2)}, u32[]{:S(2)}) collective-permute-start(f32[224,256]{1,0:T(8,128)S(1)} %collective-permute-done.4.refs_5_), channel_id=1, source_target_pairs={{1,0},{0,2},{2,4},{4,6},{6,7},{7,5},{5,3},{3,1},{9,8},{8,10},{10,1... | collective-permute-start | bytes 688136 | tf_op jit(solution)/shard_map/ppermute | solution.py:369
  29.2 3.9 %collective-permute-done.6.refs_0_ = f32[224,256]{1,0:T(8,128)S(1)} collective-permute-done((f32[224,256]{1,0:T(8,128)S(1)}, f32[224,256]{1,0:T(8,128)S(1)}, u32[]{:S(2)}, u32[]{:S(2)}) %collective-permute-start.6) | collective-permute-done | bytes 229408 | tf_op jit(solution)/shard_map/ppermute | solution.py:369
  33.7 2.5 %shard_map.63 = (f32[448,256]{1,0:T(8,128)S(1)}, bf16[2,640,256]{2,1,0:T(8,128)(2,1)S(1)}, bf16[2,640,256]{2,1,0:T(8,128)(2,1)S(1)}) custom-call(s32[1792]{0:T(1024)S(1)} %copy-done, f32[2,2376,128]{2,1,0:T(8,128)S(1)} %get-tuple-element.44.us_ref, f32[2016,128]{1,0:T(8,128)S(1)} %shard_map.62.refs_0_, f32[2016,128]{1,0:T(8,128)S(1)} %collective-permute-done.7.refs_1_), custom_call_target="tpu_custom_call" | custom-call | flops 1321205760 | bytes 6274048 | tf_op jit(solution)/shard_map/pallas_call | solution.py:327
  36.8 2.5 %collective-permute-done.9.refs_1_ = f32[576,128]{1,0:T(8,128)S(1)} collective-permute-done((f32[576,128]{1,0:T(8,128)S(1)}, f32[576,128]{1,0:T(8,128)S(1)}, u32[]{:S(2)}, u32[]{:S(2)}) %collective-permute-start.9) | collective-permute-done | bytes 294944 | tf_op jit(solution)/shard_map/ppermute | solution.py:338
  39.3 1.5 %collective-permute-start.14 = (f32[576,128]{1,0:T(8,128)S(1)}, f32[576,128]{1,0:T(8,128)S(1)}, u32[]{:S(2)}, u32[]{:S(2)}) collective-permute-start(f32[576,128]{1,0:T(8,128)S(1)} %get-tuple-element.59.refs_0_), channel_id=1, source_target_pairs={{0,16},{8,24},{16,0},{24,8},{1,17},{9,25},{17,1},{25,9},{2,18},{10... | collective-permute-start | bytes 884744 | tf_op jit(solution)/shard_map/ppermute | solution.py:346
  41.5 1.8 %shard_map.65 = (f32[448,256]{1,0:T(8,128)S(1)}, f32[112,256]{1,0:T(8,128)S(1)}, f32[112,256]{1,0:T(8,128)S(1)}, f32[112,256]{1,0:T(8,128)S(1)}) custom-call(bf16[2,640,256]{2,1,0:T(8,128)(2,1)S(1)} %get-tuple-element.46.uh_ref, bf16[2,640,256]{2,1,0:T(8,128)(2,1)S(1)} %get-tuple-element.47.ul_ref, f32[448,256]{1,0:T(8,128)S(1)} %shard_map.64.part_ref, ...), custom_call_target="tpu_custom_call" | custom-call | flops 440401920 | bytes 4005888 | tf_op jit(solution)/shard_map/pallas_call | solution.py:327
  43.8 1.5 %collective-permute-start.11 = (f32[112,256]{1,0:T(8,128)S(1)}, f32[112,256]{1,0:T(8,128)S(1)}, u32[]{:S(2)}, u32[]{:S(2)}) collective-permute-start(f32[112,256]{1,0:T(8,128)S(1)} %get-tuple-element.54), channel_id=1, source_target_pairs={{0,2},{1,3},{2,4},{3,5},{4,6},{5,7},{6,0},{7,1},{8,10},{9,11},{10,... | collective-permute-start | bytes 344072 | tf_op jit(solution)/shard_map/ppermute | solution.py:469
  45.3 2.6 %collective-permute-start.12 = (f32[112,256]{1,0:T(8,128)S(1)}, f32[112,256]{1,0:T(8,128)S(1)}, u32[]{:S(2)}, u32[]{:S(2)}) collective-permute-start(f32[112,256]{1,0:T(8,128)S(1)} %get-tuple-element.55), channel_id=1, source_target_pairs={{0,4},{1,5},{2,6},{3,7},{4,0},{5,1},{6,2},{7,3},{8,12},{9,13},{10,... | collective-permute-start | bytes 344072 | tf_op jit(solution)/shard_map/ppermute | solution.py:469
  49.2 3.5 %collective-permute-start.13 = (f32[112,256]{1,0:T(8,128)S(1)}, f32[112,256]{1,0:T(8,128)S(1)}, u32[]{:S(2)}, u32[]{:S(2)}) collective-permute-start(f32[112,256]{1,0:T(8,128)S(1)} %get-tuple-element.56), channel_id=1, source_target_pairs={{0,6},{1,7},{2,0},{3,1},{4,2},{5,3},{6,4},{7,5},{8,14},{9,15},{10,... | collective-permute-start | bytes 344072 | tf_op jit(solution)/shard_map/ppermute | solution.py:469
  53.9 2.0 %shard_map.66 = (bf16[4,128,896]{2,1,0:T(8,128)(2,1)S(1)}, bf16[4,128,896]{2,1,0:T(8,128)(2,1)S(1)}) custom-call(bf16[576,896]{1,0:T(8,128)(2,1)S(1)} %get-tuple-element.57.place_ref, f32[576,128]{1,0:T(8,128)S(1)} %get-tuple-element.59.refs_0_, f32[576,128]{1,0:T(8,128)S(1)} %collective-permute-done.9.refs_1_, ...), custom_call_target="tpu_custom_call" | custom-call | flops 1056964608 | bytes 4046848 | tf_op jit(solution)/shard_map/pallas_call | solution.py:327
  58.7 2.9 %collective-permute-start.18 = (f32[128,256]{1,0:T(8,128)S(1)}, f32[128,256]{1,0:T(8,128)S(1)}, u32[]{:S(2)}, u32[]{:S(2)}) collective-permute-start(f32[128,256]{1,0:T(8,128)S(1)} %get-tuple-element.73), channel_id=1, source_target_pairs={{0,2},{1,3},{2,4},{3,5},{4,6},{5,7},{6,0},{7,1},{8,10},{9,11},{10,... | collective-permute-start | bytes 393224 | tf_op jit(solution)/shard_map/ppermute | solution.py:496
  61.6 1.7 %collective-permute-start.19 = (f32[128,256]{1,0:T(8,128)S(1)}, f32[128,256]{1,0:T(8,128)S(1)}, u32[]{:S(2)}, u32[]{:S(2)}) collective-permute-start(f32[128,256]{1,0:T(8,128)S(1)} %get-tuple-element.74), channel_id=1, source_target_pairs={{0,4},{1,5},{2,6},{3,7},{4,0},{5,1},{6,2},{7,3},{8,12},{9,13},{10,... | collective-permute-start | bytes 393224 | tf_op jit(solution)/shard_map/ppermute | solution.py:496
  64.0 1.5 %collective-permute-done.17.other_ref = f32[224,256]{1,0:T(8,128)S(1)} collective-permute-done((f32[224,256]{1,0:T(8,128)S(1)}, f32[224,256]{1,0:T(8,128)S(1)}, u32[]{:S(2)}, u32[]{:S(2)}) %collective-permute-start.17) | collective-permute-done | bytes 229408 | tf_op jit(solution)/shard_map/ppermute | solution.py:338
  67.2 4.2 %collective-permute-done.19 = f32[128,256]{1,0:T(8,128)S(1)} collective-permute-done((f32[128,256]{1,0:T(8,128)S(1)}, f32[128,256]{1,0:T(8,128)S(1)}, u32[]{:S(2)}, u32[]{:S(2)}) %collective-permute-start.19) | collective-permute-done | bytes 131104 | tf_op jit(solution)/shard_map/ppermute | solution.py:496
  (36 shorter events, 12.7 us)
Async XLA Ops:
  0.6 8.8 %collective-permute-start = (f32[224,256]{1,0:T(8,128)}, f32[224,256]{1,0:T(8,128)S(1)}, u32[]{:S(2)}, u32[]{:S(2)}) collective-permute-start(f32[224,256]{1,0:T(8,128)} %refs_0_.1), channel_id=1, source_target_pairs={{1,0},{0,2},{2,4},{4,6},{6,7},{7,5},{5,3},{3,1},{9,8},{8,10},{10,1... | collective-permute-start | bytes 688136 | tf_op jit(solution)/shard_map/ppermute | solution.py:365
  3.7 7.3 %collective-permute-start.1 = (f32[224,256]{1,0:T(8,128)}, f32[224,256]{1,0:T(8,128)S(1)}, u32[]{:S(2)}, u32[]{:S(2)}) collective-permute-start(f32[224,256]{1,0:T(8,128)} %refs_0_.1), channel_id=1, source_target_pairs={{0,1},{2,0},{4,2},{6,4},{7,6},{5,7},{3,5},{1,3},{8,9},{10,8},{12,1... | collective-permute-start | bytes 688136 | tf_op jit(solution)/shard_map/ppermute | solution.py:365
  3.7 0.7 copy-start
  4.4 24.3 %copy-start.1 = (f32[224,256]{1,0:T(8,128)S(1)}, f32[224,256]{1,0:T(8,128)}, u32[]{:S(2)}) copy-start(f32[224,256]{1,0:T(8,128)} %refs_0_.1) | copy-start | bytes 688132
  11.0 22.7 %collective-permute-start.7 = (f32[2016,128]{1,0:T(8,128)S(1)}, f32[2016,128]{1,0:T(8,128)S(1)}, u32[]{:S(2)}, u32[]{:S(2)}) collective-permute-start(f32[2016,128]{1,0:T(8,128)S(1)} %shard_map.62.refs_0_), channel_id=1, source_target_pairs={{0,8},{8,0},{16,24},{24,16},{1,9},{9,1},{17,25},{25,17},{2,10},{10... | collective-permute-start | bytes 3096584 | tf_op jit(solution)/shard_map/ppermute | solution.py:338
  11.0 25.2 %collective-permute-start.8 = (f32[2016,128]{1,0:T(8,128)S(1)}, f32[2016,128]{1,0:T(8,128)S(1)}, u32[]{:S(2)}, u32[]{:S(2)}) collective-permute-start(f32[2016,128]{1,0:T(8,128)S(1)} %shard_map.62.refs_0_), channel_id=1, source_target_pairs={{0,16},{8,24},{16,0},{24,8},{1,17},{9,25},{17,1},{25,9},{2,18},{10... | collective-permute-start | bytes 3096584 | tf_op jit(solution)/shard_map/ppermute | solution.py:444
  12.5 7.7 %collective-permute-start.2 = (f32[224,256]{1,0:T(8,128)S(1)}, f32[224,256]{1,0:T(8,128)S(1)}, u32[]{:S(2)}, u32[]{:S(2)}) collective-permute-start(f32[224,256]{1,0:T(8,128)S(1)} %collective-permute-done.refs_1_), channel_id=1, source_target_pairs={{1,0},{0,2},{2,4},{4,6},{6,7},{7,5},{5,3},{3,1},{9,8},{8,10},{10,1... | collective-permute-start | bytes 688136 | tf_op jit(solution)/shard_map/ppermute | solution.py:365
  14.1 7.7 %collective-permute-start.3 = (f32[224,256]{1,0:T(8,128)S(1)}, f32[224,256]{1,0:T(8,128)S(1)}, u32[]{:S(2)}, u32[]{:S(2)}) collective-permute-start(f32[224,256]{1,0:T(8,128)S(1)} %collective-permute-done.1.refs_2_), channel_id=1, source_target_pairs={{0,1},{2,0},{4,2},{6,4},{7,6},{5,7},{3,5},{1,3},{8,9},{10,8},{12,1... | collective-permute-start | bytes 688136 | tf_op jit(solution)/shard_map/ppermute | solution.py:365
  20.2 6.9 %collective-permute-start.4 = (f32[224,256]{1,0:T(8,128)S(1)}, f32[224,256]{1,0:T(8,128)S(1)}, u32[]{:S(2)}, u32[]{:S(2)}) collective-permute-start(f32[224,256]{1,0:T(8,128)S(1)} %collective-permute-done.2.refs_3_), channel_id=1, source_target_pairs={{1,0},{0,2},{2,4},{4,6},{6,7},{7,5},{5,3},{3,1},{9,8},{8,10},{10,1... | collective-permute-start | bytes 688136 | tf_op jit(solution)/shard_map/ppermute | solution.py:365
  21.8 6.9 %collective-permute-start.5 = (f32[224,256]{1,0:T(8,128)S(1)}, f32[224,256]{1,0:T(8,128)S(1)}, u32[]{:S(2)}, u32[]{:S(2)}) collective-permute-start(f32[224,256]{1,0:T(8,128)S(1)} %collective-permute-done.3.refs_4_), channel_id=1, source_target_pairs={{0,1},{2,0},{4,2},{6,4},{7,6},{5,7},{3,5},{1,3},{8,9},{10,8},{12,1... | collective-permute-start | bytes 688136 | tf_op jit(solution)/shard_map/ppermute | solution.py:365
  27.2 6.0 %collective-permute-start.6 = (f32[224,256]{1,0:T(8,128)S(1)}, f32[224,256]{1,0:T(8,128)S(1)}, u32[]{:S(2)}, u32[]{:S(2)}) collective-permute-start(f32[224,256]{1,0:T(8,128)S(1)} %collective-permute-done.4.refs_5_), channel_id=1, source_target_pairs={{1,0},{0,2},{2,4},{4,6},{6,7},{7,5},{5,3},{3,1},{9,8},{8,10},{10,1... | collective-permute-start | bytes 688136 | tf_op jit(solution)/shard_map/ppermute | solution.py:369
  36.2 5.3 %collective-permute-start.10 = (f32[2016,128]{1,0:T(8,128)S(1)}, f32[2016,128]{1,0:T(8,128)S(1)}, u32[]{:S(2)}, u32[]{:S(2)}) collective-permute-start(f32[2016,128]{1,0:T(8,128)S(1)} %collective-permute-done.8.refs_0_), channel_id=1, source_target_pairs={{0,8},{8,0},{16,24},{24,16},{1,9},{9,1},{17,25},{25,17},{2,10},{10... | collective-permute-start | bytes 3096584 | tf_op jit(solution)/shard_map/ppermute | solution.py:338
  36.3 3.0 %collective-permute-start.9 = (f32[576,128]{1,0:T(8,128)S(1)}, f32[576,128]{1,0:T(8,128)S(1)}, u32[]{:S(2)}, u32[]{:S(2)}) collective-permute-start(f32[576,128]{1,0:T(8,128)S(1)} %get-tuple-element.59.refs_0_), channel_id=1, source_target_pairs={{0,8},{8,0},{16,24},{24,16},{1,9},{9,1},{17,25},{25,17},{2,10},{10... | collective-permute-start | bytes 884744 | tf_op jit(solution)/shard_map/ppermute | solution.py:338
  39.3 9.9 %collective-permute-start.14 = (f32[576,128]{1,0:T(8,128)S(1)}, f32[576,128]{1,0:T(8,128)S(1)}, u32[]{:S(2)}, u32[]{:S(2)}) collective-permute-start(f32[576,128]{1,0:T(8,128)S(1)} %get-tuple-element.59.refs_0_), channel_id=1, source_target_pairs={{0,16},{8,24},{16,0},{24,8},{1,17},{9,25},{17,1},{25,9},{2,18},{10... | collective-permute-start | bytes 884744 | tf_op jit(solution)/shard_map/ppermute | solution.py:346
  40.8 13.1 %collective-permute-start.15 = (f32[576,128]{1,0:T(8,128)S(1)}, f32[576,128]{1,0:T(8,128)S(1)}, u32[]{:S(2)}, u32[]{:S(2)}) collective-permute-start(f32[576,128]{1,0:T(8,128)S(1)} %get-tuple-element.59.refs_0_), channel_id=1, source_target_pairs={{0,24},{8,16},{16,8},{24,0},{1,25},{9,17},{17,9},{25,1},{2,26},{10... | collective-permute-start | bytes 884744 | tf_op jit(solution)/shard_map/ppermute | solution.py:346
  43.2 13.1 %collective-permute-start.16 = (f32[448,256]{1,0:T(8,128)S(1)}, f32[448,256]{1,0:T(8,128)S(1)}, u32[]{:S(2)}, u32[]{:S(2)}) collective-permute-start(f32[448,256]{1,0:T(8,128)S(1)} %get-tuple-element.61.refs_0_.mine_ref), channel_id=1, source_target_pairs={{0,1},{1,0},{2,3},{3,2},{4,5},{5,4},{6,7},{7,6},{8,9},{9,8},{10,11... | collective-permute-start | bytes 1376264 | tf_op jit(solution)/shard_map/ppermute | solution.py:338
  43.8 12.1 %collective-permute-start.11 = (f32[112,256]{1,0:T(8,128)S(1)}, f32[112,256]{1,0:T(8,128)S(1)}, u32[]{:S(2)}, u32[]{:S(2)}) collective-permute-start(f32[112,256]{1,0:T(8,128)S(1)} %get-tuple-element.54), channel_id=1, source_target_pairs={{0,2},{1,3},{2,4},{3,5},{4,6},{5,7},{6,0},{7,1},{8,10},{9,11},{10,... | collective-permute-start | bytes 344072 | tf_op jit(solution)/shard_map/ppermute | solution.py:469
  45.3 10.7 %collective-permute-start.12 = (f32[112,256]{1,0:T(8,128)S(1)}, f32[112,256]{1,0:T(8,128)S(1)}, u32[]{:S(2)}, u32[]{:S(2)}) collective-permute-start(f32[112,256]{1,0:T(8,128)S(1)} %get-tuple-element.55), channel_id=1, source_target_pairs={{0,4},{1,5},{2,6},{3,7},{4,0},{5,1},{6,2},{7,3},{8,12},{9,13},{10,... | collective-permute-start | bytes 344072 | tf_op jit(solution)/shard_map/ppermute | solution.py:469
  49.2 7.2 %collective-permute-start.13 = (f32[112,256]{1,0:T(8,128)S(1)}, f32[112,256]{1,0:T(8,128)S(1)}, u32[]{:S(2)}, u32[]{:S(2)}) collective-permute-start(f32[112,256]{1,0:T(8,128)S(1)} %get-tuple-element.56), channel_id=1, source_target_pairs={{0,6},{1,7},{2,0},{3,1},{4,2},{5,3},{6,4},{7,5},{8,14},{9,15},{10,... | collective-permute-start | bytes 344072 | tf_op jit(solution)/shard_map/ppermute | solution.py:469
  56.4 15.1 %copy-start.2 = (f32[128,256]{1,0:T(8,128)S(1)}, f32[128,256]{1,0:T(8,128)}, u32[]{:S(2)}) copy-start(f32[128,256]{1,0:T(8,128)} %param.7) | copy-start | bytes 393220
  57.4 8.1 %collective-permute-start.17 = (f32[224,256]{1,0:T(8,128)S(1)}, f32[224,256]{1,0:T(8,128)S(1)}, u32[]{:S(2)}, u32[]{:S(2)}) collective-permute-start(f32[224,256]{1,0:T(8,128)S(1)} %get-tuple-element.70), channel_id=1, source_target_pairs={{0,1},{1,0},{2,3},{3,2},{4,5},{5,4},{6,7},{7,6},{8,9},{9,8},{10,11... | collective-permute-start | bytes 688136 | tf_op jit(solution)/shard_map/ppermute | solution.py:338
  58.7 8.5 %collective-permute-start.18 = (f32[128,256]{1,0:T(8,128)S(1)}, f32[128,256]{1,0:T(8,128)S(1)}, u32[]{:S(2)}, u32[]{:S(2)}) collective-permute-start(f32[128,256]{1,0:T(8,128)S(1)} %get-tuple-element.73), channel_id=1, source_target_pairs={{0,2},{1,3},{2,4},{3,5},{4,6},{5,7},{6,0},{7,1},{8,10},{9,11},{10,... | collective-permute-start | bytes 393224 | tf_op jit(solution)/shard_map/ppermute | solution.py:496
  61.6 9.8 %collective-permute-start.19 = (f32[128,256]{1,0:T(8,128)S(1)}, f32[128,256]{1,0:T(8,128)S(1)}, u32[]{:S(2)}, u32[]{:S(2)}) collective-permute-start(f32[128,256]{1,0:T(8,128)S(1)} %get-tuple-element.74), channel_id=1, source_target_pairs={{0,4},{1,5},{2,6},{3,7},{4,0},{5,1},{6,2},{7,3},{8,12},{9,13},{10,... | collective-permute-start | bytes 393224 | tf_op jit(solution)/shard_map/ppermute | solution.py:496
  63.3 8.1 %collective-permute-start.20 = (f32[128,256]{1,0:T(8,128)S(1)}, f32[128,256]{1,0:T(8,128)S(1)}, u32[]{:S(2)}, u32[]{:S(2)}) collective-permute-start(f32[128,256]{1,0:T(8,128)S(1)} %get-tuple-element.75), channel_id=1, source_target_pairs={{0,6},{1,7},{2,0},{3,1},{4,2},{5,3},{6,4},{7,5},{8,14},{9,15},{10,... | collective-permute-start | bytes 393224 | tf_op jit(solution)/shard_map/ppermute | solution.py:496

commit v10 on v9

--- a/solution.py
+++ b/solution.py
@@ -238,25 +238,26 @@
             uh_ref[k], ul_ref[k] = cut(us_ref, names, owner, width, w)
 
 
-def far_terms(first, uh_ref, ul_ref, image, block_refs):
+def far_terms(places, uh_ref, ul_ref, image, block_refs):
     rows = image.shape[0]
-    for k, block_ref in enumerate(block_refs):
-        image = image + block_term(block_ref, uh_ref[first + 2 * k], ul_ref[first + 2 * k], rows)
+    for k, block_ref in zip(places, block_refs):
+        image = image + block_term(block_ref, uh_ref[k], ul_ref[k], rows)
     return image
 
 
-def far_kernel(first, uh_ref, ul_ref, part_ref, *refs):
-    refs[-1][...] = far_terms(first, uh_ref, ul_ref, part_ref[...], refs[:-1])
+def far_kernel(uh_ref, ul_ref, part_ref, *refs):
+    places = [0] + list(range(1, uh_ref.shape[0], 2))
+    refs[-1][...] = far_terms(places, uh_ref, ul_ref, part_ref[...], refs[:-1])
 
 
 def image_kernel(direct, uh_ref, ul_ref, part_ref, to_ref, *refs):
-    n_in = uh_ref.shape[0] // 2 if direct else 1
+    n_in = (uh_ref.shape[0] - 1) // 2 if direct else 1
     block_refs, out_refs = refs[:n_in], refs[n_in:]
     n_out = len(out_refs)
     rows = part_ref.shape[0]
     image = part_ref[...]
     if direct:
-        image = far_terms(1, uh_ref, ul_ref, image, block_refs)
+        image = far_terms(range(2, uh_ref.shape[0], 2), uh_ref, ul_ref, image, block_refs)
     else:
         stack = block_refs[0]
         add = lambda b, v: v + block_term(stack.at[b], uh_ref[b], ul_ref[b], rows)
@@ -322,7 +323,7 @@
 
 def call(kernel, out_shape, *args, flops=0, vmem=20, **kw):
     many = isinstance(out_shape, (list, tuple))
-    size = sum(v.size * v.dtype.itemsize for v in jax.tree.leaves((out_shape, args)))
+    size = flops and sum(v.size * v.dtype.itemsize for v in jax.tree.leaves((out_shape, args)))
     kw = {"in_specs": [VMEM] * len(args)} | kw
     return pl.pallas_call(
         kernel,
@@ -425,32 +426,28 @@
         *late,
         flops=term,
     )
-    halves = bf16(nr - 2 if direct else nr, WIDE, w)
-    near = []
-    if direct:
-        again, _ = lax.optimization_barrier((chosen, u_all[1]))
-        near = [chosen, swap(again, "prow", nr)]
+    halves = bf16(nr - 1 if direct else nr, WIDE, w)
+    near = [chosen] if direct else []
     image, uh, ul = call(
-        functools.partial(near_kernel, lambda r: owners(r)[:2], (lambda r: owners(r)[2:]) if direct else None),
+        functools.partial(near_kernel, lambda r: owners(r)[:1], (lambda r: owners(r)[1:]) if direct else None),
         [f32(rows, w), halves, halves],
         names,
         us,
         *near,
-        flops=3 * term,
-    )
-    if direct:
-        beside, later = [], []
+        flops=0,
+    )
+    if direct:
+        beside, later = [swap(chosen, "prow", nr)], []
         for t in range(1, nr // 2):
             far = lax.ppermute(chosen, "prow", [(k, (k + 2 * t) % nr) for k in range(nr)])
             far, _ = lax.optimization_barrier((far, image))
             beside.append(far)
             later.append(swap(far, "prow", nr))
-        image = call(functools.partial(far_kernel, 0), f32(rows, w), uh, ul, image, *beside, flops=term)
+        image = call(far_kernel, f32(rows, w), uh, ul, image, *beside, flops=1 * term)
     else:
         later = [lax.all_gather(chosen, "prow")]
     if direct:
-        owned = spread(own, nr, beside[0])
-        owned[1], to = lax.optimization_barrier((owned[1], to))
+        owned = spread(own, nr, beside[1])
     sent = call(
         functools.partial(image_kernel, direct),
         [f32(nc * slots, w)] + [f32(2 * slots, w)] * ((nz - 1) * direct),

time: 72.7 us -> 69.3 us (0.953)
  waiting for transfers between devices: 28.2 us -> 24.7 us
    ppermute x4, waiting for transfers between devices: 14.8 us -> 10.4 us  [ring_gather(): lax.ppermute(up, 'pcol', pairs)]
    ppermute x3, waiting for transfers between devices: 4.89 us -> 8.29 us  [per_device(): lax.ppermute(terms[t], 'pcol', [(k, (k + 2 * t) % nc) for k in range(nc)])]
    ppermute x5, waiting for transfers between devices: 4.06 us -> 1.96 us  [swap(): return lax.ppermute(v, axis, [(k, k ^ 1) for k in range(size)])]
    ppermute x2, waiting for transfers between devices: 2.51 us -> 1.11 us  [spread(): lax.ppermute(v, 'prow', [(k, (k + 2 * t) % size ^ flip) for k in range(si...]
    ppermute x3, waiting for transfers between devices: 0.42 us -> 1.42 us  [per_device(): lax.ppermute(sent[t], 'pcol', [(k, (k + 2 * t) % nc) for k in range(nc)])]
  transfers between devices with their start and end apart: 21 -> 21, of which waited for: 14 -> 11; matrix products, arithmetic and copies ran while one was open for 0% -> 0% of each run, Pallas kernels for 19% -> 20%
where the time goes in v10:
time: 69.3 us; the launch traced here: 69.1 us
  starting transfers between devices  27.3 us (39%)
  waiting for transfers between devices  24.7 us (36%)
  Pallas kernels  14.9 us (22%)
  between operations  0.76 us (1%)
  local copies, waits for them, and re-layouts  0.71 us (1%)
  other arithmetic  0.7 us (1%)
    pallas_call x11, Pallas kernels, call(): pl.pallas_call(kernel, out_shape=out_shape, out_specs=[VMEM] * len(out_sh...  14.9 us
    ppermute x4, waiting for transfers between devices, ring_gather(): lax.ppermute(up, 'pcol', pairs)  10.4 us
    ppermute x3, waiting for transfers between devices, per_device(): lax.ppermute(terms[t], 'pcol', [(k, (k + 2 * t) % nc) for k in range(nc)])  8.29 us
    ppermute x4, starting transfers between devices, ring_gather(): lax.ppermute(up, 'pcol', pairs)  7.81 us
    ppermute x3, starting transfers between devices, per_device(): lax.ppermute(sent[t], 'pcol', [(k, (k + 2 * t) % nc) for k in range(nc)])  7.7 us
    ppermute x3, starting transfers between devices, per_device(): lax.ppermute(terms[t], 'pcol', [(k, (k + 2 * t) % nc) for k in range(nc)])  4.64 us
    ppermute x5, starting transfers between devices, swap(): return lax.ppermute(v, axis, [(k, k ^ 1) for k in range(size)])  2.64 us
    ppermute x1, starting transfers between devices, per_device(): lax.ppermute(chosen, 'prow', [(k, (k + 2 * t) % nr) for k in range(nr)])  2.03 us
  transfers between devices with their start and end apart: 21, of which 11 were waited for; matrix products, arithmetic and copies ran while one was open for 0% of the time, Pallas kernels for 20%

profile of v10, /device:TPU:0, one launch (start us, length us, event | category | flops | bytes accessed | tf_op | source)
XLA Modules:
  0.0 69.1 jit_solution(12338424552745197622)
XLA Ops:
  0.6 3.1 %collective-permute-start = (f32[224,256]{1,0:T(8,128)}, f32[224,256]{1,0:T(8,128)S(1)}, u32[]{:S(2)}, u32[]{:S(2)}) collective-permute-start(f32[224,256]{1,0:T(8,128)} %refs_0_.1), channel_id=1, source_target_pairs={{1,0},{0,2},{2,4},{4,6},{6,7},{7,5},{5,3},{3,1},{9,8},{8,10},{10,1... | collective-permute-start | bytes 688136 | tf_op jit(solution)/shard_map/ppermute | solution.py:366
  4.4 2.7 %shard_map.62.refs_0_ = f32[2016,128]{1,0:T(8,128)S(1)} custom-call(s32[1792]{0:T(1024)S(1)} %copy-done, f32[448,896]{1,0:T(8,128)} %sigma_ref.1), custom_call_target="tpu_custom_call" | custom-call | flops 1027604480 | bytes 2644992 | tf_op jit(solution)/shard_map/pallas_call | solution.py:328
  7.1 2.0 %collective-permute-start.8 = (f32[2016,128]{1,0:T(8,128)S(1)}, f32[2016,128]{1,0:T(8,128)S(1)}, u32[]{:S(2)}, u32[]{:S(2)}) collective-permute-start(f32[2016,128]{1,0:T(8,128)S(1)} %shard_map.62.refs_0_), channel_id=1, source_target_pairs={{0,16},{8,24},{16,0},{24,8},{1,17},{9,25},{17,1},{25,9},{2,18},{10... | collective-permute-start | bytes 3096584 | tf_op jit(solution)/shard_map/ppermute | solution.py:442
  9.4 1.5 %collective-permute-done.1.refs_2_ = f32[224,256]{1,0:T(8,128)S(1)} collective-permute-done((f32[224,256]{1,0:T(8,128)}, f32[224,256]{1,0:T(8,128)S(1)}, u32[]{:S(2)}, u32[]{:S(2)}) %collective-permute-start.1) | collective-permute-done | bytes 229408 | tf_op jit(solution)/shard_map/ppermute | solution.py:366
  11.0 1.6 %collective-permute-start.2 = (f32[224,256]{1,0:T(8,128)S(1)}, f32[224,256]{1,0:T(8,128)S(1)}, u32[]{:S(2)}, u32[]{:S(2)}) collective-permute-start(f32[224,256]{1,0:T(8,128)S(1)} %collective-permute-done.refs_1_), channel_id=1, source_target_pairs={{1,0},{0,2},{2,4},{4,6},{6,7},{7,5},{5,3},{3,1},{9,8},{8,10},{10,1... | collective-permute-start | bytes 688136 | tf_op jit(solution)/shard_map/ppermute | solution.py:366
  13.0 4.1 %collective-permute-done.2.refs_3_ = f32[224,256]{1,0:T(8,128)S(1)} collective-permute-done((f32[224,256]{1,0:T(8,128)S(1)}, f32[224,256]{1,0:T(8,128)S(1)}, u32[]{:S(2)}, u32[]{:S(2)}) %collective-permute-start.2) | collective-permute-done | bytes 229408 | tf_op jit(solution)/shard_map/ppermute | solution.py:366
  17.1 1.6 %collective-permute-start.4 = (f32[224,256]{1,0:T(8,128)S(1)}, f32[224,256]{1,0:T(8,128)S(1)}, u32[]{:S(2)}, u32[]{:S(2)}) collective-permute-start(f32[224,256]{1,0:T(8,128)S(1)} %collective-permute-done.2.refs_3_), channel_id=1, source_target_pairs={{1,0},{0,2},{2,4},{4,6},{6,7},{7,5},{5,3},{3,1},{9,8},{8,10},{10,1... | collective-permute-start | bytes 688136 | tf_op jit(solution)/shard_map/ppermute | solution.py:366
  19.2 2.1 %shard_map.59 = (bf16[448,448]{1,0:T(8,128)(2,1)S(1)}, bf16[576,896]{1,0:T(8,128)(2,1)S(1)}, bf16[224,448]{1,0:T(8,128)(2,1)S(1)}) custom-call(s32[1792]{0:T(1024)S(1)} %copy-done), custom_call_target="tpu_custom_call" | custom-call | tf_op jit(solution)/shard_map/pallas_call | solution.py:328
  21.2 1.9 %collective-permute-done.4.refs_5_ = f32[224,256]{1,0:T(8,128)S(1)} collective-permute-done((f32[224,256]{1,0:T(8,128)S(1)}, f32[224,256]{1,0:T(8,128)S(1)}, u32[]{:S(2)}, u32[]{:S(2)}) %collective-permute-start.4) | collective-permute-done | bytes 229408 | tf_op jit(solution)/shard_map/ppermute | solution.py:366
  23.2 1.6 %collective-permute-start.6 = (f32[224,256]{1,0:T(8,128)S(1)}, f32[224,256]{1,0:T(8,128)S(1)}, u32[]{:S(2)}, u32[]{:S(2)}) collective-permute-start(f32[224,256]{1,0:T(8,128)S(1)} %collective-permute-done.4.refs_5_), channel_id=1, source_target_pairs={{1,0},{0,2},{2,4},{4,6},{6,7},{7,5},{5,3},{3,1},{9,8},{8,10},{10,1... | collective-permute-start | bytes 688136 | tf_op jit(solution)/shard_map/ppermute | solution.py:370
  25.2 4.1 %collective-permute-done.6.refs_0_ = f32[224,256]{1,0:T(8,128)S(1)} collective-permute-done((f32[224,256]{1,0:T(8,128)S(1)}, f32[224,256]{1,0:T(8,128)S(1)}, u32[]{:S(2)}, u32[]{:S(2)}) %collective-permute-start.6) | collective-permute-done | bytes 229408 | tf_op jit(solution)/shard_map/ppermute | solution.py:370
  29.8 2.1 %shard_map.63 = (f32[448,256]{1,0:T(8,128)S(1)}, bf16[3,640,256]{2,1,0:T(8,128)(2,1)S(1)}, bf16[3,640,256]{2,1,0:T(8,128)(2,1)S(1)}) custom-call(s32[1792]{0:T(1024)S(1)} %copy-done, f32[2,2376,128]{2,1,0:T(8,128)S(1)} %get-tuple-element.41.us_ref, f32[2016,128]{1,0:T(8,128)S(1)} %shard_map.62.refs_0_), custom_call_target="tpu_custom_call" | custom-call | tf_op jit(solution)/shard_map/pallas_call | solution.py:328
  32.5 1.5 %collective-permute-start.14 = (f32[576,128]{1,0:T(8,128)S(1)}, f32[576,128]{1,0:T(8,128)S(1)}, u32[]{:S(2)}, u32[]{:S(2)}) collective-permute-start(f32[576,128]{1,0:T(8,128)S(1)} %get-tuple-element.53.refs_0_), channel_id=1, source_target_pairs={{0,16},{8,24},{16,0},{24,8},{1,17},{9,25},{17,1},{25,9},{2,18},{10... | collective-permute-start | bytes 884744 | tf_op jit(solution)/shard_map/ppermute | solution.py:347
  34.1 1.1 %shard_map.64.part_ref = f32[448,256]{1,0:T(8,128)S(1)} custom-call(bf16[3,640,256]{2,1,0:T(8,128)(2,1)S(1)} %get-tuple-element.42.uh_ref, bf16[3,640,256]{2,1,0:T(8,128)(2,1)S(1)} %get-tuple-element.43.ul_ref, f32[448,256]{1,0:T(8,128)S(1)} %get-tuple-element.44.part_ref, f32[2016,128]{1,0:T(8,128)S(1)} %collective-permute-done.7.refs_0_, ...), custom_call_target="tpu_custom_call" | custom-call | flops 440401920 | bytes 4947968 | tf_op jit(solution)/shard_map/pallas_call | solution.py:328
  35.2 1.8 %shard_map.65 = (f32[448,256]{1,0:T(8,128)S(1)}, f32[112,256]{1,0:T(8,128)S(1)}, f32[112,256]{1,0:T(8,128)S(1)}, f32[112,256]{1,0:T(8,128)S(1)}) custom-call(bf16[3,640,256]{2,1,0:T(8,128)(2,1)S(1)} %get-tuple-element.42.uh_ref, bf16[3,640,256]{2,1,0:T(8,128)(2,1)S(1)} %get-tuple-element.43.ul_ref, f32[448,256]{1,0:T(8,128)S(1)} %shard_map.64.part_ref, ...), custom_call_target="tpu_custom_call" | custom-call | flops 440401920 | bytes 4661248 | tf_op jit(solution)/shard_map/pallas_call | solution.py:328
  37.0 1.1 %collective-permute-start.16 = (f32[448,256]{1,0:T(8,128)S(1)}, f32[448,256]{1,0:T(8,128)S(1)}, u32[]{:S(2)}, u32[]{:S(2)}) collective-permute-start(f32[448,256]{1,0:T(8,128)S(1)} %get-tuple-element.55.refs_0_.mine_ref), channel_id=1, source_target_pairs={{0,1},{1,0},{2,3},{3,2},{4,5},{5,4},{6,7},{7,6},{8,9},{9,8},{10,11... | collective-permute-start | bytes 1376264 | tf_op jit(solution)/shard_map/ppermute | solution.py:339
  38.2 1.6 %collective-permute-start.10 = (f32[112,256]{1,0:T(8,128)S(1)}, f32[112,256]{1,0:T(8,128)S(1)}, u32[]{:S(2)}, u32[]{:S(2)}) collective-permute-start(f32[112,256]{1,0:T(8,128)S(1)} %get-tuple-element.48), channel_id=1, source_target_pairs={{0,2},{1,3},{2,4},{3,5},{4,6},{5,7},{6,0},{7,1},{8,10},{9,11},{10,... | collective-permute-start | bytes 344072 | tf_op jit(solution)/shard_map/ppermute | solution.py:466
  39.7 2.6 %collective-permute-start.11 = (f32[112,256]{1,0:T(8,128)S(1)}, f32[112,256]{1,0:T(8,128)S(1)}, u32[]{:S(2)}, u32[]{:S(2)}) collective-permute-start(f32[112,256]{1,0:T(8,128)S(1)} %get-tuple-element.49), channel_id=1, source_target_pairs={{0,4},{1,5},{2,6},{3,7},{4,0},{5,1},{6,2},{7,3},{8,12},{9,13},{10,... | collective-permute-start | bytes 344072 | tf_op jit(solution)/shard_map/ppermute | solution.py:466
  42.4 3.5 %collective-permute-start.12 = (f32[112,256]{1,0:T(8,128)S(1)}, f32[112,256]{1,0:T(8,128)S(1)}, u32[]{:S(2)}, u32[]{:S(2)}) collective-permute-start(f32[112,256]{1,0:T(8,128)S(1)} %get-tuple-element.50), channel_id=1, source_target_pairs={{0,6},{1,7},{2,0},{3,1},{4,2},{5,3},{6,4},{7,5},{8,14},{9,15},{10,... | collective-permute-start | bytes 344072 | tf_op jit(solution)/shard_map/ppermute | solution.py:466
  47.0 2.0 %shard_map.66 = (bf16[4,128,896]{2,1,0:T(8,128)(2,1)S(1)}, bf16[4,128,896]{2,1,0:T(8,128)(2,1)S(1)}) custom-call(bf16[576,896]{1,0:T(8,128)(2,1)S(1)} %get-tuple-element.51.place_ref, f32[576,128]{1,0:T(8,128)S(1)} %get-tuple-element.53.refs_0_, f32[576,128]{1,0:T(8,128)S(1)} %collective-permute-done.13.refs_1_, ...), custom_call_target="tpu_custom_call" | custom-call | flops 1056964608 | bytes 4046848 | tf_op jit(solution)/shard_map/pallas_call | solution.py:328
  49.0 1.4 %collective-permute-done.11.refs_2_ = f32[112,256]{1,0:T(8,128)S(1)} collective-permute-done((f32[112,256]{1,0:T(8,128)S(1)}, f32[112,256]{1,0:T(8,128)S(1)}, u32[]{:S(2)}, u32[]{:S(2)}) %collective-permute-start.11) | collective-permute-done | bytes 114720 | tf_op jit(solution)/shard_map/ppermute | solution.py:466
  52.4 4.1 %collective-permute-start.20 = (f32[128,256]{1,0:T(8,128)S(1)}, f32[128,256]{1,0:T(8,128)S(1)}, u32[]{:S(2)}, u32[]{:S(2)}) collective-permute-start(f32[128,256]{1,0:T(8,128)S(1)} %get-tuple-element.69), channel_id=1, source_target_pairs={{0,6},{1,7},{2,0},{3,1},{4,2},{5,3},{6,4},{7,5},{8,14},{9,15},{10,... | collective-permute-start | bytes 393224 | tf_op jit(solution)/shard_map/ppermute | solution.py:493
  57.1 1.9 %collective-permute-done.17.other_ref = f32[224,256]{1,0:T(8,128)S(1)} collective-permute-done((f32[224,256]{1,0:T(8,128)S(1)}, f32[224,256]{1,0:T(8,128)S(1)}, u32[]{:S(2)}, u32[]{:S(2)}) %collective-permute-start.17) | collective-permute-done | bytes 229408 | tf_op jit(solution)/shard_map/ppermute | solution.py:339
  60.4 7.9 %collective-permute-done.19 = f32[128,256]{1,0:T(8,128)S(1)} collective-permute-done((f32[128,256]{1,0:T(8,128)S(1)}, f32[128,256]{1,0:T(8,128)S(1)}, u32[]{:S(2)}, u32[]{:S(2)}) %collective-permute-start.19) | collective-permute-done | bytes 131104 | tf_op jit(solution)/shard_map/ppermute | solution.py:493
  (36 shorter events, 9.2 us)
Async XLA Ops:
  0.6 8.8 %collective-permute-start = (f32[224,256]{1,0:T(8,128)}, f32[224,256]{1,0:T(8,128)S(1)}, u32[]{:S(2)}, u32[]{:S(2)}) collective-permute-start(f32[224,256]{1,0:T(8,128)} %refs_0_.1), channel_id=1, source_target_pairs={{1,0},{0,2},{2,4},{4,6},{6,7},{7,5},{5,3},{3,1},{9,8},{8,10},{10,1... | collective-permute-start | bytes 688136 | tf_op jit(solution)/shard_map/ppermute | solution.py:366
  3.7 7.3 %collective-permute-start.1 = (f32[224,256]{1,0:T(8,128)}, f32[224,256]{1,0:T(8,128)S(1)}, u32[]{:S(2)}, u32[]{:S(2)}) collective-permute-start(f32[224,256]{1,0:T(8,128)} %refs_0_.1), channel_id=1, source_target_pairs={{0,1},{2,0},{4,2},{6,4},{7,6},{5,7},{3,5},{1,3},{8,9},{10,8},{12,1... | collective-permute-start | bytes 688136 | tf_op jit(solution)/shard_map/ppermute | solution.py:366
  3.7 0.7 %copy-start = (s32[1792]{0:T(1024)S(1)}, s32[1792]{0:T(1024)}, u32[]{:S(2)}) copy-start(s32[1792]{0:T(1024)} %structure_ref.7) | copy-start | bytes 21508
  4.4 20.3 %copy-start.1 = (f32[224,256]{1,0:T(8,128)S(1)}, f32[224,256]{1,0:T(8,128)}, u32[]{:S(2)}) copy-start(f32[224,256]{1,0:T(8,128)} %refs_0_.1) | copy-start | bytes 688132
  7.1 24.8 %collective-permute-start.8 = (f32[2016,128]{1,0:T(8,128)S(1)}, f32[2016,128]{1,0:T(8,128)S(1)}, u32[]{:S(2)}, u32[]{:S(2)}) collective-permute-start(f32[2016,128]{1,0:T(8,128)S(1)} %shard_map.62.refs_0_), channel_id=1, source_target_pairs={{0,16},{8,24},{16,0},{24,8},{1,17},{9,25},{17,1},{25,9},{2,18},{10... | collective-permute-start | bytes 3096584 | tf_op jit(solution)/shard_map/ppermute | solution.py:442
  11.0 6.2 %collective-permute-start.2 = (f32[224,256]{1,0:T(8,128)S(1)}, f32[224,256]{1,0:T(8,128)S(1)}, u32[]{:S(2)}, u32[]{:S(2)}) collective-permute-start(f32[224,256]{1,0:T(8,128)S(1)} %collective-permute-done.refs_1_), channel_id=1, source_target_pairs={{1,0},{0,2},{2,4},{4,6},{6,7},{7,5},{5,3},{3,1},{9,8},{8,10},{10,1... | collective-permute-start | bytes 688136 | tf_op jit(solution)/shard_map/ppermute | solution.py:366
  12.6 6.2 %collective-permute-start.3 = (f32[224,256]{1,0:T(8,128)S(1)}, f32[224,256]{1,0:T(8,128)S(1)}, u32[]{:S(2)}, u32[]{:S(2)}) collective-permute-start(f32[224,256]{1,0:T(8,128)S(1)} %collective-permute-done.1.refs_2_), channel_id=1, source_target_pairs={{0,1},{2,0},{4,2},{6,4},{7,6},{5,7},{3,5},{1,3},{8,9},{10,8},{12,1... | collective-permute-start | bytes 688136 | tf_op jit(solution)/shard_map/ppermute | solution.py:366
  17.1 6.0 %collective-permute-start.4 = (f32[224,256]{1,0:T(8,128)S(1)}, f32[224,256]{1,0:T(8,128)S(1)}, u32[]{:S(2)}, u32[]{:S(2)}) collective-permute-start(f32[224,256]{1,0:T(8,128)S(1)} %collective-permute-done.2.refs_3_), channel_id=1, source_target_pairs={{1,0},{0,2},{2,4},{4,6},{6,7},{7,5},{5,3},{3,1},{9,8},{8,10},{10,1... | collective-permute-start | bytes 688136 | tf_op jit(solution)/shard_map/ppermute | solution.py:366
  18.7 6.0 %collective-permute-start.5 = (f32[224,256]{1,0:T(8,128)S(1)}, f32[224,256]{1,0:T(8,128)S(1)}, u32[]{:S(2)}, u32[]{:S(2)}) collective-permute-start(f32[224,256]{1,0:T(8,128)S(1)} %collective-permute-done.3.refs_4_), channel_id=1, source_target_pairs={{0,1},{2,0},{4,2},{6,4},{7,6},{5,7},{3,5},{1,3},{8,9},{10,8},{12,1... | collective-permute-start | bytes 688136 | tf_op jit(solution)/shard_map/ppermute | solution.py:366
  19.2 14.9 %collective-permute-start.7 = (f32[2016,128]{1,0:T(8,128)S(1)}, f32[2016,128]{1,0:T(8,128)S(1)}, u32[]{:S(2)}, u32[]{:S(2)}) collective-permute-start(f32[2016,128]{1,0:T(8,128)S(1)} %shard_map.62.refs_0_), channel_id=1, source_target_pairs={{0,8},{8,0},{16,24},{24,16},{1,9},{9,1},{17,25},{25,17},{2,10},{10... | collective-permute-start | bytes 3096584 | tf_op jit(solution)/shard_map/ppermute | solution.py:339
  23.2 6.2 %collective-permute-start.6 = (f32[224,256]{1,0:T(8,128)S(1)}, f32[224,256]{1,0:T(8,128)S(1)}, u32[]{:S(2)}, u32[]{:S(2)}) collective-permute-start(f32[224,256]{1,0:T(8,128)S(1)} %collective-permute-done.4.refs_5_), channel_id=1, source_target_pairs={{1,0},{0,2},{2,4},{4,6},{6,7},{7,5},{5,3},{3,1},{9,8},{8,10},{10,1... | collective-permute-start | bytes 688136 | tf_op jit(solution)/shard_map/ppermute | solution.py:370
  32.0 3.3 %collective-permute-start.9 = (f32[2016,128]{1,0:T(8,128)S(1)}, f32[2016,128]{1,0:T(8,128)S(1)}, u32[]{:S(2)}, u32[]{:S(2)}) collective-permute-start(f32[2016,128]{1,0:T(8,128)S(1)} %collective-permute-done.8.refs_1_), channel_id=1, source_target_pairs={{0,8},{8,0},{16,24},{24,16},{1,9},{9,1},{17,25},{25,17},{2,10},{10... | collective-permute-start | bytes 3096584 | tf_op jit(solution)/shard_map/ppermute | solution.py:339
  32.0 7.7 %collective-permute-start.13 = (f32[576,128]{1,0:T(8,128)S(1)}, f32[576,128]{1,0:T(8,128)S(1)}, u32[]{:S(2)}, u32[]{:S(2)}) collective-permute-start(f32[576,128]{1,0:T(8,128)S(1)} %get-tuple-element.53.refs_0_), channel_id=1, source_target_pairs={{0,8},{8,0},{16,24},{24,16},{1,9},{9,1},{17,25},{25,17},{2,10},{10... | collective-permute-start | bytes 884744 | tf_op jit(solution)/shard_map/ppermute | solution.py:339
  32.5 9.9 %collective-permute-start.14 = (f32[576,128]{1,0:T(8,128)S(1)}, f32[576,128]{1,0:T(8,128)S(1)}, u32[]{:S(2)}, u32[]{:S(2)}) collective-permute-start(f32[576,128]{1,0:T(8,128)S(1)} %get-tuple-element.53.refs_0_), channel_id=1, source_target_pairs={{0,16},{8,24},{16,0},{24,8},{1,17},{9,25},{17,1},{25,9},{2,18},{10... | collective-permute-start | bytes 884744 | tf_op jit(solution)/shard_map/ppermute | solution.py:347
  34.1 12.9 %collective-permute-start.15 = (f32[576,128]{1,0:T(8,128)S(1)}, f32[576,128]{1,0:T(8,128)S(1)}, u32[]{:S(2)}, u32[]{:S(2)}) collective-permute-start(f32[576,128]{1,0:T(8,128)S(1)} %get-tuple-element.53.refs_0_), channel_id=1, source_target_pairs={{0,24},{8,16},{16,8},{24,0},{1,25},{9,17},{17,9},{25,1},{2,26},{10... | collective-permute-start | bytes 884744 | tf_op jit(solution)/shard_map/ppermute | solution.py:347
  37.0 13.5 %collective-permute-start.16 = (f32[448,256]{1,0:T(8,128)S(1)}, f32[448,256]{1,0:T(8,128)S(1)}, u32[]{:S(2)}, u32[]{:S(2)}) collective-permute-start(f32[448,256]{1,0:T(8,128)S(1)} %get-tuple-element.55.refs_0_.mine_ref), channel_id=1, source_target_pairs={{0,1},{1,0},{2,3},{3,2},{4,5},{5,4},{6,7},{7,6},{8,9},{9,8},{10,11... | collective-permute-start | bytes 1376264 | tf_op jit(solution)/shard_map/ppermute | solution.py:339
  38.2 10.8 %collective-permute-start.10 = (f32[112,256]{1,0:T(8,128)S(1)}, f32[112,256]{1,0:T(8,128)S(1)}, u32[]{:S(2)}, u32[]{:S(2)}) collective-permute-start(f32[112,256]{1,0:T(8,128)S(1)} %get-tuple-element.48), channel_id=1, source_target_pairs={{0,2},{1,3},{2,4},{3,5},{4,6},{5,7},{6,0},{7,1},{8,10},{9,11},{10,... | collective-permute-start | bytes 344072 | tf_op jit(solution)/shard_map/ppermute | solution.py:466
  39.7 10.7 %collective-permute-start.11 = (f32[112,256]{1,0:T(8,128)S(1)}, f32[112,256]{1,0:T(8,128)S(1)}, u32[]{:S(2)}, u32[]{:S(2)}) collective-permute-start(f32[112,256]{1,0:T(8,128)S(1)} %get-tuple-element.49), channel_id=1, source_target_pairs={{0,4},{1,5},{2,6},{3,7},{4,0},{5,1},{6,2},{7,3},{8,12},{9,13},{10,... | collective-permute-start | bytes 344072 | tf_op jit(solution)/shard_map/ppermute | solution.py:466
  42.4 8.0 %collective-permute-start.12 = (f32[112,256]{1,0:T(8,128)S(1)}, f32[112,256]{1,0:T(8,128)S(1)}, u32[]{:S(2)}, u32[]{:S(2)}) collective-permute-start(f32[112,256]{1,0:T(8,128)S(1)} %get-tuple-element.50), channel_id=1, source_target_pairs={{0,6},{1,7},{2,0},{3,1},{4,2},{5,3},{6,4},{7,5},{8,14},{9,15},{10,... | collective-permute-start | bytes 344072 | tf_op jit(solution)/shard_map/ppermute | solution.py:466
  50.5 17.9 %copy-start.2 = (f32[128,256]{1,0:T(8,128)S(1)}, f32[128,256]{1,0:T(8,128)}, u32[]{:S(2)}) copy-start(f32[128,256]{1,0:T(8,128)} %param.7) | copy-start | bytes 393220
  51.5 7.5 %collective-permute-start.17 = (f32[224,256]{1,0:T(8,128)S(1)}, f32[224,256]{1,0:T(8,128)S(1)}, u32[]{:S(2)}, u32[]{:S(2)}) collective-permute-start(f32[224,256]{1,0:T(8,128)S(1)} %get-tuple-element.64), channel_id=1, source_target_pairs={{0,1},{1,0},{2,3},{3,2},{4,5},{5,4},{6,7},{7,6},{8,9},{9,8},{10,11... | collective-permute-start | bytes 688136 | tf_op jit(solution)/shard_map/ppermute | solution.py:339
  52.4 8.0 %collective-permute-start.20 = (f32[128,256]{1,0:T(8,128)S(1)}, f32[128,256]{1,0:T(8,128)S(1)}, u32[]{:S(2)}, u32[]{:S(2)}) collective-permute-start(f32[128,256]{1,0:T(8,128)S(1)} %get-tuple-element.69), channel_id=1, source_target_pairs={{0,6},{1,7},{2,0},{3,1},{4,2},{5,3},{6,4},{7,5},{8,14},{9,15},{10,... | collective-permute-start | bytes 393224 | tf_op jit(solution)/shard_map/ppermute | solution.py:493
  56.5 11.9 %collective-permute-start.19 = (f32[128,256]{1,0:T(8,128)S(1)}, f32[128,256]{1,0:T(8,128)S(1)}, u32[]{:S(2)}, u32[]{:S(2)}) collective-permute-start(f32[128,256]{1,0:T(8,128)S(1)} %get-tuple-element.68), channel_id=1, source_target_pairs={{0,4},{1,5},{2,6},{3,7},{4,0},{5,1},{6,2},{7,3},{8,12},{9,13},{10,... | collective-permute-start | bytes 393224 | tf_op jit(solution)/shard_map/ppermute | solution.py:493
  56.8 11.6 %collective-permute-start.18 = (f32[128,256]{1,0:T(8,128)S(1)}, f32[128,256]{1,0:T(8,128)S(1)}, u32[]{:S(2)}, u32[]{:S(2)}) collective-permute-start(f32[128,256]{1,0:T(8,128)S(1)} %get-tuple-element.67), channel_id=1, source_target_pairs={{0,2},{1,3},{2,4},{3,5},{4,6},{5,7},{6,0},{7,1},{8,10},{9,11},{10,... | collective-permute-start | bytes 393224 | tf_op jit(solution)/shard_map/ppermute | solution.py:493

commit v11 on v10

--- a/solution.py
+++ b/solution.py
@@ -275,7 +275,7 @@
     z = lax.axis_index("pcol") // 2
 
     def put(owner, u_ref):
-        where = ((owner - z) & (nz - 1)) if direct else owner
+        where = (owner ^ z) if direct else owner
         high, low = split(u_ref[...].T)
         held_ref[pl.ds(pl.multiple_of(where * wd, wd), wd), :] = high
         held_ref[pl.ds(pl.multiple_of((where + nz) * wd, wd), wd), :] = low
@@ -293,13 +293,33 @@
         return dot(high_ref[t], sh) + (dot(high_ref[t], sl) + dot(low_ref[t], sh))
 
     if len(out_refs) > 1:
-        for t, out_ref in enumerate(out_refs):
-            out_ref[...] = term(t)
+        terms = [term(t) for t in range(4)]
+        half = terms[0].shape[1] // 2
+        for k, out_ref in enumerate(out_refs):
+            lanes = slice(0, half) if k < 2 else slice(half, None)
+            picked = ((0, 1), (2, 3), (0, 2), (1, 3))[k]
+            out_ref[...] = jnp.concatenate([terms[t][:, lanes] for t in picked], axis=0)
     else:
 
         @pl.loop(0, out_refs[0].shape[0])
         def _(t):
             out_refs[0][t] = term(t)
+
+
+def add_kernel(kept_ref, got_ref, mine_ref, next_ref):
+    n = mine_ref.shape[0]
+    mine_ref[...] = kept_ref[:n, :] + got_ref[:n, :]
+    next_ref[...] = kept_ref[n:, :] + got_ref[n:, :]
+
+
+def sum_kernel(kept_ref, got_ref, out_ref):
+    out_ref[...] = kept_ref[...] + got_ref[...]
+
+
+def final_kernel(d_ref, left_ref, got_ref, right_ref, out_ref):
+    half = left_ref.shape[1]
+    out_ref[:, :half] = d_ref[:, :half] + (left_ref[...] + got_ref[...])
+    out_ref[:, half:] = d_ref[:, half:] + right_ref[...]
 
 
 def part_kernel(slots, *refs):
@@ -390,7 +410,7 @@
     wd = w // 2
     n = structure.shape[0]
     slots = -(-rows // nc)
-    direct = nc <= 8
+    direct = (nr, nc) == (4, 8)
     names = structure
     groups = [[2 * k + x for k in range(nz)] for x in range(2)]
     owners = functools.partial(relative_owners, nr)
@@ -480,22 +500,26 @@
         scratch_shapes=[pltpu.VMEM((2 * nz * wd, CAP), BF16)],
         flops=8 * nz * wd * nc * slots * CAP,
     )
-    parts = [f32(wd, w)] * nz if direct else [f32(nz, wd, w)]
+    parts = [f32(2 * wd, w // 2)] * 4 if direct else [f32(nz, wd, w)]
     got, _ = lax.optimization_barrier((got, high))
     mine, theirs = call(functools.partial(part_kernel, slots), [f32(nz * slots, w)] * 2, *got, flops=2 * term)
     other, _ = lax.optimization_barrier((other, mine))
     terms = call(correction_kernel, parts, high, low, whole, other, flops=term)
     theirs, _ = lax.optimization_barrier((theirs, terms[0]))
     sigma_sj = call(pick_kernel, f32(m, w), source, mine, swap(theirs, "pcol", nc), flops=term // 4)
-    if direct:
-        total = terms[0]
-        for t in range(1, nz):
-            total = total + lax.ppermute(terms[t], "pcol", [(k, (k + 2 * t) % nc) for k in range(nc)])
-    else:
-        terms = lax.all_to_all(terms[0], "pcol", split_axis=0, concat_axis=0, axis_index_groups=groups, tiled=True)
-        total = jnp.sum(terms, axis=0)
     sigma_sj, d_term = lax.optimization_barrier((sigma_sj, d_term))
-    return sigma_sj, d_term + total
+    if direct:
+        meet = lambda v, by: lax.ppermute(v, "pcol", [(k, k ^ by) for k in range(nc)])
+        pieces = [f32(wd, w // 2)] * 2
+        from_far, from_near = meet(terms[1], 4), meet(terms[3], 2)
+        right, right_next = call(add_kernel, pieces, terms[2], from_near)
+        from_far, _ = lax.optimization_barrier((from_far, right))
+        left, left_next = call(add_kernel, pieces, terms[0], from_far)
+        right = call(sum_kernel, pieces[0], right, meet(right_next, 4), flops=4 * term)
+        sigma_jj = call(final_kernel, f32(wd, w), d_term, left, meet(left_next, 2), right)
+        return sigma_sj, sigma_jj
+    terms = lax.all_to_all(terms[0], "pcol", split_axis=0, concat_axis=0, axis_index_groups=groups, tiled=True)
+    return sigma_sj, d_term + jnp.sum(terms, axis=0)
 
 
 def solution(mesh):

time: 69.3 us -> 69.8 us (level)
  starting transfers between devices: 27.3 us -> 30.4 us
  waiting for transfers between devices: 24.7 us -> 21.9 us
  Pallas kernels: 14.9 us -> 15.8 us
  other arithmetic: 0.7 us -> 0 us
    ppermute x3 -> x4, starting transfers between devices: 4.64 us -> 7.79 us  [per_device(): lax.ppermute(v, 'pcol', [(k, k ^ by) for k in range(nc)])]
    ppermute x3 -> x4, waiting for transfers between devices: 8.29 us -> 5.99 us  [per_device(): lax.ppermute(v, 'pcol', [(k, k ^ by) for k in range(nc)])]
    pallas_call x11 -> x15, Pallas kernels: 14.9 us -> 15.8 us  [call(): pl.pallas_call(kernel, out_shape=out_shape, out_specs=[VMEM] * len(out_sh...]
  transfers between devices with their start and end apart: 21 -> 22, of which waited for: 11 -> 13; matrix products, arithmetic and copies ran while one was open for 0% -> 0% of each run, Pallas kernels for 20% -> 20%
where the time goes in v11:
time: 69.8 us; the launch traced here: 69.6 us
  starting transfers between devices  30.4 us (44%)
  waiting for transfers between devices  21.9 us (31%)
  Pallas kernels  15.8 us (23%)
  between operations  0.78 us (1%)
  local copies, waits for them, and re-layouts  0.71 us (1%)
    pallas_call x15, Pallas kernels, call(): pl.pallas_call(kernel, out_shape=out_shape, out_specs=[VMEM] * len(out_sh...  15.8 us
    ppermute x4, waiting for transfers between devices, ring_gather(): lax.ppermute(up, 'pcol', pairs)  10.4 us
    ppermute x4, starting transfers between devices, ring_gather(): lax.ppermute(up, 'pcol', pairs)  7.81 us
    ppermute x4, starting transfers between devices, per_device(): lax.ppermute(v, 'pcol', [(k, k ^ by) for k in range(nc)])  7.79 us
    ppermute x3, starting transfers between devices, per_device(): lax.ppermute(sent[t], 'pcol', [(k, (k + 2 * t) % nc) for k in range(nc)])  7.7 us
    ppermute x4, waiting for transfers between devices, per_device(): lax.ppermute(v, 'pcol', [(k, k ^ by) for k in range(nc)])  5.99 us
    ppermute x5, starting transfers between devices, swap(): return lax.ppermute(v, axis, [(k, k ^ 1) for k in range(size)])  2.64 us
    ppermute x1, starting transfers between devices, per_device(): lax.ppermute(chosen, 'prow', [(k, (k + 2 * t) % nr) for k in range(nr)])  2.03 us
  transfers between devices with their start and end apart: 22, of which 13 were waited for; matrix products, arithmetic and copies ran while one was open for 0% of the time, Pallas kernels for 20%

profile of v11, /device:TPU:0, one launch (start us, length us, event | category | flops | bytes accessed | tf_op | source)
XLA Modules:
  0.0 69.6 jit_solution(893142682834411679)
XLA Ops:
  0.6 3.1 %collective-permute-start = (f32[224,256]{1,0:T(8,128)}, f32[224,256]{1,0:T(8,128)S(1)}, u32[]{:S(2)}, u32[]{:S(2)}) collective-permute-start(f32[224,256]{1,0:T(8,128)} %refs_0_.1), channel_id=1, source_target_pairs={{1,0},{0,2},{2,4},{4,6},{6,7},{7,5},{5,3},{3,1},{9,8},{8,10},{10,1... | collective-permute-start | bytes 688136 | tf_op jit(solution)/shard_map/ppermute | solution.py:386
  4.4 2.7 %shard_map.62.refs_0_ = f32[2016,128]{1,0:T(8,128)S(1)} custom-call(s32[1792]{0:T(1024)S(1)} %copy-done.1, f32[448,896]{1,0:T(8,128)} %sigma_ref.1), custom_call_target="tpu_custom_call" | custom-call | flops 1027604480 | bytes 2644992 | tf_op jit(solution)/shard_map/pallas_call | solution.py:348
  7.1 2.0 %collective-permute-start.8 = (f32[2016,128]{1,0:T(8,128)S(1)}, f32[2016,128]{1,0:T(8,128)S(1)}, u32[]{:S(2)}, u32[]{:S(2)}) collective-permute-start(f32[2016,128]{1,0:T(8,128)S(1)} %shard_map.62.refs_0_), channel_id=1, source_target_pairs={{0,16},{8,24},{16,0},{24,8},{1,17},{9,25},{17,1},{25,9},{2,18},{10... | collective-permute-start | bytes 3096584 | tf_op jit(solution)/shard_map/ppermute | solution.py:462
  9.4 1.5 %collective-permute-done.1.refs_2_ = f32[224,256]{1,0:T(8,128)S(1)} collective-permute-done((f32[224,256]{1,0:T(8,128)}, f32[224,256]{1,0:T(8,128)S(1)}, u32[]{:S(2)}, u32[]{:S(2)}) %collective-permute-start.1) | collective-permute-done | bytes 229408 | tf_op jit(solution)/shard_map/ppermute | solution.py:386
  11.0 1.6 %collective-permute-start.2 = (f32[224,256]{1,0:T(8,128)S(1)}, f32[224,256]{1,0:T(8,128)S(1)}, u32[]{:S(2)}, u32[]{:S(2)}) collective-permute-start(f32[224,256]{1,0:T(8,128)S(1)} %collective-permute-done.refs_1_), channel_id=1, source_target_pairs={{1,0},{0,2},{2,4},{4,6},{6,7},{7,5},{5,3},{3,1},{9,8},{8,10},{10,1... | collective-permute-start | bytes 688136 | tf_op jit(solution)/shard_map/ppermute | solution.py:386
  13.0 4.1 %collective-permute-done.2.refs_3_ = f32[224,256]{1,0:T(8,128)S(1)} collective-permute-done((f32[224,256]{1,0:T(8,128)S(1)}, f32[224,256]{1,0:T(8,128)S(1)}, u32[]{:S(2)}, u32[]{:S(2)}) %collective-permute-start.2) | collective-permute-done | bytes 229408 | tf_op jit(solution)/shard_map/ppermute | solution.py:386
  17.1 1.6 %collective-permute-start.4 = (f32[224,256]{1,0:T(8,128)S(1)}, f32[224,256]{1,0:T(8,128)S(1)}, u32[]{:S(2)}, u32[]{:S(2)}) collective-permute-start(f32[224,256]{1,0:T(8,128)S(1)} %collective-permute-done.2.refs_3_), channel_id=1, source_target_pairs={{1,0},{0,2},{2,4},{4,6},{6,7},{7,5},{5,3},{3,1},{9,8},{8,10},{10,1... | collective-permute-start | bytes 688136 | tf_op jit(solution)/shard_map/ppermute | solution.py:386
  19.2 2.1 %shard_map.59 = (bf16[448,448]{1,0:T(8,128)(2,1)S(1)}, bf16[576,896]{1,0:T(8,128)(2,1)S(1)}, bf16[224,448]{1,0:T(8,128)(2,1)S(1)}) custom-call(s32[1792]{0:T(1024)S(1)} %copy-done.1), custom_call_target="tpu_custom_call" | custom-call | tf_op jit(solution)/shard_map/pallas_call | solution.py:348
  21.2 1.9 %collective-permute-done.4.refs_5_ = f32[224,256]{1,0:T(8,128)S(1)} collective-permute-done((f32[224,256]{1,0:T(8,128)S(1)}, f32[224,256]{1,0:T(8,128)S(1)}, u32[]{:S(2)}, u32[]{:S(2)}) %collective-permute-start.4) | collective-permute-done | bytes 229408 | tf_op jit(solution)/shard_map/ppermute | solution.py:386
  23.2 1.6 %collective-permute-start.6 = (f32[224,256]{1,0:T(8,128)S(1)}, f32[224,256]{1,0:T(8,128)S(1)}, u32[]{:S(2)}, u32[]{:S(2)}) collective-permute-start(f32[224,256]{1,0:T(8,128)S(1)} %collective-permute-done.4.refs_5_), channel_id=1, source_target_pairs={{1,0},{0,2},{2,4},{4,6},{6,7},{7,5},{5,3},{3,1},{9,8},{8,10},{10,1... | collective-permute-start | bytes 688136 | tf_op jit(solution)/shard_map/ppermute | solution.py:390
  25.2 4.1 %collective-permute-done.6.refs_0_ = f32[224,256]{1,0:T(8,128)S(1)} collective-permute-done((f32[224,256]{1,0:T(8,128)S(1)}, f32[224,256]{1,0:T(8,128)S(1)}, u32[]{:S(2)}, u32[]{:S(2)}) %collective-permute-start.6) | collective-permute-done | bytes 229408 | tf_op jit(solution)/shard_map/ppermute | solution.py:390
  29.8 2.1 %shard_map.63 = (f32[448,256]{1,0:T(8,128)S(1)}, bf16[3,640,256]{2,1,0:T(8,128)(2,1)S(1)}, bf16[3,640,256]{2,1,0:T(8,128)(2,1)S(1)}) custom-call(s32[1792]{0:T(1024)S(1)} %copy-done.1, f32[2,2376,128]{2,1,0:T(8,128)S(1)} %get-tuple-element.46.us_ref, f32[2016,128]{1,0:T(8,128)S(1)} %shard_map.62.refs_0_), custom_call_target="tpu_custom_call" | custom-call | tf_op jit(solution)/shard_map/pallas_call | solution.py:348
  32.5 1.5 %collective-permute-start.14 = (f32[576,128]{1,0:T(8,128)S(1)}, f32[576,128]{1,0:T(8,128)S(1)}, u32[]{:S(2)}, u32[]{:S(2)}) collective-permute-start(f32[576,128]{1,0:T(8,128)S(1)} %get-tuple-element.58.refs_0_), channel_id=1, source_target_pairs={{0,16},{8,24},{16,0},{24,8},{1,17},{9,25},{17,1},{25,9},{2,18},{10... | collective-permute-start | bytes 884744 | tf_op jit(solution)/shard_map/ppermute | solution.py:367
  35.2 1.8 %shard_map.65 = (f32[448,256]{1,0:T(8,128)S(1)}, f32[112,256]{1,0:T(8,128)S(1)}, f32[112,256]{1,0:T(8,128)S(1)}, f32[112,256]{1,0:T(8,128)S(1)}) custom-call(bf16[3,640,256]{2,1,0:T(8,128)(2,1)S(1)} %get-tuple-element.47.uh_ref, bf16[3,640,256]{2,1,0:T(8,128)(2,1)S(1)} %get-tuple-element.48.ul_ref, f32[448,256]{1,0:T(8,128)S(1)} %shard_map.64.part_ref, ...), custom_call_target="tpu_custom_call" | custom-call | flops 440401920 | bytes 4661248 | tf_op jit(solution)/shard_map/pallas_call | solution.py:348
  38.2 1.6 %collective-permute-start.10 = (f32[112,256]{1,0:T(8,128)S(1)}, f32[112,256]{1,0:T(8,128)S(1)}, u32[]{:S(2)}, u32[]{:S(2)}) collective-permute-start(f32[112,256]{1,0:T(8,128)S(1)} %get-tuple-element.53), channel_id=1, source_target_pairs={{0,2},{1,3},{2,4},{3,5},{4,6},{5,7},{6,0},{7,1},{8,10},{9,11},{10,... | collective-permute-start | bytes 344072 | tf_op jit(solution)/shard_map/ppermute | solution.py:486
  39.7 2.6 %collective-permute-start.11 = (f32[112,256]{1,0:T(8,128)S(1)}, f32[112,256]{1,0:T(8,128)S(1)}, u32[]{:S(2)}, u32[]{:S(2)}) collective-permute-start(f32[112,256]{1,0:T(8,128)S(1)} %get-tuple-element.54), channel_id=1, source_target_pairs={{0,4},{1,5},{2,6},{3,7},{4,0},{5,1},{6,2},{7,3},{8,12},{9,13},{10,... | collective-permute-start | bytes 344072 | tf_op jit(solution)/shard_map/ppermute | solution.py:486
  42.4 3.5 %collective-permute-start.12 = (f32[112,256]{1,0:T(8,128)S(1)}, f32[112,256]{1,0:T(8,128)S(1)}, u32[]{:S(2)}, u32[]{:S(2)}) collective-permute-start(f32[112,256]{1,0:T(8,128)S(1)} %get-tuple-element.55), channel_id=1, source_target_pairs={{0,6},{1,7},{2,0},{3,1},{4,2},{5,3},{6,4},{7,5},{8,14},{9,15},{10,... | collective-permute-start | bytes 344072 | tf_op jit(solution)/shard_map/ppermute | solution.py:486
  47.0 2.2 %shard_map.66 = (bf16[4,128,896]{2,1,0:T(8,128)(2,1)S(1)}, bf16[4,128,896]{2,1,0:T(8,128)(2,1)S(1)}) custom-call(bf16[576,896]{1,0:T(8,128)(2,1)S(1)} %get-tuple-element.56.place_ref, f32[576,128]{1,0:T(8,128)S(1)} %get-tuple-element.58.refs_0_, f32[576,128]{1,0:T(8,128)S(1)} %collective-permute-done.13.refs_1_, ...), custom_call_target="tpu_custom_call" | custom-call | flops 1056964608 | bytes 4046848 | tf_op jit(solution)/shard_map/pallas_call | solution.py:348
  51.5 3.0 %collective-permute-start.19 = (f32[256,128]{1,0:T(8,128)S(1)}, f32[256,128]{1,0:T(8,128)S(1)}, u32[]{:S(2)}, u32[]{:S(2)}) collective-permute-start(f32[256,128]{1,0:T(8,128)S(1)} %get-tuple-element.74), channel_id=1, source_target_pairs={{0,2},{1,3},{2,0},{3,1},{4,6},{5,7},{6,4},{7,5},{8,10},{9,11},{10,... | collective-permute-start | bytes 393224 | tf_op jit(solution)/shard_map/ppermute | solution.py:512
  54.5 1.6 %collective-permute-start.18 = (f32[256,128]{1,0:T(8,128)S(1)}, f32[256,128]{1,0:T(8,128)S(1)}, u32[]{:S(2)}, u32[]{:S(2)}) collective-permute-start(f32[256,128]{1,0:T(8,128)S(1)} %get-tuple-element.72), channel_id=1, source_target_pairs={{0,4},{1,5},{2,6},{3,7},{4,0},{5,1},{6,2},{7,3},{8,12},{9,13},{10,... | collective-permute-start | bytes 393224 | tf_op jit(solution)/shard_map/ppermute | solution.py:512
  56.1 2.5 %collective-permute-done.19.got_ref = f32[256,128]{1,0:T(8,128)S(1)} collective-permute-done((f32[256,128]{1,0:T(8,128)S(1)}, f32[256,128]{1,0:T(8,128)S(1)}, u32[]{:S(2)}, u32[]{:S(2)}) %collective-permute-start.19) | collective-permute-done | bytes 131104 | tf_op jit(solution)/shard_map/ppermute | solution.py:512
  58.6 2.8 %collective-permute-start.21 = (f32[128,128]{1,0:T(8,128)S(1)}, f32[128,128]{1,0:T(8,128)S(1)}, u32[]{:S(2)}, u32[]{:S(2)}) collective-permute-start(f32[128,128]{1,0:T(8,128)S(1)} %get-tuple-element.79), channel_id=1, source_target_pairs={{0,4},{1,5},{2,6},{3,7},{4,0},{5,1},{6,2},{7,3},{8,12},{9,13},{10,... | collective-permute-start | bytes 196616 | tf_op jit(solution)/shard_map/ppermute | solution.py:512
  62.4 2.2 %collective-permute-done.18.got_ref = f32[256,128]{1,0:T(8,128)S(1)} collective-permute-done((f32[256,128]{1,0:T(8,128)S(1)}, f32[256,128]{1,0:T(8,128)S(1)}, u32[]{:S(2)}, u32[]{:S(2)}) %collective-permute-start.18) | collective-permute-done | bytes 131104 | tf_op jit(solution)/shard_map/ppermute | solution.py:512
  65.8 1.6 %collective-permute-done.17.other_ref = f32[224,256]{1,0:T(8,128)S(1)} collective-permute-done((f32[224,256]{1,0:T(8,128)S(1)}, f32[224,256]{1,0:T(8,128)S(1)}, u32[]{:S(2)}, u32[]{:S(2)}) %collective-permute-start.17) | collective-permute-done | bytes 229408 | tf_op jit(solution)/shard_map/ppermute | solution.py:359
  (41 shorter events, 13.5 us)
Async XLA Ops:
  0.6 8.8 %collective-permute-start = (f32[224,256]{1,0:T(8,128)}, f32[224,256]{1,0:T(8,128)S(1)}, u32[]{:S(2)}, u32[]{:S(2)}) collective-permute-start(f32[224,256]{1,0:T(8,128)} %refs_0_.1), channel_id=1, source_target_pairs={{1,0},{0,2},{2,4},{4,6},{6,7},{7,5},{5,3},{3,1},{9,8},{8,10},{10,1... | collective-permute-start | bytes 688136 | tf_op jit(solution)/shard_map/ppermute | solution.py:386
  3.7 7.3 %collective-permute-start.1 = (f32[224,256]{1,0:T(8,128)}, f32[224,256]{1,0:T(8,128)S(1)}, u32[]{:S(2)}, u32[]{:S(2)}) collective-permute-start(f32[224,256]{1,0:T(8,128)} %refs_0_.1), channel_id=1, source_target_pairs={{0,1},{2,0},{4,2},{6,4},{7,6},{5,7},{3,5},{1,3},{8,9},{10,8},{12,1... | collective-permute-start | bytes 688136 | tf_op jit(solution)/shard_map/ppermute | solution.py:386
  4.4 20.3 %copy-start.2 = (f32[224,256]{1,0:T(8,128)S(1)}, f32[224,256]{1,0:T(8,128)}, u32[]{:S(2)}) copy-start(f32[224,256]{1,0:T(8,128)} %refs_0_.1) | copy-start | bytes 688132
  7.1 24.8 %collective-permute-start.8 = (f32[2016,128]{1,0:T(8,128)S(1)}, f32[2016,128]{1,0:T(8,128)S(1)}, u32[]{:S(2)}, u32[]{:S(2)}) collective-permute-start(f32[2016,128]{1,0:T(8,128)S(1)} %shard_map.62.refs_0_), channel_id=1, source_target_pairs={{0,16},{8,24},{16,0},{24,8},{1,17},{9,25},{17,1},{25,9},{2,18},{10... | collective-permute-start | bytes 3096584 | tf_op jit(solution)/shard_map/ppermute | solution.py:462
  11.0 6.2 %collective-permute-start.2 = (f32[224,256]{1,0:T(8,128)S(1)}, f32[224,256]{1,0:T(8,128)S(1)}, u32[]{:S(2)}, u32[]{:S(2)}) collective-permute-start(f32[224,256]{1,0:T(8,128)S(1)} %collective-permute-done.refs_1_), channel_id=1, source_target_pairs={{1,0},{0,2},{2,4},{4,6},{6,7},{7,5},{5,3},{3,1},{9,8},{8,10},{10,1... | collective-permute-start | bytes 688136 | tf_op jit(solution)/shard_map/ppermute | solution.py:386
  12.6 6.2 %collective-permute-start.3 = (f32[224,256]{1,0:T(8,128)S(1)}, f32[224,256]{1,0:T(8,128)S(1)}, u32[]{:S(2)}, u32[]{:S(2)}) collective-permute-start(f32[224,256]{1,0:T(8,128)S(1)} %collective-permute-done.1.refs_2_), channel_id=1, source_target_pairs={{0,1},{2,0},{4,2},{6,4},{7,6},{5,7},{3,5},{1,3},{8,9},{10,8},{12,1... | collective-permute-start | bytes 688136 | tf_op jit(solution)/shard_map/ppermute | solution.py:386
  17.1 6.0 %collective-permute-start.4 = (f32[224,256]{1,0:T(8,128)S(1)}, f32[224,256]{1,0:T(8,128)S(1)}, u32[]{:S(2)}, u32[]{:S(2)}) collective-permute-start(f32[224,256]{1,0:T(8,128)S(1)} %collective-permute-done.2.refs_3_), channel_id=1, source_target_pairs={{1,0},{0,2},{2,4},{4,6},{6,7},{7,5},{5,3},{3,1},{9,8},{8,10},{10,1... | collective-permute-start | bytes 688136 | tf_op jit(solution)/shard_map/ppermute | solution.py:386
  18.7 6.0 %collective-permute-start.5 = (f32[224,256]{1,0:T(8,128)S(1)}, f32[224,256]{1,0:T(8,128)S(1)}, u32[]{:S(2)}, u32[]{:S(2)}) collective-permute-start(f32[224,256]{1,0:T(8,128)S(1)} %collective-permute-done.3.refs_4_), channel_id=1, source_target_pairs={{0,1},{2,0},{4,2},{6,4},{7,6},{5,7},{3,5},{1,3},{8,9},{10,8},{12,1... | collective-permute-start | bytes 688136 | tf_op jit(solution)/shard_map/ppermute | solution.py:386
  19.2 14.9 %collective-permute-start.7 = (f32[2016,128]{1,0:T(8,128)S(1)}, f32[2016,128]{1,0:T(8,128)S(1)}, u32[]{:S(2)}, u32[]{:S(2)}) collective-permute-start(f32[2016,128]{1,0:T(8,128)S(1)} %shard_map.62.refs_0_), channel_id=1, source_target_pairs={{0,8},{8,0},{16,24},{24,16},{1,9},{9,1},{17,25},{25,17},{2,10},{10... | collective-permute-start | bytes 3096584 | tf_op jit(solution)/shard_map/ppermute | solution.py:359
  23.2 6.2 %collective-permute-start.6 = (f32[224,256]{1,0:T(8,128)S(1)}, f32[224,256]{1,0:T(8,128)S(1)}, u32[]{:S(2)}, u32[]{:S(2)}) collective-permute-start(f32[224,256]{1,0:T(8,128)S(1)} %collective-permute-done.4.refs_5_), channel_id=1, source_target_pairs={{1,0},{0,2},{2,4},{4,6},{6,7},{7,5},{5,3},{3,1},{9,8},{8,10},{10,1... | collective-permute-start | bytes 688136 | tf_op jit(solution)/shard_map/ppermute | solution.py:390
  32.0 3.3 %collective-permute-start.9 = (f32[2016,128]{1,0:T(8,128)S(1)}, f32[2016,128]{1,0:T(8,128)S(1)}, u32[]{:S(2)}, u32[]{:S(2)}) collective-permute-start(f32[2016,128]{1,0:T(8,128)S(1)} %collective-permute-done.8.refs_1_), channel_id=1, source_target_pairs={{0,8},{8,0},{16,24},{24,16},{1,9},{9,1},{17,25},{25,17},{2,10},{10... | collective-permute-start | bytes 3096584 | tf_op jit(solution)/shard_map/ppermute | solution.py:359
  32.0 7.7 %collective-permute-start.13 = (f32[576,128]{1,0:T(8,128)S(1)}, f32[576,128]{1,0:T(8,128)S(1)}, u32[]{:S(2)}, u32[]{:S(2)}) collective-permute-start(f32[576,128]{1,0:T(8,128)S(1)} %get-tuple-element.58.refs_0_), channel_id=1, source_target_pairs={{0,8},{8,0},{16,24},{24,16},{1,9},{9,1},{17,25},{25,17},{2,10},{10... | collective-permute-start | bytes 884744 | tf_op jit(solution)/shard_map/ppermute | solution.py:359
  32.5 9.9 %collective-permute-start.14 = (f32[576,128]{1,0:T(8,128)S(1)}, f32[576,128]{1,0:T(8,128)S(1)}, u32[]{:S(2)}, u32[]{:S(2)}) collective-permute-start(f32[576,128]{1,0:T(8,128)S(1)} %get-tuple-element.58.refs_0_), channel_id=1, source_target_pairs={{0,16},{8,24},{16,0},{24,8},{1,17},{9,25},{17,1},{25,9},{2,18},{10... | collective-permute-start | bytes 884744 | tf_op jit(solution)/shard_map/ppermute | solution.py:367
  34.1 12.9 %collective-permute-start.15 = (f32[576,128]{1,0:T(8,128)S(1)}, f32[576,128]{1,0:T(8,128)S(1)}, u32[]{:S(2)}, u32[]{:S(2)}) collective-permute-start(f32[576,128]{1,0:T(8,128)S(1)} %get-tuple-element.58.refs_0_), channel_id=1, source_target_pairs={{0,24},{8,16},{16,8},{24,0},{1,25},{9,17},{17,9},{25,1},{2,26},{10... | collective-permute-start | bytes 884744 | tf_op jit(solution)/shard_map/ppermute | solution.py:367
  37.0 13.5 %collective-permute-start.16 = (f32[448,256]{1,0:T(8,128)S(1)}, f32[448,256]{1,0:T(8,128)S(1)}, u32[]{:S(2)}, u32[]{:S(2)}) collective-permute-start(f32[448,256]{1,0:T(8,128)S(1)} %get-tuple-element.60.refs_0_.mine_ref), channel_id=1, source_target_pairs={{0,1},{1,0},{2,3},{3,2},{4,5},{5,4},{6,7},{7,6},{8,9},{9,8},{10,11... | collective-permute-start | bytes 1376264 | tf_op jit(solution)/shard_map/ppermute | solution.py:359
  38.2 11.0 %collective-permute-start.10 = (f32[112,256]{1,0:T(8,128)S(1)}, f32[112,256]{1,0:T(8,128)S(1)}, u32[]{:S(2)}, u32[]{:S(2)}) collective-permute-start(f32[112,256]{1,0:T(8,128)S(1)} %get-tuple-element.53), channel_id=1, source_target_pairs={{0,2},{1,3},{2,4},{3,5},{4,6},{5,7},{6,0},{7,1},{8,10},{9,11},{10,... | collective-permute-start | bytes 344072 | tf_op jit(solution)/shard_map/ppermute | solution.py:486
  39.7 10.7 %collective-permute-start.11 = (f32[112,256]{1,0:T(8,128)S(1)}, f32[112,256]{1,0:T(8,128)S(1)}, u32[]{:S(2)}, u32[]{:S(2)}) collective-permute-start(f32[112,256]{1,0:T(8,128)S(1)} %get-tuple-element.54), channel_id=1, source_target_pairs={{0,4},{1,5},{2,6},{3,7},{4,0},{5,1},{6,2},{7,3},{8,12},{9,13},{10,... | collective-permute-start | bytes 344072 | tf_op jit(solution)/shard_map/ppermute | solution.py:486
  42.4 8.0 %collective-permute-start.12 = (f32[112,256]{1,0:T(8,128)S(1)}, f32[112,256]{1,0:T(8,128)S(1)}, u32[]{:S(2)}, u32[]{:S(2)}) collective-permute-start(f32[112,256]{1,0:T(8,128)S(1)} %get-tuple-element.55), channel_id=1, source_target_pairs={{0,6},{1,7},{2,0},{3,1},{4,2},{5,3},{6,4},{7,5},{8,14},{9,15},{10,... | collective-permute-start | bytes 344072 | tf_op jit(solution)/shard_map/ppermute | solution.py:486
  51.5 7.1 %collective-permute-start.19 = (f32[256,128]{1,0:T(8,128)S(1)}, f32[256,128]{1,0:T(8,128)S(1)}, u32[]{:S(2)}, u32[]{:S(2)}) collective-permute-start(f32[256,128]{1,0:T(8,128)S(1)} %get-tuple-element.74), channel_id=1, source_target_pairs={{0,2},{1,3},{2,0},{3,1},{4,6},{5,7},{6,4},{7,5},{8,10},{9,11},{10,... | collective-permute-start | bytes 393224 | tf_op jit(solution)/shard_map/ppermute | solution.py:512
  54.5 10.1 %collective-permute-start.18 = (f32[256,128]{1,0:T(8,128)S(1)}, f32[256,128]{1,0:T(8,128)S(1)}, u32[]{:S(2)}, u32[]{:S(2)}) collective-permute-start(f32[256,128]{1,0:T(8,128)S(1)} %get-tuple-element.72), channel_id=1, source_target_pairs={{0,4},{1,5},{2,6},{3,7},{4,0},{5,1},{6,2},{7,3},{8,12},{9,13},{10,... | collective-permute-start | bytes 393224 | tf_op jit(solution)/shard_map/ppermute | solution.py:512
  58.6 7.2 %collective-permute-start.21 = (f32[128,128]{1,0:T(8,128)S(1)}, f32[128,128]{1,0:T(8,128)S(1)}, u32[]{:S(2)}, u32[]{:S(2)}) collective-permute-start(f32[128,128]{1,0:T(8,128)S(1)} %get-tuple-element.79), channel_id=1, source_target_pairs={{0,4},{1,5},{2,6},{3,7},{4,0},{5,1},{6,2},{7,3},{8,12},{9,13},{10,... | collective-permute-start | bytes 196616 | tf_op jit(solution)/shard_map/ppermute | solution.py:512
  61.5 6.0 %collective-permute-start.17 = (f32[224,256]{1,0:T(8,128)S(1)}, f32[224,256]{1,0:T(8,128)S(1)}, u32[]{:S(2)}, u32[]{:S(2)}) collective-permute-start(f32[224,256]{1,0:T(8,128)S(1)} %get-tuple-element.69), channel_id=1, source_target_pairs={{0,1},{1,0},{2,3},{3,2},{4,5},{5,4},{6,7},{7,6},{8,9},{9,8},{10,11... | collective-permute-start | bytes 688136 | tf_op jit(solution)/shard_map/ppermute | solution.py:359
  64.6 4.3 %copy-start = (f32[128,256]{1,0:T(8,128)S(1)}, f32[128,256]{1,0:T(8,128)}, u32[]{:S(2)}) copy-start(f32[128,256]{1,0:T(8,128)} %d_ref) | copy-start | bytes 393220
  64.6 4.3 %collective-permute-start.20 = (f32[128,128]{1,0:T(8,128)S(1)}, f32[128,128]{1,0:T(8,128)S(1)}, u32[]{:S(2)}, u32[]{:S(2)}) collective-permute-start(f32[128,128]{1,0:T(8,128)S(1)} %get-tuple-element.78), channel_id=1, source_target_pairs={{0,2},{1,3},{2,0},{3,1},{4,6},{5,7},{6,4},{7,5},{8,10},{9,11},{10,... | collective-permute-start | bytes 196616 | tf_op jit(solution)/shard_map/ppermute | solution.py:512
  (1 other events, 0.7 us)

commit v12 on v10

--- a/solution.py
+++ b/solution.py
@@ -167,7 +167,7 @@
     ahead = (count(names < c * rows) - turn + nc - 1) >> lg
     block = turn >> 1
     if direct:
-        block = (block - z) & (nc // 2 - 1)
+        block = block ^ z
     block = 2 * block + (turn & 1)
     slot = jnp.where(member > 0.5, block * slots + (rank >> lg) - ahead, -1)
     at = lax.broadcasted_iota(jnp.int32, (rows, nc * slots), 1)
@@ -194,7 +194,7 @@
     ahead = (jnp.where(half == 1, middle, start) - turn + nc - 1) >> lg
     block = turn >> 1
     if direct:
-        block = (block - z) & (nz - 1)
+        block = block ^ z
     slot = (2 * block + (turn & 1)) * slots + (index >> lg) - ahead + (half ^ x) * rows
     slot = jnp.where((named >= 2 * z * rows) & (named < (2 * z + 2) * rows), slot, -1)
     at = lax.broadcasted_iota(jnp.int32, (2 * rows, CAP), 0)
@@ -210,7 +210,7 @@
         before = jnp.where(less, before, count(less))
     block = source >> 1
     if direct:
-        block = (z - block) & (nz - 1)
+        block = z ^ block
     block = block + nz * ((source ^ c) & 1)
     slot = block * slots + lax.broadcasted_iota(jnp.int32, (m, 1), 0) - before
     at = lax.broadcasted_iota(jnp.int32, (m, rows), 1)
@@ -275,7 +275,7 @@
     z = lax.axis_index("pcol") // 2
 
     def put(owner, u_ref):
-        where = ((owner - z) & (nz - 1)) if direct else owner
+        where = (owner ^ z) if direct else owner
         high, low = split(u_ref[...].T)
         held_ref[pl.ds(pl.multiple_of(where * wd, wd), wd), :] = high
         held_ref[pl.ds(pl.multiple_of((where + nz) * wd, wd), wd), :] = low
@@ -300,6 +300,13 @@
         @pl.loop(0, out_refs[0].shape[0])
         def _(t):
             out_refs[0][t] = term(t)
+
+
+def sum_kernel(*refs):
+    total = refs[0][...]
+    for ref in refs[1:-1]:
+        total = total + ref[...]
+    refs[-1][...] = total
 
 
 def part_kernel(slots, *refs):
@@ -390,7 +397,7 @@
     wd = w // 2
     n = structure.shape[0]
     slots = -(-rows // nc)
-    direct = nc <= 8
+    direct = (nr, nc) == (4, 8)
     names = structure
     groups = [[2 * k + x for k in range(nz)] for x in range(2)]
     owners = functools.partial(relative_owners, nr)
@@ -458,12 +465,13 @@
         *later,
         flops=term,
     )
+    meet = lambda v, t: lax.ppermute(v, "pcol", [(k, k ^ (2 * t)) for k in range(nc)])
     whole = sent[0]
     other = swap(whole, "pcol", nc)
     if direct:
         got = [whole]
         for t in range(1, nz):
-            got.append(lax.ppermute(sent[t], "pcol", [(k, (k + 2 * t) % nc) for k in range(nc)]))
+            got.append(meet(sent[t], t))
     else:
         blocks = whole.reshape(nz, 2 * slots, w)
         blocks = lax.all_to_all(blocks, "pcol", split_axis=0, concat_axis=0, axis_index_groups=groups, tiled=True)
@@ -487,15 +495,12 @@
     terms = call(correction_kernel, parts, high, low, whole, other, flops=term)
     theirs, _ = lax.optimization_barrier((theirs, terms[0]))
     sigma_sj = call(pick_kernel, f32(m, w), source, mine, swap(theirs, "pcol", nc), flops=term // 4)
-    if direct:
-        total = terms[0]
-        for t in range(1, nz):
-            total = total + lax.ppermute(terms[t], "pcol", [(k, (k + 2 * t) % nc) for k in range(nc)])
-    else:
-        terms = lax.all_to_all(terms[0], "pcol", split_axis=0, concat_axis=0, axis_index_groups=groups, tiled=True)
-        total = jnp.sum(terms, axis=0)
     sigma_sj, d_term = lax.optimization_barrier((sigma_sj, d_term))
-    return sigma_sj, d_term + total
+    if direct:
+        total = call(sum_kernel, f32(wd, w), terms[0], *[meet(terms[t], t) for t in range(2, nz)], flops=4 * term)
+        return sigma_sj, d_term + (total + meet(terms[1], 1))
+    terms = lax.all_to_all(terms[0], "pcol", split_axis=0, concat_axis=0, axis_index_groups=groups, tiled=True)
+    return sigma_sj, d_term + jnp.sum(terms, axis=0)
 
 
 def solution(mesh):

time: 69.3 us -> 67.6 us (0.975)
  waiting for transfers between devices: 24.7 us -> 23 us
    ppermute x5, waiting for transfers between devices: 1.96 us -> 0.01 us  [swap(): return lax.ppermute(v, axis, [(k, k ^ 1) for k in range(size)])]
    pallas_call x11 -> x12, Pallas kernels: 14.9 us -> 15.1 us  [call(): pl.pallas_call(kernel, out_shape=out_shape, out_specs=[VMEM] * len(out_sh...]
  transfers between devices with their start and end apart: 21 -> 21, of which waited for: 11 -> 9; matrix products, arithmetic and copies ran while one was open for 0% -> 0% of each run, Pallas kernels for 20% -> 21%
where the time goes in v12:
time: 67.6 us; the launch traced here: 67.4 us
  starting transfers between devices  27.2 us (40%)
  waiting for transfers between devices  23 us (34%)
  Pallas kernels  15.1 us (22%)
  between operations  0.77 us (1%)
  local copies, waits for them, and re-layouts  0.7 us (1%)
  other arithmetic  0.68 us (1%)
    pallas_call x12, Pallas kernels, call(): pl.pallas_call(kernel, out_shape=out_shape, out_specs=[VMEM] * len(out_sh...  15.1 us
    ppermute x6, starting transfers between devices, per_device(): lax.ppermute(v, 'pcol', [(k, k ^ 2 * t) for k in range(nc)])  12.2 us
    ppermute x4, waiting for transfers between devices, ring_gather(): lax.ppermute(up, 'pcol', pairs)  10.6 us
    ppermute x6, waiting for transfers between devices, per_device(): lax.ppermute(v, 'pcol', [(k, k ^ 2 * t) for k in range(nc)])  9.58 us
    ppermute x4, starting transfers between devices, ring_gather(): lax.ppermute(up, 'pcol', pairs)  7.81 us
    ppermute x5, starting transfers between devices, swap(): return lax.ppermute(v, axis, [(k, k ^ 1) for k in range(size)])  2.66 us
    ppermute x1, starting transfers between devices, per_device(): lax.ppermute(chosen, 'prow', [(k, (k + 2 * t) % nr) for k in range(nr)])  2.03 us
    ppermute x3, waiting for transfers between devices, ring_gather(): lax.ppermute(down, 'pcol', back)  1.55 us
  transfers between devices with their start and end apart: 21, of which 9 were waited for; matrix products, arithmetic and copies ran while one was open for 0% of the time, Pallas kernels for 21%

profile of v12, /device:TPU:0, one launch (start us, length us, event | category | flops | bytes accessed | tf_op | source)
XLA Modules:
  0.0 67.4 jit_solution(13107026875809869269)
XLA Ops:
  0.6 3.1 %collective-permute-start = (f32[224,256]{1,0:T(8,128)}, f32[224,256]{1,0:T(8,128)S(1)}, u32[]{:S(2)}, u32[]{:S(2)}) collective-permute-start(f32[224,256]{1,0:T(8,128)} %refs_0_.1), channel_id=1, source_target_pairs={{1,0},{0,2},{2,4},{4,6},{6,7},{7,5},{5,3},{3,1},{9,8},{8,10},{10,1... | collective-permute-start | bytes 688136 | tf_op jit(solution)/shard_map/ppermute | solution.py:373
  4.4 2.7 %shard_map.62.refs_0_ = f32[2016,128]{1,0:T(8,128)S(1)} custom-call(s32[1792]{0:T(1024)S(1)} %copy-done, f32[448,896]{1,0:T(8,128)} %sigma_ref.1), custom_call_target="tpu_custom_call" | custom-call | flops 1027604480 | bytes 2644992 | tf_op jit(solution)/shard_map/pallas_call | solution.py:335
  7.1 2.0 %collective-permute-start.8 = (f32[2016,128]{1,0:T(8,128)S(1)}, f32[2016,128]{1,0:T(8,128)S(1)}, u32[]{:S(2)}, u32[]{:S(2)}) collective-permute-start(f32[2016,128]{1,0:T(8,128)S(1)} %shard_map.62.refs_0_), channel_id=1, source_target_pairs={{0,16},{8,24},{16,0},{24,8},{1,17},{9,25},{17,1},{25,9},{2,18},{10... | collective-permute-start | bytes 3096584 | tf_op jit(solution)/shard_map/ppermute | solution.py:449
  9.4 1.5 %collective-permute-done.1.refs_2_ = f32[224,256]{1,0:T(8,128)S(1)} collective-permute-done((f32[224,256]{1,0:T(8,128)}, f32[224,256]{1,0:T(8,128)S(1)}, u32[]{:S(2)}, u32[]{:S(2)}) %collective-permute-start.1) | collective-permute-done | bytes 229408 | tf_op jit(solution)/shard_map/ppermute | solution.py:373
  11.0 1.6 %collective-permute-start.2 = (f32[224,256]{1,0:T(8,128)S(1)}, f32[224,256]{1,0:T(8,128)S(1)}, u32[]{:S(2)}, u32[]{:S(2)}) collective-permute-start(f32[224,256]{1,0:T(8,128)S(1)} %collective-permute-done.refs_1_), channel_id=1, source_target_pairs={{1,0},{0,2},{2,4},{4,6},{6,7},{7,5},{5,3},{3,1},{9,8},{8,10},{10,1... | collective-permute-start | bytes 688136 | tf_op jit(solution)/shard_map/ppermute | solution.py:373
  13.0 4.1 %collective-permute-done.2.refs_3_ = f32[224,256]{1,0:T(8,128)S(1)} collective-permute-done((f32[224,256]{1,0:T(8,128)S(1)}, f32[224,256]{1,0:T(8,128)S(1)}, u32[]{:S(2)}, u32[]{:S(2)}) %collective-permute-start.2) | collective-permute-done | bytes 229408 | tf_op jit(solution)/shard_map/ppermute | solution.py:373
  17.1 1.6 %collective-permute-start.4 = (f32[224,256]{1,0:T(8,128)S(1)}, f32[224,256]{1,0:T(8,128)S(1)}, u32[]{:S(2)}, u32[]{:S(2)}) collective-permute-start(f32[224,256]{1,0:T(8,128)S(1)} %collective-permute-done.2.refs_3_), channel_id=1, source_target_pairs={{1,0},{0,2},{2,4},{4,6},{6,7},{7,5},{5,3},{3,1},{9,8},{8,10},{10,1... | collective-permute-start | bytes 688136 | tf_op jit(solution)/shard_map/ppermute | solution.py:373
  19.2 2.1 %shard_map.59 = (bf16[448,448]{1,0:T(8,128)(2,1)S(1)}, bf16[576,896]{1,0:T(8,128)(2,1)S(1)}, bf16[224,448]{1,0:T(8,128)(2,1)S(1)}) custom-call(s32[1792]{0:T(1024)S(1)} %copy-done), custom_call_target="tpu_custom_call" | custom-call | tf_op jit(solution)/shard_map/pallas_call | solution.py:335
  21.2 1.9 %collective-permute-done.4.refs_5_ = f32[224,256]{1,0:T(8,128)S(1)} collective-permute-done((f32[224,256]{1,0:T(8,128)S(1)}, f32[224,256]{1,0:T(8,128)S(1)}, u32[]{:S(2)}, u32[]{:S(2)}) %collective-permute-start.4) | collective-permute-done | bytes 229408 | tf_op jit(solution)/shard_map/ppermute | solution.py:373
  23.2 1.6 %collective-permute-start.6 = (f32[224,256]{1,0:T(8,128)S(1)}, f32[224,256]{1,0:T(8,128)S(1)}, u32[]{:S(2)}, u32[]{:S(2)}) collective-permute-start(f32[224,256]{1,0:T(8,128)S(1)} %collective-permute-done.4.refs_5_), channel_id=1, source_target_pairs={{1,0},{0,2},{2,4},{4,6},{6,7},{7,5},{5,3},{3,1},{9,8},{8,10},{10,1... | collective-permute-start | bytes 688136 | tf_op jit(solution)/shard_map/ppermute | solution.py:377
  25.2 4.3 %collective-permute-done.6.refs_0_ = f32[224,256]{1,0:T(8,128)S(1)} collective-permute-done((f32[224,256]{1,0:T(8,128)S(1)}, f32[224,256]{1,0:T(8,128)S(1)}, u32[]{:S(2)}, u32[]{:S(2)}) %collective-permute-start.6) | collective-permute-done | bytes 229408 | tf_op jit(solution)/shard_map/ppermute | solution.py:377
  30.0 2.1 %shard_map.63 = (f32[448,256]{1,0:T(8,128)S(1)}, bf16[3,640,256]{2,1,0:T(8,128)(2,1)S(1)}, bf16[3,640,256]{2,1,0:T(8,128)(2,1)S(1)}) custom-call(s32[1792]{0:T(1024)S(1)} %copy-done, f32[2,2376,128]{2,1,0:T(8,128)S(1)} %get-tuple-element.41.us_ref, f32[2016,128]{1,0:T(8,128)S(1)} %shard_map.62.refs_0_), custom_call_target="tpu_custom_call" | custom-call | tf_op jit(solution)/shard_map/pallas_call | solution.py:335
  32.7 1.5 %collective-permute-start.14 = (f32[576,128]{1,0:T(8,128)S(1)}, f32[576,128]{1,0:T(8,128)S(1)}, u32[]{:S(2)}, u32[]{:S(2)}) collective-permute-start(f32[576,128]{1,0:T(8,128)S(1)} %get-tuple-element.53.refs_0_), channel_id=1, source_target_pairs={{0,16},{8,24},{16,0},{24,8},{1,17},{9,25},{17,1},{25,9},{2,18},{10... | collective-permute-start | bytes 884744 | tf_op jit(solution)/shard_map/ppermute | solution.py:354
  34.2 1.2 %shard_map.64.part_ref = f32[448,256]{1,0:T(8,128)S(1)} custom-call(bf16[3,640,256]{2,1,0:T(8,128)(2,1)S(1)} %get-tuple-element.42.uh_ref, bf16[3,640,256]{2,1,0:T(8,128)(2,1)S(1)} %get-tuple-element.43.ul_ref, f32[448,256]{1,0:T(8,128)S(1)} %get-tuple-element.44.part_ref, f32[2016,128]{1,0:T(8,128)S(1)} %collective-permute-done.7.refs_0_, ...), custom_call_target="tpu_custom_call" | custom-call | flops 440401920 | bytes 4947968 | tf_op jit(solution)/shard_map/pallas_call | solution.py:335
  35.4 1.8 %shard_map.65 = (f32[448,256]{1,0:T(8,128)S(1)}, f32[112,256]{1,0:T(8,128)S(1)}, f32[112,256]{1,0:T(8,128)S(1)}, f32[112,256]{1,0:T(8,128)S(1)}) custom-call(bf16[3,640,256]{2,1,0:T(8,128)(2,1)S(1)} %get-tuple-element.42.uh_ref, bf16[3,640,256]{2,1,0:T(8,128)(2,1)S(1)} %get-tuple-element.43.ul_ref, f32[448,256]{1,0:T(8,128)S(1)} %shard_map.64.part_ref, ...), custom_call_target="tpu_custom_call" | custom-call | flops 440401920 | bytes 4661248 | tf_op jit(solution)/shard_map/pallas_call | solution.py:335
  38.2 1.6 %collective-permute-start.10 = (f32[112,256]{1,0:T(8,128)S(1)}, f32[112,256]{1,0:T(8,128)S(1)}, u32[]{:S(2)}, u32[]{:S(2)}) collective-permute-start(f32[112,256]{1,0:T(8,128)S(1)} %get-tuple-element.48), channel_id=1, source_target_pairs={{0,2},{1,3},{2,0},{3,1},{4,6},{5,7},{6,4},{7,5},{8,10},{9,11},{10,... | collective-permute-start | bytes 344072 | tf_op jit(solution)/shard_map/ppermute | solution.py:468
  39.7 2.6 %collective-permute-start.11 = (f32[112,256]{1,0:T(8,128)S(1)}, f32[112,256]{1,0:T(8,128)S(1)}, u32[]{:S(2)}, u32[]{:S(2)}) collective-permute-start(f32[112,256]{1,0:T(8,128)S(1)} %get-tuple-element.49), channel_id=1, source_target_pairs={{0,4},{1,5},{2,6},{3,7},{4,0},{5,1},{6,2},{7,3},{8,12},{9,13},{10,... | collective-permute-start | bytes 344072 | tf_op jit(solution)/shard_map/ppermute | solution.py:468
  42.6 3.5 %collective-permute-start.12 = (f32[112,256]{1,0:T(8,128)S(1)}, f32[112,256]{1,0:T(8,128)S(1)}, u32[]{:S(2)}, u32[]{:S(2)}) collective-permute-start(f32[112,256]{1,0:T(8,128)S(1)} %get-tuple-element.50), channel_id=1, source_target_pairs={{0,6},{1,7},{2,4},{3,5},{4,2},{5,3},{6,0},{7,1},{8,14},{9,15},{10,... | collective-permute-start | bytes 344072 | tf_op jit(solution)/shard_map/ppermute | solution.py:468
  47.2 2.2 %shard_map.66 = (bf16[4,128,896]{2,1,0:T(8,128)(2,1)S(1)}, bf16[4,128,896]{2,1,0:T(8,128)(2,1)S(1)}) custom-call(bf16[576,896]{1,0:T(8,128)(2,1)S(1)} %get-tuple-element.51.place_ref, f32[576,128]{1,0:T(8,128)S(1)} %get-tuple-element.53.refs_0_, f32[576,128]{1,0:T(8,128)S(1)} %collective-permute-done.13.refs_1_, ...), custom_call_target="tpu_custom_call" | custom-call | flops 1056964608 | bytes 4046848 | tf_op jit(solution)/shard_map/pallas_call | solution.py:335
  49.3 2.3 %collective-permute-done.11.refs_2_ = f32[112,256]{1,0:T(8,128)S(1)} collective-permute-done((f32[112,256]{1,0:T(8,128)S(1)}, f32[112,256]{1,0:T(8,128)S(1)}, u32[]{:S(2)}, u32[]{:S(2)}) %collective-permute-start.11) | collective-permute-done | bytes 114720 | tf_op jit(solution)/shard_map/ppermute | solution.py:468
  52.7 3.2 %collective-permute-start.18 = (f32[128,256]{1,0:T(8,128)S(1)}, f32[128,256]{1,0:T(8,128)S(1)}, u32[]{:S(2)}, u32[]{:S(2)}) collective-permute-start(f32[128,256]{1,0:T(8,128)S(1)} %get-tuple-element.67), channel_id=1, source_target_pairs={{0,4},{1,5},{2,6},{3,7},{4,0},{5,1},{6,2},{7,3},{8,12},{9,13},{10,... | collective-permute-start | bytes 393224 | tf_op jit(solution)/shard_map/ppermute | solution.py:468
  55.9 1.3 %collective-permute-start.19 = (f32[128,256]{1,0:T(8,128)S(1)}, f32[128,256]{1,0:T(8,128)S(1)}, u32[]{:S(2)}, u32[]{:S(2)}) collective-permute-start(f32[128,256]{1,0:T(8,128)S(1)} %get-tuple-element.68), channel_id=1, source_target_pairs={{0,6},{1,7},{2,4},{3,5},{4,2},{5,3},{6,0},{7,1},{8,14},{9,15},{10,... | collective-permute-start | bytes 393224 | tf_op jit(solution)/shard_map/ppermute | solution.py:468
  57.2 1.1 %collective-permute-start.17 = (f32[224,256]{1,0:T(8,128)S(1)}, f32[224,256]{1,0:T(8,128)S(1)}, u32[]{:S(2)}, u32[]{:S(2)}) collective-permute-start(f32[224,256]{1,0:T(8,128)S(1)} %get-tuple-element.64), channel_id=1, source_target_pairs={{0,1},{1,0},{2,3},{3,2},{4,5},{5,4},{6,7},{7,6},{8,9},{9,8},{10,11... | collective-permute-start | bytes 688136 | tf_op jit(solution)/shard_map/ppermute | solution.py:346
  58.3 7.3 %collective-permute-done.18.refs_1_ = f32[128,256]{1,0:T(8,128)S(1)} collective-permute-done((f32[128,256]{1,0:T(8,128)S(1)}, f32[128,256]{1,0:T(8,128)S(1)}, u32[]{:S(2)}, u32[]{:S(2)}) %collective-permute-start.18) | collective-permute-done | bytes 131104 | tf_op jit(solution)/shard_map/ppermute | solution.py:468
  (37 shorter events, 8.5 us)
Async XLA Ops:
  0.6 8.8 %collective-permute-start = (f32[224,256]{1,0:T(8,128)}, f32[224,256]{1,0:T(8,128)S(1)}, u32[]{:S(2)}, u32[]{:S(2)}) collective-permute-start(f32[224,256]{1,0:T(8,128)} %refs_0_.1), channel_id=1, source_target_pairs={{1,0},{0,2},{2,4},{4,6},{6,7},{7,5},{5,3},{3,1},{9,8},{8,10},{10,1... | collective-permute-start | bytes 688136 | tf_op jit(solution)/shard_map/ppermute | solution.py:373
  3.7 7.3 %collective-permute-start.1 = (f32[224,256]{1,0:T(8,128)}, f32[224,256]{1,0:T(8,128)S(1)}, u32[]{:S(2)}, u32[]{:S(2)}) collective-permute-start(f32[224,256]{1,0:T(8,128)} %refs_0_.1), channel_id=1, source_target_pairs={{0,1},{2,0},{4,2},{6,4},{7,6},{5,7},{3,5},{1,3},{8,9},{10,8},{12,1... | collective-permute-start | bytes 688136 | tf_op jit(solution)/shard_map/ppermute | solution.py:373
  3.7 0.7 %copy-start = (s32[1792]{0:T(1024)S(1)}, s32[1792]{0:T(1024)}, u32[]{:S(2)}) copy-start(s32[1792]{0:T(1024)} %structure_ref.7) | copy-start | bytes 21508
  4.4 20.3 %copy-start.1 = (f32[224,256]{1,0:T(8,128)S(1)}, f32[224,256]{1,0:T(8,128)}, u32[]{:S(2)}) copy-start(f32[224,256]{1,0:T(8,128)} %refs_0_.1) | copy-start | bytes 688132
  7.1 25.0 %collective-permute-start.8 = (f32[2016,128]{1,0:T(8,128)S(1)}, f32[2016,128]{1,0:T(8,128)S(1)}, u32[]{:S(2)}, u32[]{:S(2)}) collective-permute-start(f32[2016,128]{1,0:T(8,128)S(1)} %shard_map.62.refs_0_), channel_id=1, source_target_pairs={{0,16},{8,24},{16,0},{24,8},{1,17},{9,25},{17,1},{25,9},{2,18},{10... | collective-permute-start | bytes 3096584 | tf_op jit(solution)/shard_map/ppermute | solution.py:449
  11.0 6.2 %collective-permute-start.2 = (f32[224,256]{1,0:T(8,128)S(1)}, f32[224,256]{1,0:T(8,128)S(1)}, u32[]{:S(2)}, u32[]{:S(2)}) collective-permute-start(f32[224,256]{1,0:T(8,128)S(1)} %collective-permute-done.refs_1_), channel_id=1, source_target_pairs={{1,0},{0,2},{2,4},{4,6},{6,7},{7,5},{5,3},{3,1},{9,8},{8,10},{10,1... | collective-permute-start | bytes 688136 | tf_op jit(solution)/shard_map/ppermute | solution.py:373
  12.6 6.2 %collective-permute-start.3 = (f32[224,256]{1,0:T(8,128)S(1)}, f32[224,256]{1,0:T(8,128)S(1)}, u32[]{:S(2)}, u32[]{:S(2)}) collective-permute-start(f32[224,256]{1,0:T(8,128)S(1)} %collective-permute-done.1.refs_2_), channel_id=1, source_target_pairs={{0,1},{2,0},{4,2},{6,4},{7,6},{5,7},{3,5},{1,3},{8,9},{10,8},{12,1... | collective-permute-start | bytes 688136 | tf_op jit(solution)/shard_map/ppermute | solution.py:373
  17.1 6.0 %collective-permute-start.4 = (f32[224,256]{1,0:T(8,128)S(1)}, f32[224,256]{1,0:T(8,128)S(1)}, u32[]{:S(2)}, u32[]{:S(2)}) collective-permute-start(f32[224,256]{1,0:T(8,128)S(1)} %collective-permute-done.2.refs_3_), channel_id=1, source_target_pairs={{1,0},{0,2},{2,4},{4,6},{6,7},{7,5},{5,3},{3,1},{9,8},{8,10},{10,1... | collective-permute-start | bytes 688136 | tf_op jit(solution)/shard_map/ppermute | solution.py:373
  18.7 6.0 %collective-permute-start.5 = (f32[224,256]{1,0:T(8,128)S(1)}, f32[224,256]{1,0:T(8,128)S(1)}, u32[]{:S(2)}, u32[]{:S(2)}) collective-permute-start(f32[224,256]{1,0:T(8,128)S(1)} %collective-permute-done.3.refs_4_), channel_id=1, source_target_pairs={{0,1},{2,0},{4,2},{6,4},{7,6},{5,7},{3,5},{1,3},{8,9},{10,8},{12,1... | collective-permute-start | bytes 688136 | tf_op jit(solution)/shard_map/ppermute | solution.py:373
  19.2 15.1 %collective-permute-start.7 = (f32[2016,128]{1,0:T(8,128)S(1)}, f32[2016,128]{1,0:T(8,128)S(1)}, u32[]{:S(2)}, u32[]{:S(2)}) collective-permute-start(f32[2016,128]{1,0:T(8,128)S(1)} %shard_map.62.refs_0_), channel_id=1, source_target_pairs={{0,8},{8,0},{16,24},{24,16},{1,9},{9,1},{17,25},{25,17},{2,10},{10... | collective-permute-start | bytes 3096584 | tf_op jit(solution)/shard_map/ppermute | solution.py:346
  23.2 6.3 %collective-permute-start.6 = (f32[224,256]{1,0:T(8,128)S(1)}, f32[224,256]{1,0:T(8,128)S(1)}, u32[]{:S(2)}, u32[]{:S(2)}) collective-permute-start(f32[224,256]{1,0:T(8,128)S(1)} %collective-permute-done.4.refs_5_), channel_id=1, source_target_pairs={{1,0},{0,2},{2,4},{4,6},{6,7},{7,5},{5,3},{3,1},{9,8},{8,10},{10,1... | collective-permute-start | bytes 688136 | tf_op jit(solution)/shard_map/ppermute | solution.py:377
  32.1 3.3 %collective-permute-start.9 = (f32[2016,128]{1,0:T(8,128)S(1)}, f32[2016,128]{1,0:T(8,128)S(1)}, u32[]{:S(2)}, u32[]{:S(2)}) collective-permute-start(f32[2016,128]{1,0:T(8,128)S(1)} %collective-permute-done.8.refs_1_), channel_id=1, source_target_pairs={{0,8},{8,0},{16,24},{24,16},{1,9},{9,1},{17,25},{25,17},{2,10},{10... | collective-permute-start | bytes 3096584 | tf_op jit(solution)/shard_map/ppermute | solution.py:346
  32.2 7.5 %collective-permute-start.13 = (f32[576,128]{1,0:T(8,128)S(1)}, f32[576,128]{1,0:T(8,128)S(1)}, u32[]{:S(2)}, u32[]{:S(2)}) collective-permute-start(f32[576,128]{1,0:T(8,128)S(1)} %get-tuple-element.53.refs_0_), channel_id=1, source_target_pairs={{0,8},{8,0},{16,24},{24,16},{1,9},{9,1},{17,25},{25,17},{2,10},{10... | collective-permute-start | bytes 884744 | tf_op jit(solution)/shard_map/ppermute | solution.py:346
  32.7 9.9 %collective-permute-start.14 = (f32[576,128]{1,0:T(8,128)S(1)}, f32[576,128]{1,0:T(8,128)S(1)}, u32[]{:S(2)}, u32[]{:S(2)}) collective-permute-start(f32[576,128]{1,0:T(8,128)S(1)} %get-tuple-element.53.refs_0_), channel_id=1, source_target_pairs={{0,16},{8,24},{16,0},{24,8},{1,17},{9,25},{17,1},{25,9},{2,18},{10... | collective-permute-start | bytes 884744 | tf_op jit(solution)/shard_map/ppermute | solution.py:354
  34.2 12.9 %collective-permute-start.15 = (f32[576,128]{1,0:T(8,128)S(1)}, f32[576,128]{1,0:T(8,128)S(1)}, u32[]{:S(2)}, u32[]{:S(2)}) collective-permute-start(f32[576,128]{1,0:T(8,128)S(1)} %get-tuple-element.53.refs_0_), channel_id=1, source_target_pairs={{0,24},{8,16},{16,8},{24,0},{1,25},{9,17},{17,9},{25,1},{2,26},{10... | collective-permute-start | bytes 884744 | tf_op jit(solution)/shard_map/ppermute | solution.py:354
  37.2 14.5 %collective-permute-start.16 = (f32[448,256]{1,0:T(8,128)S(1)}, f32[448,256]{1,0:T(8,128)S(1)}, u32[]{:S(2)}, u32[]{:S(2)}) collective-permute-start(f32[448,256]{1,0:T(8,128)S(1)} %get-tuple-element.55.refs_0_.mine_ref), channel_id=1, source_target_pairs={{0,1},{1,0},{2,3},{3,2},{4,5},{5,4},{6,7},{7,6},{8,9},{9,8},{10,11... | collective-permute-start | bytes 1376264 | tf_op jit(solution)/shard_map/ppermute | solution.py:346
  38.2 11.2 %collective-permute-start.10 = (f32[112,256]{1,0:T(8,128)S(1)}, f32[112,256]{1,0:T(8,128)S(1)}, u32[]{:S(2)}, u32[]{:S(2)}) collective-permute-start(f32[112,256]{1,0:T(8,128)S(1)} %get-tuple-element.48), channel_id=1, source_target_pairs={{0,2},{1,3},{2,0},{3,1},{4,6},{5,7},{6,4},{7,5},{8,10},{9,11},{10,... | collective-permute-start | bytes 344072 | tf_op jit(solution)/shard_map/ppermute | solution.py:468
  39.7 11.9 %collective-permute-start.11 = (f32[112,256]{1,0:T(8,128)S(1)}, f32[112,256]{1,0:T(8,128)S(1)}, u32[]{:S(2)}, u32[]{:S(2)}) collective-permute-start(f32[112,256]{1,0:T(8,128)S(1)} %get-tuple-element.49), channel_id=1, source_target_pairs={{0,4},{1,5},{2,6},{3,7},{4,0},{5,1},{6,2},{7,3},{8,12},{9,13},{10,... | collective-permute-start | bytes 344072 | tf_op jit(solution)/shard_map/ppermute | solution.py:468
  42.6 9.0 %collective-permute-start.12 = (f32[112,256]{1,0:T(8,128)S(1)}, f32[112,256]{1,0:T(8,128)S(1)}, u32[]{:S(2)}, u32[]{:S(2)}) collective-permute-start(f32[112,256]{1,0:T(8,128)S(1)} %get-tuple-element.50), channel_id=1, source_target_pairs={{0,6},{1,7},{2,4},{3,5},{4,2},{5,3},{6,0},{7,1},{8,14},{9,15},{10,... | collective-permute-start | bytes 344072 | tf_op jit(solution)/shard_map/ppermute | solution.py:468
  52.7 13.0 %collective-permute-start.18 = (f32[128,256]{1,0:T(8,128)S(1)}, f32[128,256]{1,0:T(8,128)S(1)}, u32[]{:S(2)}, u32[]{:S(2)}) collective-permute-start(f32[128,256]{1,0:T(8,128)S(1)} %get-tuple-element.67), channel_id=1, source_target_pairs={{0,4},{1,5},{2,6},{3,7},{4,0},{5,1},{6,2},{7,3},{8,12},{9,13},{10,... | collective-permute-start | bytes 393224 | tf_op jit(solution)/shard_map/ppermute | solution.py:468
  55.9 9.8 %collective-permute-start.19 = (f32[128,256]{1,0:T(8,128)S(1)}, f32[128,256]{1,0:T(8,128)S(1)}, u32[]{:S(2)}, u32[]{:S(2)}) collective-permute-start(f32[128,256]{1,0:T(8,128)S(1)} %get-tuple-element.68), channel_id=1, source_target_pairs={{0,6},{1,7},{2,4},{3,5},{4,2},{5,3},{6,0},{7,1},{8,14},{9,15},{10,... | collective-permute-start | bytes 393224 | tf_op jit(solution)/shard_map/ppermute | solution.py:468
  57.2 8.5 %collective-permute-start.17 = (f32[224,256]{1,0:T(8,128)S(1)}, f32[224,256]{1,0:T(8,128)S(1)}, u32[]{:S(2)}, u32[]{:S(2)}) collective-permute-start(f32[224,256]{1,0:T(8,128)S(1)} %get-tuple-element.64), channel_id=1, source_target_pairs={{0,1},{1,0},{2,3},{3,2},{4,5},{5,4},{6,7},{7,6},{8,9},{9,8},{10,11... | collective-permute-start | bytes 688136 | tf_op jit(solution)/shard_map/ppermute | solution.py:346
  58.3 8.4 %copy-start.2 = (f32[128,256]{1,0:T(8,128)S(1)}, f32[128,256]{1,0:T(8,128)}, u32[]{:S(2)}) copy-start(f32[128,256]{1,0:T(8,128)} %param.7) | copy-start | bytes 393220
  58.3 8.4 %collective-permute-start.20 = (f32[128,256]{1,0:T(8,128)S(1)}, f32[128,256]{1,0:T(8,128)S(1)}, u32[]{:S(2)}, u32[]{:S(2)}) collective-permute-start(f32[128,256]{1,0:T(8,128)S(1)} %get-tuple-element.69), channel_id=1, source_target_pairs={{0,2},{1,3},{2,0},{3,1},{4,6},{5,7},{6,4},{7,5},{8,10},{9,11},{10,... | collective-permute-start | bytes 393224 | tf_op jit(solution)/shard_map/ppermute | solution.py:468

commit v13 on v12

--- a/solution.py
+++ b/solution.py
@@ -156,6 +156,13 @@
     own_ref[...] = rows_of(us_ref, names, c // 2, width, [c & 1] if len(refs) > 2 else [0])[:, :w]
 
 
+AWAY = (0, 2, 3, 1)
+
+
+def place_of(t):
+    return jnp.where(t == 1, 3, jnp.where(t > 1, t - 1, 0))
+
+
 def row_order(names, c, rows, nc, slots, direct):
     n = names.shape[1]
     z = c // 2
@@ -167,7 +174,7 @@
     ahead = (count(names < c * rows) - turn + nc - 1) >> lg
     block = turn >> 1
     if direct:
-        block = block ^ z
+        block = place_of(block ^ z)
     block = 2 * block + (turn & 1)
     slot = jnp.where(member > 0.5, block * slots + (rank >> lg) - ahead, -1)
     at = lax.broadcasted_iota(jnp.int32, (rows, nc * slots), 1)
@@ -194,7 +201,7 @@
     ahead = (jnp.where(half == 1, middle, start) - turn + nc - 1) >> lg
     block = turn >> 1
     if direct:
-        block = block ^ z
+        block = place_of(block ^ z)
     slot = (2 * block + (turn & 1)) * slots + (index >> lg) - ahead + (half ^ x) * rows
     slot = jnp.where((named >= 2 * z * rows) & (named < (2 * z + 2) * rows), slot, -1)
     at = lax.broadcasted_iota(jnp.int32, (2 * rows, CAP), 0)
@@ -210,7 +217,7 @@
         before = jnp.where(less, before, count(less))
     block = source >> 1
     if direct:
-        block = z ^ block
+        block = place_of(block ^ z)
     block = block + nz * ((source ^ c) & 1)
     slot = block * slots + lax.broadcasted_iota(jnp.int32, (m, 1), 0) - before
     at = lax.broadcasted_iota(jnp.int32, (m, rows), 1)
@@ -262,7 +269,8 @@
         stack = block_refs[0]
         add = lambda b, v: v + block_term(stack.at[b], uh_ref[b], ul_ref[b], rows)
         image = lax.fori_loop(0, stack.shape[0], add, image)
-    image = pick_rows(to_ref[...], image)
+    high, low = split(image)
+    image = dot(to_ref[...], high) + dot(to_ref[...], low)
     out_refs[0][...] = image
     size = image.shape[0] // n_out
     for k in range(1, n_out):
@@ -469,9 +477,7 @@
     whole = sent[0]
     other = swap(whole, "pcol", nc)
     if direct:
-        got = [whole]
-        for t in range(1, nz):
-            got.append(meet(sent[t], t))
+        got = [whole] + [meet(v, t) for v, t in zip(sent[1:], AWAY[1:])]
     else:
         blocks = whole.reshape(nz, 2 * slots, w)
         blocks = lax.all_to_all(blocks, "pcol", split_axis=0, concat_axis=0, axis_index_groups=groups, tiled=True)
@@ -497,7 +503,9 @@
     sigma_sj = call(pick_kernel, f32(m, w), source, mine, swap(theirs, "pcol", nc), flops=term // 4)
     sigma_sj, d_term = lax.optimization_barrier((sigma_sj, d_term))
     if direct:
-        total = call(sum_kernel, f32(wd, w), terms[0], *[meet(terms[t], t) for t in range(2, nz)], flops=4 * term)
+        far = [meet(terms[t], t) for t in range(2, nz)]
+        far, _ = lax.optimization_barrier((far, sigma_sj))
+        total = call(sum_kernel, f32(wd, w), terms[0], *far, flops=4 * term)
         return sigma_sj, d_term + (total + meet(terms[1], 1))
     terms = lax.all_to_all(terms[0], "pcol", split_axis=0, concat_axis=0, axis_index_groups=groups, tiled=True)
     return sigma_sj, d_term + jnp.sum(terms, axis=0)

time: 67.6 us -> 67.7 us (level)
  waiting for transfers between devices: 23 us -> 25.8 us
  starting transfers between devices: 27.2 us -> 24.8 us
    ppermute x2, waiting for transfers between devices: 1.29 us -> 3.85 us  [spread(): lax.ppermute(v, 'prow', [(k, (k + 2 * t) % size ^ flip) for k in range(si...]
    ppermute x6, starting transfers between devices: 12.2 us -> 9.82 us  [per_device(): lax.ppermute(v, 'pcol', [(k, k ^ 2 * t) for k in range(nc)])]
    ppermute x5, waiting for transfers between devices: 0.01 us -> 2.08 us  [swap(): return lax.ppermute(v, axis, [(k, k ^ 1) for k in range(size)])]
    ppermute x6, waiting for transfers between devices: 9.58 us -> 7.74 us  [per_device(): lax.ppermute(v, 'pcol', [(k, k ^ 2 * t) for k in range(nc)])]
  transfers between devices with their start and end apart: 21 -> 21, of which waited for: 9 -> 12; matrix products, arithmetic and copies ran while one was open for 0% -> 0% of each run, Pallas kernels for 21% -> 20%
where the time goes in v13:
time: 67.7 us; the launch traced here: 67.5 us
  waiting for transfers between devices  25.8 us (38%)
  starting transfers between devices  24.8 us (37%)
  Pallas kernels  14.8 us (22%)
  between operations  0.75 us (1%)
  local copies, waits for them, and re-layouts  0.7 us (1%)
  other arithmetic  0.68 us (1%)
    pallas_call x12, Pallas kernels, call(): pl.pallas_call(kernel, out_shape=out_shape, out_specs=[VMEM] * len(out_sh...  14.8 us
    ppermute x4, waiting for transfers between devices, ring_gather(): lax.ppermute(up, 'pcol', pairs)  10.6 us
    ppermute x6, starting transfers between devices, per_device(): lax.ppermute(v, 'pcol', [(k, k ^ 2 * t) for k in range(nc)])  9.82 us
    ppermute x4, starting transfers between devices, ring_gather(): lax.ppermute(up, 'pcol', pairs)  7.81 us
    ppermute x6, waiting for transfers between devices, per_device(): lax.ppermute(v, 'pcol', [(k, k ^ 2 * t) for k in range(nc)])  7.74 us
    ppermute x2, waiting for transfers between devices, spread(): lax.ppermute(v, 'prow', [(k, (k + 2 * t) % size ^ flip) for k in range(si...  3.85 us
    ppermute x5, starting transfers between devices, swap(): return lax.ppermute(v, axis, [(k, k ^ 1) for k in range(size)])  2.73 us
    ppermute x5, waiting for transfers between devices, swap(): return lax.ppermute(v, axis, [(k, k ^ 1) for k in range(size)])  2.08 us
  transfers between devices with their start and end apart: 21, of which 12 were waited for; matrix products, arithmetic and copies ran while one was open for 0% of the time, Pallas kernels for 20%

profile of v13, /device:TPU:0, one launch (start us, length us, event | category | flops | bytes accessed | tf_op | source)
XLA Modules:
  0.0 67.5 jit_solution(11569641415669302103)
XLA Ops:
  0.6 3.1 %collective-permute-start = (f32[224,256]{1,0:T(8,128)}, f32[224,256]{1,0:T(8,128)S(1)}, u32[]{:S(2)}, u32[]{:S(2)}) collective-permute-start(f32[224,256]{1,0:T(8,128)} %refs_0_.1), channel_id=1, source_target_pairs={{1,0},{0,2},{2,4},{4,6},{6,7},{7,5},{5,3},{3,1},{9,8},{8,10},{10,1... | collective-permute-start | bytes 688136 | tf_op jit(solution)/shard_map/ppermute | solution.py:381
  4.4 2.7 %shard_map.62.refs_0_ = f32[2016,128]{1,0:T(8,128)S(1)} custom-call(s32[1792]{0:T(1024)S(1)} %copy-done, f32[448,896]{1,0:T(8,128)} %sigma_ref.1), custom_call_target="tpu_custom_call" | custom-call | flops 1027604480 | bytes 2644992 | tf_op jit(solution)/shard_map/pallas_call | solution.py:343
  7.1 2.0 %collective-permute-start.8 = (f32[2016,128]{1,0:T(8,128)S(1)}, f32[2016,128]{1,0:T(8,128)S(1)}, u32[]{:S(2)}, u32[]{:S(2)}) collective-permute-start(f32[2016,128]{1,0:T(8,128)S(1)} %shard_map.62.refs_0_), channel_id=1, source_target_pairs={{0,16},{8,24},{16,0},{24,8},{1,17},{9,25},{17,1},{25,9},{2,18},{10... | collective-permute-start | bytes 3096584 | tf_op jit(solution)/shard_map/ppermute | solution.py:457
  9.4 1.5 %collective-permute-done.1.refs_2_ = f32[224,256]{1,0:T(8,128)S(1)} collective-permute-done((f32[224,256]{1,0:T(8,128)}, f32[224,256]{1,0:T(8,128)S(1)}, u32[]{:S(2)}, u32[]{:S(2)}) %collective-permute-start.1) | collective-permute-done | bytes 229408 | tf_op jit(solution)/shard_map/ppermute | solution.py:381
  11.0 1.6 %collective-permute-start.2 = (f32[224,256]{1,0:T(8,128)S(1)}, f32[224,256]{1,0:T(8,128)S(1)}, u32[]{:S(2)}, u32[]{:S(2)}) collective-permute-start(f32[224,256]{1,0:T(8,128)S(1)} %collective-permute-done.refs_1_), channel_id=1, source_target_pairs={{1,0},{0,2},{2,4},{4,6},{6,7},{7,5},{5,3},{3,1},{9,8},{8,10},{10,1... | collective-permute-start | bytes 688136 | tf_op jit(solution)/shard_map/ppermute | solution.py:381
  13.0 4.1 %collective-permute-done.2.refs_3_ = f32[224,256]{1,0:T(8,128)S(1)} collective-permute-done((f32[224,256]{1,0:T(8,128)S(1)}, f32[224,256]{1,0:T(8,128)S(1)}, u32[]{:S(2)}, u32[]{:S(2)}) %collective-permute-start.2) | collective-permute-done | bytes 229408 | tf_op jit(solution)/shard_map/ppermute | solution.py:381
  17.1 1.6 %collective-permute-start.4 = (f32[224,256]{1,0:T(8,128)S(1)}, f32[224,256]{1,0:T(8,128)S(1)}, u32[]{:S(2)}, u32[]{:S(2)}) collective-permute-start(f32[224,256]{1,0:T(8,128)S(1)} %collective-permute-done.2.refs_3_), channel_id=1, source_target_pairs={{1,0},{0,2},{2,4},{4,6},{6,7},{7,5},{5,3},{3,1},{9,8},{8,10},{10,1... | collective-permute-start | bytes 688136 | tf_op jit(solution)/shard_map/ppermute | solution.py:381
  19.2 2.1 %shard_map.59 = (bf16[448,448]{1,0:T(8,128)(2,1)S(1)}, bf16[576,896]{1,0:T(8,128)(2,1)S(1)}, bf16[224,448]{1,0:T(8,128)(2,1)S(1)}) custom-call(s32[1792]{0:T(1024)S(1)} %copy-done), custom_call_target="tpu_custom_call" | custom-call | tf_op jit(solution)/shard_map/pallas_call | solution.py:343
  21.3 1.9 %collective-permute-done.4.refs_5_ = f32[224,256]{1,0:T(8,128)S(1)} collective-permute-done((f32[224,256]{1,0:T(8,128)S(1)}, f32[224,256]{1,0:T(8,128)S(1)}, u32[]{:S(2)}, u32[]{:S(2)}) %collective-permute-start.4) | collective-permute-done | bytes 229408 | tf_op jit(solution)/shard_map/ppermute | solution.py:381
  23.2 1.6 %collective-permute-start.6 = (f32[224,256]{1,0:T(8,128)S(1)}, f32[224,256]{1,0:T(8,128)S(1)}, u32[]{:S(2)}, u32[]{:S(2)}) collective-permute-start(f32[224,256]{1,0:T(8,128)S(1)} %collective-permute-done.4.refs_5_), channel_id=1, source_target_pairs={{1,0},{0,2},{2,4},{4,6},{6,7},{7,5},{5,3},{3,1},{9,8},{8,10},{10,1... | collective-permute-start | bytes 688136 | tf_op jit(solution)/shard_map/ppermute | solution.py:385
  25.2 4.3 %collective-permute-done.6.refs_0_ = f32[224,256]{1,0:T(8,128)S(1)} collective-permute-done((f32[224,256]{1,0:T(8,128)S(1)}, f32[224,256]{1,0:T(8,128)S(1)}, u32[]{:S(2)}, u32[]{:S(2)}) %collective-permute-start.6) | collective-permute-done | bytes 229408 | tf_op jit(solution)/shard_map/ppermute | solution.py:385
  30.0 2.1 %shard_map.63 = (f32[448,256]{1,0:T(8,128)S(1)}, bf16[3,640,256]{2,1,0:T(8,128)(2,1)S(1)}, bf16[3,640,256]{2,1,0:T(8,128)(2,1)S(1)}) custom-call(s32[1792]{0:T(1024)S(1)} %copy-done, f32[2,2376,128]{2,1,0:T(8,128)S(1)} %get-tuple-element.43.us_ref, f32[2016,128]{1,0:T(8,128)S(1)} %shard_map.62.refs_0_), custom_call_target="tpu_custom_call" | custom-call | tf_op jit(solution)/shard_map/pallas_call | solution.py:343
  32.7 1.5 %collective-permute-start.14 = (f32[576,128]{1,0:T(8,128)S(1)}, f32[576,128]{1,0:T(8,128)S(1)}, u32[]{:S(2)}, u32[]{:S(2)}) collective-permute-start(f32[576,128]{1,0:T(8,128)S(1)} %get-tuple-element.55.refs_0_), channel_id=1, source_target_pairs={{0,16},{8,24},{16,0},{24,8},{1,17},{9,25},{17,1},{25,9},{2,18},{10... | collective-permute-start | bytes 884744 | tf_op jit(solution)/shard_map/ppermute | solution.py:362
  34.3 1.1 %shard_map.64.part_ref = f32[448,256]{1,0:T(8,128)S(1)} custom-call(bf16[3,640,256]{2,1,0:T(8,128)(2,1)S(1)} %get-tuple-element.44.uh_ref, bf16[3,640,256]{2,1,0:T(8,128)(2,1)S(1)} %get-tuple-element.45.ul_ref, f32[448,256]{1,0:T(8,128)S(1)} %get-tuple-element.46.part_ref, f32[2016,128]{1,0:T(8,128)S(1)} %collective-permute-done.7.refs_0_, ...), custom_call_target="tpu_custom_call" | custom-call | flops 440401920 | bytes 4947968 | tf_op jit(solution)/shard_map/pallas_call | solution.py:343
  35.4 1.4 %shard_map.65 = (f32[448,256]{1,0:T(8,128)S(1)}, f32[112,256]{1,0:T(8,128)S(1)}, f32[112,256]{1,0:T(8,128)S(1)}, f32[112,256]{1,0:T(8,128)S(1)}) custom-call(bf16[3,640,256]{2,1,0:T(8,128)(2,1)S(1)} %get-tuple-element.44.uh_ref, bf16[3,640,256]{2,1,0:T(8,128)(2,1)S(1)} %get-tuple-element.45.ul_ref, f32[448,256]{1,0:T(8,128)S(1)} %shard_map.64.part_ref, ...), custom_call_target="tpu_custom_call" | custom-call | flops 440401920 | bytes 4661248 | tf_op jit(solution)/shard_map/pallas_call | solution.py:343
  37.8 2.6 %collective-permute-start.10 = (f32[112,256]{1,0:T(8,128)S(1)}, f32[112,256]{1,0:T(8,128)S(1)}, u32[]{:S(2)}, u32[]{:S(2)}) collective-permute-start(f32[112,256]{1,0:T(8,128)S(1)} %get-tuple-element.50), channel_id=1, source_target_pairs={{0,4},{1,5},{2,6},{3,7},{4,0},{5,1},{6,2},{7,3},{8,12},{9,13},{10,... | collective-permute-start | bytes 344072 | tf_op jit(solution)/shard_map/ppermute | solution.py:476
  40.4 1.3 %collective-permute-start.11 = (f32[112,256]{1,0:T(8,128)S(1)}, f32[112,256]{1,0:T(8,128)S(1)}, u32[]{:S(2)}, u32[]{:S(2)}) collective-permute-start(f32[112,256]{1,0:T(8,128)S(1)} %get-tuple-element.51), channel_id=1, source_target_pairs={{0,6},{1,7},{2,4},{3,5},{4,2},{5,3},{6,0},{7,1},{8,14},{9,15},{10,... | collective-permute-start | bytes 344072 | tf_op jit(solution)/shard_map/ppermute | solution.py:476
  42.6 1.6 %collective-permute-start.12 = (f32[112,256]{1,0:T(8,128)S(1)}, f32[112,256]{1,0:T(8,128)S(1)}, u32[]{:S(2)}, u32[]{:S(2)}) collective-permute-start(f32[112,256]{1,0:T(8,128)S(1)} %get-tuple-element.52), channel_id=1, source_target_pairs={{0,2},{1,3},{2,0},{3,1},{4,6},{5,7},{6,4},{7,5},{8,10},{9,11},{10,... | collective-permute-start | bytes 344072 | tf_op jit(solution)/shard_map/ppermute | solution.py:476
  44.2 3.0 %collective-permute-done.15.refs_3_ = f32[576,128]{1,0:T(8,128)S(1)} collective-permute-done((f32[576,128]{1,0:T(8,128)S(1)}, f32[576,128]{1,0:T(8,128)S(1)}, u32[]{:S(2)}, u32[]{:S(2)}) %collective-permute-start.15) | collective-permute-done | bytes 294944 | tf_op jit(solution)/shard_map/ppermute | solution.py:362
  47.2 2.2 %shard_map.66 = (bf16[4,128,896]{2,1,0:T(8,128)(2,1)S(1)}, bf16[4,128,896]{2,1,0:T(8,128)(2,1)S(1)}) custom-call(bf16[576,896]{1,0:T(8,128)(2,1)S(1)} %get-tuple-element.53.place_ref, f32[576,128]{1,0:T(8,128)S(1)} %get-tuple-element.55.refs_0_, f32[576,128]{1,0:T(8,128)S(1)} %collective-permute-done.13.refs_1_, ...), custom_call_target="tpu_custom_call" | custom-call | flops 1056964608 | bytes 4046848 | tf_op jit(solution)/shard_map/pallas_call | solution.py:343
  51.4 1.2 %collective-permute-start.17 = (f32[224,256]{1,0:T(8,128)S(1)}, f32[224,256]{1,0:T(8,128)S(1)}, u32[]{:S(2)}, u32[]{:S(2)}) collective-permute-start(f32[224,256]{1,0:T(8,128)S(1)} %get-tuple-element.66), channel_id=1, source_target_pairs={{0,1},{1,0},{2,3},{3,2},{4,5},{5,4},{6,7},{7,6},{8,9},{9,8},{10,11... | collective-permute-start | bytes 688136 | tf_op jit(solution)/shard_map/ppermute | solution.py:354
  52.6 3.7 %collective-permute-start.18 = (f32[128,256]{1,0:T(8,128)S(1)}, f32[128,256]{1,0:T(8,128)S(1)}, u32[]{:S(2)}, u32[]{:S(2)}) collective-permute-start(f32[128,256]{1,0:T(8,128)S(1)} %get-tuple-element.69), channel_id=1, source_target_pairs={{0,4},{1,5},{2,6},{3,7},{4,0},{5,1},{6,2},{7,3},{8,12},{9,13},{10,... | collective-permute-start | bytes 393224 | tf_op jit(solution)/shard_map/ppermute | solution.py:476
  56.9 2.1 %collective-permute-done.17.other_ref = f32[224,256]{1,0:T(8,128)S(1)} collective-permute-done((f32[224,256]{1,0:T(8,128)S(1)}, f32[224,256]{1,0:T(8,128)S(1)}, u32[]{:S(2)}, u32[]{:S(2)}) %collective-permute-start.17) | collective-permute-done | bytes 229408 | tf_op jit(solution)/shard_map/ppermute | solution.py:354
  60.1 5.6 %collective-permute-done.18.refs_1_ = f32[128,256]{1,0:T(8,128)S(1)} collective-permute-done((f32[128,256]{1,0:T(8,128)S(1)}, f32[128,256]{1,0:T(8,128)S(1)}, u32[]{:S(2)}, u32[]{:S(2)}) %collective-permute-start.18) | collective-permute-done | bytes 131104 | tf_op jit(solution)/shard_map/ppermute | solution.py:476
  (37 shorter events, 10.7 us)
Async XLA Ops:
  0.6 8.8 %collective-permute-start = (f32[224,256]{1,0:T(8,128)}, f32[224,256]{1,0:T(8,128)S(1)}, u32[]{:S(2)}, u32[]{:S(2)}) collective-permute-start(f32[224,256]{1,0:T(8,128)} %refs_0_.1), channel_id=1, source_target_pairs={{1,0},{0,2},{2,4},{4,6},{6,7},{7,5},{5,3},{3,1},{9,8},{8,10},{10,1... | collective-permute-start | bytes 688136 | tf_op jit(solution)/shard_map/ppermute | solution.py:381
  3.7 7.3 %collective-permute-start.1 = (f32[224,256]{1,0:T(8,128)}, f32[224,256]{1,0:T(8,128)S(1)}, u32[]{:S(2)}, u32[]{:S(2)}) collective-permute-start(f32[224,256]{1,0:T(8,128)} %refs_0_.1), channel_id=1, source_target_pairs={{0,1},{2,0},{4,2},{6,4},{7,6},{5,7},{3,5},{1,3},{8,9},{10,8},{12,1... | collective-permute-start | bytes 688136 | tf_op jit(solution)/shard_map/ppermute | solution.py:381
  3.7 0.7 %copy-start = (s32[1792]{0:T(1024)S(1)}, s32[1792]{0:T(1024)}, u32[]{:S(2)}) copy-start(s32[1792]{0:T(1024)} %structure_ref.7) | copy-start | bytes 21508
  4.4 20.3 %copy-start.1 = (f32[224,256]{1,0:T(8,128)S(1)}, f32[224,256]{1,0:T(8,128)}, u32[]{:S(2)}) copy-start(f32[224,256]{1,0:T(8,128)} %refs_0_.1) | copy-start | bytes 688132
  7.1 25.0 %collective-permute-start.8 = (f32[2016,128]{1,0:T(8,128)S(1)}, f32[2016,128]{1,0:T(8,128)S(1)}, u32[]{:S(2)}, u32[]{:S(2)}) collective-permute-start(f32[2016,128]{1,0:T(8,128)S(1)} %shard_map.62.refs_0_), channel_id=1, source_target_pairs={{0,16},{8,24},{16,0},{24,8},{1,17},{9,25},{17,1},{25,9},{2,18},{10... | collective-permute-start | bytes 3096584 | tf_op jit(solution)/shard_map/ppermute | solution.py:457
  11.0 6.2 %collective-permute-start.2 = (f32[224,256]{1,0:T(8,128)S(1)}, f32[224,256]{1,0:T(8,128)S(1)}, u32[]{:S(2)}, u32[]{:S(2)}) collective-permute-start(f32[224,256]{1,0:T(8,128)S(1)} %collective-permute-done.refs_1_), channel_id=1, source_target_pairs={{1,0},{0,2},{2,4},{4,6},{6,7},{7,5},{5,3},{3,1},{9,8},{8,10},{10,1... | collective-permute-start | bytes 688136 | tf_op jit(solution)/shard_map/ppermute | solution.py:381
  12.6 6.2 %collective-permute-start.3 = (f32[224,256]{1,0:T(8,128)S(1)}, f32[224,256]{1,0:T(8,128)S(1)}, u32[]{:S(2)}, u32[]{:S(2)}) collective-permute-start(f32[224,256]{1,0:T(8,128)S(1)} %collective-permute-done.1.refs_2_), channel_id=1, source_target_pairs={{0,1},{2,0},{4,2},{6,4},{7,6},{5,7},{3,5},{1,3},{8,9},{10,8},{12,1... | collective-permute-start | bytes 688136 | tf_op jit(solution)/shard_map/ppermute | solution.py:381
  17.1 6.0 %collective-permute-start.4 = (f32[224,256]{1,0:T(8,128)S(1)}, f32[224,256]{1,0:T(8,128)S(1)}, u32[]{:S(2)}, u32[]{:S(2)}) collective-permute-start(f32[224,256]{1,0:T(8,128)S(1)} %collective-permute-done.2.refs_3_), channel_id=1, source_target_pairs={{1,0},{0,2},{2,4},{4,6},{6,7},{7,5},{5,3},{3,1},{9,8},{8,10},{10,1... | collective-permute-start | bytes 688136 | tf_op jit(solution)/shard_map/ppermute | solution.py:381
  18.7 6.0 %collective-permute-start.5 = (f32[224,256]{1,0:T(8,128)S(1)}, f32[224,256]{1,0:T(8,128)S(1)}, u32[]{:S(2)}, u32[]{:S(2)}) collective-permute-start(f32[224,256]{1,0:T(8,128)S(1)} %collective-permute-done.3.refs_4_), channel_id=1, source_target_pairs={{0,1},{2,0},{4,2},{6,4},{7,6},{5,7},{3,5},{1,3},{8,9},{10,8},{12,1... | collective-permute-start | bytes 688136 | tf_op jit(solution)/shard_map/ppermute | solution.py:381
  19.2 15.1 %collective-permute-start.7 = (f32[2016,128]{1,0:T(8,128)S(1)}, f32[2016,128]{1,0:T(8,128)S(1)}, u32[]{:S(2)}, u32[]{:S(2)}) collective-permute-start(f32[2016,128]{1,0:T(8,128)S(1)} %shard_map.62.refs_0_), channel_id=1, source_target_pairs={{0,8},{8,0},{16,24},{24,16},{1,9},{9,1},{17,25},{25,17},{2,10},{10... | collective-permute-start | bytes 3096584 | tf_op jit(solution)/shard_map/ppermute | solution.py:354
  23.2 6.4 %collective-permute-start.6 = (f32[224,256]{1,0:T(8,128)S(1)}, f32[224,256]{1,0:T(8,128)S(1)}, u32[]{:S(2)}, u32[]{:S(2)}) collective-permute-start(f32[224,256]{1,0:T(8,128)S(1)} %collective-permute-done.4.refs_5_), channel_id=1, source_target_pairs={{1,0},{0,2},{2,4},{4,6},{6,7},{7,5},{5,3},{3,1},{9,8},{8,10},{10,1... | collective-permute-start | bytes 688136 | tf_op jit(solution)/shard_map/ppermute | solution.py:385
  32.2 3.3 %collective-permute-start.9 = (f32[2016,128]{1,0:T(8,128)S(1)}, f32[2016,128]{1,0:T(8,128)S(1)}, u32[]{:S(2)}, u32[]{:S(2)}) collective-permute-start(f32[2016,128]{1,0:T(8,128)S(1)} %collective-permute-done.8.refs_1_), channel_id=1, source_target_pairs={{0,8},{8,0},{16,24},{24,16},{1,9},{9,1},{17,25},{25,17},{2,10},{10... | collective-permute-start | bytes 3096584 | tf_op jit(solution)/shard_map/ppermute | solution.py:354
  32.2 8.2 %collective-permute-start.13 = (f32[576,128]{1,0:T(8,128)S(1)}, f32[576,128]{1,0:T(8,128)S(1)}, u32[]{:S(2)}, u32[]{:S(2)}) collective-permute-start(f32[576,128]{1,0:T(8,128)S(1)} %get-tuple-element.55.refs_0_), channel_id=1, source_target_pairs={{0,8},{8,0},{16,24},{24,16},{1,9},{9,1},{17,25},{25,17},{2,10},{10... | collective-permute-start | bytes 884744 | tf_op jit(solution)/shard_map/ppermute | solution.py:354
  32.7 9.9 %collective-permute-start.14 = (f32[576,128]{1,0:T(8,128)S(1)}, f32[576,128]{1,0:T(8,128)S(1)}, u32[]{:S(2)}, u32[]{:S(2)}) collective-permute-start(f32[576,128]{1,0:T(8,128)S(1)} %get-tuple-element.55.refs_0_), channel_id=1, source_target_pairs={{0,16},{8,24},{16,0},{24,8},{1,17},{9,25},{17,1},{25,9},{2,18},{10... | collective-permute-start | bytes 884744 | tf_op jit(solution)/shard_map/ppermute | solution.py:362
  34.3 12.9 %collective-permute-start.15 = (f32[576,128]{1,0:T(8,128)S(1)}, f32[576,128]{1,0:T(8,128)S(1)}, u32[]{:S(2)}, u32[]{:S(2)}) collective-permute-start(f32[576,128]{1,0:T(8,128)S(1)} %get-tuple-element.55.refs_0_), channel_id=1, source_target_pairs={{0,24},{8,16},{16,8},{24,0},{1,25},{9,17},{17,9},{25,1},{2,26},{10... | collective-permute-start | bytes 884744 | tf_op jit(solution)/shard_map/ppermute | solution.py:362
  36.8 13.6 %collective-permute-start.16 = (f32[448,256]{1,0:T(8,128)S(1)}, f32[448,256]{1,0:T(8,128)S(1)}, u32[]{:S(2)}, u32[]{:S(2)}) collective-permute-start(f32[448,256]{1,0:T(8,128)S(1)} %get-tuple-element.57.refs_0_.mine_ref), channel_id=1, source_target_pairs={{0,1},{1,0},{2,3},{3,2},{4,5},{5,4},{6,7},{7,6},{8,9},{9,8},{10,11... | collective-permute-start | bytes 1376264 | tf_op jit(solution)/shard_map/ppermute | solution.py:354
  37.8 11.8 %collective-permute-start.10 = (f32[112,256]{1,0:T(8,128)S(1)}, f32[112,256]{1,0:T(8,128)S(1)}, u32[]{:S(2)}, u32[]{:S(2)}) collective-permute-start(f32[112,256]{1,0:T(8,128)S(1)} %get-tuple-element.50), channel_id=1, source_target_pairs={{0,4},{1,5},{2,6},{3,7},{4,0},{5,1},{6,2},{7,3},{8,12},{9,13},{10,... | collective-permute-start | bytes 344072 | tf_op jit(solution)/shard_map/ppermute | solution.py:476
  40.4 9.2 %collective-permute-start.11 = (f32[112,256]{1,0:T(8,128)S(1)}, f32[112,256]{1,0:T(8,128)S(1)}, u32[]{:S(2)}, u32[]{:S(2)}) collective-permute-start(f32[112,256]{1,0:T(8,128)S(1)} %get-tuple-element.51), channel_id=1, source_target_pairs={{0,6},{1,7},{2,4},{3,5},{4,2},{5,3},{6,0},{7,1},{8,14},{9,15},{10,... | collective-permute-start | bytes 344072 | tf_op jit(solution)/shard_map/ppermute | solution.py:476
  42.6 7.8 %collective-permute-start.12 = (f32[112,256]{1,0:T(8,128)S(1)}, f32[112,256]{1,0:T(8,128)S(1)}, u32[]{:S(2)}, u32[]{:S(2)}) collective-permute-start(f32[112,256]{1,0:T(8,128)S(1)} %get-tuple-element.52), channel_id=1, source_target_pairs={{0,2},{1,3},{2,0},{3,1},{4,6},{5,7},{6,4},{7,5},{8,10},{9,11},{10,... | collective-permute-start | bytes 344072 | tf_op jit(solution)/shard_map/ppermute | solution.py:476
  51.4 7.6 %collective-permute-start.17 = (f32[224,256]{1,0:T(8,128)S(1)}, f32[224,256]{1,0:T(8,128)S(1)}, u32[]{:S(2)}, u32[]{:S(2)}) collective-permute-start(f32[224,256]{1,0:T(8,128)S(1)} %get-tuple-element.66), channel_id=1, source_target_pairs={{0,1},{1,0},{2,3},{3,2},{4,5},{5,4},{6,7},{7,6},{8,9},{9,8},{10,11... | collective-permute-start | bytes 688136 | tf_op jit(solution)/shard_map/ppermute | solution.py:354
  52.6 13.1 %collective-permute-start.18 = (f32[128,256]{1,0:T(8,128)S(1)}, f32[128,256]{1,0:T(8,128)S(1)}, u32[]{:S(2)}, u32[]{:S(2)}) collective-permute-start(f32[128,256]{1,0:T(8,128)S(1)} %get-tuple-element.69), channel_id=1, source_target_pairs={{0,4},{1,5},{2,6},{3,7},{4,0},{5,1},{6,2},{7,3},{8,12},{9,13},{10,... | collective-permute-start | bytes 393224 | tf_op jit(solution)/shard_map/ppermute | solution.py:476
  56.4 9.4 %collective-permute-start.19 = (f32[128,256]{1,0:T(8,128)S(1)}, f32[128,256]{1,0:T(8,128)S(1)}, u32[]{:S(2)}, u32[]{:S(2)}) collective-permute-start(f32[128,256]{1,0:T(8,128)S(1)} %get-tuple-element.70), channel_id=1, source_target_pairs={{0,6},{1,7},{2,4},{3,5},{4,2},{5,3},{6,0},{7,1},{8,14},{9,15},{10,... | collective-permute-start | bytes 393224 | tf_op jit(solution)/shard_map/ppermute | solution.py:476
  56.8 10.0 %collective-permute-start.20 = (f32[128,256]{1,0:T(8,128)S(1)}, f32[128,256]{1,0:T(8,128)S(1)}, u32[]{:S(2)}, u32[]{:S(2)}) collective-permute-start(f32[128,256]{1,0:T(8,128)S(1)} %get-tuple-element.73), channel_id=1, source_target_pairs={{0,2},{1,3},{2,0},{3,1},{4,6},{5,7},{6,4},{7,5},{8,10},{9,11},{10,... | collective-permute-start | bytes 393224 | tf_op jit(solution)/shard_map/ppermute | solution.py:476
  60.1 6.7 %copy-start.2 = (f32[128,256]{1,0:T(8,128)S(1)}, f32[128,256]{1,0:T(8,128)}, u32[]{:S(2)}) copy-start(f32[128,256]{1,0:T(8,128)} %param.7) | copy-start | bytes 393220

commit v14 on v13

--- a/solution.py
+++ b/solution.py
@@ -332,8 +332,9 @@
     theirs_ref[...] = jnp.concatenate(theirs, axis=0)
 
 
-def pick_kernel(from_ref, mine_ref, other_ref, out_ref):
-    out_ref[...] = -pick_rows(from_ref[...], jnp.concatenate([mine_ref[...], other_ref[...]], axis=0))
+def last_sum_kernel(from_ref, mine_ref, other_ref, d_ref, total_ref, got_ref, sj_ref, jj_ref):
+    sj_ref[...] = -pick_rows(from_ref[...], jnp.concatenate([mine_ref[...], other_ref[...]], axis=0))
+    jj_ref[...] = d_ref[...] + (total_ref[...] + got_ref[...])
 
 
 def call(kernel, out_shape, *args, flops=0, vmem=20, **kw):
@@ -500,15 +501,16 @@
     other, _ = lax.optimization_barrier((other, mine))
     terms = call(correction_kernel, parts, high, low, whole, other, flops=term)
     theirs, _ = lax.optimization_barrier((theirs, terms[0]))
-    sigma_sj = call(pick_kernel, f32(m, w), source, mine, swap(theirs, "pcol", nc), flops=term // 4)
-    sigma_sj, d_term = lax.optimization_barrier((sigma_sj, d_term))
+    theirs = swap(theirs, "pcol", nc)
     if direct:
         far = [meet(terms[t], t) for t in range(2, nz)]
-        far, _ = lax.optimization_barrier((far, sigma_sj))
         total = call(sum_kernel, f32(wd, w), terms[0], *far, flops=4 * term)
-        return sigma_sj, d_term + (total + meet(terms[1], 1))
-    terms = lax.all_to_all(terms[0], "pcol", split_axis=0, concat_axis=0, axis_index_groups=groups, tiled=True)
-    return sigma_sj, d_term + jnp.sum(terms, axis=0)
+        rest = meet(terms[1], 1)
+    else:
+        terms = lax.all_to_all(terms[0], "pcol", split_axis=0, concat_axis=0, axis_index_groups=groups, tiled=True)
+        total, rest = jnp.sum(terms[1:], axis=0), terms[0]
+    outs = [f32(m, w), f32(wd, w)]
+    return tuple(call(last_sum_kernel, outs, source, mine, theirs, d_term, total, rest, flops=term // 4))
 
 
 def solution(mesh):

time: 67.7 us -> 68.1 us (level)
  waiting for transfers between devices: 25.8 us -> 26.8 us
    ppermute x6, waiting for transfers between devices: 7.74 us -> 10.8 us  [per_device(): lax.ppermute(v, 'pcol', [(k, k ^ 2 * t) for k in range(nc)])]
    ppermute x5, waiting for transfers between devices: 2.08 us -> 0.01 us  [swap(): return lax.ppermute(v, axis, [(k, k ^ 1) for k in range(size)])]
  transfers between devices with their start and end apart: 21 -> 21, of which waited for: 12 -> 11; matrix products, arithmetic and copies ran while one was open for 0% -> 0% of each run, Pallas kernels for 20% -> 19%
where the time goes in v14:
time: 68.1 us; the launch traced here: 67.9 us
  waiting for transfers between devices  26.8 us (39%)
  starting transfers between devices  24.9 us (37%)
  Pallas kernels  14.8 us (22%)
  between operations  0.75 us (1%)
  local copies, waits for them, and re-layouts  0.7 us (1%)
    pallas_call x12, Pallas kernels, call(): pl.pallas_call(kernel, out_shape=out_shape, out_specs=[VMEM] * len(out_sh...  14.8 us
    ppermute x6, waiting for transfers between devices, per_device(): lax.ppermute(v, 'pcol', [(k, k ^ 2 * t) for k in range(nc)])  10.8 us
    ppermute x4, waiting for transfers between devices, ring_gather(): lax.ppermute(up, 'pcol', pairs)  10.6 us
    ppermute x6, starting transfers between devices, per_device(): lax.ppermute(v, 'pcol', [(k, k ^ 2 * t) for k in range(nc)])  9.95 us
    ppermute x4, starting transfers between devices, ring_gather(): lax.ppermute(up, 'pcol', pairs)  7.81 us
    ppermute x2, waiting for transfers between devices, spread(): lax.ppermute(v, 'prow', [(k, (k + 2 * t) % size ^ flip) for k in range(si...  3.85 us
    ppermute x5, starting transfers between devices, swap(): return lax.ppermute(v, axis, [(k, k ^ 1) for k in range(size)])  2.67 us
    ppermute x1, starting transfers between devices, per_device(): lax.ppermute(chosen, 'prow', [(k, (k + 2 * t) % nr) for k in range(nr)])  2.03 us
  transfers between devices with their start and end apart: 21, of which 11 were waited for; matrix products, arithmetic and copies ran while one was open for 0% of the time, Pallas kernels for 19%

profile of v14, /device:TPU:0, one launch (start us, length us, event | category | flops | bytes accessed | tf_op | source)
XLA Modules:
  0.0 67.9 jit_solution(13853168341479824882)
XLA Ops:
  0.6 3.1 %collective-permute-start = (f32[224,256]{1,0:T(8,128)}, f32[224,256]{1,0:T(8,128)S(1)}, u32[]{:S(2)}, u32[]{:S(2)}) collective-permute-start(f32[224,256]{1,0:T(8,128)} %refs_0_.1), channel_id=1, source_target_pairs={{1,0},{0,2},{2,4},{4,6},{6,7},{7,5},{5,3},{3,1},{9,8},{8,10},{10,1... | collective-permute-start | bytes 688136 | tf_op jit(solution)/shard_map/ppermute | solution.py:382
  4.4 2.7 %shard_map.62.refs_0_ = f32[2016,128]{1,0:T(8,128)S(1)} custom-call(s32[1792]{0:T(1024)S(1)} %copy-done.1, f32[448,896]{1,0:T(8,128)} %sigma_ref.1), custom_call_target="tpu_custom_call" | custom-call | flops 1027604480 | bytes 2644992 | tf_op jit(solution)/shard_map/pallas_call | solution.py:344
  7.1 2.0 %collective-permute-start.8 = (f32[2016,128]{1,0:T(8,128)S(1)}, f32[2016,128]{1,0:T(8,128)S(1)}, u32[]{:S(2)}, u32[]{:S(2)}) collective-permute-start(f32[2016,128]{1,0:T(8,128)S(1)} %shard_map.62.refs_0_), channel_id=1, source_target_pairs={{0,16},{8,24},{16,0},{24,8},{1,17},{9,25},{17,1},{25,9},{2,18},{10... | collective-permute-start | bytes 3096584 | tf_op jit(solution)/shard_map/ppermute | solution.py:458
  9.4 1.5 %collective-permute-done.1.refs_2_ = f32[224,256]{1,0:T(8,128)S(1)} collective-permute-done((f32[224,256]{1,0:T(8,128)}, f32[224,256]{1,0:T(8,128)S(1)}, u32[]{:S(2)}, u32[]{:S(2)}) %collective-permute-start.1) | collective-permute-done | bytes 229408 | tf_op jit(solution)/shard_map/ppermute | solution.py:382
  11.0 1.6 %collective-permute-start.2 = (f32[224,256]{1,0:T(8,128)S(1)}, f32[224,256]{1,0:T(8,128)S(1)}, u32[]{:S(2)}, u32[]{:S(2)}) collective-permute-start(f32[224,256]{1,0:T(8,128)S(1)} %collective-permute-done.refs_1_), channel_id=1, source_target_pairs={{1,0},{0,2},{2,4},{4,6},{6,7},{7,5},{5,3},{3,1},{9,8},{8,10},{10,1... | collective-permute-start | bytes 688136 | tf_op jit(solution)/shard_map/ppermute | solution.py:382
  13.0 4.1 %collective-permute-done.2.refs_3_ = f32[224,256]{1,0:T(8,128)S(1)} collective-permute-done((f32[224,256]{1,0:T(8,128)S(1)}, f32[224,256]{1,0:T(8,128)S(1)}, u32[]{:S(2)}, u32[]{:S(2)}) %collective-permute-start.2) | collective-permute-done | bytes 229408 | tf_op jit(solution)/shard_map/ppermute | solution.py:382
  17.1 1.6 %collective-permute-start.4 = (f32[224,256]{1,0:T(8,128)S(1)}, f32[224,256]{1,0:T(8,128)S(1)}, u32[]{:S(2)}, u32[]{:S(2)}) collective-permute-start(f32[224,256]{1,0:T(8,128)S(1)} %collective-permute-done.2.refs_3_), channel_id=1, source_target_pairs={{1,0},{0,2},{2,4},{4,6},{6,7},{7,5},{5,3},{3,1},{9,8},{8,10},{10,1... | collective-permute-start | bytes 688136 | tf_op jit(solution)/shard_map/ppermute | solution.py:382
  19.2 2.1 %shard_map.59 = (bf16[448,448]{1,0:T(8,128)(2,1)S(1)}, bf16[576,896]{1,0:T(8,128)(2,1)S(1)}, bf16[224,448]{1,0:T(8,128)(2,1)S(1)}) custom-call(s32[1792]{0:T(1024)S(1)} %copy-done.1), custom_call_target="tpu_custom_call" | custom-call | tf_op jit(solution)/shard_map/pallas_call | solution.py:344
  21.3 1.9 %collective-permute-done.4.refs_5_ = f32[224,256]{1,0:T(8,128)S(1)} collective-permute-done((f32[224,256]{1,0:T(8,128)S(1)}, f32[224,256]{1,0:T(8,128)S(1)}, u32[]{:S(2)}, u32[]{:S(2)}) %collective-permute-start.4) | collective-permute-done | bytes 229408 | tf_op jit(solution)/shard_map/ppermute | solution.py:382
  23.2 1.6 %collective-permute-start.6 = (f32[224,256]{1,0:T(8,128)S(1)}, f32[224,256]{1,0:T(8,128)S(1)}, u32[]{:S(2)}, u32[]{:S(2)}) collective-permute-start(f32[224,256]{1,0:T(8,128)S(1)} %collective-permute-done.4.refs_5_), channel_id=1, source_target_pairs={{1,0},{0,2},{2,4},{4,6},{6,7},{7,5},{5,3},{3,1},{9,8},{8,10},{10,1... | collective-permute-start | bytes 688136 | tf_op jit(solution)/shard_map/ppermute | solution.py:386
  25.2 4.3 %collective-permute-done.6.refs_0_ = f32[224,256]{1,0:T(8,128)S(1)} collective-permute-done((f32[224,256]{1,0:T(8,128)S(1)}, f32[224,256]{1,0:T(8,128)S(1)}, u32[]{:S(2)}, u32[]{:S(2)}) %collective-permute-start.6) | collective-permute-done | bytes 229408 | tf_op jit(solution)/shard_map/ppermute | solution.py:386
  30.0 2.1 %shard_map.63 = (f32[448,256]{1,0:T(8,128)S(1)}, bf16[3,640,256]{2,1,0:T(8,128)(2,1)S(1)}, bf16[3,640,256]{2,1,0:T(8,128)(2,1)S(1)}) custom-call(s32[1792]{0:T(1024)S(1)} %copy-done.1, f32[2,2376,128]{2,1,0:T(8,128)S(1)} %get-tuple-element.39.us_ref, f32[2016,128]{1,0:T(8,128)S(1)} %shard_map.62.refs_0_), custom_call_target="tpu_custom_call" | custom-call | tf_op jit(solution)/shard_map/pallas_call | solution.py:344
  32.7 1.5 %collective-permute-start.14 = (f32[576,128]{1,0:T(8,128)S(1)}, f32[576,128]{1,0:T(8,128)S(1)}, u32[]{:S(2)}, u32[]{:S(2)}) collective-permute-start(f32[576,128]{1,0:T(8,128)S(1)} %get-tuple-element.51.refs_0_), channel_id=1, source_target_pairs={{0,16},{8,24},{16,0},{24,8},{1,17},{9,25},{17,1},{25,9},{2,18},{10... | collective-permute-start | bytes 884744 | tf_op jit(solution)/shard_map/ppermute | solution.py:363
  34.3 1.2 %shard_map.64.part_ref = f32[448,256]{1,0:T(8,128)S(1)} custom-call(bf16[3,640,256]{2,1,0:T(8,128)(2,1)S(1)} %get-tuple-element.40.uh_ref, bf16[3,640,256]{2,1,0:T(8,128)(2,1)S(1)} %get-tuple-element.41.ul_ref, f32[448,256]{1,0:T(8,128)S(1)} %get-tuple-element.42.part_ref, f32[2016,128]{1,0:T(8,128)S(1)} %collective-permute-done.7.refs_0_, ...), custom_call_target="tpu_custom_call" | custom-call | flops 440401920 | bytes 4947968 | tf_op jit(solution)/shard_map/pallas_call | solution.py:344
  35.4 1.4 %shard_map.65 = (f32[448,256]{1,0:T(8,128)S(1)}, f32[112,256]{1,0:T(8,128)S(1)}, f32[112,256]{1,0:T(8,128)S(1)}, f32[112,256]{1,0:T(8,128)S(1)}) custom-call(bf16[3,640,256]{2,1,0:T(8,128)(2,1)S(1)} %get-tuple-element.40.uh_ref, bf16[3,640,256]{2,1,0:T(8,128)(2,1)S(1)} %get-tuple-element.41.ul_ref, f32[448,256]{1,0:T(8,128)S(1)} %shard_map.64.part_ref, ...), custom_call_target="tpu_custom_call" | custom-call | flops 440401920 | bytes 4661248 | tf_op jit(solution)/shard_map/pallas_call | solution.py:344
  37.8 2.6 %collective-permute-start.10 = (f32[112,256]{1,0:T(8,128)S(1)}, f32[112,256]{1,0:T(8,128)S(1)}, u32[]{:S(2)}, u32[]{:S(2)}) collective-permute-start(f32[112,256]{1,0:T(8,128)S(1)} %get-tuple-element.46), channel_id=1, source_target_pairs={{0,4},{1,5},{2,6},{3,7},{4,0},{5,1},{6,2},{7,3},{8,12},{9,13},{10,... | collective-permute-start | bytes 344072 | tf_op jit(solution)/shard_map/ppermute | solution.py:477
  40.4 1.3 %collective-permute-start.11 = (f32[112,256]{1,0:T(8,128)S(1)}, f32[112,256]{1,0:T(8,128)S(1)}, u32[]{:S(2)}, u32[]{:S(2)}) collective-permute-start(f32[112,256]{1,0:T(8,128)S(1)} %get-tuple-element.47), channel_id=1, source_target_pairs={{0,6},{1,7},{2,4},{3,5},{4,2},{5,3},{6,0},{7,1},{8,14},{9,15},{10,... | collective-permute-start | bytes 344072 | tf_op jit(solution)/shard_map/ppermute | solution.py:477
  42.6 1.6 %collective-permute-start.12 = (f32[112,256]{1,0:T(8,128)S(1)}, f32[112,256]{1,0:T(8,128)S(1)}, u32[]{:S(2)}, u32[]{:S(2)}) collective-permute-start(f32[112,256]{1,0:T(8,128)S(1)} %get-tuple-element.48), channel_id=1, source_target_pairs={{0,2},{1,3},{2,0},{3,1},{4,6},{5,7},{6,4},{7,5},{8,10},{9,11},{10,... | collective-permute-start | bytes 344072 | tf_op jit(solution)/shard_map/ppermute | solution.py:477
  44.2 3.0 %collective-permute-done.15.refs_3_ = f32[576,128]{1,0:T(8,128)S(1)} collective-permute-done((f32[576,128]{1,0:T(8,128)S(1)}, f32[576,128]{1,0:T(8,128)S(1)}, u32[]{:S(2)}, u32[]{:S(2)}) %collective-permute-start.15) | collective-permute-done | bytes 294944 | tf_op jit(solution)/shard_map/ppermute | solution.py:363
  47.2 2.2 %shard_map.66 = (bf16[4,128,896]{2,1,0:T(8,128)(2,1)S(1)}, bf16[4,128,896]{2,1,0:T(8,128)(2,1)S(1)}) custom-call(bf16[576,896]{1,0:T(8,128)(2,1)S(1)} %get-tuple-element.49.place_ref, f32[576,128]{1,0:T(8,128)S(1)} %get-tuple-element.51.refs_0_, f32[576,128]{1,0:T(8,128)S(1)} %collective-permute-done.13.refs_1_, ...), custom_call_target="tpu_custom_call" | custom-call | flops 1056964608 | bytes 4046848 | tf_op jit(solution)/shard_map/pallas_call | solution.py:344
  51.4 3.8 %collective-permute-start.18 = (f32[128,256]{1,0:T(8,128)S(1)}, f32[128,256]{1,0:T(8,128)S(1)}, u32[]{:S(2)}, u32[]{:S(2)}) collective-permute-start(f32[128,256]{1,0:T(8,128)S(1)} %get-tuple-element.63), channel_id=1, source_target_pairs={{0,4},{1,5},{2,6},{3,7},{4,0},{5,1},{6,2},{7,3},{8,12},{9,13},{10,... | collective-permute-start | bytes 393224 | tf_op jit(solution)/shard_map/ppermute | solution.py:477
  55.7 1.1 %collective-permute-start.17 = (f32[224,256]{1,0:T(8,128)S(1)}, f32[224,256]{1,0:T(8,128)S(1)}, u32[]{:S(2)}, u32[]{:S(2)}) collective-permute-start(f32[224,256]{1,0:T(8,128)S(1)} %get-tuple-element.62), channel_id=1, source_target_pairs={{0,1},{1,0},{2,3},{3,2},{4,5},{5,4},{6,7},{7,6},{8,9},{9,8},{10,11... | collective-permute-start | bytes 688136 | tf_op jit(solution)/shard_map/ppermute | solution.py:355
  57.0 7.8 %collective-permute-done.18.refs_1_ = f32[128,256]{1,0:T(8,128)S(1)} collective-permute-done((f32[128,256]{1,0:T(8,128)S(1)}, f32[128,256]{1,0:T(8,128)S(1)}, u32[]{:S(2)}, u32[]{:S(2)}) %collective-permute-start.18) | collective-permute-done | bytes 131104 | tf_op jit(solution)/shard_map/ppermute | solution.py:477
  64.9 1.9 %collective-permute-done.20.got_ref = f32[128,256]{1,0:T(8,128)S(1)} collective-permute-done((f32[128,256]{1,0:T(8,128)S(1)}, f32[128,256]{1,0:T(8,128)S(1)}, u32[]{:S(2)}, u32[]{:S(2)}) %collective-permute-start.20) | collective-permute-done | bytes 131104 | tf_op jit(solution)/shard_map/ppermute | solution.py:477
  (36 shorter events, 9.1 us)
Async XLA Ops:
  0.6 8.8 %collective-permute-start = (f32[224,256]{1,0:T(8,128)}, f32[224,256]{1,0:T(8,128)S(1)}, u32[]{:S(2)}, u32[]{:S(2)}) collective-permute-start(f32[224,256]{1,0:T(8,128)} %refs_0_.1), channel_id=1, source_target_pairs={{1,0},{0,2},{2,4},{4,6},{6,7},{7,5},{5,3},{3,1},{9,8},{8,10},{10,1... | collective-permute-start | bytes 688136 | tf_op jit(solution)/shard_map/ppermute | solution.py:382
  3.7 7.3 %collective-permute-start.1 = (f32[224,256]{1,0:T(8,128)}, f32[224,256]{1,0:T(8,128)S(1)}, u32[]{:S(2)}, u32[]{:S(2)}) collective-permute-start(f32[224,256]{1,0:T(8,128)} %refs_0_.1), channel_id=1, source_target_pairs={{0,1},{2,0},{4,2},{6,4},{7,6},{5,7},{3,5},{1,3},{8,9},{10,8},{12,1... | collective-permute-start | bytes 688136 | tf_op jit(solution)/shard_map/ppermute | solution.py:382
  3.7 0.7 %copy-start.1 = (s32[1792]{0:T(1024)S(1)}, s32[1792]{0:T(1024)}, u32[]{:S(2)}) copy-start(s32[1792]{0:T(1024)} %structure_ref.7) | copy-start | bytes 21508
  4.4 20.3 %copy-start.2 = (f32[224,256]{1,0:T(8,128)S(1)}, f32[224,256]{1,0:T(8,128)}, u32[]{:S(2)}) copy-start(f32[224,256]{1,0:T(8,128)} %refs_0_.1) | copy-start | bytes 688132
  7.1 25.0 %collective-permute-start.8 = (f32[2016,128]{1,0:T(8,128)S(1)}, f32[2016,128]{1,0:T(8,128)S(1)}, u32[]{:S(2)}, u32[]{:S(2)}) collective-permute-start(f32[2016,128]{1,0:T(8,128)S(1)} %shard_map.62.refs_0_), channel_id=1, source_target_pairs={{0,16},{8,24},{16,0},{24,8},{1,17},{9,25},{17,1},{25,9},{2,18},{10... | collective-permute-start | bytes 3096584 | tf_op jit(solution)/shard_map/ppermute | solution.py:458
  11.0 6.2 %collective-permute-start.2 = (f32[224,256]{1,0:T(8,128)S(1)}, f32[224,256]{1,0:T(8,128)S(1)}, u32[]{:S(2)}, u32[]{:S(2)}) collective-permute-start(f32[224,256]{1,0:T(8,128)S(1)} %collective-permute-done.refs_1_), channel_id=1, source_target_pairs={{1,0},{0,2},{2,4},{4,6},{6,7},{7,5},{5,3},{3,1},{9,8},{8,10},{10,1... | collective-permute-start | bytes 688136 | tf_op jit(solution)/shard_map/ppermute | solution.py:382
  12.6 6.2 %collective-permute-start.3 = (f32[224,256]{1,0:T(8,128)S(1)}, f32[224,256]{1,0:T(8,128)S(1)}, u32[]{:S(2)}, u32[]{:S(2)}) collective-permute-start(f32[224,256]{1,0:T(8,128)S(1)} %collective-permute-done.1.refs_2_), channel_id=1, source_target_pairs={{0,1},{2,0},{4,2},{6,4},{7,6},{5,7},{3,5},{1,3},{8,9},{10,8},{12,1... | collective-permute-start | bytes 688136 | tf_op jit(solution)/shard_map/ppermute | solution.py:382
  17.1 6.0 %collective-permute-start.4 = (f32[224,256]{1,0:T(8,128)S(1)}, f32[224,256]{1,0:T(8,128)S(1)}, u32[]{:S(2)}, u32[]{:S(2)}) collective-permute-start(f32[224,256]{1,0:T(8,128)S(1)} %collective-permute-done.2.refs_3_), channel_id=1, source_target_pairs={{1,0},{0,2},{2,4},{4,6},{6,7},{7,5},{5,3},{3,1},{9,8},{8,10},{10,1... | collective-permute-start | bytes 688136 | tf_op jit(solution)/shard_map/ppermute | solution.py:382
  18.7 6.0 %collective-permute-start.5 = (f32[224,256]{1,0:T(8,128)S(1)}, f32[224,256]{1,0:T(8,128)S(1)}, u32[]{:S(2)}, u32[]{:S(2)}) collective-permute-start(f32[224,256]{1,0:T(8,128)S(1)} %collective-permute-done.3.refs_4_), channel_id=1, source_target_pairs={{0,1},{2,0},{4,2},{6,4},{7,6},{5,7},{3,5},{1,3},{8,9},{10,8},{12,1... | collective-permute-start | bytes 688136 | tf_op jit(solution)/shard_map/ppermute | solution.py:382
  19.2 15.1 %collective-permute-start.7 = (f32[2016,128]{1,0:T(8,128)S(1)}, f32[2016,128]{1,0:T(8,128)S(1)}, u32[]{:S(2)}, u32[]{:S(2)}) collective-permute-start(f32[2016,128]{1,0:T(8,128)S(1)} %shard_map.62.refs_0_), channel_id=1, source_target_pairs={{0,8},{8,0},{16,24},{24,16},{1,9},{9,1},{17,25},{25,17},{2,10},{10... | collective-permute-start | bytes 3096584 | tf_op jit(solution)/shard_map/ppermute | solution.py:355
  23.2 6.4 %collective-permute-start.6 = (f32[224,256]{1,0:T(8,128)S(1)}, f32[224,256]{1,0:T(8,128)S(1)}, u32[]{:S(2)}, u32[]{:S(2)}) collective-permute-start(f32[224,256]{1,0:T(8,128)S(1)} %collective-permute-done.4.refs_5_), channel_id=1, source_target_pairs={{1,0},{0,2},{2,4},{4,6},{6,7},{7,5},{5,3},{3,1},{9,8},{8,10},{10,1... | collective-permute-start | bytes 688136 | tf_op jit(solution)/shard_map/ppermute | solution.py:386
  32.2 3.3 %collective-permute-start.9 = (f32[2016,128]{1,0:T(8,128)S(1)}, f32[2016,128]{1,0:T(8,128)S(1)}, u32[]{:S(2)}, u32[]{:S(2)}) collective-permute-start(f32[2016,128]{1,0:T(8,128)S(1)} %collective-permute-done.8.refs_1_), channel_id=1, source_target_pairs={{0,8},{8,0},{16,24},{24,16},{1,9},{9,1},{17,25},{25,17},{2,10},{10... | collective-permute-start | bytes 3096584 | tf_op jit(solution)/shard_map/ppermute | solution.py:355
  32.2 8.2 %collective-permute-start.13 = (f32[576,128]{1,0:T(8,128)S(1)}, f32[576,128]{1,0:T(8,128)S(1)}, u32[]{:S(2)}, u32[]{:S(2)}) collective-permute-start(f32[576,128]{1,0:T(8,128)S(1)} %get-tuple-element.51.refs_0_), channel_id=1, source_target_pairs={{0,8},{8,0},{16,24},{24,16},{1,9},{9,1},{17,25},{25,17},{2,10},{10... | collective-permute-start | bytes 884744 | tf_op jit(solution)/shard_map/ppermute | solution.py:355
  32.7 9.9 %collective-permute-start.14 = (f32[576,128]{1,0:T(8,128)S(1)}, f32[576,128]{1,0:T(8,128)S(1)}, u32[]{:S(2)}, u32[]{:S(2)}) collective-permute-start(f32[576,128]{1,0:T(8,128)S(1)} %get-tuple-element.51.refs_0_), channel_id=1, source_target_pairs={{0,16},{8,24},{16,0},{24,8},{1,17},{9,25},{17,1},{25,9},{2,18},{10... | collective-permute-start | bytes 884744 | tf_op jit(solution)/shard_map/ppermute | solution.py:363
  34.3 12.9 %collective-permute-start.15 = (f32[576,128]{1,0:T(8,128)S(1)}, f32[576,128]{1,0:T(8,128)S(1)}, u32[]{:S(2)}, u32[]{:S(2)}) collective-permute-start(f32[576,128]{1,0:T(8,128)S(1)} %get-tuple-element.51.refs_0_), channel_id=1, source_target_pairs={{0,24},{8,16},{16,8},{24,0},{1,25},{9,17},{17,9},{25,1},{2,26},{10... | collective-permute-start | bytes 884744 | tf_op jit(solution)/shard_map/ppermute | solution.py:363
  36.8 13.6 %collective-permute-start.16 = (f32[448,256]{1,0:T(8,128)S(1)}, f32[448,256]{1,0:T(8,128)S(1)}, u32[]{:S(2)}, u32[]{:S(2)}) collective-permute-start(f32[448,256]{1,0:T(8,128)S(1)} %get-tuple-element.53.refs_0_.mine_ref), channel_id=1, source_target_pairs={{0,1},{1,0},{2,3},{3,2},{4,5},{5,4},{6,7},{7,6},{8,9},{9,8},{10,11... | collective-permute-start | bytes 1376264 | tf_op jit(solution)/shard_map/ppermute | solution.py:355
  37.8 11.8 %collective-permute-start.10 = (f32[112,256]{1,0:T(8,128)S(1)}, f32[112,256]{1,0:T(8,128)S(1)}, u32[]{:S(2)}, u32[]{:S(2)}) collective-permute-start(f32[112,256]{1,0:T(8,128)S(1)} %get-tuple-element.46), channel_id=1, source_target_pairs={{0,4},{1,5},{2,6},{3,7},{4,0},{5,1},{6,2},{7,3},{8,12},{9,13},{10,... | collective-permute-start | bytes 344072 | tf_op jit(solution)/shard_map/ppermute | solution.py:477
  40.4 9.2 %collective-permute-start.11 = (f32[112,256]{1,0:T(8,128)S(1)}, f32[112,256]{1,0:T(8,128)S(1)}, u32[]{:S(2)}, u32[]{:S(2)}) collective-permute-start(f32[112,256]{1,0:T(8,128)S(1)} %get-tuple-element.47), channel_id=1, source_target_pairs={{0,6},{1,7},{2,4},{3,5},{4,2},{5,3},{6,0},{7,1},{8,14},{9,15},{10,... | collective-permute-start | bytes 344072 | tf_op jit(solution)/shard_map/ppermute | solution.py:477
  42.6 7.8 %collective-permute-start.12 = (f32[112,256]{1,0:T(8,128)S(1)}, f32[112,256]{1,0:T(8,128)S(1)}, u32[]{:S(2)}, u32[]{:S(2)}) collective-permute-start(f32[112,256]{1,0:T(8,128)S(1)} %get-tuple-element.48), channel_id=1, source_target_pairs={{0,2},{1,3},{2,0},{3,1},{4,6},{5,7},{6,4},{7,5},{8,10},{9,11},{10,... | collective-permute-start | bytes 344072 | tf_op jit(solution)/shard_map/ppermute | solution.py:477
  51.4 13.4 %collective-permute-start.18 = (f32[128,256]{1,0:T(8,128)S(1)}, f32[128,256]{1,0:T(8,128)S(1)}, u32[]{:S(2)}, u32[]{:S(2)}) collective-permute-start(f32[128,256]{1,0:T(8,128)S(1)} %get-tuple-element.63), channel_id=1, source_target_pairs={{0,4},{1,5},{2,6},{3,7},{4,0},{5,1},{6,2},{7,3},{8,12},{9,13},{10,... | collective-permute-start | bytes 393224 | tf_op jit(solution)/shard_map/ppermute | solution.py:477
  55.2 9.6 %collective-permute-start.19 = (f32[128,256]{1,0:T(8,128)S(1)}, f32[128,256]{1,0:T(8,128)S(1)}, u32[]{:S(2)}, u32[]{:S(2)}) collective-permute-start(f32[128,256]{1,0:T(8,128)S(1)} %get-tuple-element.64), channel_id=1, source_target_pairs={{0,6},{1,7},{2,4},{3,5},{4,2},{5,3},{6,0},{7,1},{8,14},{9,15},{10,... | collective-permute-start | bytes 393224 | tf_op jit(solution)/shard_map/ppermute | solution.py:477
  55.7 11.1 %collective-permute-start.17 = (f32[224,256]{1,0:T(8,128)S(1)}, f32[224,256]{1,0:T(8,128)S(1)}, u32[]{:S(2)}, u32[]{:S(2)}) collective-permute-start(f32[224,256]{1,0:T(8,128)S(1)} %get-tuple-element.62), channel_id=1, source_target_pairs={{0,1},{1,0},{2,3},{3,2},{4,5},{5,4},{6,7},{7,6},{8,9},{9,8},{10,11... | collective-permute-start | bytes 688136 | tf_op jit(solution)/shard_map/ppermute | solution.py:355
  56.8 10.0 %copy-start = (f32[128,256]{1,0:T(8,128)S(1)}, f32[128,256]{1,0:T(8,128)}, u32[]{:S(2)}) copy-start(f32[128,256]{1,0:T(8,128)} %d_ref.1) | copy-start | bytes 393220
  56.8 10.0 %collective-permute-start.20 = (f32[128,256]{1,0:T(8,128)S(1)}, f32[128,256]{1,0:T(8,128)S(1)}, u32[]{:S(2)}, u32[]{:S(2)}) collective-permute-start(f32[128,256]{1,0:T(8,128)S(1)} %get-tuple-element.65), channel_id=1, source_target_pairs={{0,2},{1,3},{2,0},{3,1},{4,6},{5,7},{6,4},{7,5},{8,10},{9,11},{10,... | collective-permute-start | bytes 393224 | tf_op jit(solution)/shard_map/ppermute | solution.py:477

commit v15 on v14

--- a/solution.py
+++ b/solution.py
@@ -156,13 +156,6 @@
     own_ref[...] = rows_of(us_ref, names, c // 2, width, [c & 1] if len(refs) > 2 else [0])[:, :w]
 
 
-AWAY = (0, 2, 3, 1)
-
-
-def place_of(t):
-    return jnp.where(t == 1, 3, jnp.where(t > 1, t - 1, 0))
-
-
 def row_order(names, c, rows, nc, slots, direct):
     n = names.shape[1]
     z = c // 2
@@ -174,7 +167,7 @@
     ahead = (count(names < c * rows) - turn + nc - 1) >> lg
     block = turn >> 1
     if direct:
-        block = place_of(block ^ z)
+        block = block ^ z
     block = 2 * block + (turn & 1)
     slot = jnp.where(member > 0.5, block * slots + (rank >> lg) - ahead, -1)
     at = lax.broadcasted_iota(jnp.int32, (rows, nc * slots), 1)
@@ -201,7 +194,7 @@
     ahead = (jnp.where(half == 1, middle, start) - turn + nc - 1) >> lg
     block = turn >> 1
     if direct:
-        block = place_of(block ^ z)
+        block = block ^ z
     slot = (2 * block + (turn & 1)) * slots + (index >> lg) - ahead + (half ^ x) * rows
     slot = jnp.where((named >= 2 * z * rows) & (named < (2 * z + 2) * rows), slot, -1)
     at = lax.broadcasted_iota(jnp.int32, (2 * rows, CAP), 0)
@@ -217,7 +210,7 @@
         before = jnp.where(less, before, count(less))
     block = source >> 1
     if direct:
-        block = place_of(block ^ z)
+        block = block ^ z
     block = block + nz * ((source ^ c) & 1)
     slot = block * slots + lax.broadcasted_iota(jnp.int32, (m, 1), 0) - before
     at = lax.broadcasted_iota(jnp.int32, (m, rows), 1)
@@ -478,7 +471,7 @@
     whole = sent[0]
     other = swap(whole, "pcol", nc)
     if direct:
-        got = [whole] + [meet(v, t) for v, t in zip(sent[1:], AWAY[1:])]
+        got = [whole] + [meet(sent[t], t) for t in range(1, nz)]
     else:
         blocks = whole.reshape(nz, 2 * slots, w)
         blocks = lax.all_to_all(blocks, "pcol", split_axis=0, concat_axis=0, axis_index_groups=groups, tiled=True)

time: 68.1 us -> 67.2 us (0.987)
  waiting for transfers between devices: 26.8 us -> 23.6 us
  starting transfers between devices: 24.9 us -> 27.2 us
    ppermute x6, starting transfers between devices: 9.95 us -> 12.3 us  [per_device(): lax.ppermute(v, 'pcol', [(k, k ^ 2 * t) for k in range(nc)])]
    ppermute x2, waiting for transfers between devices: 3.85 us -> 1.65 us  [spread(): lax.ppermute(v, 'prow', [(k, (k + 2 * t) % size ^ flip) for k in range(si...]
    ppermute x6, waiting for transfers between devices: 10.8 us -> 9.78 us  [per_device(): lax.ppermute(v, 'pcol', [(k, k ^ 2 * t) for k in range(nc)])]
  transfers between devices with their start and end apart: 21 -> 21, of which waited for: 11 -> 10; matrix products, arithmetic and copies ran while one was open for 0% -> 0% of each run, Pallas kernels for 19% -> 19%
where the time goes in v15:
time: 67.2 us; the launch traced here: 67 us
  starting transfers between devices  27.2 us (40%)
  waiting for transfers between devices  23.6 us (35%)
  Pallas kernels  14.8 us (22%)
  between operations  0.76 us (1%)
  local copies, waits for them, and re-layouts  0.7 us (1%)
    pallas_call x12, Pallas kernels, call(): pl.pallas_call(kernel, out_shape=out_shape, out_specs=[VMEM] * len(out_sh...  14.8 us
    ppermute x6, starting transfers between devices, per_device(): lax.ppermute(v, 'pcol', [(k, k ^ 2 * t) for k in range(nc)])  12.3 us
    ppermute x4, waiting for transfers between devices, ring_gather(): lax.ppermute(up, 'pcol', pairs)  10.6 us
    ppermute x6, waiting for transfers between devices, per_device(): lax.ppermute(v, 'pcol', [(k, k ^ 2 * t) for k in range(nc)])  9.78 us
    ppermute x4, starting transfers between devices, ring_gather(): lax.ppermute(up, 'pcol', pairs)  7.81 us
    ppermute x5, starting transfers between devices, swap(): return lax.ppermute(v, axis, [(k, k ^ 1) for k in range(size)])  2.66 us
    ppermute x1, starting transfers between devices, per_device(): lax.ppermute(chosen, 'prow', [(k, (k + 2 * t) % nr) for k in range(nr)])  2.03 us
    ppermute x2, waiting for transfers between devices, spread(): lax.ppermute(v, 'prow', [(k, (k + 2 * t) % size ^ flip) for k in range(si...  1.65 us
  transfers between devices with their start and end apart: 21, of which 10 were waited for; matrix products, arithmetic and copies ran while one was open for 0% of the time, Pallas kernels for 19%

profile of v15, /device:TPU:0, one launch (start us, length us, event | category | flops | bytes accessed | tf_op | source)
XLA Modules:
  0.0 67.0 jit_solution(11998819912417374020)
XLA Ops:
  0.6 3.1 %collective-permute-start = (f32[224,256]{1,0:T(8,128)}, f32[224,256]{1,0:T(8,128)S(1)}, u32[]{:S(2)}, u32[]{:S(2)}) collective-permute-start(f32[224,256]{1,0:T(8,128)} %refs_0_.1), channel_id=1, source_target_pairs={{1,0},{0,2},{2,4},{4,6},{6,7},{7,5},{5,3},{3,1},{9,8},{8,10},{10,1... | collective-permute-start | bytes 688136 | tf_op jit(solution)/shard_map/ppermute | solution.py:375
  4.4 2.7 %shard_map.62.refs_0_ = f32[2016,128]{1,0:T(8,128)S(1)} custom-call(s32[1792]{0:T(1024)S(1)} %copy-done.1, f32[448,896]{1,0:T(8,128)} %sigma_ref.1), custom_call_target="tpu_custom_call" | custom-call | flops 1027604480 | bytes 2644992 | tf_op jit(solution)/shard_map/pallas_call | solution.py:337
  7.1 2.0 %collective-permute-start.8 = (f32[2016,128]{1,0:T(8,128)S(1)}, f32[2016,128]{1,0:T(8,128)S(1)}, u32[]{:S(2)}, u32[]{:S(2)}) collective-permute-start(f32[2016,128]{1,0:T(8,128)S(1)} %shard_map.62.refs_0_), channel_id=1, source_target_pairs={{0,16},{8,24},{16,0},{24,8},{1,17},{9,25},{17,1},{25,9},{2,18},{10... | collective-permute-start | bytes 3096584 | tf_op jit(solution)/shard_map/ppermute | solution.py:451
  9.4 1.5 %collective-permute-done.1.refs_2_ = f32[224,256]{1,0:T(8,128)S(1)} collective-permute-done((f32[224,256]{1,0:T(8,128)}, f32[224,256]{1,0:T(8,128)S(1)}, u32[]{:S(2)}, u32[]{:S(2)}) %collective-permute-start.1) | collective-permute-done | bytes 229408 | tf_op jit(solution)/shard_map/ppermute | solution.py:375
  11.0 1.6 %collective-permute-start.2 = (f32[224,256]{1,0:T(8,128)S(1)}, f32[224,256]{1,0:T(8,128)S(1)}, u32[]{:S(2)}, u32[]{:S(2)}) collective-permute-start(f32[224,256]{1,0:T(8,128)S(1)} %collective-permute-done.refs_1_), channel_id=1, source_target_pairs={{1,0},{0,2},{2,4},{4,6},{6,7},{7,5},{5,3},{3,1},{9,8},{8,10},{10,1... | collective-permute-start | bytes 688136 | tf_op jit(solution)/shard_map/ppermute | solution.py:375
  13.0 4.1 %collective-permute-done.2.refs_3_ = f32[224,256]{1,0:T(8,128)S(1)} collective-permute-done((f32[224,256]{1,0:T(8,128)S(1)}, f32[224,256]{1,0:T(8,128)S(1)}, u32[]{:S(2)}, u32[]{:S(2)}) %collective-permute-start.2) | collective-permute-done | bytes 229408 | tf_op jit(solution)/shard_map/ppermute | solution.py:375
  17.1 1.6 %collective-permute-start.4 = (f32[224,256]{1,0:T(8,128)S(1)}, f32[224,256]{1,0:T(8,128)S(1)}, u32[]{:S(2)}, u32[]{:S(2)}) collective-permute-start(f32[224,256]{1,0:T(8,128)S(1)} %collective-permute-done.2.refs_3_), channel_id=1, source_target_pairs={{1,0},{0,2},{2,4},{4,6},{6,7},{7,5},{5,3},{3,1},{9,8},{8,10},{10,1... | collective-permute-start | bytes 688136 | tf_op jit(solution)/shard_map/ppermute | solution.py:375
  19.2 2.1 %shard_map.59 = (bf16[448,448]{1,0:T(8,128)(2,1)S(1)}, bf16[576,896]{1,0:T(8,128)(2,1)S(1)}, bf16[224,448]{1,0:T(8,128)(2,1)S(1)}) custom-call(s32[1792]{0:T(1024)S(1)} %copy-done.1), custom_call_target="tpu_custom_call" | custom-call | tf_op jit(solution)/shard_map/pallas_call | solution.py:337
  21.2 1.9 %collective-permute-done.4.refs_5_ = f32[224,256]{1,0:T(8,128)S(1)} collective-permute-done((f32[224,256]{1,0:T(8,128)S(1)}, f32[224,256]{1,0:T(8,128)S(1)}, u32[]{:S(2)}, u32[]{:S(2)}) %collective-permute-start.4) | collective-permute-done | bytes 229408 | tf_op jit(solution)/shard_map/ppermute | solution.py:375
  23.2 1.6 %collective-permute-start.6 = (f32[224,256]{1,0:T(8,128)S(1)}, f32[224,256]{1,0:T(8,128)S(1)}, u32[]{:S(2)}, u32[]{:S(2)}) collective-permute-start(f32[224,256]{1,0:T(8,128)S(1)} %collective-permute-done.4.refs_5_), channel_id=1, source_target_pairs={{1,0},{0,2},{2,4},{4,6},{6,7},{7,5},{5,3},{3,1},{9,8},{8,10},{10,1... | collective-permute-start | bytes 688136 | tf_op jit(solution)/shard_map/ppermute | solution.py:379
  25.2 4.3 %collective-permute-done.6.refs_0_ = f32[224,256]{1,0:T(8,128)S(1)} collective-permute-done((f32[224,256]{1,0:T(8,128)S(1)}, f32[224,256]{1,0:T(8,128)S(1)}, u32[]{:S(2)}, u32[]{:S(2)}) %collective-permute-start.6) | collective-permute-done | bytes 229408 | tf_op jit(solution)/shard_map/ppermute | solution.py:379
  30.0 2.1 %shard_map.63 = (f32[448,256]{1,0:T(8,128)S(1)}, bf16[3,640,256]{2,1,0:T(8,128)(2,1)S(1)}, bf16[3,640,256]{2,1,0:T(8,128)(2,1)S(1)}) custom-call(s32[1792]{0:T(1024)S(1)} %copy-done.1, f32[2,2376,128]{2,1,0:T(8,128)S(1)} %get-tuple-element.39.us_ref, f32[2016,128]{1,0:T(8,128)S(1)} %shard_map.62.refs_0_), custom_call_target="tpu_custom_call" | custom-call | tf_op jit(solution)/shard_map/pallas_call | solution.py:337
  32.7 1.5 %collective-permute-start.14 = (f32[576,128]{1,0:T(8,128)S(1)}, f32[576,128]{1,0:T(8,128)S(1)}, u32[]{:S(2)}, u32[]{:S(2)}) collective-permute-start(f32[576,128]{1,0:T(8,128)S(1)} %get-tuple-element.51.refs_0_), channel_id=1, source_target_pairs={{0,16},{8,24},{16,0},{24,8},{1,17},{9,25},{17,1},{25,9},{2,18},{10... | collective-permute-start | bytes 884744 | tf_op jit(solution)/shard_map/ppermute | solution.py:356
  34.2 1.1 %shard_map.64.part_ref = f32[448,256]{1,0:T(8,128)S(1)} custom-call(bf16[3,640,256]{2,1,0:T(8,128)(2,1)S(1)} %get-tuple-element.40.uh_ref, bf16[3,640,256]{2,1,0:T(8,128)(2,1)S(1)} %get-tuple-element.41.ul_ref, f32[448,256]{1,0:T(8,128)S(1)} %get-tuple-element.42.part_ref, f32[2016,128]{1,0:T(8,128)S(1)} %collective-permute-done.7.refs_0_, ...), custom_call_target="tpu_custom_call" | custom-call | flops 440401920 | bytes 4947968 | tf_op jit(solution)/shard_map/pallas_call | solution.py:337
  35.4 1.4 %shard_map.65 = (f32[448,256]{1,0:T(8,128)S(1)}, f32[112,256]{1,0:T(8,128)S(1)}, f32[112,256]{1,0:T(8,128)S(1)}, f32[112,256]{1,0:T(8,128)S(1)}) custom-call(bf16[3,640,256]{2,1,0:T(8,128)(2,1)S(1)} %get-tuple-element.40.uh_ref, bf16[3,640,256]{2,1,0:T(8,128)(2,1)S(1)} %get-tuple-element.41.ul_ref, f32[448,256]{1,0:T(8,128)S(1)} %shard_map.64.part_ref, ...), custom_call_target="tpu_custom_call" | custom-call | flops 440401920 | bytes 4661248 | tf_op jit(solution)/shard_map/pallas_call | solution.py:337
  37.8 1.6 %collective-permute-start.10 = (f32[112,256]{1,0:T(8,128)S(1)}, f32[112,256]{1,0:T(8,128)S(1)}, u32[]{:S(2)}, u32[]{:S(2)}) collective-permute-start(f32[112,256]{1,0:T(8,128)S(1)} %get-tuple-element.46), channel_id=1, source_target_pairs={{0,2},{1,3},{2,0},{3,1},{4,6},{5,7},{6,4},{7,5},{8,10},{9,11},{10,... | collective-permute-start | bytes 344072 | tf_op jit(solution)/shard_map/ppermute | solution.py:470
  39.4 2.6 %collective-permute-start.11 = (f32[112,256]{1,0:T(8,128)S(1)}, f32[112,256]{1,0:T(8,128)S(1)}, u32[]{:S(2)}, u32[]{:S(2)}) collective-permute-start(f32[112,256]{1,0:T(8,128)S(1)} %get-tuple-element.47), channel_id=1, source_target_pairs={{0,4},{1,5},{2,6},{3,7},{4,0},{5,1},{6,2},{7,3},{8,12},{9,13},{10,... | collective-permute-start | bytes 344072 | tf_op jit(solution)/shard_map/ppermute | solution.py:470
  42.6 3.5 %collective-permute-start.12 = (f32[112,256]{1,0:T(8,128)S(1)}, f32[112,256]{1,0:T(8,128)S(1)}, u32[]{:S(2)}, u32[]{:S(2)}) collective-permute-start(f32[112,256]{1,0:T(8,128)S(1)} %get-tuple-element.48), channel_id=1, source_target_pairs={{0,6},{1,7},{2,4},{3,5},{4,2},{5,3},{6,0},{7,1},{8,14},{9,15},{10,... | collective-permute-start | bytes 344072 | tf_op jit(solution)/shard_map/ppermute | solution.py:470
  47.2 2.2 %shard_map.66 = (bf16[4,128,896]{2,1,0:T(8,128)(2,1)S(1)}, bf16[4,128,896]{2,1,0:T(8,128)(2,1)S(1)}) custom-call(bf16[576,896]{1,0:T(8,128)(2,1)S(1)} %get-tuple-element.49.place_ref, f32[576,128]{1,0:T(8,128)S(1)} %get-tuple-element.51.refs_0_, f32[576,128]{1,0:T(8,128)S(1)} %collective-permute-done.13.refs_1_, ...), custom_call_target="tpu_custom_call" | custom-call | flops 1056964608 | bytes 4046848 | tf_op jit(solution)/shard_map/pallas_call | solution.py:337
  49.3 1.9 %collective-permute-done.11.refs_2_ = f32[112,256]{1,0:T(8,128)S(1)} collective-permute-done((f32[112,256]{1,0:T(8,128)S(1)}, f32[112,256]{1,0:T(8,128)S(1)}, u32[]{:S(2)}, u32[]{:S(2)}) %collective-permute-start.11) | collective-permute-done | bytes 114720 | tf_op jit(solution)/shard_map/ppermute | solution.py:470
  52.3 3.2 %collective-permute-start.18 = (f32[128,256]{1,0:T(8,128)S(1)}, f32[128,256]{1,0:T(8,128)S(1)}, u32[]{:S(2)}, u32[]{:S(2)}) collective-permute-start(f32[128,256]{1,0:T(8,128)S(1)} %get-tuple-element.63), channel_id=1, source_target_pairs={{0,4},{1,5},{2,6},{3,7},{4,0},{5,1},{6,2},{7,3},{8,12},{9,13},{10,... | collective-permute-start | bytes 393224 | tf_op jit(solution)/shard_map/ppermute | solution.py:470
  55.5 1.3 %collective-permute-start.19 = (f32[128,256]{1,0:T(8,128)S(1)}, f32[128,256]{1,0:T(8,128)S(1)}, u32[]{:S(2)}, u32[]{:S(2)}) collective-permute-start(f32[128,256]{1,0:T(8,128)S(1)} %get-tuple-element.64), channel_id=1, source_target_pairs={{0,6},{1,7},{2,4},{3,5},{4,2},{5,3},{6,0},{7,1},{8,14},{9,15},{10,... | collective-permute-start | bytes 393224 | tf_op jit(solution)/shard_map/ppermute | solution.py:470
  56.9 1.1 %collective-permute-start.17 = (f32[224,256]{1,0:T(8,128)S(1)}, f32[224,256]{1,0:T(8,128)S(1)}, u32[]{:S(2)}, u32[]{:S(2)}) collective-permute-start(f32[224,256]{1,0:T(8,128)S(1)} %get-tuple-element.62), channel_id=1, source_target_pairs={{0,1},{1,0},{2,3},{3,2},{4,5},{5,4},{6,7},{7,6},{8,9},{9,8},{10,11... | collective-permute-start | bytes 688136 | tf_op jit(solution)/shard_map/ppermute | solution.py:348
  58.0 7.3 %collective-permute-done.18.refs_1_ = f32[128,256]{1,0:T(8,128)S(1)} collective-permute-done((f32[128,256]{1,0:T(8,128)S(1)}, f32[128,256]{1,0:T(8,128)S(1)}, u32[]{:S(2)}, u32[]{:S(2)}) %collective-permute-start.18) | collective-permute-done | bytes 131104 | tf_op jit(solution)/shard_map/ppermute | solution.py:470
  (36 shorter events, 8.8 us)
Async XLA Ops:
  0.6 8.8 %collective-permute-start = (f32[224,256]{1,0:T(8,128)}, f32[224,256]{1,0:T(8,128)S(1)}, u32[]{:S(2)}, u32[]{:S(2)}) collective-permute-start(f32[224,256]{1,0:T(8,128)} %refs_0_.1), channel_id=1, source_target_pairs={{1,0},{0,2},{2,4},{4,6},{6,7},{7,5},{5,3},{3,1},{9,8},{8,10},{10,1... | collective-permute-start | bytes 688136 | tf_op jit(solution)/shard_map/ppermute | solution.py:375
  3.7 7.3 %collective-permute-start.1 = (f32[224,256]{1,0:T(8,128)}, f32[224,256]{1,0:T(8,128)S(1)}, u32[]{:S(2)}, u32[]{:S(2)}) collective-permute-start(f32[224,256]{1,0:T(8,128)} %refs_0_.1), channel_id=1, source_target_pairs={{0,1},{2,0},{4,2},{6,4},{7,6},{5,7},{3,5},{1,3},{8,9},{10,8},{12,1... | collective-permute-start | bytes 688136 | tf_op jit(solution)/shard_map/ppermute | solution.py:375
  3.7 0.7 %copy-start.1 = (s32[1792]{0:T(1024)S(1)}, s32[1792]{0:T(1024)}, u32[]{:S(2)}) copy-start(s32[1792]{0:T(1024)} %structure_ref.7) | copy-start | bytes 21508
  4.4 20.3 %copy-start.2 = (f32[224,256]{1,0:T(8,128)S(1)}, f32[224,256]{1,0:T(8,128)}, u32[]{:S(2)}) copy-start(f32[224,256]{1,0:T(8,128)} %refs_0_.1) | copy-start | bytes 688132
  7.1 25.0 %collective-permute-start.8 = (f32[2016,128]{1,0:T(8,128)S(1)}, f32[2016,128]{1,0:T(8,128)S(1)}, u32[]{:S(2)}, u32[]{:S(2)}) collective-permute-start(f32[2016,128]{1,0:T(8,128)S(1)} %shard_map.62.refs_0_), channel_id=1, source_target_pairs={{0,16},{8,24},{16,0},{24,8},{1,17},{9,25},{17,1},{25,9},{2,18},{10... | collective-permute-start | bytes 3096584 | tf_op jit(solution)/shard_map/ppermute | solution.py:451
  11.0 6.2 %collective-permute-start.2 = (f32[224,256]{1,0:T(8,128)S(1)}, f32[224,256]{1,0:T(8,128)S(1)}, u32[]{:S(2)}, u32[]{:S(2)}) collective-permute-start(f32[224,256]{1,0:T(8,128)S(1)} %collective-permute-done.refs_1_), channel_id=1, source_target_pairs={{1,0},{0,2},{2,4},{4,6},{6,7},{7,5},{5,3},{3,1},{9,8},{8,10},{10,1... | collective-permute-start | bytes 688136 | tf_op jit(solution)/shard_map/ppermute | solution.py:375
  12.6 6.2 %collective-permute-start.3 = (f32[224,256]{1,0:T(8,128)S(1)}, f32[224,256]{1,0:T(8,128)S(1)}, u32[]{:S(2)}, u32[]{:S(2)}) collective-permute-start(f32[224,256]{1,0:T(8,128)S(1)} %collective-permute-done.1.refs_2_), channel_id=1, source_target_pairs={{0,1},{2,0},{4,2},{6,4},{7,6},{5,7},{3,5},{1,3},{8,9},{10,8},{12,1... | collective-permute-start | bytes 688136 | tf_op jit(solution)/shard_map/ppermute | solution.py:375
  17.1 6.0 %collective-permute-start.4 = (f32[224,256]{1,0:T(8,128)S(1)}, f32[224,256]{1,0:T(8,128)S(1)}, u32[]{:S(2)}, u32[]{:S(2)}) collective-permute-start(f32[224,256]{1,0:T(8,128)S(1)} %collective-permute-done.2.refs_3_), channel_id=1, source_target_pairs={{1,0},{0,2},{2,4},{4,6},{6,7},{7,5},{5,3},{3,1},{9,8},{8,10},{10,1... | collective-permute-start | bytes 688136 | tf_op jit(solution)/shard_map/ppermute | solution.py:375
  18.7 6.0 %collective-permute-start.5 = (f32[224,256]{1,0:T(8,128)S(1)}, f32[224,256]{1,0:T(8,128)S(1)}, u32[]{:S(2)}, u32[]{:S(2)}) collective-permute-start(f32[224,256]{1,0:T(8,128)S(1)} %collective-permute-done.3.refs_4_), channel_id=1, source_target_pairs={{0,1},{2,0},{4,2},{6,4},{7,6},{5,7},{3,5},{1,3},{8,9},{10,8},{12,1... | collective-permute-start | bytes 688136 | tf_op jit(solution)/shard_map/ppermute | solution.py:375
  19.2 15.1 %collective-permute-start.7 = (f32[2016,128]{1,0:T(8,128)S(1)}, f32[2016,128]{1,0:T(8,128)S(1)}, u32[]{:S(2)}, u32[]{:S(2)}) collective-permute-start(f32[2016,128]{1,0:T(8,128)S(1)} %shard_map.62.refs_0_), channel_id=1, source_target_pairs={{0,8},{8,0},{16,24},{24,16},{1,9},{9,1},{17,25},{25,17},{2,10},{10... | collective-permute-start | bytes 3096584 | tf_op jit(solution)/shard_map/ppermute | solution.py:348
  23.2 6.3 %collective-permute-start.6 = (f32[224,256]{1,0:T(8,128)S(1)}, f32[224,256]{1,0:T(8,128)S(1)}, u32[]{:S(2)}, u32[]{:S(2)}) collective-permute-start(f32[224,256]{1,0:T(8,128)S(1)} %collective-permute-done.4.refs_5_), channel_id=1, source_target_pairs={{1,0},{0,2},{2,4},{4,6},{6,7},{7,5},{5,3},{3,1},{9,8},{8,10},{10,1... | collective-permute-start | bytes 688136 | tf_op jit(solution)/shard_map/ppermute | solution.py:379
  32.1 3.3 %collective-permute-start.9 = (f32[2016,128]{1,0:T(8,128)S(1)}, f32[2016,128]{1,0:T(8,128)S(1)}, u32[]{:S(2)}, u32[]{:S(2)}) collective-permute-start(f32[2016,128]{1,0:T(8,128)S(1)} %collective-permute-done.8.refs_1_), channel_id=1, source_target_pairs={{0,8},{8,0},{16,24},{24,16},{1,9},{9,1},{17,25},{25,17},{2,10},{10... | collective-permute-start | bytes 3096584 | tf_op jit(solution)/shard_map/ppermute | solution.py:348
  32.2 7.2 %collective-permute-start.13 = (f32[576,128]{1,0:T(8,128)S(1)}, f32[576,128]{1,0:T(8,128)S(1)}, u32[]{:S(2)}, u32[]{:S(2)}) collective-permute-start(f32[576,128]{1,0:T(8,128)S(1)} %get-tuple-element.51.refs_0_), channel_id=1, source_target_pairs={{0,8},{8,0},{16,24},{24,16},{1,9},{9,1},{17,25},{25,17},{2,10},{10... | collective-permute-start | bytes 884744 | tf_op jit(solution)/shard_map/ppermute | solution.py:348
  32.7 9.9 %collective-permute-start.14 = (f32[576,128]{1,0:T(8,128)S(1)}, f32[576,128]{1,0:T(8,128)S(1)}, u32[]{:S(2)}, u32[]{:S(2)}) collective-permute-start(f32[576,128]{1,0:T(8,128)S(1)} %get-tuple-element.51.refs_0_), channel_id=1, source_target_pairs={{0,16},{8,24},{16,0},{24,8},{1,17},{9,25},{17,1},{25,9},{2,18},{10... | collective-permute-start | bytes 884744 | tf_op jit(solution)/shard_map/ppermute | solution.py:356
  34.2 12.9 %collective-permute-start.15 = (f32[576,128]{1,0:T(8,128)S(1)}, f32[576,128]{1,0:T(8,128)S(1)}, u32[]{:S(2)}, u32[]{:S(2)}) collective-permute-start(f32[576,128]{1,0:T(8,128)S(1)} %get-tuple-element.51.refs_0_), channel_id=1, source_target_pairs={{0,24},{8,16},{16,8},{24,0},{1,25},{9,17},{17,9},{25,1},{2,26},{10... | collective-permute-start | bytes 884744 | tf_op jit(solution)/shard_map/ppermute | solution.py:356
  36.8 14.5 %collective-permute-start.16 = (f32[448,256]{1,0:T(8,128)S(1)}, f32[448,256]{1,0:T(8,128)S(1)}, u32[]{:S(2)}, u32[]{:S(2)}) collective-permute-start(f32[448,256]{1,0:T(8,128)S(1)} %get-tuple-element.53.refs_0_.mine_ref), channel_id=1, source_target_pairs={{0,1},{1,0},{2,3},{3,2},{4,5},{5,4},{6,7},{7,6},{8,9},{9,8},{10,11... | collective-permute-start | bytes 1376264 | tf_op jit(solution)/shard_map/ppermute | solution.py:348
  37.8 11.5 %collective-permute-start.10 = (f32[112,256]{1,0:T(8,128)S(1)}, f32[112,256]{1,0:T(8,128)S(1)}, u32[]{:S(2)}, u32[]{:S(2)}) collective-permute-start(f32[112,256]{1,0:T(8,128)S(1)} %get-tuple-element.46), channel_id=1, source_target_pairs={{0,2},{1,3},{2,0},{3,1},{4,6},{5,7},{6,4},{7,5},{8,10},{9,11},{10,... | collective-permute-start | bytes 344072 | tf_op jit(solution)/shard_map/ppermute | solution.py:470
  39.4 11.9 %collective-permute-start.11 = (f32[112,256]{1,0:T(8,128)S(1)}, f32[112,256]{1,0:T(8,128)S(1)}, u32[]{:S(2)}, u32[]{:S(2)}) collective-permute-start(f32[112,256]{1,0:T(8,128)S(1)} %get-tuple-element.47), channel_id=1, source_target_pairs={{0,4},{1,5},{2,6},{3,7},{4,0},{5,1},{6,2},{7,3},{8,12},{9,13},{10,... | collective-permute-start | bytes 344072 | tf_op jit(solution)/shard_map/ppermute | solution.py:470
  42.6 8.7 %collective-permute-start.12 = (f32[112,256]{1,0:T(8,128)S(1)}, f32[112,256]{1,0:T(8,128)S(1)}, u32[]{:S(2)}, u32[]{:S(2)}) collective-permute-start(f32[112,256]{1,0:T(8,128)S(1)} %get-tuple-element.48), channel_id=1, source_target_pairs={{0,6},{1,7},{2,4},{3,5},{4,2},{5,3},{6,0},{7,1},{8,14},{9,15},{10,... | collective-permute-start | bytes 344072 | tf_op jit(solution)/shard_map/ppermute | solution.py:470
  52.3 13.0 %collective-permute-start.18 = (f32[128,256]{1,0:T(8,128)S(1)}, f32[128,256]{1,0:T(8,128)S(1)}, u32[]{:S(2)}, u32[]{:S(2)}) collective-permute-start(f32[128,256]{1,0:T(8,128)S(1)} %get-tuple-element.63), channel_id=1, source_target_pairs={{0,4},{1,5},{2,6},{3,7},{4,0},{5,1},{6,2},{7,3},{8,12},{9,13},{10,... | collective-permute-start | bytes 393224 | tf_op jit(solution)/shard_map/ppermute | solution.py:470
  55.5 9.8 %collective-permute-start.19 = (f32[128,256]{1,0:T(8,128)S(1)}, f32[128,256]{1,0:T(8,128)S(1)}, u32[]{:S(2)}, u32[]{:S(2)}) collective-permute-start(f32[128,256]{1,0:T(8,128)S(1)} %get-tuple-element.64), channel_id=1, source_target_pairs={{0,6},{1,7},{2,4},{3,5},{4,2},{5,3},{6,0},{7,1},{8,14},{9,15},{10,... | collective-permute-start | bytes 393224 | tf_op jit(solution)/shard_map/ppermute | solution.py:470
  56.9 9.0 %collective-permute-start.17 = (f32[224,256]{1,0:T(8,128)S(1)}, f32[224,256]{1,0:T(8,128)S(1)}, u32[]{:S(2)}, u32[]{:S(2)}) collective-permute-start(f32[224,256]{1,0:T(8,128)S(1)} %get-tuple-element.62), channel_id=1, source_target_pairs={{0,1},{1,0},{2,3},{3,2},{4,5},{5,4},{6,7},{7,6},{8,9},{9,8},{10,11... | collective-permute-start | bytes 688136 | tf_op jit(solution)/shard_map/ppermute | solution.py:348
  58.0 7.9 %copy-start = (f32[128,256]{1,0:T(8,128)S(1)}, f32[128,256]{1,0:T(8,128)}, u32[]{:S(2)}) copy-start(f32[128,256]{1,0:T(8,128)} %d_ref.1) | copy-start | bytes 393220
  58.0 7.9 %collective-permute-start.20 = (f32[128,256]{1,0:T(8,128)S(1)}, f32[128,256]{1,0:T(8,128)S(1)}, u32[]{:S(2)}, u32[]{:S(2)}) collective-permute-start(f32[128,256]{1,0:T(8,128)S(1)} %get-tuple-element.65), channel_id=1, source_target_pairs={{0,2},{1,3},{2,0},{3,1},{4,6},{5,7},{6,4},{7,5},{8,10},{9,11},{10,... | collective-permute-start | bytes 393224 | tf_op jit(solution)/shard_map/ppermute | solution.py:470

commit v16 on v15

--- a/solution.py
+++ b/solution.py
@@ -496,9 +496,9 @@
     theirs, _ = lax.optimization_barrier((theirs, terms[0]))
     theirs = swap(theirs, "pcol", nc)
     if direct:
-        far = [meet(terms[t], t) for t in range(2, nz)]
-        total = call(sum_kernel, f32(wd, w), terms[0], *far, flops=4 * term)
-        rest = meet(terms[1], 1)
+        some = [meet(terms[t], t) for t in range(1, nz - 1)]
+        total = call(sum_kernel, f32(wd, w), terms[0], *some, flops=4 * term)
+        rest = meet(terms[nz - 1], nz - 1)
     else:
         terms = lax.all_to_all(terms[0], "pcol", split_axis=0, concat_axis=0, axis_index_groups=groups, tiled=True)
         total, rest = jnp.sum(terms[1:], axis=0), terms[0]

time: 67.2 us -> 68.1 us (1.013)
  waiting for transfers between devices: 23.6 us -> 24.4 us
    ppermute x6, waiting for transfers between devices: 9.78 us -> 10.6 us  [per_device(): lax.ppermute(v, 'pcol', [(k, k ^ 2 * t) for k in range(nc)])]
where the time goes in v16:
time: 68.1 us; the launch traced here: 67.9 us
  starting transfers between devices  27.3 us (40%)
  waiting for transfers between devices  24.4 us (36%)
  Pallas kernels  14.8 us (22%)
  between operations  0.78 us (1%)
  local copies, waits for them, and re-layouts  0.7 us (1%)
    pallas_call x12, Pallas kernels, call(): pl.pallas_call(kernel, out_shape=out_shape, out_specs=[VMEM] * len(out_sh...  14.8 us
    ppermute x6, starting transfers between devices, per_device(): lax.ppermute(v, 'pcol', [(k, k ^ 2 * t) for k in range(nc)])  12.4 us
    ppermute x6, waiting for transfers between devices, per_device(): lax.ppermute(v, 'pcol', [(k, k ^ 2 * t) for k in range(nc)])  10.6 us
    ppermute x4, waiting for transfers between devices, ring_gather(): lax.ppermute(up, 'pcol', pairs)  10.6 us
    ppermute x4, starting transfers between devices, ring_gather(): lax.ppermute(up, 'pcol', pairs)  7.81 us
    ppermute x5, starting transfers between devices, swap(): return lax.ppermute(v, axis, [(k, k ^ 1) for k in range(size)])  2.64 us
    ppermute x1, starting transfers between devices, per_device(): lax.ppermute(chosen, 'prow', [(k, (k + 2 * t) % nr) for k in range(nr)])  2.03 us
    ppermute x2, waiting for transfers between devices, spread(): lax.ppermute(v, 'prow', [(k, (k + 2 * t) % size ^ flip) for k in range(si...  1.64 us
  transfers between devices with their start and end apart: 21, of which 10 were waited for; matrix products, arithmetic and copies ran while one was open for 0% of the time, Pallas kernels for 19%

profile of v16, /device:TPU:0, one launch (start us, length us, event | category | flops | bytes accessed | tf_op | source)
XLA Modules:
  0.0 67.9 jit_solution(10104300726735496381)
XLA Ops:
  0.6 3.1 %collective-permute-start = (f32[224,256]{1,0:T(8,128)}, f32[224,256]{1,0:T(8,128)S(1)}, u32[]{:S(2)}, u32[]{:S(2)}) collective-permute-start(f32[224,256]{1,0:T(8,128)} %refs_0_.1), channel_id=1, source_target_pairs={{1,0},{0,2},{2,4},{4,6},{6,7},{7,5},{5,3},{3,1},{9,8},{8,10},{10,1... | collective-permute-start | bytes 688136 | tf_op jit(solution)/shard_map/ppermute | solution.py:375
  4.4 2.7 %shard_map.62.refs_0_ = f32[2016,128]{1,0:T(8,128)S(1)} custom-call(s32[1792]{0:T(1024)S(1)} %copy-done.1, f32[448,896]{1,0:T(8,128)} %sigma_ref.1), custom_call_target="tpu_custom_call" | custom-call | flops 1027604480 | bytes 2644992 | tf_op jit(solution)/shard_map/pallas_call | solution.py:337
  7.1 2.0 %collective-permute-start.8 = (f32[2016,128]{1,0:T(8,128)S(1)}, f32[2016,128]{1,0:T(8,128)S(1)}, u32[]{:S(2)}, u32[]{:S(2)}) collective-permute-start(f32[2016,128]{1,0:T(8,128)S(1)} %shard_map.62.refs_0_), channel_id=1, source_target_pairs={{0,16},{8,24},{16,0},{24,8},{1,17},{9,25},{17,1},{25,9},{2,18},{10... | collective-permute-start | bytes 3096584 | tf_op jit(solution)/shard_map/ppermute | solution.py:451
  9.4 1.5 %collective-permute-done.1.refs_2_ = f32[224,256]{1,0:T(8,128)S(1)} collective-permute-done((f32[224,256]{1,0:T(8,128)}, f32[224,256]{1,0:T(8,128)S(1)}, u32[]{:S(2)}, u32[]{:S(2)}) %collective-permute-start.1) | collective-permute-done | bytes 229408 | tf_op jit(solution)/shard_map/ppermute | solution.py:375
  11.0 1.6 %collective-permute-start.2 = (f32[224,256]{1,0:T(8,128)S(1)}, f32[224,256]{1,0:T(8,128)S(1)}, u32[]{:S(2)}, u32[]{:S(2)}) collective-permute-start(f32[224,256]{1,0:T(8,128)S(1)} %collective-permute-done.refs_1_), channel_id=1, source_target_pairs={{1,0},{0,2},{2,4},{4,6},{6,7},{7,5},{5,3},{3,1},{9,8},{8,10},{10,1... | collective-permute-start | bytes 688136 | tf_op jit(solution)/shard_map/ppermute | solution.py:375
  13.0 4.1 %collective-permute-done.2.refs_3_ = f32[224,256]{1,0:T(8,128)S(1)} collective-permute-done((f32[224,256]{1,0:T(8,128)S(1)}, f32[224,256]{1,0:T(8,128)S(1)}, u32[]{:S(2)}, u32[]{:S(2)}) %collective-permute-start.2) | collective-permute-done | bytes 229408 | tf_op jit(solution)/shard_map/ppermute | solution.py:375
  17.1 1.6 %collective-permute-start.4 = (f32[224,256]{1,0:T(8,128)S(1)}, f32[224,256]{1,0:T(8,128)S(1)}, u32[]{:S(2)}, u32[]{:S(2)}) collective-permute-start(f32[224,256]{1,0:T(8,128)S(1)} %collective-permute-done.2.refs_3_), channel_id=1, source_target_pairs={{1,0},{0,2},{2,4},{4,6},{6,7},{7,5},{5,3},{3,1},{9,8},{8,10},{10,1... | collective-permute-start | bytes 688136 | tf_op jit(solution)/shard_map/ppermute | solution.py:375
  19.2 2.1 %shard_map.59 = (bf16[448,448]{1,0:T(8,128)(2,1)S(1)}, bf16[576,896]{1,0:T(8,128)(2,1)S(1)}, bf16[224,448]{1,0:T(8,128)(2,1)S(1)}) custom-call(s32[1792]{0:T(1024)S(1)} %copy-done.1), custom_call_target="tpu_custom_call" | custom-call | tf_op jit(solution)/shard_map/pallas_call | solution.py:337
  21.2 1.9 %collective-permute-done.4.refs_5_ = f32[224,256]{1,0:T(8,128)S(1)} collective-permute-done((f32[224,256]{1,0:T(8,128)S(1)}, f32[224,256]{1,0:T(8,128)S(1)}, u32[]{:S(2)}, u32[]{:S(2)}) %collective-permute-start.4) | collective-permute-done | bytes 229408 | tf_op jit(solution)/shard_map/ppermute | solution.py:375
  23.2 1.6 %collective-permute-start.6 = (f32[224,256]{1,0:T(8,128)S(1)}, f32[224,256]{1,0:T(8,128)S(1)}, u32[]{:S(2)}, u32[]{:S(2)}) collective-permute-start(f32[224,256]{1,0:T(8,128)S(1)} %collective-permute-done.4.refs_5_), channel_id=1, source_target_pairs={{1,0},{0,2},{2,4},{4,6},{6,7},{7,5},{5,3},{3,1},{9,8},{8,10},{10,1... | collective-permute-start | bytes 688136 | tf_op jit(solution)/shard_map/ppermute | solution.py:379
  25.2 4.3 %collective-permute-done.6.refs_0_ = f32[224,256]{1,0:T(8,128)S(1)} collective-permute-done((f32[224,256]{1,0:T(8,128)S(1)}, f32[224,256]{1,0:T(8,128)S(1)}, u32[]{:S(2)}, u32[]{:S(2)}) %collective-permute-start.6) | collective-permute-done | bytes 229408 | tf_op jit(solution)/shard_map/ppermute | solution.py:379
  30.0 2.1 %shard_map.63 = (f32[448,256]{1,0:T(8,128)S(1)}, bf16[3,640,256]{2,1,0:T(8,128)(2,1)S(1)}, bf16[3,640,256]{2,1,0:T(8,128)(2,1)S(1)}) custom-call(s32[1792]{0:T(1024)S(1)} %copy-done.1, f32[2,2376,128]{2,1,0:T(8,128)S(1)} %get-tuple-element.39.us_ref, f32[2016,128]{1,0:T(8,128)S(1)} %shard_map.62.refs_0_), custom_call_target="tpu_custom_call" | custom-call | tf_op jit(solution)/shard_map/pallas_call | solution.py:337
  32.7 1.5 %collective-permute-start.14 = (f32[576,128]{1,0:T(8,128)S(1)}, f32[576,128]{1,0:T(8,128)S(1)}, u32[]{:S(2)}, u32[]{:S(2)}) collective-permute-start(f32[576,128]{1,0:T(8,128)S(1)} %get-tuple-element.51.refs_0_), channel_id=1, source_target_pairs={{0,16},{8,24},{16,0},{24,8},{1,17},{9,25},{17,1},{25,9},{2,18},{10... | collective-permute-start | bytes 884744 | tf_op jit(solution)/shard_map/ppermute | solution.py:356
  34.2 1.2 %shard_map.64.part_ref = f32[448,256]{1,0:T(8,128)S(1)} custom-call(bf16[3,640,256]{2,1,0:T(8,128)(2,1)S(1)} %get-tuple-element.40.uh_ref, bf16[3,640,256]{2,1,0:T(8,128)(2,1)S(1)} %get-tuple-element.41.ul_ref, f32[448,256]{1,0:T(8,128)S(1)} %get-tuple-element.42.part_ref, f32[2016,128]{1,0:T(8,128)S(1)} %collective-permute-done.7.refs_0_, ...), custom_call_target="tpu_custom_call" | custom-call | flops 440401920 | bytes 4947968 | tf_op jit(solution)/shard_map/pallas_call | solution.py:337
  35.4 1.4 %shard_map.65 = (f32[448,256]{1,0:T(8,128)S(1)}, f32[112,256]{1,0:T(8,128)S(1)}, f32[112,256]{1,0:T(8,128)S(1)}, f32[112,256]{1,0:T(8,128)S(1)}) custom-call(bf16[3,640,256]{2,1,0:T(8,128)(2,1)S(1)} %get-tuple-element.40.uh_ref, bf16[3,640,256]{2,1,0:T(8,128)(2,1)S(1)} %get-tuple-element.41.ul_ref, f32[448,256]{1,0:T(8,128)S(1)} %shard_map.64.part_ref, ...), custom_call_target="tpu_custom_call" | custom-call | flops 440401920 | bytes 4661248 | tf_op jit(solution)/shard_map/pallas_call | solution.py:337
  37.8 1.6 %collective-permute-start.10 = (f32[112,256]{1,0:T(8,128)S(1)}, f32[112,256]{1,0:T(8,128)S(1)}, u32[]{:S(2)}, u32[]{:S(2)}) collective-permute-start(f32[112,256]{1,0:T(8,128)S(1)} %get-tuple-element.46), channel_id=1, source_target_pairs={{0,2},{1,3},{2,0},{3,1},{4,6},{5,7},{6,4},{7,5},{8,10},{9,11},{10,... | collective-permute-start | bytes 344072 | tf_op jit(solution)/shard_map/ppermute | solution.py:470
  39.4 2.6 %collective-permute-start.11 = (f32[112,256]{1,0:T(8,128)S(1)}, f32[112,256]{1,0:T(8,128)S(1)}, u32[]{:S(2)}, u32[]{:S(2)}) collective-permute-start(f32[112,256]{1,0:T(8,128)S(1)} %get-tuple-element.47), channel_id=1, source_target_pairs={{0,4},{1,5},{2,6},{3,7},{4,0},{5,1},{6,2},{7,3},{8,12},{9,13},{10,... | collective-permute-start | bytes 344072 | tf_op jit(solution)/shard_map/ppermute | solution.py:470
  42.6 3.5 %collective-permute-start.12 = (f32[112,256]{1,0:T(8,128)S(1)}, f32[112,256]{1,0:T(8,128)S(1)}, u32[]{:S(2)}, u32[]{:S(2)}) collective-permute-start(f32[112,256]{1,0:T(8,128)S(1)} %get-tuple-element.48), channel_id=1, source_target_pairs={{0,6},{1,7},{2,4},{3,5},{4,2},{5,3},{6,0},{7,1},{8,14},{9,15},{10,... | collective-permute-start | bytes 344072 | tf_op jit(solution)/shard_map/ppermute | solution.py:470
  47.2 2.2 %shard_map.66 = (bf16[4,128,896]{2,1,0:T(8,128)(2,1)S(1)}, bf16[4,128,896]{2,1,0:T(8,128)(2,1)S(1)}) custom-call(bf16[576,896]{1,0:T(8,128)(2,1)S(1)} %get-tuple-element.49.place_ref, f32[576,128]{1,0:T(8,128)S(1)} %get-tuple-element.51.refs_0_, f32[576,128]{1,0:T(8,128)S(1)} %collective-permute-done.13.refs_1_, ...), custom_call_target="tpu_custom_call" | custom-call | flops 1056964608 | bytes 4046848 | tf_op jit(solution)/shard_map/pallas_call | solution.py:337
  49.3 1.9 %collective-permute-done.11.refs_2_ = f32[112,256]{1,0:T(8,128)S(1)} collective-permute-done((f32[112,256]{1,0:T(8,128)S(1)}, f32[112,256]{1,0:T(8,128)S(1)}, u32[]{:S(2)}, u32[]{:S(2)}) %collective-permute-start.11) | collective-permute-done | bytes 114720 | tf_op jit(solution)/shard_map/ppermute | solution.py:470
  52.3 2.2 %collective-permute-start.18 = (f32[128,256]{1,0:T(8,128)S(1)}, f32[128,256]{1,0:T(8,128)S(1)}, u32[]{:S(2)}, u32[]{:S(2)}) collective-permute-start(f32[128,256]{1,0:T(8,128)S(1)} %get-tuple-element.63), channel_id=1, source_target_pairs={{0,2},{1,3},{2,0},{3,1},{4,6},{5,7},{6,4},{7,5},{8,10},{9,11},{10,... | collective-permute-start | bytes 393224 | tf_op jit(solution)/shard_map/ppermute | solution.py:470
  54.5 1.1 %collective-permute-start.19 = (f32[128,256]{1,0:T(8,128)S(1)}, f32[128,256]{1,0:T(8,128)S(1)}, u32[]{:S(2)}, u32[]{:S(2)}) collective-permute-start(f32[128,256]{1,0:T(8,128)S(1)} %get-tuple-element.64), channel_id=1, source_target_pairs={{0,4},{1,5},{2,6},{3,7},{4,0},{5,1},{6,2},{7,3},{8,12},{9,13},{10,... | collective-permute-start | bytes 393224 | tf_op jit(solution)/shard_map/ppermute | solution.py:470
  56.7 1.4 %collective-permute-start.20 = (f32[128,256]{1,0:T(8,128)S(1)}, f32[128,256]{1,0:T(8,128)S(1)}, u32[]{:S(2)}, u32[]{:S(2)}) collective-permute-start(f32[128,256]{1,0:T(8,128)S(1)} %get-tuple-element.65), channel_id=1, source_target_pairs={{0,6},{1,7},{2,4},{3,5},{4,2},{5,3},{6,0},{7,1},{8,14},{9,15},{10,... | collective-permute-start | bytes 393224 | tf_op jit(solution)/shard_map/ppermute | solution.py:470
  58.7 8.1 %collective-permute-done.19.refs_2_ = f32[128,256]{1,0:T(8,128)S(1)} collective-permute-done((f32[128,256]{1,0:T(8,128)S(1)}, f32[128,256]{1,0:T(8,128)S(1)}, u32[]{:S(2)}, u32[]{:S(2)}) %collective-permute-start.19) | collective-permute-done | bytes 131104 | tf_op jit(solution)/shard_map/ppermute | solution.py:470
  (36 shorter events, 10.0 us)
Async XLA Ops:
  0.6 8.8 %collective-permute-start = (f32[224,256]{1,0:T(8,128)}, f32[224,256]{1,0:T(8,128)S(1)}, u32[]{:S(2)}, u32[]{:S(2)}) collective-permute-start(f32[224,256]{1,0:T(8,128)} %refs_0_.1), channel_id=1, source_target_pairs={{1,0},{0,2},{2,4},{4,6},{6,7},{7,5},{5,3},{3,1},{9,8},{8,10},{10,1... | collective-permute-start | bytes 688136 | tf_op jit(solution)/shard_map/ppermute | solution.py:375
  3.7 7.3 %collective-permute-start.1 = (f32[224,256]{1,0:T(8,128)}, f32[224,256]{1,0:T(8,128)S(1)}, u32[]{:S(2)}, u32[]{:S(2)}) collective-permute-start(f32[224,256]{1,0:T(8,128)} %refs_0_.1), channel_id=1, source_target_pairs={{0,1},{2,0},{4,2},{6,4},{7,6},{5,7},{3,5},{1,3},{8,9},{10,8},{12,1... | collective-permute-start | bytes 688136 | tf_op jit(solution)/shard_map/ppermute | solution.py:375
  3.7 0.7 %copy-start.1 = (s32[1792]{0:T(1024)S(1)}, s32[1792]{0:T(1024)}, u32[]{:S(2)}) copy-start(s32[1792]{0:T(1024)} %structure_ref.7) | copy-start | bytes 21508
  4.4 20.3 %copy-start.2 = (f32[224,256]{1,0:T(8,128)S(1)}, f32[224,256]{1,0:T(8,128)}, u32[]{:S(2)}) copy-start(f32[224,256]{1,0:T(8,128)} %refs_0_.1) | copy-start | bytes 688132
  7.1 25.0 %collective-permute-start.8 = (f32[2016,128]{1,0:T(8,128)S(1)}, f32[2016,128]{1,0:T(8,128)S(1)}, u32[]{:S(2)}, u32[]{:S(2)}) collective-permute-start(f32[2016,128]{1,0:T(8,128)S(1)} %shard_map.62.refs_0_), channel_id=1, source_target_pairs={{0,16},{8,24},{16,0},{24,8},{1,17},{9,25},{17,1},{25,9},{2,18},{10... | collective-permute-start | bytes 3096584 | tf_op jit(solution)/shard_map/ppermute | solution.py:451
  11.0 6.2 %collective-permute-start.2 = (f32[224,256]{1,0:T(8,128)S(1)}, f32[224,256]{1,0:T(8,128)S(1)}, u32[]{:S(2)}, u32[]{:S(2)}) collective-permute-start(f32[224,256]{1,0:T(8,128)S(1)} %collective-permute-done.refs_1_), channel_id=1, source_target_pairs={{1,0},{0,2},{2,4},{4,6},{6,7},{7,5},{5,3},{3,1},{9,8},{8,10},{10,1... | collective-permute-start | bytes 688136 | tf_op jit(solution)/shard_map/ppermute | solution.py:375
  12.6 6.2 %collective-permute-start.3 = (f32[224,256]{1,0:T(8,128)S(1)}, f32[224,256]{1,0:T(8,128)S(1)}, u32[]{:S(2)}, u32[]{:S(2)}) collective-permute-start(f32[224,256]{1,0:T(8,128)S(1)} %collective-permute-done.1.refs_2_), channel_id=1, source_target_pairs={{0,1},{2,0},{4,2},{6,4},{7,6},{5,7},{3,5},{1,3},{8,9},{10,8},{12,1... | collective-permute-start | bytes 688136 | tf_op jit(solution)/shard_map/ppermute | solution.py:375
  17.1 6.0 %collective-permute-start.4 = (f32[224,256]{1,0:T(8,128)S(1)}, f32[224,256]{1,0:T(8,128)S(1)}, u32[]{:S(2)}, u32[]{:S(2)}) collective-permute-start(f32[224,256]{1,0:T(8,128)S(1)} %collective-permute-done.2.refs_3_), channel_id=1, source_target_pairs={{1,0},{0,2},{2,4},{4,6},{6,7},{7,5},{5,3},{3,1},{9,8},{8,10},{10,1... | collective-permute-start | bytes 688136 | tf_op jit(solution)/shard_map/ppermute | solution.py:375
  18.7 6.0 %collective-permute-start.5 = (f32[224,256]{1,0:T(8,128)S(1)}, f32[224,256]{1,0:T(8,128)S(1)}, u32[]{:S(2)}, u32[]{:S(2)}) collective-permute-start(f32[224,256]{1,0:T(8,128)S(1)} %collective-permute-done.3.refs_4_), channel_id=1, source_target_pairs={{0,1},{2,0},{4,2},{6,4},{7,6},{5,7},{3,5},{1,3},{8,9},{10,8},{12,1... | collective-permute-start | bytes 688136 | tf_op jit(solution)/shard_map/ppermute | solution.py:375
  19.2 15.1 %collective-permute-start.7 = (f32[2016,128]{1,0:T(8,128)S(1)}, f32[2016,128]{1,0:T(8,128)S(1)}, u32[]{:S(2)}, u32[]{:S(2)}) collective-permute-start(f32[2016,128]{1,0:T(8,128)S(1)} %shard_map.62.refs_0_), channel_id=1, source_target_pairs={{0,8},{8,0},{16,24},{24,16},{1,9},{9,1},{17,25},{25,17},{2,10},{10... | collective-permute-start | bytes 3096584 | tf_op jit(solution)/shard_map/ppermute | solution.py:348
  23.2 6.3 %collective-permute-start.6 = (f32[224,256]{1,0:T(8,128)S(1)}, f32[224,256]{1,0:T(8,128)S(1)}, u32[]{:S(2)}, u32[]{:S(2)}) collective-permute-start(f32[224,256]{1,0:T(8,128)S(1)} %collective-permute-done.4.refs_5_), channel_id=1, source_target_pairs={{1,0},{0,2},{2,4},{4,6},{6,7},{7,5},{5,3},{3,1},{9,8},{8,10},{10,1... | collective-permute-start | bytes 688136 | tf_op jit(solution)/shard_map/ppermute | solution.py:379
  32.1 3.3 %collective-permute-start.9 = (f32[2016,128]{1,0:T(8,128)S(1)}, f32[2016,128]{1,0:T(8,128)S(1)}, u32[]{:S(2)}, u32[]{:S(2)}) collective-permute-start(f32[2016,128]{1,0:T(8,128)S(1)} %collective-permute-done.8.refs_1_), channel_id=1, source_target_pairs={{0,8},{8,0},{16,24},{24,16},{1,9},{9,1},{17,25},{25,17},{2,10},{10... | collective-permute-start | bytes 3096584 | tf_op jit(solution)/shard_map/ppermute | solution.py:348
  32.2 7.2 %collective-permute-start.13 = (f32[576,128]{1,0:T(8,128)S(1)}, f32[576,128]{1,0:T(8,128)S(1)}, u32[]{:S(2)}, u32[]{:S(2)}) collective-permute-start(f32[576,128]{1,0:T(8,128)S(1)} %get-tuple-element.51.refs_0_), channel_id=1, source_target_pairs={{0,8},{8,0},{16,24},{24,16},{1,9},{9,1},{17,25},{25,17},{2,10},{10... | collective-permute-start | bytes 884744 | tf_op jit(solution)/shard_map/ppermute | solution.py:348
  32.7 9.9 %collective-permute-start.14 = (f32[576,128]{1,0:T(8,128)S(1)}, f32[576,128]{1,0:T(8,128)S(1)}, u32[]{:S(2)}, u32[]{:S(2)}) collective-permute-start(f32[576,128]{1,0:T(8,128)S(1)} %get-tuple-element.51.refs_0_), channel_id=1, source_target_pairs={{0,16},{8,24},{16,0},{24,8},{1,17},{9,25},{17,1},{25,9},{2,18},{10... | collective-permute-start | bytes 884744 | tf_op jit(solution)/shard_map/ppermute | solution.py:356
  34.2 12.9 %collective-permute-start.15 = (f32[576,128]{1,0:T(8,128)S(1)}, f32[576,128]{1,0:T(8,128)S(1)}, u32[]{:S(2)}, u32[]{:S(2)}) collective-permute-start(f32[576,128]{1,0:T(8,128)S(1)} %get-tuple-element.51.refs_0_), channel_id=1, source_target_pairs={{0,24},{8,16},{16,8},{24,0},{1,25},{9,17},{17,9},{25,1},{2,26},{10... | collective-permute-start | bytes 884744 | tf_op jit(solution)/shard_map/ppermute | solution.py:356
  36.8 14.5 %collective-permute-start.16 = (f32[448,256]{1,0:T(8,128)S(1)}, f32[448,256]{1,0:T(8,128)S(1)}, u32[]{:S(2)}, u32[]{:S(2)}) collective-permute-start(f32[448,256]{1,0:T(8,128)S(1)} %get-tuple-element.53.refs_0_.mine_ref), channel_id=1, source_target_pairs={{0,1},{1,0},{2,3},{3,2},{4,5},{5,4},{6,7},{7,6},{8,9},{9,8},{10,11... | collective-permute-start | bytes 1376264 | tf_op jit(solution)/shard_map/ppermute | solution.py:348
  37.8 11.5 %collective-permute-start.10 = (f32[112,256]{1,0:T(8,128)S(1)}, f32[112,256]{1,0:T(8,128)S(1)}, u32[]{:S(2)}, u32[]{:S(2)}) collective-permute-start(f32[112,256]{1,0:T(8,128)S(1)} %get-tuple-element.46), channel_id=1, source_target_pairs={{0,2},{1,3},{2,0},{3,1},{4,6},{5,7},{6,4},{7,5},{8,10},{9,11},{10,... | collective-permute-start | bytes 344072 | tf_op jit(solution)/shard_map/ppermute | solution.py:470
  39.4 11.9 %collective-permute-start.11 = (f32[112,256]{1,0:T(8,128)S(1)}, f32[112,256]{1,0:T(8,128)S(1)}, u32[]{:S(2)}, u32[]{:S(2)}) collective-permute-start(f32[112,256]{1,0:T(8,128)S(1)} %get-tuple-element.47), channel_id=1, source_target_pairs={{0,4},{1,5},{2,6},{3,7},{4,0},{5,1},{6,2},{7,3},{8,12},{9,13},{10,... | collective-permute-start | bytes 344072 | tf_op jit(solution)/shard_map/ppermute | solution.py:470
  42.6 8.7 %collective-permute-start.12 = (f32[112,256]{1,0:T(8,128)S(1)}, f32[112,256]{1,0:T(8,128)S(1)}, u32[]{:S(2)}, u32[]{:S(2)}) collective-permute-start(f32[112,256]{1,0:T(8,128)S(1)} %get-tuple-element.48), channel_id=1, source_target_pairs={{0,6},{1,7},{2,4},{3,5},{4,2},{5,3},{6,0},{7,1},{8,14},{9,15},{10,... | collective-permute-start | bytes 344072 | tf_op jit(solution)/shard_map/ppermute | solution.py:470
  52.3 6.4 %collective-permute-start.18 = (f32[128,256]{1,0:T(8,128)S(1)}, f32[128,256]{1,0:T(8,128)S(1)}, u32[]{:S(2)}, u32[]{:S(2)}) collective-permute-start(f32[128,256]{1,0:T(8,128)S(1)} %get-tuple-element.63), channel_id=1, source_target_pairs={{0,2},{1,3},{2,0},{3,1},{4,6},{5,7},{6,4},{7,5},{8,10},{9,11},{10,... | collective-permute-start | bytes 393224 | tf_op jit(solution)/shard_map/ppermute | solution.py:470
  54.5 12.3 %collective-permute-start.19 = (f32[128,256]{1,0:T(8,128)S(1)}, f32[128,256]{1,0:T(8,128)S(1)}, u32[]{:S(2)}, u32[]{:S(2)}) collective-permute-start(f32[128,256]{1,0:T(8,128)S(1)} %get-tuple-element.64), channel_id=1, source_target_pairs={{0,4},{1,5},{2,6},{3,7},{4,0},{5,1},{6,2},{7,3},{8,12},{9,13},{10,... | collective-permute-start | bytes 393224 | tf_op jit(solution)/shard_map/ppermute | solution.py:470
  55.6 11.2 %collective-permute-start.17 = (f32[224,256]{1,0:T(8,128)S(1)}, f32[224,256]{1,0:T(8,128)S(1)}, u32[]{:S(2)}, u32[]{:S(2)}) collective-permute-start(f32[224,256]{1,0:T(8,128)S(1)} %get-tuple-element.62), channel_id=1, source_target_pairs={{0,1},{1,0},{2,3},{3,2},{4,5},{5,4},{6,7},{7,6},{8,9},{9,8},{10,11... | collective-permute-start | bytes 688136 | tf_op jit(solution)/shard_map/ppermute | solution.py:348
  56.7 10.2 %copy-start = (f32[128,256]{1,0:T(8,128)S(1)}, f32[128,256]{1,0:T(8,128)}, u32[]{:S(2)}) copy-start(f32[128,256]{1,0:T(8,128)} %d_ref.1) | copy-start | bytes 393220
  56.7 10.1 %collective-permute-start.20 = (f32[128,256]{1,0:T(8,128)S(1)}, f32[128,256]{1,0:T(8,128)S(1)}, u32[]{:S(2)}, u32[]{:S(2)}) collective-permute-start(f32[128,256]{1,0:T(8,128)S(1)} %get-tuple-element.65), channel_id=1, source_target_pairs={{0,6},{1,7},{2,4},{3,5},{4,2},{5,3},{6,0},{7,1},{8,14},{9,15},{10,... | collective-permute-start | bytes 393224 | tf_op jit(solution)/shard_map/ppermute | solution.py:470

commit v17 on v15

--- a/solution.py
+++ b/solution.py
@@ -153,7 +153,7 @@
         place_rows(us_ref, refs[0][...], ring_owners(nc, c)[-1])
     names = structure_ref[...].reshape(1, -1)
     w = own_ref.shape[1]
-    own_ref[...] = rows_of(us_ref, names, c // 2, width, [c & 1] if len(refs) > 2 else [0])[:, :w]
+    own_ref[...] = rows_of(us_ref, names, c // 2, width, [c & 1] if len(refs) > 2 else range(us_ref.shape[0]))[:, :w]
 
 
 def row_order(names, c, rows, nc, slots, direct):
@@ -496,7 +496,7 @@
     theirs, _ = lax.optimization_barrier((theirs, terms[0]))
     theirs = swap(theirs, "pcol", nc)
     if direct:
-        far = [meet(terms[t], t) for t in range(2, nz)]
+        far = [meet(terms[t], t) for t in reversed(range(2, nz))]
         total = call(sum_kernel, f32(wd, w), terms[0], *far, flops=4 * term)
         rest = meet(terms[1], 1)
     else:

time: 67.2 us -> 68.3 us (1.016)
  waiting for transfers between devices: 23.6 us -> 24.8 us
    ppermute x6, waiting for transfers between devices: 9.78 us -> 11 us  [per_device(): lax.ppermute(v, 'pcol', [(k, k ^ 2 * t) for k in range(nc)])]
where the time goes in v17:
time: 68.3 us; the launch traced here: 68.1 us
  starting transfers between devices  27 us (40%)
  waiting for transfers between devices  24.8 us (36%)
  Pallas kernels  14.8 us (22%)
  between operations  0.78 us (1%)
  local copies, waits for them, and re-layouts  0.7 us (1%)
    pallas_call x12, Pallas kernels, call(): pl.pallas_call(kernel, out_shape=out_shape, out_specs=[VMEM] * len(out_sh...  14.8 us
    ppermute x6, starting transfers between devices, per_device(): lax.ppermute(v, 'pcol', [(k, k ^ 2 * t) for k in range(nc)])  12.1 us
    ppermute x6, waiting for transfers between devices, per_device(): lax.ppermute(v, 'pcol', [(k, k ^ 2 * t) for k in range(nc)])  11 us
    ppermute x4, waiting for transfers between devices, ring_gather(): lax.ppermute(up, 'pcol', pairs)  10.6 us
    ppermute x4, starting transfers between devices, ring_gather(): lax.ppermute(up, 'pcol', pairs)  7.81 us
    ppermute x5, starting transfers between devices, swap(): return lax.ppermute(v, axis, [(k, k ^ 1) for k in range(size)])  2.65 us
    ppermute x1, starting transfers between devices, per_device(): lax.ppermute(chosen, 'prow', [(k, (k + 2 * t) % nr) for k in range(nr)])  2.03 us
    ppermute x2, waiting for transfers between devices, spread(): lax.ppermute(v, 'prow', [(k, (k + 2 * t) % size ^ flip) for k in range(si...  1.65 us
  transfers between devices with their start and end apart: 21, of which 10 were waited for; matrix products, arithmetic and copies ran while one was open for 0% of the time, Pallas kernels for 19%

profile of v17, /device:TPU:0, one launch (start us, length us, event | category | flops | bytes accessed | tf_op | source)
XLA Modules:
  0.0 68.1 jit_solution(6087944129473346480)
XLA Ops:
  0.6 3.1 %collective-permute-start = (f32[224,256]{1,0:T(8,128)}, f32[224,256]{1,0:T(8,128)S(1)}, u32[]{:S(2)}, u32[]{:S(2)}) collective-permute-start(f32[224,256]{1,0:T(8,128)} %refs_0_.1), channel_id=1, source_target_pairs={{1,0},{0,2},{2,4},{4,6},{6,7},{7,5},{5,3},{3,1},{9,8},{8,10},{10,1... | collective-permute-start | bytes 688136 | tf_op jit(solution)/shard_map/ppermute | solution.py:375
  4.4 2.7 %shard_map.62.refs_0_ = f32[2016,128]{1,0:T(8,128)S(1)} custom-call(s32[1792]{0:T(1024)S(1)} %copy-done.1, f32[448,896]{1,0:T(8,128)} %sigma_ref.1), custom_call_target="tpu_custom_call" | custom-call | flops 1027604480 | bytes 2644992 | tf_op jit(solution)/shard_map/pallas_call | solution.py:337
  7.1 2.0 %collective-permute-start.8 = (f32[2016,128]{1,0:T(8,128)S(1)}, f32[2016,128]{1,0:T(8,128)S(1)}, u32[]{:S(2)}, u32[]{:S(2)}) collective-permute-start(f32[2016,128]{1,0:T(8,128)S(1)} %shard_map.62.refs_0_), channel_id=1, source_target_pairs={{0,16},{8,24},{16,0},{24,8},{1,17},{9,25},{17,1},{25,9},{2,18},{10... | collective-permute-start | bytes 3096584 | tf_op jit(solution)/shard_map/ppermute | solution.py:451
  9.4 1.5 %collective-permute-done.1.refs_2_ = f32[224,256]{1,0:T(8,128)S(1)} collective-permute-done((f32[224,256]{1,0:T(8,128)}, f32[224,256]{1,0:T(8,128)S(1)}, u32[]{:S(2)}, u32[]{:S(2)}) %collective-permute-start.1) | collective-permute-done | bytes 229408 | tf_op jit(solution)/shard_map/ppermute | solution.py:375
  11.0 1.6 %collective-permute-start.2 = (f32[224,256]{1,0:T(8,128)S(1)}, f32[224,256]{1,0:T(8,128)S(1)}, u32[]{:S(2)}, u32[]{:S(2)}) collective-permute-start(f32[224,256]{1,0:T(8,128)S(1)} %collective-permute-done.refs_1_), channel_id=1, source_target_pairs={{1,0},{0,2},{2,4},{4,6},{6,7},{7,5},{5,3},{3,1},{9,8},{8,10},{10,1... | collective-permute-start | bytes 688136 | tf_op jit(solution)/shard_map/ppermute | solution.py:375
  13.0 4.1 %collective-permute-done.2.refs_3_ = f32[224,256]{1,0:T(8,128)S(1)} collective-permute-done((f32[224,256]{1,0:T(8,128)S(1)}, f32[224,256]{1,0:T(8,128)S(1)}, u32[]{:S(2)}, u32[]{:S(2)}) %collective-permute-start.2) | collective-permute-done | bytes 229408 | tf_op jit(solution)/shard_map/ppermute | solution.py:375
  17.1 1.6 %collective-permute-start.4 = (f32[224,256]{1,0:T(8,128)S(1)}, f32[224,256]{1,0:T(8,128)S(1)}, u32[]{:S(2)}, u32[]{:S(2)}) collective-permute-start(f32[224,256]{1,0:T(8,128)S(1)} %collective-permute-done.2.refs_3_), channel_id=1, source_target_pairs={{1,0},{0,2},{2,4},{4,6},{6,7},{7,5},{5,3},{3,1},{9,8},{8,10},{10,1... | collective-permute-start | bytes 688136 | tf_op jit(solution)/shard_map/ppermute | solution.py:375
  19.2 2.1 %shard_map.59 = (bf16[448,448]{1,0:T(8,128)(2,1)S(1)}, bf16[576,896]{1,0:T(8,128)(2,1)S(1)}, bf16[224,448]{1,0:T(8,128)(2,1)S(1)}) custom-call(s32[1792]{0:T(1024)S(1)} %copy-done.1), custom_call_target="tpu_custom_call" | custom-call | tf_op jit(solution)/shard_map/pallas_call | solution.py:337
  21.2 1.9 %collective-permute-done.4.refs_5_ = f32[224,256]{1,0:T(8,128)S(1)} collective-permute-done((f32[224,256]{1,0:T(8,128)S(1)}, f32[224,256]{1,0:T(8,128)S(1)}, u32[]{:S(2)}, u32[]{:S(2)}) %collective-permute-start.4) | collective-permute-done | bytes 229408 | tf_op jit(solution)/shard_map/ppermute | solution.py:375
  23.2 1.6 %collective-permute-start.6 = (f32[224,256]{1,0:T(8,128)S(1)}, f32[224,256]{1,0:T(8,128)S(1)}, u32[]{:S(2)}, u32[]{:S(2)}) collective-permute-start(f32[224,256]{1,0:T(8,128)S(1)} %collective-permute-done.4.refs_5_), channel_id=1, source_target_pairs={{1,0},{0,2},{2,4},{4,6},{6,7},{7,5},{5,3},{3,1},{9,8},{8,10},{10,1... | collective-permute-start | bytes 688136 | tf_op jit(solution)/shard_map/ppermute | solution.py:379
  25.2 4.3 %collective-permute-done.6.refs_0_ = f32[224,256]{1,0:T(8,128)S(1)} collective-permute-done((f32[224,256]{1,0:T(8,128)S(1)}, f32[224,256]{1,0:T(8,128)S(1)}, u32[]{:S(2)}, u32[]{:S(2)}) %collective-permute-start.6) | collective-permute-done | bytes 229408 | tf_op jit(solution)/shard_map/ppermute | solution.py:379
  30.0 2.1 %shard_map.63 = (f32[448,256]{1,0:T(8,128)S(1)}, bf16[3,640,256]{2,1,0:T(8,128)(2,1)S(1)}, bf16[3,640,256]{2,1,0:T(8,128)(2,1)S(1)}) custom-call(s32[1792]{0:T(1024)S(1)} %copy-done.1, f32[2,2376,128]{2,1,0:T(8,128)S(1)} %get-tuple-element.39.us_ref, f32[2016,128]{1,0:T(8,128)S(1)} %shard_map.62.refs_0_), custom_call_target="tpu_custom_call" | custom-call | tf_op jit(solution)/shard_map/pallas_call | solution.py:337
  32.7 1.5 %collective-permute-start.14 = (f32[576,128]{1,0:T(8,128)S(1)}, f32[576,128]{1,0:T(8,128)S(1)}, u32[]{:S(2)}, u32[]{:S(2)}) collective-permute-start(f32[576,128]{1,0:T(8,128)S(1)} %get-tuple-element.51.refs_0_), channel_id=1, source_target_pairs={{0,16},{8,24},{16,0},{24,8},{1,17},{9,25},{17,1},{25,9},{2,18},{10... | collective-permute-start | bytes 884744 | tf_op jit(solution)/shard_map/ppermute | solution.py:356
  34.2 1.1 %shard_map.64.part_ref = f32[448,256]{1,0:T(8,128)S(1)} custom-call(bf16[3,640,256]{2,1,0:T(8,128)(2,1)S(1)} %get-tuple-element.40.uh_ref, bf16[3,640,256]{2,1,0:T(8,128)(2,1)S(1)} %get-tuple-element.41.ul_ref, f32[448,256]{1,0:T(8,128)S(1)} %get-tuple-element.42.part_ref, f32[2016,128]{1,0:T(8,128)S(1)} %collective-permute-done.7.refs_0_, ...), custom_call_target="tpu_custom_call" | custom-call | flops 440401920 | bytes 4947968 | tf_op jit(solution)/shard_map/pallas_call | solution.py:337
  35.4 1.4 %shard_map.65 = (f32[448,256]{1,0:T(8,128)S(1)}, f32[112,256]{1,0:T(8,128)S(1)}, f32[112,256]{1,0:T(8,128)S(1)}, f32[112,256]{1,0:T(8,128)S(1)}) custom-call(bf16[3,640,256]{2,1,0:T(8,128)(2,1)S(1)} %get-tuple-element.40.uh_ref, bf16[3,640,256]{2,1,0:T(8,128)(2,1)S(1)} %get-tuple-element.41.ul_ref, f32[448,256]{1,0:T(8,128)S(1)} %shard_map.64.part_ref, ...), custom_call_target="tpu_custom_call" | custom-call | flops 440401920 | bytes 4661248 | tf_op jit(solution)/shard_map/pallas_call | solution.py:337
  37.8 1.6 %collective-permute-start.10 = (f32[112,256]{1,0:T(8,128)S(1)}, f32[112,256]{1,0:T(8,128)S(1)}, u32[]{:S(2)}, u32[]{:S(2)}) collective-permute-start(f32[112,256]{1,0:T(8,128)S(1)} %get-tuple-element.46), channel_id=1, source_target_pairs={{0,2},{1,3},{2,0},{3,1},{4,6},{5,7},{6,4},{7,5},{8,10},{9,11},{10,... | collective-permute-start | bytes 344072 | tf_op jit(solution)/shard_map/ppermute | solution.py:470
  39.4 2.6 %collective-permute-start.11 = (f32[112,256]{1,0:T(8,128)S(1)}, f32[112,256]{1,0:T(8,128)S(1)}, u32[]{:S(2)}, u32[]{:S(2)}) collective-permute-start(f32[112,256]{1,0:T(8,128)S(1)} %get-tuple-element.47), channel_id=1, source_target_pairs={{0,4},{1,5},{2,6},{3,7},{4,0},{5,1},{6,2},{7,3},{8,12},{9,13},{10,... | collective-permute-start | bytes 344072 | tf_op jit(solution)/shard_map/ppermute | solution.py:470
  42.6 3.5 %collective-permute-start.12 = (f32[112,256]{1,0:T(8,128)S(1)}, f32[112,256]{1,0:T(8,128)S(1)}, u32[]{:S(2)}, u32[]{:S(2)}) collective-permute-start(f32[112,256]{1,0:T(8,128)S(1)} %get-tuple-element.48), channel_id=1, source_target_pairs={{0,6},{1,7},{2,4},{3,5},{4,2},{5,3},{6,0},{7,1},{8,14},{9,15},{10,... | collective-permute-start | bytes 344072 | tf_op jit(solution)/shard_map/ppermute | solution.py:470
  47.2 2.2 %shard_map.66 = (bf16[4,128,896]{2,1,0:T(8,128)(2,1)S(1)}, bf16[4,128,896]{2,1,0:T(8,128)(2,1)S(1)}) custom-call(bf16[576,896]{1,0:T(8,128)(2,1)S(1)} %get-tuple-element.49.place_ref, f32[576,128]{1,0:T(8,128)S(1)} %get-tuple-element.51.refs_0_, f32[576,128]{1,0:T(8,128)S(1)} %collective-permute-done.13.refs_1_, ...), custom_call_target="tpu_custom_call" | custom-call | flops 1056964608 | bytes 4046848 | tf_op jit(solution)/shard_map/pallas_call | solution.py:337
  49.3 1.9 %collective-permute-done.11.refs_2_ = f32[112,256]{1,0:T(8,128)S(1)} collective-permute-done((f32[112,256]{1,0:T(8,128)S(1)}, f32[112,256]{1,0:T(8,128)S(1)}, u32[]{:S(2)}, u32[]{:S(2)}) %collective-permute-start.11) | collective-permute-done | bytes 114720 | tf_op jit(solution)/shard_map/ppermute | solution.py:470
  52.3 2.5 %collective-permute-start.18 = (f32[128,256]{1,0:T(8,128)S(1)}, f32[128,256]{1,0:T(8,128)S(1)}, u32[]{:S(2)}, u32[]{:S(2)}) collective-permute-start(f32[128,256]{1,0:T(8,128)S(1)} %get-tuple-element.63), channel_id=1, source_target_pairs={{0,6},{1,7},{2,4},{3,5},{4,2},{5,3},{6,0},{7,1},{8,14},{9,15},{10,... | collective-permute-start | bytes 393224 | tf_op jit(solution)/shard_map/ppermute | solution.py:470
  54.8 1.1 %collective-permute-start.19 = (f32[128,256]{1,0:T(8,128)S(1)}, f32[128,256]{1,0:T(8,128)S(1)}, u32[]{:S(2)}, u32[]{:S(2)}) collective-permute-start(f32[128,256]{1,0:T(8,128)S(1)} %get-tuple-element.64), channel_id=1, source_target_pairs={{0,4},{1,5},{2,6},{3,7},{4,0},{5,1},{6,2},{7,3},{8,12},{9,13},{10,... | collective-permute-start | bytes 393224 | tf_op jit(solution)/shard_map/ppermute | solution.py:470
  57.9 2.6 %collective-permute-done.18.refs_1_ = f32[128,256]{1,0:T(8,128)S(1)} collective-permute-done((f32[128,256]{1,0:T(8,128)S(1)}, f32[128,256]{1,0:T(8,128)S(1)}, u32[]{:S(2)}, u32[]{:S(2)}) %collective-permute-start.18) | collective-permute-done | bytes 131104 | tf_op jit(solution)/shard_map/ppermute | solution.py:470
  60.4 6.5 %collective-permute-done.19.refs_2_ = f32[128,256]{1,0:T(8,128)S(1)} collective-permute-done((f32[128,256]{1,0:T(8,128)S(1)}, f32[128,256]{1,0:T(8,128)S(1)}, u32[]{:S(2)}, u32[]{:S(2)}) %collective-permute-start.19) | collective-permute-done | bytes 131104 | tf_op jit(solution)/shard_map/ppermute | solution.py:470
  (36 shorter events, 10.1 us)
Async XLA Ops:
  0.6 8.8 %collective-permute-start = (f32[224,256]{1,0:T(8,128)}, f32[224,256]{1,0:T(8,128)S(1)}, u32[]{:S(2)}, u32[]{:S(2)}) collective-permute-start(f32[224,256]{1,0:T(8,128)} %refs_0_.1), channel_id=1, source_target_pairs={{1,0},{0,2},{2,4},{4,6},{6,7},{7,5},{5,3},{3,1},{9,8},{8,10},{10,1... | collective-permute-start | bytes 688136 | tf_op jit(solution)/shard_map/ppermute | solution.py:375
  3.7 7.3 %collective-permute-start.1 = (f32[224,256]{1,0:T(8,128)}, f32[224,256]{1,0:T(8,128)S(1)}, u32[]{:S(2)}, u32[]{:S(2)}) collective-permute-start(f32[224,256]{1,0:T(8,128)} %refs_0_.1), channel_id=1, source_target_pairs={{0,1},{2,0},{4,2},{6,4},{7,6},{5,7},{3,5},{1,3},{8,9},{10,8},{12,1... | collective-permute-start | bytes 688136 | tf_op jit(solution)/shard_map/ppermute | solution.py:375
  3.7 0.7 %copy-start.1 = (s32[1792]{0:T(1024)S(1)}, s32[1792]{0:T(1024)}, u32[]{:S(2)}) copy-start(s32[1792]{0:T(1024)} %structure_ref.7) | copy-start | bytes 21508
  4.4 20.3 %copy-start.2 = (f32[224,256]{1,0:T(8,128)S(1)}, f32[224,256]{1,0:T(8,128)}, u32[]{:S(2)}) copy-start(f32[224,256]{1,0:T(8,128)} %refs_0_.1) | copy-start | bytes 688132
  7.1 25.0 %collective-permute-start.8 = (f32[2016,128]{1,0:T(8,128)S(1)}, f32[2016,128]{1,0:T(8,128)S(1)}, u32[]{:S(2)}, u32[]{:S(2)}) collective-permute-start(f32[2016,128]{1,0:T(8,128)S(1)} %shard_map.62.refs_0_), channel_id=1, source_target_pairs={{0,16},{8,24},{16,0},{24,8},{1,17},{9,25},{17,1},{25,9},{2,18},{10... | collective-permute-start | bytes 3096584 | tf_op jit(solution)/shard_map/ppermute | solution.py:451
  11.0 6.2 %collective-permute-start.2 = (f32[224,256]{1,0:T(8,128)S(1)}, f32[224,256]{1,0:T(8,128)S(1)}, u32[]{:S(2)}, u32[]{:S(2)}) collective-permute-start(f32[224,256]{1,0:T(8,128)S(1)} %collective-permute-done.refs_1_), channel_id=1, source_target_pairs={{1,0},{0,2},{2,4},{4,6},{6,7},{7,5},{5,3},{3,1},{9,8},{8,10},{10,1... | collective-permute-start | bytes 688136 | tf_op jit(solution)/shard_map/ppermute | solution.py:375
  12.6 6.2 %collective-permute-start.3 = (f32[224,256]{1,0:T(8,128)S(1)}, f32[224,256]{1,0:T(8,128)S(1)}, u32[]{:S(2)}, u32[]{:S(2)}) collective-permute-start(f32[224,256]{1,0:T(8,128)S(1)} %collective-permute-done.1.refs_2_), channel_id=1, source_target_pairs={{0,1},{2,0},{4,2},{6,4},{7,6},{5,7},{3,5},{1,3},{8,9},{10,8},{12,1... | collective-permute-start | bytes 688136 | tf_op jit(solution)/shard_map/ppermute | solution.py:375
  17.1 6.0 %collective-permute-start.4 = (f32[224,256]{1,0:T(8,128)S(1)}, f32[224,256]{1,0:T(8,128)S(1)}, u32[]{:S(2)}, u32[]{:S(2)}) collective-permute-start(f32[224,256]{1,0:T(8,128)S(1)} %collective-permute-done.2.refs_3_), channel_id=1, source_target_pairs={{1,0},{0,2},{2,4},{4,6},{6,7},{7,5},{5,3},{3,1},{9,8},{8,10},{10,1... | collective-permute-start | bytes 688136 | tf_op jit(solution)/shard_map/ppermute | solution.py:375
  18.7 6.0 %collective-permute-start.5 = (f32[224,256]{1,0:T(8,128)S(1)}, f32[224,256]{1,0:T(8,128)S(1)}, u32[]{:S(2)}, u32[]{:S(2)}) collective-permute-start(f32[224,256]{1,0:T(8,128)S(1)} %collective-permute-done.3.refs_4_), channel_id=1, source_target_pairs={{0,1},{2,0},{4,2},{6,4},{7,6},{5,7},{3,5},{1,3},{8,9},{10,8},{12,1... | collective-permute-start | bytes 688136 | tf_op jit(solution)/shard_map/ppermute | solution.py:375
  19.2 15.1 %collective-permute-start.7 = (f32[2016,128]{1,0:T(8,128)S(1)}, f32[2016,128]{1,0:T(8,128)S(1)}, u32[]{:S(2)}, u32[]{:S(2)}) collective-permute-start(f32[2016,128]{1,0:T(8,128)S(1)} %shard_map.62.refs_0_), channel_id=1, source_target_pairs={{0,8},{8,0},{16,24},{24,16},{1,9},{9,1},{17,25},{25,17},{2,10},{10... | collective-permute-start | bytes 3096584 | tf_op jit(solution)/shard_map/ppermute | solution.py:348
  23.2 6.3 %collective-permute-start.6 = (f32[224,256]{1,0:T(8,128)S(1)}, f32[224,256]{1,0:T(8,128)S(1)}, u32[]{:S(2)}, u32[]{:S(2)}) collective-permute-start(f32[224,256]{1,0:T(8,128)S(1)} %collective-permute-done.4.refs_5_), channel_id=1, source_target_pairs={{1,0},{0,2},{2,4},{4,6},{6,7},{7,5},{5,3},{3,1},{9,8},{8,10},{10,1... | collective-permute-start | bytes 688136 | tf_op jit(solution)/shard_map/ppermute | solution.py:379
  32.1 3.3 %collective-permute-start.9 = (f32[2016,128]{1,0:T(8,128)S(1)}, f32[2016,128]{1,0:T(8,128)S(1)}, u32[]{:S(2)}, u32[]{:S(2)}) collective-permute-start(f32[2016,128]{1,0:T(8,128)S(1)} %collective-permute-done.8.refs_1_), channel_id=1, source_target_pairs={{0,8},{8,0},{16,24},{24,16},{1,9},{9,1},{17,25},{25,17},{2,10},{10... | collective-permute-start | bytes 3096584 | tf_op jit(solution)/shard_map/ppermute | solution.py:348
  32.2 7.2 %collective-permute-start.13 = (f32[576,128]{1,0:T(8,128)S(1)}, f32[576,128]{1,0:T(8,128)S(1)}, u32[]{:S(2)}, u32[]{:S(2)}) collective-permute-start(f32[576,128]{1,0:T(8,128)S(1)} %get-tuple-element.51.refs_0_), channel_id=1, source_target_pairs={{0,8},{8,0},{16,24},{24,16},{1,9},{9,1},{17,25},{25,17},{2,10},{10... | collective-permute-start | bytes 884744 | tf_op jit(solution)/shard_map/ppermute | solution.py:348
  32.7 9.9 %collective-permute-start.14 = (f32[576,128]{1,0:T(8,128)S(1)}, f32[576,128]{1,0:T(8,128)S(1)}, u32[]{:S(2)}, u32[]{:S(2)}) collective-permute-start(f32[576,128]{1,0:T(8,128)S(1)} %get-tuple-element.51.refs_0_), channel_id=1, source_target_pairs={{0,16},{8,24},{16,0},{24,8},{1,17},{9,25},{17,1},{25,9},{2,18},{10... | collective-permute-start | bytes 884744 | tf_op jit(solution)/shard_map/ppermute | solution.py:356
  34.2 12.9 %collective-permute-start.15 = (f32[576,128]{1,0:T(8,128)S(1)}, f32[576,128]{1,0:T(8,128)S(1)}, u32[]{:S(2)}, u32[]{:S(2)}) collective-permute-start(f32[576,128]{1,0:T(8,128)S(1)} %get-tuple-element.51.refs_0_), channel_id=1, source_target_pairs={{0,24},{8,16},{16,8},{24,0},{1,25},{9,17},{17,9},{25,1},{2,26},{10... | collective-permute-start | bytes 884744 | tf_op jit(solution)/shard_map/ppermute | solution.py:356
  36.8 14.5 %collective-permute-start.16 = (f32[448,256]{1,0:T(8,128)S(1)}, f32[448,256]{1,0:T(8,128)S(1)}, u32[]{:S(2)}, u32[]{:S(2)}) collective-permute-start(f32[448,256]{1,0:T(8,128)S(1)} %get-tuple-element.53.refs_0_.mine_ref), channel_id=1, source_target_pairs={{0,1},{1,0},{2,3},{3,2},{4,5},{5,4},{6,7},{7,6},{8,9},{9,8},{10,11... | collective-permute-start | bytes 1376264 | tf_op jit(solution)/shard_map/ppermute | solution.py:348
  37.8 11.5 %collective-permute-start.10 = (f32[112,256]{1,0:T(8,128)S(1)}, f32[112,256]{1,0:T(8,128)S(1)}, u32[]{:S(2)}, u32[]{:S(2)}) collective-permute-start(f32[112,256]{1,0:T(8,128)S(1)} %get-tuple-element.46), channel_id=1, source_target_pairs={{0,2},{1,3},{2,0},{3,1},{4,6},{5,7},{6,4},{7,5},{8,10},{9,11},{10,... | collective-permute-start | bytes 344072 | tf_op jit(solution)/shard_map/ppermute | solution.py:470
  39.4 11.9 %collective-permute-start.11 = (f32[112,256]{1,0:T(8,128)S(1)}, f32[112,256]{1,0:T(8,128)S(1)}, u32[]{:S(2)}, u32[]{:S(2)}) collective-permute-start(f32[112,256]{1,0:T(8,128)S(1)} %get-tuple-element.47), channel_id=1, source_target_pairs={{0,4},{1,5},{2,6},{3,7},{4,0},{5,1},{6,2},{7,3},{8,12},{9,13},{10,... | collective-permute-start | bytes 344072 | tf_op jit(solution)/shard_map/ppermute | solution.py:470
  42.6 8.7 %collective-permute-start.12 = (f32[112,256]{1,0:T(8,128)S(1)}, f32[112,256]{1,0:T(8,128)S(1)}, u32[]{:S(2)}, u32[]{:S(2)}) collective-permute-start(f32[112,256]{1,0:T(8,128)S(1)} %get-tuple-element.48), channel_id=1, source_target_pairs={{0,6},{1,7},{2,4},{3,5},{4,2},{5,3},{6,0},{7,1},{8,14},{9,15},{10,... | collective-permute-start | bytes 344072 | tf_op jit(solution)/shard_map/ppermute | solution.py:470
  52.3 8.1 %collective-permute-start.18 = (f32[128,256]{1,0:T(8,128)S(1)}, f32[128,256]{1,0:T(8,128)S(1)}, u32[]{:S(2)}, u32[]{:S(2)}) collective-permute-start(f32[128,256]{1,0:T(8,128)S(1)} %get-tuple-element.63), channel_id=1, source_target_pairs={{0,6},{1,7},{2,4},{3,5},{4,2},{5,3},{6,0},{7,1},{8,14},{9,15},{10,... | collective-permute-start | bytes 393224 | tf_op jit(solution)/shard_map/ppermute | solution.py:470
  54.8 12.1 %collective-permute-start.19 = (f32[128,256]{1,0:T(8,128)S(1)}, f32[128,256]{1,0:T(8,128)S(1)}, u32[]{:S(2)}, u32[]{:S(2)}) collective-permute-start(f32[128,256]{1,0:T(8,128)S(1)} %get-tuple-element.64), channel_id=1, source_target_pairs={{0,4},{1,5},{2,6},{3,7},{4,0},{5,1},{6,2},{7,3},{8,12},{9,13},{10,... | collective-permute-start | bytes 393224 | tf_op jit(solution)/shard_map/ppermute | solution.py:470
  56.0 11.0 %collective-permute-start.17 = (f32[224,256]{1,0:T(8,128)S(1)}, f32[224,256]{1,0:T(8,128)S(1)}, u32[]{:S(2)}, u32[]{:S(2)}) collective-permute-start(f32[224,256]{1,0:T(8,128)S(1)} %get-tuple-element.62), channel_id=1, source_target_pairs={{0,1},{1,0},{2,3},{3,2},{4,5},{5,4},{6,7},{7,6},{8,9},{9,8},{10,11... | collective-permute-start | bytes 688136 | tf_op jit(solution)/shard_map/ppermute | solution.py:348
  57.1 9.9 %copy-start = (f32[128,256]{1,0:T(8,128)S(1)}, f32[128,256]{1,0:T(8,128)}, u32[]{:S(2)}) copy-start(f32[128,256]{1,0:T(8,128)} %d_ref.1) | copy-start | bytes 393220
  57.1 9.9 %collective-permute-start.20 = (f32[128,256]{1,0:T(8,128)S(1)}, f32[128,256]{1,0:T(8,128)S(1)}, u32[]{:S(2)}, u32[]{:S(2)}) collective-permute-start(f32[128,256]{1,0:T(8,128)S(1)} %get-tuple-element.65), channel_id=1, source_target_pairs={{0,2},{1,3},{2,0},{3,1},{4,6},{5,7},{6,4},{7,5},{8,10},{9,11},{10,... | collective-permute-start | bytes 393224 | tf_op jit(solution)/shard_map/ppermute | solution.py:470

commit v18 on v15

--- a/solution.py
+++ b/solution.py
@@ -41,8 +41,8 @@
 
 
 def pick_rows(place, v):
-    high, mid, low = split3(v)
-    return dot(place, high) + (dot(place, mid) + dot(place, low))
+    high, low = split(v)
+    return dot(place, high) + dot(place, low)
 
 
 def one_hot(mask):
@@ -153,7 +153,7 @@
         place_rows(us_ref, refs[0][...], ring_owners(nc, c)[-1])
     names = structure_ref[...].reshape(1, -1)
     w = own_ref.shape[1]
-    own_ref[...] = rows_of(us_ref, names, c // 2, width, [c & 1] if len(refs) > 2 else [0])[:, :w]
+    own_ref[...] = rows_of(us_ref, names, c // 2, width, [c & 1] if len(refs) > 2 else range(us_ref.shape[0]))[:BLOCK_CAP, :w]
 
 
 def row_order(names, c, rows, nc, slots, direct):
@@ -198,7 +198,7 @@
     slot = (2 * block + (turn & 1)) * slots + (index >> lg) - ahead + (half ^ x) * rows
     slot = jnp.where((named >= 2 * z * rows) & (named < (2 * z + 2) * rows), slot, -1)
     at = lax.broadcasted_iota(jnp.int32, (2 * rows, CAP), 0)
-    place_ref[...] = one_hot(at == slot).T.astype(BF16)
+    place_ref[...] = one_hot(at == slot).T.astype(BF16)[:BLOCK_CAP]
 
     own = lax.broadcasted_iota(jnp.int32, (m, n), 1) - nc * lax.broadcasted_iota(jnp.int32, (m, n), 0)
     mine = jnp.sum(jnp.where(own == c, names, 0).astype(jnp.float32), axis=1, keepdims=True)
@@ -416,7 +416,7 @@
     )
     to, place, source = call(
         functools.partial(order_kernel, direct, slots),
-        [bf16(nc * slots, rows), bf16(CAP, 2 * nc * slots), bf16(m, nc * slots)],
+        [bf16(nc * slots, rows), bf16(BLOCK_CAP, 2 * nc * slots), bf16(m, nc * slots)],
         names,
     )
     if direct:
@@ -429,7 +429,7 @@
     before = call(functools.partial(place_kernel, direct, nc), placed, *early, flops=8 * term)
     us, own = call(
         functools.partial(last_kernel, nc, cols),
-        [placed, f32(CAP, wd if direct else w)],
+        [placed, f32(BLOCK_CAP, wd if direct else w)],
         names,
         before,
         *late,
@@ -485,7 +485,7 @@
         [turned, turned],
         place,
         *owned,
-        scratch_shapes=[pltpu.VMEM((2 * nz * wd, CAP), BF16)],
+        scratch_shapes=[pltpu.VMEM((2 * nz * wd, BLOCK_CAP), BF16)],
         flops=8 * nz * wd * nc * slots * CAP,
     )
     parts = [f32(wd, w)] * nz if direct else [f32(nz, wd, w)]

time: 67.2 us -> 67.1 us (level)
  no operation moved by 1% of the time
where the time goes in v18:
time: 67.1 us; the launch traced here: 66.9 us
  starting transfers between devices  27.2 us (41%)
  waiting for transfers between devices  23.6 us (35%)
  Pallas kernels  14.7 us (22%)
  between operations  0.76 us (1%)
  local copies, waits for them, and re-layouts  0.7 us (1%)
    pallas_call x12, Pallas kernels, call(): pl.pallas_call(kernel, out_shape=out_shape, out_specs=[VMEM] * len(out_sh...  14.7 us
    ppermute x6, starting transfers between devices, per_device(): lax.ppermute(v, 'pcol', [(k, k ^ 2 * t) for k in range(nc)])  12.3 us
    ppermute x4, waiting for transfers between devices, ring_gather(): lax.ppermute(up, 'pcol', pairs)  10.6 us
    ppermute x6, waiting for transfers between devices, per_device(): lax.ppermute(v, 'pcol', [(k, k ^ 2 * t) for k in range(nc)])  10.1 us
    ppermute x4, starting transfers between devices, ring_gather(): lax.ppermute(up, 'pcol', pairs)  7.81 us
    ppermute x5, starting transfers between devices, swap(): return lax.ppermute(v, axis, [(k, k ^ 1) for k in range(size)])  2.66 us
    ppermute x1, starting transfers between devices, per_device(): lax.ppermute(chosen, 'prow', [(k, (k + 2 * t) % nr) for k in range(nr)])  2.03 us
    ppermute x3, waiting for transfers between devices, ring_gather(): lax.ppermute(down, 'pcol', back)  1.55 us
  transfers between devices with their start and end apart: 21, of which 10 were waited for; matrix products, arithmetic and copies ran while one was open for 0% of the time, Pallas kernels for 19%

profile of v18, /device:TPU:0, one launch (start us, length us, event | category | flops | bytes accessed | tf_op | source)
XLA Modules:
  0.0 66.9 jit_solution(125346723141523164)
XLA Ops:
  0.6 3.1 %collective-permute-start = (f32[224,256]{1,0:T(8,128)}, f32[224,256]{1,0:T(8,128)S(1)}, u32[]{:S(2)}, u32[]{:S(2)}) collective-permute-start(f32[224,256]{1,0:T(8,128)} %refs_0_.1), channel_id=1, source_target_pairs={{1,0},{0,2},{2,4},{4,6},{6,7},{7,5},{5,3},{3,1},{9,8},{8,10},{10,1... | collective-permute-start | bytes 688136 | tf_op jit(solution)/shard_map/ppermute | solution.py:375
  4.4 2.7 %shard_map.62.refs_0_ = f32[2016,128]{1,0:T(8,128)S(1)} custom-call(s32[1792]{0:T(1024)S(1)} %copy-done.1, f32[448,896]{1,0:T(8,128)} %sigma_ref.1), custom_call_target="tpu_custom_call" | custom-call | flops 1027604480 | bytes 2644992 | tf_op jit(solution)/shard_map/pallas_call | solution.py:337
  7.1 2.0 %collective-permute-start.8 = (f32[2016,128]{1,0:T(8,128)S(1)}, f32[2016,128]{1,0:T(8,128)S(1)}, u32[]{:S(2)}, u32[]{:S(2)}) collective-permute-start(f32[2016,128]{1,0:T(8,128)S(1)} %shard_map.62.refs_0_), channel_id=1, source_target_pairs={{0,16},{8,24},{16,0},{24,8},{1,17},{9,25},{17,1},{25,9},{2,18},{10... | collective-permute-start | bytes 3096584 | tf_op jit(solution)/shard_map/ppermute | solution.py:451
  9.4 1.5 %collective-permute-done.1.refs_2_ = f32[224,256]{1,0:T(8,128)S(1)} collective-permute-done((f32[224,256]{1,0:T(8,128)}, f32[224,256]{1,0:T(8,128)S(1)}, u32[]{:S(2)}, u32[]{:S(2)}) %collective-permute-start.1) | collective-permute-done | bytes 229408 | tf_op jit(solution)/shard_map/ppermute | solution.py:375
  11.0 1.6 %collective-permute-start.2 = (f32[224,256]{1,0:T(8,128)S(1)}, f32[224,256]{1,0:T(8,128)S(1)}, u32[]{:S(2)}, u32[]{:S(2)}) collective-permute-start(f32[224,256]{1,0:T(8,128)S(1)} %collective-permute-done.refs_1_), channel_id=1, source_target_pairs={{1,0},{0,2},{2,4},{4,6},{6,7},{7,5},{5,3},{3,1},{9,8},{8,10},{10,1... | collective-permute-start | bytes 688136 | tf_op jit(solution)/shard_map/ppermute | solution.py:375
  13.0 4.1 %collective-permute-done.2.refs_3_ = f32[224,256]{1,0:T(8,128)S(1)} collective-permute-done((f32[224,256]{1,0:T(8,128)S(1)}, f32[224,256]{1,0:T(8,128)S(1)}, u32[]{:S(2)}, u32[]{:S(2)}) %collective-permute-start.2) | collective-permute-done | bytes 229408 | tf_op jit(solution)/shard_map/ppermute | solution.py:375
  17.1 1.6 %collective-permute-start.4 = (f32[224,256]{1,0:T(8,128)S(1)}, f32[224,256]{1,0:T(8,128)S(1)}, u32[]{:S(2)}, u32[]{:S(2)}) collective-permute-start(f32[224,256]{1,0:T(8,128)S(1)} %collective-permute-done.2.refs_3_), channel_id=1, source_target_pairs={{1,0},{0,2},{2,4},{4,6},{6,7},{7,5},{5,3},{3,1},{9,8},{8,10},{10,1... | collective-permute-start | bytes 688136 | tf_op jit(solution)/shard_map/ppermute | solution.py:375
  19.2 2.1 %shard_map.59 = (bf16[448,448]{1,0:T(8,128)(2,1)S(1)}, bf16[560,896]{1,0:T(8,128)(2,1)S(1)}, bf16[224,448]{1,0:T(8,128)(2,1)S(1)}) custom-call(s32[1792]{0:T(1024)S(1)} %copy-done.1), custom_call_target="tpu_custom_call" | custom-call | tf_op jit(solution)/shard_map/pallas_call | solution.py:337
  21.2 1.9 %collective-permute-done.4.refs_5_ = f32[224,256]{1,0:T(8,128)S(1)} collective-permute-done((f32[224,256]{1,0:T(8,128)S(1)}, f32[224,256]{1,0:T(8,128)S(1)}, u32[]{:S(2)}, u32[]{:S(2)}) %collective-permute-start.4) | collective-permute-done | bytes 229408 | tf_op jit(solution)/shard_map/ppermute | solution.py:375
  23.2 1.6 %collective-permute-start.6 = (f32[224,256]{1,0:T(8,128)S(1)}, f32[224,256]{1,0:T(8,128)S(1)}, u32[]{:S(2)}, u32[]{:S(2)}) collective-permute-start(f32[224,256]{1,0:T(8,128)S(1)} %collective-permute-done.4.refs_5_), channel_id=1, source_target_pairs={{1,0},{0,2},{2,4},{4,6},{6,7},{7,5},{5,3},{3,1},{9,8},{8,10},{10,1... | collective-permute-start | bytes 688136 | tf_op jit(solution)/shard_map/ppermute | solution.py:379
  25.2 4.2 %collective-permute-done.6.refs_0_ = f32[224,256]{1,0:T(8,128)S(1)} collective-permute-done((f32[224,256]{1,0:T(8,128)S(1)}, f32[224,256]{1,0:T(8,128)S(1)}, u32[]{:S(2)}, u32[]{:S(2)}) %collective-permute-start.6) | collective-permute-done | bytes 229408 | tf_op jit(solution)/shard_map/ppermute | solution.py:379
  30.0 2.1 %shard_map.63 = (f32[448,256]{1,0:T(8,128)S(1)}, bf16[3,640,256]{2,1,0:T(8,128)(2,1)S(1)}, bf16[3,640,256]{2,1,0:T(8,128)(2,1)S(1)}) custom-call(s32[1792]{0:T(1024)S(1)} %copy-done.1, f32[2,2376,128]{2,1,0:T(8,128)S(1)} %get-tuple-element.39.us_ref, f32[2016,128]{1,0:T(8,128)S(1)} %shard_map.62.refs_0_), custom_call_target="tpu_custom_call" | custom-call | tf_op jit(solution)/shard_map/pallas_call | solution.py:337
  32.7 1.5 %collective-permute-start.14 = (f32[560,128]{1,0:T(8,128)S(1)}, f32[560,128]{1,0:T(8,128)S(1)}, u32[]{:S(2)}, u32[]{:S(2)}) collective-permute-start(f32[560,128]{1,0:T(8,128)S(1)} %get-tuple-element.51.refs_0_), channel_id=1, source_target_pairs={{0,16},{8,24},{16,0},{24,8},{1,17},{9,25},{17,1},{25,9},{2,18},{10... | collective-permute-start | bytes 860168 | tf_op jit(solution)/shard_map/ppermute | solution.py:356
  34.2 1.1 %shard_map.64.part_ref = f32[448,256]{1,0:T(8,128)S(1)} custom-call(bf16[3,640,256]{2,1,0:T(8,128)(2,1)S(1)} %get-tuple-element.40.uh_ref, bf16[3,640,256]{2,1,0:T(8,128)(2,1)S(1)} %get-tuple-element.41.ul_ref, f32[448,256]{1,0:T(8,128)S(1)} %get-tuple-element.42.part_ref, f32[2016,128]{1,0:T(8,128)S(1)} %collective-permute-done.7.refs_0_, ...), custom_call_target="tpu_custom_call" | custom-call | flops 440401920 | bytes 4947968 | tf_op jit(solution)/shard_map/pallas_call | solution.py:337
  35.4 1.4 %shard_map.65 = (f32[448,256]{1,0:T(8,128)S(1)}, f32[112,256]{1,0:T(8,128)S(1)}, f32[112,256]{1,0:T(8,128)S(1)}, f32[112,256]{1,0:T(8,128)S(1)}) custom-call(bf16[3,640,256]{2,1,0:T(8,128)(2,1)S(1)} %get-tuple-element.40.uh_ref, bf16[3,640,256]{2,1,0:T(8,128)(2,1)S(1)} %get-tuple-element.41.ul_ref, f32[448,256]{1,0:T(8,128)S(1)} %shard_map.64.part_ref, ...), custom_call_target="tpu_custom_call" | custom-call | flops 440401920 | bytes 4661248 | tf_op jit(solution)/shard_map/pallas_call | solution.py:337
  37.8 1.6 %collective-permute-start.10 = (f32[112,256]{1,0:T(8,128)S(1)}, f32[112,256]{1,0:T(8,128)S(1)}, u32[]{:S(2)}, u32[]{:S(2)}) collective-permute-start(f32[112,256]{1,0:T(8,128)S(1)} %get-tuple-element.46), channel_id=1, source_target_pairs={{0,2},{1,3},{2,0},{3,1},{4,6},{5,7},{6,4},{7,5},{8,10},{9,11},{10,... | collective-permute-start | bytes 344072 | tf_op jit(solution)/shard_map/ppermute | solution.py:470
  39.4 2.6 %collective-permute-start.11 = (f32[112,256]{1,0:T(8,128)S(1)}, f32[112,256]{1,0:T(8,128)S(1)}, u32[]{:S(2)}, u32[]{:S(2)}) collective-permute-start(f32[112,256]{1,0:T(8,128)S(1)} %get-tuple-element.47), channel_id=1, source_target_pairs={{0,4},{1,5},{2,6},{3,7},{4,0},{5,1},{6,2},{7,3},{8,12},{9,13},{10,... | collective-permute-start | bytes 344072 | tf_op jit(solution)/shard_map/ppermute | solution.py:470
  42.4 3.5 %collective-permute-start.12 = (f32[112,256]{1,0:T(8,128)S(1)}, f32[112,256]{1,0:T(8,128)S(1)}, u32[]{:S(2)}, u32[]{:S(2)}) collective-permute-start(f32[112,256]{1,0:T(8,128)S(1)} %get-tuple-element.48), channel_id=1, source_target_pairs={{0,6},{1,7},{2,4},{3,5},{4,2},{5,3},{6,0},{7,1},{8,14},{9,15},{10,... | collective-permute-start | bytes 344072 | tf_op jit(solution)/shard_map/ppermute | solution.py:470
  46.8 2.2 %shard_map.66 = (bf16[4,128,896]{2,1,0:T(8,128)(2,1)S(1)}, bf16[4,128,896]{2,1,0:T(8,128)(2,1)S(1)}) custom-call(bf16[560,896]{1,0:T(8,128)(2,1)S(1)} %get-tuple-element.49.place_ref, f32[560,128]{1,0:T(8,128)S(1)} %get-tuple-element.51.refs_0_, f32[560,128]{1,0:T(8,128)S(1)} %collective-permute-done.13.refs_1_, ...), custom_call_target="tpu_custom_call" | custom-call | flops 1056964608 | bytes 3985408 | tf_op jit(solution)/shard_map/pallas_call | solution.py:337
  49.0 2.3 %collective-permute-done.11.refs_2_ = f32[112,256]{1,0:T(8,128)S(1)} collective-permute-done((f32[112,256]{1,0:T(8,128)S(1)}, f32[112,256]{1,0:T(8,128)S(1)}, u32[]{:S(2)}, u32[]{:S(2)}) %collective-permute-start.11) | collective-permute-done | bytes 114720 | tf_op jit(solution)/shard_map/ppermute | solution.py:470
  52.3 3.2 %collective-permute-start.18 = (f32[128,256]{1,0:T(8,128)S(1)}, f32[128,256]{1,0:T(8,128)S(1)}, u32[]{:S(2)}, u32[]{:S(2)}) collective-permute-start(f32[128,256]{1,0:T(8,128)S(1)} %get-tuple-element.63), channel_id=1, source_target_pairs={{0,4},{1,5},{2,6},{3,7},{4,0},{5,1},{6,2},{7,3},{8,12},{9,13},{10,... | collective-permute-start | bytes 393224 | tf_op jit(solution)/shard_map/ppermute | solution.py:470
  55.5 1.4 %collective-permute-start.19 = (f32[128,256]{1,0:T(8,128)S(1)}, f32[128,256]{1,0:T(8,128)S(1)}, u32[]{:S(2)}, u32[]{:S(2)}) collective-permute-start(f32[128,256]{1,0:T(8,128)S(1)} %get-tuple-element.64), channel_id=1, source_target_pairs={{0,6},{1,7},{2,4},{3,5},{4,2},{5,3},{6,0},{7,1},{8,14},{9,15},{10,... | collective-permute-start | bytes 393224 | tf_op jit(solution)/shard_map/ppermute | solution.py:470
  56.9 1.1 %collective-permute-start.17 = (f32[224,256]{1,0:T(8,128)S(1)}, f32[224,256]{1,0:T(8,128)S(1)}, u32[]{:S(2)}, u32[]{:S(2)}) collective-permute-start(f32[224,256]{1,0:T(8,128)S(1)} %get-tuple-element.62), channel_id=1, source_target_pairs={{0,1},{1,0},{2,3},{3,2},{4,5},{5,4},{6,7},{7,6},{8,9},{9,8},{10,11... | collective-permute-start | bytes 688136 | tf_op jit(solution)/shard_map/ppermute | solution.py:348
  58.0 7.3 %collective-permute-done.18.refs_1_ = f32[128,256]{1,0:T(8,128)S(1)} collective-permute-done((f32[128,256]{1,0:T(8,128)S(1)}, f32[128,256]{1,0:T(8,128)S(1)}, u32[]{:S(2)}, u32[]{:S(2)}) %collective-permute-start.18) | collective-permute-done | bytes 131104 | tf_op jit(solution)/shard_map/ppermute | solution.py:470
  (36 shorter events, 8.3 us)
Async XLA Ops:
  0.6 8.8 %collective-permute-start = (f32[224,256]{1,0:T(8,128)}, f32[224,256]{1,0:T(8,128)S(1)}, u32[]{:S(2)}, u32[]{:S(2)}) collective-permute-start(f32[224,256]{1,0:T(8,128)} %refs_0_.1), channel_id=1, source_target_pairs={{1,0},{0,2},{2,4},{4,6},{6,7},{7,5},{5,3},{3,1},{9,8},{8,10},{10,1... | collective-permute-start | bytes 688136 | tf_op jit(solution)/shard_map/ppermute | solution.py:375
  3.7 7.3 %collective-permute-start.1 = (f32[224,256]{1,0:T(8,128)}, f32[224,256]{1,0:T(8,128)S(1)}, u32[]{:S(2)}, u32[]{:S(2)}) collective-permute-start(f32[224,256]{1,0:T(8,128)} %refs_0_.1), channel_id=1, source_target_pairs={{0,1},{2,0},{4,2},{6,4},{7,6},{5,7},{3,5},{1,3},{8,9},{10,8},{12,1... | collective-permute-start | bytes 688136 | tf_op jit(solution)/shard_map/ppermute | solution.py:375
  3.7 0.7 %copy-start.1 = (s32[1792]{0:T(1024)S(1)}, s32[1792]{0:T(1024)}, u32[]{:S(2)}) copy-start(s32[1792]{0:T(1024)} %structure_ref.7) | copy-start | bytes 21508
  4.4 20.3 %copy-start.2 = (f32[224,256]{1,0:T(8,128)S(1)}, f32[224,256]{1,0:T(8,128)}, u32[]{:S(2)}) copy-start(f32[224,256]{1,0:T(8,128)} %refs_0_.1) | copy-start | bytes 688132
  7.1 25.0 %collective-permute-start.8 = (f32[2016,128]{1,0:T(8,128)S(1)}, f32[2016,128]{1,0:T(8,128)S(1)}, u32[]{:S(2)}, u32[]{:S(2)}) collective-permute-start(f32[2016,128]{1,0:T(8,128)S(1)} %shard_map.62.refs_0_), channel_id=1, source_target_pairs={{0,16},{8,24},{16,0},{24,8},{1,17},{9,25},{17,1},{25,9},{2,18},{10... | collective-permute-start | bytes 3096584 | tf_op jit(solution)/shard_map/ppermute | solution.py:451
  11.0 6.2 %collective-permute-start.2 = (f32[224,256]{1,0:T(8,128)S(1)}, f32[224,256]{1,0:T(8,128)S(1)}, u32[]{:S(2)}, u32[]{:S(2)}) collective-permute-start(f32[224,256]{1,0:T(8,128)S(1)} %collective-permute-done.refs_1_), channel_id=1, source_target_pairs={{1,0},{0,2},{2,4},{4,6},{6,7},{7,5},{5,3},{3,1},{9,8},{8,10},{10,1... | collective-permute-start | bytes 688136 | tf_op jit(solution)/shard_map/ppermute | solution.py:375
  12.6 6.2 %collective-permute-start.3 = (f32[224,256]{1,0:T(8,128)S(1)}, f32[224,256]{1,0:T(8,128)S(1)}, u32[]{:S(2)}, u32[]{:S(2)}) collective-permute-start(f32[224,256]{1,0:T(8,128)S(1)} %collective-permute-done.1.refs_2_), channel_id=1, source_target_pairs={{0,1},{2,0},{4,2},{6,4},{7,6},{5,7},{3,5},{1,3},{8,9},{10,8},{12,1... | collective-permute-start | bytes 688136 | tf_op jit(solution)/shard_map/ppermute | solution.py:375
  17.1 6.0 %collective-permute-start.4 = (f32[224,256]{1,0:T(8,128)S(1)}, f32[224,256]{1,0:T(8,128)S(1)}, u32[]{:S(2)}, u32[]{:S(2)}) collective-permute-start(f32[224,256]{1,0:T(8,128)S(1)} %collective-permute-done.2.refs_3_), channel_id=1, source_target_pairs={{1,0},{0,2},{2,4},{4,6},{6,7},{7,5},{5,3},{3,1},{9,8},{8,10},{10,1... | collective-permute-start | bytes 688136 | tf_op jit(solution)/shard_map/ppermute | solution.py:375
  18.7 6.0 %collective-permute-start.5 = (f32[224,256]{1,0:T(8,128)S(1)}, f32[224,256]{1,0:T(8,128)S(1)}, u32[]{:S(2)}, u32[]{:S(2)}) collective-permute-start(f32[224,256]{1,0:T(8,128)S(1)} %collective-permute-done.3.refs_4_), channel_id=1, source_target_pairs={{0,1},{2,0},{4,2},{6,4},{7,6},{5,7},{3,5},{1,3},{8,9},{10,8},{12,1... | collective-permute-start | bytes 688136 | tf_op jit(solution)/shard_map/ppermute | solution.py:375
  19.2 15.1 %collective-permute-start.7 = (f32[2016,128]{1,0:T(8,128)S(1)}, f32[2016,128]{1,0:T(8,128)S(1)}, u32[]{:S(2)}, u32[]{:S(2)}) collective-permute-start(f32[2016,128]{1,0:T(8,128)S(1)} %shard_map.62.refs_0_), channel_id=1, source_target_pairs={{0,8},{8,0},{16,24},{24,16},{1,9},{9,1},{17,25},{25,17},{2,10},{10... | collective-permute-start | bytes 3096584 | tf_op jit(solution)/shard_map/ppermute | solution.py:348
  23.2 6.3 %collective-permute-start.6 = (f32[224,256]{1,0:T(8,128)S(1)}, f32[224,256]{1,0:T(8,128)S(1)}, u32[]{:S(2)}, u32[]{:S(2)}) collective-permute-start(f32[224,256]{1,0:T(8,128)S(1)} %collective-permute-done.4.refs_5_), channel_id=1, source_target_pairs={{1,0},{0,2},{2,4},{4,6},{6,7},{7,5},{5,3},{3,1},{9,8},{8,10},{10,1... | collective-permute-start | bytes 688136 | tf_op jit(solution)/shard_map/ppermute | solution.py:379
  32.1 3.3 %collective-permute-start.9 = (f32[2016,128]{1,0:T(8,128)S(1)}, f32[2016,128]{1,0:T(8,128)S(1)}, u32[]{:S(2)}, u32[]{:S(2)}) collective-permute-start(f32[2016,128]{1,0:T(8,128)S(1)} %collective-permute-done.8.refs_1_), channel_id=1, source_target_pairs={{0,8},{8,0},{16,24},{24,16},{1,9},{9,1},{17,25},{25,17},{2,10},{10... | collective-permute-start | bytes 3096584 | tf_op jit(solution)/shard_map/ppermute | solution.py:348
  32.2 7.2 %collective-permute-start.13 = (f32[560,128]{1,0:T(8,128)S(1)}, f32[560,128]{1,0:T(8,128)S(1)}, u32[]{:S(2)}, u32[]{:S(2)}) collective-permute-start(f32[560,128]{1,0:T(8,128)S(1)} %get-tuple-element.51.refs_0_), channel_id=1, source_target_pairs={{0,8},{8,0},{16,24},{24,16},{1,9},{9,1},{17,25},{25,17},{2,10},{10... | collective-permute-start | bytes 860168 | tf_op jit(solution)/shard_map/ppermute | solution.py:348
  32.7 9.7 %collective-permute-start.14 = (f32[560,128]{1,0:T(8,128)S(1)}, f32[560,128]{1,0:T(8,128)S(1)}, u32[]{:S(2)}, u32[]{:S(2)}) collective-permute-start(f32[560,128]{1,0:T(8,128)S(1)} %get-tuple-element.51.refs_0_), channel_id=1, source_target_pairs={{0,16},{8,24},{16,0},{24,8},{1,17},{9,25},{17,1},{25,9},{2,18},{10... | collective-permute-start | bytes 860168 | tf_op jit(solution)/shard_map/ppermute | solution.py:356
  34.2 12.6 %collective-permute-start.15 = (f32[560,128]{1,0:T(8,128)S(1)}, f32[560,128]{1,0:T(8,128)S(1)}, u32[]{:S(2)}, u32[]{:S(2)}) collective-permute-start(f32[560,128]{1,0:T(8,128)S(1)} %get-tuple-element.51.refs_0_), channel_id=1, source_target_pairs={{0,24},{8,16},{16,8},{24,0},{1,25},{9,17},{17,9},{25,1},{2,26},{10... | collective-permute-start | bytes 860168 | tf_op jit(solution)/shard_map/ppermute | solution.py:356
  36.8 14.5 %collective-permute-start.16 = (f32[448,256]{1,0:T(8,128)S(1)}, f32[448,256]{1,0:T(8,128)S(1)}, u32[]{:S(2)}, u32[]{:S(2)}) collective-permute-start(f32[448,256]{1,0:T(8,128)S(1)} %get-tuple-element.53.refs_0_.mine_ref), channel_id=1, source_target_pairs={{0,1},{1,0},{2,3},{3,2},{4,5},{5,4},{6,7},{7,6},{8,9},{9,8},{10,11... | collective-permute-start | bytes 1376264 | tf_op jit(solution)/shard_map/ppermute | solution.py:348
  37.8 11.2 %collective-permute-start.10 = (f32[112,256]{1,0:T(8,128)S(1)}, f32[112,256]{1,0:T(8,128)S(1)}, u32[]{:S(2)}, u32[]{:S(2)}) collective-permute-start(f32[112,256]{1,0:T(8,128)S(1)} %get-tuple-element.46), channel_id=1, source_target_pairs={{0,2},{1,3},{2,0},{3,1},{4,6},{5,7},{6,4},{7,5},{8,10},{9,11},{10,... | collective-permute-start | bytes 344072 | tf_op jit(solution)/shard_map/ppermute | solution.py:470
  39.4 11.9 %collective-permute-start.11 = (f32[112,256]{1,0:T(8,128)S(1)}, f32[112,256]{1,0:T(8,128)S(1)}, u32[]{:S(2)}, u32[]{:S(2)}) collective-permute-start(f32[112,256]{1,0:T(8,128)S(1)} %get-tuple-element.47), channel_id=1, source_target_pairs={{0,4},{1,5},{2,6},{3,7},{4,0},{5,1},{6,2},{7,3},{8,12},{9,13},{10,... | collective-permute-start | bytes 344072 | tf_op jit(solution)/shard_map/ppermute | solution.py:470
  42.4 8.8 %collective-permute-start.12 = (f32[112,256]{1,0:T(8,128)S(1)}, f32[112,256]{1,0:T(8,128)S(1)}, u32[]{:S(2)}, u32[]{:S(2)}) collective-permute-start(f32[112,256]{1,0:T(8,128)S(1)} %get-tuple-element.48), channel_id=1, source_target_pairs={{0,6},{1,7},{2,4},{3,5},{4,2},{5,3},{6,0},{7,1},{8,14},{9,15},{10,... | collective-permute-start | bytes 344072 | tf_op jit(solution)/shard_map/ppermute | solution.py:470
  52.3 13.0 %collective-permute-start.18 = (f32[128,256]{1,0:T(8,128)S(1)}, f32[128,256]{1,0:T(8,128)S(1)}, u32[]{:S(2)}, u32[]{:S(2)}) collective-permute-start(f32[128,256]{1,0:T(8,128)S(1)} %get-tuple-element.63), channel_id=1, source_target_pairs={{0,4},{1,5},{2,6},{3,7},{4,0},{5,1},{6,2},{7,3},{8,12},{9,13},{10,... | collective-permute-start | bytes 393224 | tf_op jit(solution)/shard_map/ppermute | solution.py:470
  55.5 9.8 %collective-permute-start.19 = (f32[128,256]{1,0:T(8,128)S(1)}, f32[128,256]{1,0:T(8,128)S(1)}, u32[]{:S(2)}, u32[]{:S(2)}) collective-permute-start(f32[128,256]{1,0:T(8,128)S(1)} %get-tuple-element.64), channel_id=1, source_target_pairs={{0,6},{1,7},{2,4},{3,5},{4,2},{5,3},{6,0},{7,1},{8,14},{9,15},{10,... | collective-permute-start | bytes 393224 | tf_op jit(solution)/shard_map/ppermute | solution.py:470
  56.9 9.0 %collective-permute-start.17 = (f32[224,256]{1,0:T(8,128)S(1)}, f32[224,256]{1,0:T(8,128)S(1)}, u32[]{:S(2)}, u32[]{:S(2)}) collective-permute-start(f32[224,256]{1,0:T(8,128)S(1)} %get-tuple-element.62), channel_id=1, source_target_pairs={{0,1},{1,0},{2,3},{3,2},{4,5},{5,4},{6,7},{7,6},{8,9},{9,8},{10,11... | collective-permute-start | bytes 688136 | tf_op jit(solution)/shard_map/ppermute | solution.py:348
  58.0 7.9 %copy-start = (f32[128,256]{1,0:T(8,128)S(1)}, f32[128,256]{1,0:T(8,128)}, u32[]{:S(2)}) copy-start(f32[128,256]{1,0:T(8,128)} %d_ref.1) | copy-start | bytes 393220
  58.0 7.9 %collective-permute-start.20 = (f32[128,256]{1,0:T(8,128)S(1)}, f32[128,256]{1,0:T(8,128)S(1)}, u32[]{:S(2)}, u32[]{:S(2)}) collective-permute-start(f32[128,256]{1,0:T(8,128)S(1)} %get-tuple-element.65), channel_id=1, source_target_pairs={{0,2},{1,3},{2,0},{3,1},{4,6},{5,7},{6,4},{7,5},{8,10},{9,11},{10,... | collective-permute-start | bytes 393224 | tf_op jit(solution)/shard_map/ppermute | solution.py:470
